TPU v7x, 32 devices: a whole 2x2x4 slice. The times are simulated.
32 devices in a mesh: replica: 4 (over y, core), shard: 8 (over z, x).
Axes of the slice: x: 2, y: 2, z: 4, core: 2. Of those that a mesh axis runs over, the one named last changes fastest.
Arguments:
- images: bfloat16 [256, 197, 768], P(('replica', 'shard')), may hold values from -6 to 6
- image_adapter_index: int32 [256], P(('replica', 'shard')), may hold values from 0 to 7
- device_image_count: int32 [32], P(('replica', 'shard')), may hold values from 1 to 8, as said below
- cotangent: bfloat16 [256, 197, 768], P(('replica', 'shard')), may hold values from -6 to 6
- query_key_value_weight: bfloat16 [768, 2304], P('shard'), may hold values from -0.21875 to 0.21875
- frozen_output_weight: bfloat16 [768, 768], P('shard'), may hold values from -0.875 to 0.875
- frozen_dispatch_weight: bfloat16 [768, 16], P('shard'), may hold values from -0.109375 to 0.109375
- query_key_value_first: bfloat16 [768, 128], P('shard'), may hold values from -0.21875 to 0.21875
- query_key_value_second: bfloat16 [128, 2304], P(None, 'shard'), may hold values from -0.75 to 0.75
- output_adapter_first: bfloat16 [768, 128], P('shard'), may hold values from -0.875 to 0.875
- output_adapter_second: bfloat16 [128, 768], P(None, 'shard'), may hold values from -0.75 to 0.75
- dispatch_adapter_first: bfloat16 [768, 128], P('shard'), may hold values from -0.21875 to 0.21875
- dispatch_adapter_second: bfloat16 [128, 16], P(None, 'shard'), may hold values from -0.375 to 0.375
- frozen_up_weight: bfloat16 [16, 768, 3072], P('shard'), may hold values from -2.5 to 2.5
- frozen_down_weight: bfloat16 [16, 3072, 768], P('shard'), may hold values from -0.875 to 0.875
- up_adapter_first: bfloat16 [16, 768, 128], P('shard'), may hold values from -2.5 to 2.5
- up_adapter_second: bfloat16 [16, 128, 3072], P('shard'), may hold values from -0.75 to 0.75
- down_adapter_first: bfloat16 [16, 3072, 128], P('shard'), may hold values from -0.109375 to 0.109375
- down_adapter_second: bfloat16 [16, 128, 768], P('shard'), may hold values from -4 to 4
Outputs:
- block_out: bfloat16 [256, 197, 768], P(('replica', 'shard'))
- input_grad: float32 [256, 197, 768], P(('replica', 'shard'))
- grad_qkv_a: float32 [768, 128], P('shard')
- grad_qkv_b: float32 [128, 2304], P(None, 'shard')
- grad_out_a: float32 [768, 128], P('shard')
- grad_out_b: float32 [128, 768], P(None, 'shard')
- grad_route_a: float32 [768, 128], P('shard')
- grad_route_b: float32 [128, 16], P(None, 'shard')
- grad_up_a: float32 [16, 768, 128], P('shard')
- grad_up_b: float32 [16, 128, 3072], P('shard')
- grad_down_a: float32 [16, 3072, 128], P('shard')
- grad_down_b: float32 [16, 128, 768], P('shard')
Inputs may be any that keep to these rules, and one draw needn't show every extreme that they name: `device_image_count`: each device's live images are its first slots; some device holds 8 live images.
All inputs are finite; a program needn't handle non-finite values.
Results may differ from a plain program's by a relative error of at most 0.025.
Values may be sent and summed in bfloat16 or wider, within the bound.
No kernel may reach another device: no remote copies, remote signals or barrier semaphores. Data moves between devices by JAX's collectives and lax.ppermute only.
A program may use at most 256 MiB of HBM per device.

v0:
```python
import jax
import jax.numpy as jnp
from jax import lax
from jax.sharding import PartitionSpec as P

HEADS = 12
RANK = 16


def layer_norm(inputs):
    centre = inputs - jnp.mean(inputs, axis=-1, keepdims=True)
    spread = jnp.mean(centre * centre, axis=-1, keepdims=True)
    return centre * lax.rsqrt(spread + 1e-06)


def norm_back(inputs, upstream):
    return jax.vjp(layer_norm, inputs)[1](upstream)[0]


def softmax_along(inputs, axis):
    shifted = inputs - jnp.max(inputs, axis=axis, keepdims=True)
    powers = jnp.exp(shifted)
    return powers / jnp.sum(powers, axis=axis, keepdims=True)


def project(left, right):
    return jnp.einsum("btd,dk->btk", left, right, preferred_element_type=jnp.float32)


def project_back(left, right):
    return jnp.einsum("btk,dk->btd", left, right, preferred_element_type=jnp.float32)


def outer_sum(left, right):
    return jnp.einsum("btd,btk->dk", left, right, preferred_element_type=jnp.float32)


def per_device(
    images,
    image_adapter_index,
    device_image_count,
    cotangent,
    query_key_value_weight,
    frozen_output_weight,
    frozen_dispatch_weight,
    query_key_value_first,
    query_key_value_second,
    output_adapter_first,
    output_adapter_second,
    dispatch_adapter_first,
    dispatch_adapter_second,
    frozen_up_weight,
    frozen_down_weight,
    up_adapter_first,
    up_adapter_second,
    down_adapter_first,
    down_adapter_second,
):
    n_img, n_tok, width = images.shape
    every_rank_lane = query_key_value_first.shape[1]
    head_dim = width // HEADS
    shared = (
        query_key_value_weight,
        frozen_output_weight,
        frozen_dispatch_weight,
        query_key_value_first,
        output_adapter_first,
        dispatch_adapter_first,
        query_key_value_second,
        output_adapter_second,
        dispatch_adapter_second,
    )
    gathered = (
        lax.all_gather(shared[0], "shard", axis=0, tiled=True),
        lax.all_gather(shared[1], "shard", axis=0, tiled=True),
        lax.all_gather(shared[2], "shard", axis=0, tiled=True),
        lax.all_gather(shared[3], "shard", axis=0, tiled=True),
        lax.all_gather(shared[4], "shard", axis=0, tiled=True),
        lax.all_gather(shared[5], "shard", axis=0, tiled=True),
        lax.all_gather(shared[6], "shard", axis=1, tiled=True),
        lax.all_gather(shared[7], "shard", axis=1, tiled=True),
        lax.all_gather(shared[8], "shard", axis=1, tiled=True),
    )
    (
        full_qkv,
        full_out,
        full_route,
        full_qkv_a,
        full_out_a,
        full_route_a,
        full_qkv_b,
        full_out_b,
        full_route_b,
    ) = gathered
    n_experts = full_route.shape[1]
    lane_group = lax.broadcasted_iota(jnp.int32, (n_img, every_rank_lane), 1) // RANK
    selector = (image_adapter_index[:, None] == lane_group).astype(jnp.bfloat16)[:, None, :]
    selector_f = selector.astype(jnp.float32)
    living = (lax.iota(jnp.int32, n_img) < device_image_count[0]).astype(jnp.float32)[:, None, None]
    inputs_f = images.astype(jnp.float32)
    normed = layer_norm(inputs_f).astype(jnp.bfloat16)
    low_qkv = project(normed, full_qkv_a).astype(jnp.bfloat16) * selector
    joined = (project(normed, full_qkv) + project(low_qkv, full_qkv_b)).astype(jnp.bfloat16)
    query_h = joined[:, :, :width].reshape(n_img, n_tok, HEADS, head_dim)
    key_h = joined[:, :, width : 2 * width].reshape(n_img, n_tok, HEADS, head_dim)
    value_h = joined[:, :, 2 * width :].reshape(n_img, n_tok, HEADS, head_dim)
    scores = (
        jnp.einsum("bthd,bshd->bhts", query_h, key_h, preferred_element_type=jnp.float32) * 0.125
    )
    probs = softmax_along(scores, 3)
    probs_low = probs.astype(jnp.bfloat16)
    attended = (
        jnp.einsum("bhts,bshd->bthd", probs_low, value_h, preferred_element_type=jnp.float32)
        .reshape(n_img, n_tok, width)
        .astype(jnp.bfloat16)
    )
    low_out = project(attended, full_out_a).astype(jnp.bfloat16) * selector
    middle = inputs_f + project(attended, full_out) + project(low_out, full_out_b)
    normed_two = layer_norm(middle).astype(jnp.bfloat16)
    low_route = project(normed_two, full_route_a).astype(jnp.bfloat16) * selector
    logits = project(normed_two, full_route) + project(low_route, full_route_b)
    dispatch = softmax_along(logits, 1)
    combine = softmax_along(logits, 2)
    dispatch_low = dispatch.astype(jnp.bfloat16)
    combine_low = combine.astype(jnp.bfloat16)
    slot_vals = jnp.einsum(
        "bte,btd->bed", dispatch_low, normed_two, preferred_element_type=jnp.float32
    ).astype(jnp.bfloat16)
    route_ids = jnp.broadcast_to(image_adapter_index[:, None], (n_img, n_experts))
    slot_received, ids_recv = (
        lax.all_to_all(slot_vals, "shard", split_axis=1, concat_axis=0, tiled=True),
        lax.all_to_all(route_ids, "shard", split_axis=1, concat_axis=0, tiled=True),
    )
    expert_lane = lax.broadcasted_iota(jnp.int32, (1, 1, every_rank_lane), 2) // RANK
    expert_sel = (ids_recv[:, :, None] == expert_lane).astype(jnp.bfloat16)
    expert_sel_f = expert_sel.astype(jnp.float32)
    rank_up_output = (
        jnp.einsum(
            "rza,zab->rzb", slot_received, up_adapter_first, preferred_element_type=jnp.float32
        ).astype(jnp.bfloat16)
        * expert_sel
    )
    preact = jnp.einsum(
        "ned,edf->nef", slot_received, frozen_up_weight, preferred_element_type=jnp.float32
    ) + jnp.einsum(
        "bwd,wda->bwa", rank_up_output, up_adapter_second, preferred_element_type=jnp.float32
    )
    hidden_units = jax.nn.gelu(preact).astype(jnp.bfloat16)
    rank_down_output = (
        jnp.einsum(
            "ywj,wjq->ywq", hidden_units, down_adapter_first, preferred_element_type=jnp.float32
        ).astype(jnp.bfloat16)
        * expert_sel
    )
    expert_out = (
        jnp.einsum(
            "nef,efd->ned", hidden_units, frozen_down_weight, preferred_element_type=jnp.float32
        )
        + jnp.einsum(
            "yxz,xzr->yxr",
            rank_down_output,
            down_adapter_second,
            preferred_element_type=jnp.float32,
        )
    ).astype(jnp.bfloat16)
    returned = lax.all_to_all(expert_out, "shard", split_axis=0, concat_axis=1, tiled=True)
    mixed = jnp.einsum("bte,bed->btd", combine_low, returned, preferred_element_type=jnp.float32)
    block_out = (living * (middle + mixed)).astype(jnp.bfloat16)
    again = (
        lax.all_gather(shared[0], "shard", axis=0, tiled=True),
        lax.all_gather(shared[1], "shard", axis=0, tiled=True),
        lax.all_gather(shared[2], "shard", axis=0, tiled=True),
        lax.all_gather(shared[3], "shard", axis=0, tiled=True),
        lax.all_gather(shared[4], "shard", axis=0, tiled=True),
        lax.all_gather(shared[5], "shard", axis=0, tiled=True),
        lax.all_gather(shared[6], "shard", axis=1, tiled=True),
        lax.all_gather(shared[7], "shard", axis=1, tiled=True),
        lax.all_gather(shared[8], "shard", axis=1, tiled=True),
    )
    (
        full_qkv,
        full_out,
        full_route,
        full_qkv_a,
        full_out_a,
        full_route_a,
        full_qkv_b,
        full_out_b,
        full_route_b,
    ) = again
    upstream = living * cotangent.astype(jnp.float32)
    upstream_low = upstream.astype(jnp.bfloat16)
    grad_comb = jnp.einsum(
        "btd,bed->bte", upstream_low, returned, preferred_element_type=jnp.float32
    )
    grad_expert = jnp.einsum(
        "bte,btd->bed", combine_low, upstream_low, preferred_element_type=jnp.float32
    ).astype(jnp.bfloat16)
    gradient_received = lax.all_to_all(
        grad_expert, "shard", split_axis=1, concat_axis=0, tiled=True
    )
    grad_down_b = jnp.einsum(
        "nek,ned->ekd", rank_down_output, gradient_received, preferred_element_type=jnp.float32
    )
    gradient_rank_down = (
        jnp.einsum(
            "orf,rzf->orz",
            gradient_received,
            down_adapter_second,
            preferred_element_type=jnp.float32,
        )
        * expert_sel_f
    ).astype(jnp.bfloat16)
    grad_down_a = jnp.einsum(
        "nef,nek->efk", hidden_units, gradient_rank_down, preferred_element_type=jnp.float32
    )
    grad_hidden = jnp.einsum(
        "ned,efd->nef", gradient_received, frozen_down_weight, preferred_element_type=jnp.float32
    ) + jnp.einsum(
        "bog,opg->bop", gradient_rank_down, down_adapter_first, preferred_element_type=jnp.float32
    )
    gradient_preactivation = jax.vjp(jax.nn.gelu, preact)[1](grad_hidden)[0].astype(jnp.bfloat16)
    grad_up_b = jnp.einsum(
        "nek,nef->ekf", rank_up_output, gradient_preactivation, preferred_element_type=jnp.float32
    )
    gradient_rank_up = (
        jnp.einsum(
            "ciu,ivu->civ",
            gradient_preactivation,
            up_adapter_second,
            preferred_element_type=jnp.float32,
        )
        * expert_sel_f
    ).astype(jnp.bfloat16)
    grad_up_a = jnp.einsum(
        "ned,nek->edk", slot_received, gradient_rank_up, preferred_element_type=jnp.float32
    )
    grad_slot_recv = (
        jnp.einsum(
            "nef,edf->ned",
            gradient_preactivation,
            frozen_up_weight,
            preferred_element_type=jnp.float32,
        )
        + jnp.einsum(
            "pjx,jsx->pjs", gradient_rank_up, up_adapter_first, preferred_element_type=jnp.float32
        )
    ).astype(jnp.bfloat16)
    grad_slots = lax.all_to_all(grad_slot_recv, "shard", split_axis=0, concat_axis=1, tiled=True)
    grad_disp = jnp.einsum(
        "bed,btd->bte", grad_slots, normed_two, preferred_element_type=jnp.float32
    )
    grad_normed_two = jnp.einsum(
        "bte,bed->btd", dispatch_low, grad_slots, preferred_element_type=jnp.float32
    )
    grad_logits = dispatch * (grad_disp - jnp.sum(grad_disp * dispatch, axis=1, keepdims=True))
    grad_logits = grad_logits + combine * (
        grad_comb - jnp.sum(grad_comb * combine, axis=2, keepdims=True)
    )
    grad_logits = grad_logits.astype(jnp.bfloat16)
    grad_low_route = (project_back(grad_logits, full_route_b) * selector_f).astype(jnp.bfloat16)
    grad_route_b = outer_sum(low_route, grad_logits)
    grad_route_a = outer_sum(normed_two, grad_low_route)
    grad_normed_two = (
        grad_normed_two
        + project_back(grad_logits, full_route)
        + project_back(grad_low_route, full_route_a)
    )
    grad_middle = upstream + norm_back(middle, grad_normed_two)
    grad_branch = grad_middle.astype(jnp.bfloat16)
    grad_out_b = outer_sum(low_out, grad_branch)
    grad_low_out = (project_back(grad_branch, full_out_b) * selector_f).astype(jnp.bfloat16)
    grad_out_a = outer_sum(attended, grad_low_out)
    grad_attended = (
        project_back(grad_branch, full_out) + project_back(grad_low_out, full_out_a)
    ).astype(jnp.bfloat16)
    grad_heads = grad_attended.reshape(n_img, n_tok, HEADS, head_dim)
    grad_value = jnp.einsum(
        "bhts,bthd->bshd", probs_low, grad_heads, preferred_element_type=jnp.float32
    )
    grad_probs = jnp.einsum(
        "bthd,bshd->bhts", grad_heads, value_h, preferred_element_type=jnp.float32
    )
    grad_scores = (
        probs * (grad_probs - jnp.sum(grad_probs * probs, axis=3, keepdims=True))
    ).astype(jnp.bfloat16)
    grad_query = (
        jnp.einsum("bhts,bshd->bthd", grad_scores, key_h, preferred_element_type=jnp.float32)
        * 0.125
    )
    grad_key = (
        jnp.einsum("bhts,bthd->bshd", grad_scores, query_h, preferred_element_type=jnp.float32)
        * 0.125
    )
    grad_joined = jnp.concatenate(
        (
            grad_query.reshape(n_img, n_tok, width),
            grad_key.reshape(n_img, n_tok, width),
            grad_value.reshape(n_img, n_tok, width),
        ),
        axis=2,
    ).astype(jnp.bfloat16)
    grad_qkv_b = outer_sum(low_qkv, grad_joined)
    grad_low_qkv = (project_back(grad_joined, full_qkv_b) * selector_f).astype(jnp.bfloat16)
    grad_qkv_a = outer_sum(normed, grad_low_qkv)
    grad_normed = project_back(grad_joined, full_qkv) + project_back(grad_low_qkv, full_qkv_a)
    input_grad = grad_middle + norm_back(inputs_f, grad_normed)
    owned = (
        lax.psum_scatter(
            grad_qkv_a.astype(jnp.bfloat16), "shard", scatter_dimension=0, tiled=True
        ).astype(jnp.float32),
        lax.psum_scatter(
            grad_out_a.astype(jnp.bfloat16), "shard", scatter_dimension=0, tiled=True
        ).astype(jnp.float32),
        lax.psum_scatter(
            grad_route_a.astype(jnp.bfloat16), "shard", scatter_dimension=0, tiled=True
        ).astype(jnp.float32),
        lax.psum_scatter(
            grad_qkv_b.astype(jnp.bfloat16), "shard", scatter_dimension=1, tiled=True
        ).astype(jnp.float32),
        lax.psum_scatter(
            grad_out_b.astype(jnp.bfloat16), "shard", scatter_dimension=1, tiled=True
        ).astype(jnp.float32),
        lax.psum_scatter(
            grad_route_b.astype(jnp.bfloat16), "shard", scatter_dimension=1, tiled=True
        ).astype(jnp.float32),
    )
    summed = (
        lax.psum(owned[0].astype(jnp.bfloat16), "replica").astype(jnp.float32),
        lax.psum(owned[1].astype(jnp.bfloat16), "replica").astype(jnp.float32),
        lax.psum(owned[2].astype(jnp.bfloat16), "replica").astype(jnp.float32),
        lax.psum(owned[3].astype(jnp.bfloat16), "replica").astype(jnp.float32),
        lax.psum(owned[4].astype(jnp.bfloat16), "replica").astype(jnp.float32),
        lax.psum(owned[5].astype(jnp.bfloat16), "replica").astype(jnp.float32),
        lax.psum(grad_up_a.astype(jnp.bfloat16), "replica").astype(jnp.float32),
        lax.psum(grad_up_b.astype(jnp.bfloat16), "replica").astype(jnp.float32),
        lax.psum(grad_down_a.astype(jnp.bfloat16), "replica").astype(jnp.float32),
        lax.psum(grad_down_b.astype(jnp.bfloat16), "replica").astype(jnp.float32),
    )
    owned_qkv_a, owned_out_a, owned_route_a, owned_qkv_b, owned_out_b, owned_route_b = (
        summed[0],
        summed[1],
        summed[2],
        summed[3],
        summed[4],
        summed[5],
    )
    final_up_a, final_up_b, final_down_a, final_down_b = (
        summed[6],
        summed[7],
        summed[8],
        summed[9],
    )
    return (
        block_out,
        input_grad,
        owned_qkv_a,
        owned_qkv_b,
        owned_out_a,
        owned_out_b,
        owned_route_a,
        owned_route_b,
        final_up_a,
        final_up_b,
        final_down_a,
        final_down_b,
    )


def solution(mesh):
    in_specs = (
        P(("replica", "shard"), None, None),
        P(("replica", "shard")),
        P(("replica", "shard")),
        P(("replica", "shard"), None, None),
        P("shard", None),
        P("shard", None),
        P("shard", None),
        P("shard", None),
        P(None, "shard"),
        P("shard", None),
        P(None, "shard"),
        P("shard", None),
        P(None, "shard"),
        P("shard", None, None),
        P("shard", None, None),
        P("shard", None, None),
        P("shard", None, None),
        P("shard", None, None),
        P("shard", None, None),
    )
    out_specs = (
        P(("replica", "shard"), None, None),
        P(("replica", "shard"), None, None),
        P("shard", None),
        P(None, "shard"),
        P("shard", None),
        P(None, "shard"),
        P("shard", None),
        P(None, "shard"),
        P("shard", None, None),
        P("shard", None, None),
        P("shard", None, None),
        P("shard", None, None),
    )
    return jax.shard_map(
        per_device, mesh=mesh, in_specs=in_specs, out_specs=out_specs, check_vma=False
    )
```

profile of v0, /device:TPU:1, one launch (start us, length us, event | category | flops | bytes accessed | tf_op | source)
XLA Modules:
  0.0 893.3 jit_solution(17985423125891223566)
XLA Ops:
  9.2 6.4 all-to-all-start.1
  20.7 24.5 %all-gather = bf16[8,96,16]{1,2,0:T(8,128)(2,1)S(1)} all-gather(bf16[1,96,16]{1,2,0:T(8,128)(2,1)S(1)} %bitcast.258), channel_id=1, replica_groups=mesh['replica'=4,'shard'=8] {'shard'}, dimensions={0}, use_global_device_ids=true | all-gather | bytes 27648 | tf_op jit(solution)/shard_map/all_gather | solution.py:76
  45.2 25.3 %all_gather.37 = bf16[768,128]{1,0:T(8,128)(2,1)S(1)} all-gather(bf16[96,128]{1,0:T(8,128)(2,1)S(1)} %copy-done.64), channel_id=1, replica_groups=mesh['replica'=4,'shard'=8] {'shard'}, dimensions={0}, use_global_device_ids=true | all-gather | bytes 221184 | tf_op jit(solution)/shard_map/all_gather | solution.py:77
  70.5 24.9 %all_gather.40 = bf16[768,128]{1,0:T(8,128)(2,1)S(1)} all-gather(bf16[96,128]{1,0:T(8,128)(2,1)S(1)} %copy-done.65), channel_id=1, replica_groups=mesh['replica'=4,'shard'=8] {'shard'}, dimensions={0}, use_global_device_ids=true | all-gather | bytes 221184 | tf_op jit(solution)/shard_map/all_gather | solution.py:78
  95.5 24.8 %all_gather.41 = bf16[128,768]{0,1:T(8,128)(2,1)S(1)} all-gather(bf16[128,96]{0,1:T(8,128)(2,1)S(1)} %copy-done.66), channel_id=1, replica_groups=mesh['replica'=4,'shard'=8] {'shard'}, dimensions={1}, use_global_device_ids=true | all-gather | bytes 221184 | tf_op jit(solution)/shard_map/all_gather | solution.py:81
  120.3 24.6 %all_gather.43 = bf16[768,128]{1,0:T(8,128)(2,1)S(1)} all-gather(bf16[96,128]{1,0:T(8,128)(2,1)S(1)} %copy-done.67), channel_id=1, replica_groups=mesh['replica'=4,'shard'=8] {'shard'}, dimensions={0}, use_global_device_ids=true | all-gather | bytes 221184 | tf_op jit(solution)/shard_map/all_gather | solution.py:79
  144.9 25.0 %all_gather.38 = bf16[128,2304]{0,1:T(8,128)(2,1)S(1)} all-gather(bf16[128,288]{0,1:T(8,128)(2,1)S(1)} %copy-done.57), channel_id=1, replica_groups=mesh['replica'=4,'shard'=8] {'shard'}, dimensions={1}, use_global_device_ids=true | all-gather | bytes 663552 | tf_op jit(solution)/shard_map/all_gather | solution.py:80
  172.3 16.8 %all-gather.1 = bf16[8,2,128]{2,1,0:T(2,128)(2,1)S(1)} all-gather(bf16[1,2,128]{2,1,0:T(2,128)(2,1)S(1)} %bitcast.259), channel_id=1, replica_groups=mesh['replica'=4,'shard'=8] {'shard'}, dimensions={0}, use_global_device_ids=true | all-gather | bytes 4608 | tf_op jit(solution)/shard_map/all_gather | solution.py:82
  190.7 12.9 %fusion.27 = f32[8,197,2304]{2,1,0:T(8,128)} fusion(bf16[768,2304]{1,0:T(8,128)(2,1)} %all-gather.5.cloned.1.call-done, f32[8,197]{1,0:T(8,128)S(1)} %fusion.139, f32[8,197]{1,0:T(8,128)S(1)} %broadcast_multiply_fusion.1, bf16[8,197,768]{2,0,1:T(8,128)(2,1)} %param.19), kind=kOutput, calls=%fused_computation.53 | convolution fusion | flops 5582217216 | bytes 20496704 | tf_op jit(solution)/shard_map/btd,dk->btk/dot_general | solution.py:27
  203.6 7.3 add_convert_fusion
  214.1 4.5 copy.84
  218.6 4.5 copy.83
  223.1 4.5 copy.82
  227.6 13.0 %fusion.151 = (f32[8,12,197]{2,1,0:T(8,128)S(1)}, f32[8,12,197,197]{2,3,1,0:T(8,128)}) fusion(bf16[8,197,12,64]{1,3,2,0:T(8,128)(2,1)} %bitcast.237, bf16[8,197,12,64]{1,3,2,0:T(8,128)(2,1)} %bitcast.234), kind=kOutput, calls=%fused_computation.203 | convolution fusion | flops 488062176 | bytes 19819776 | tf_op jit(solution)/shard_map/sub | solution.py:21
  240.6 9.7 %fusion.30 = bf16[8,12,64,197]{3,2,1,0:T(8,128)(2,1)S(1)} fusion(bf16[8,197,12,64]{1,3,2,0:T(8,128)(2,1)} %bitcast.246, f32[8,12,197,197]{2,3,1,0:T(8,128)} %get-tuple-element.66, f32[8,12,197]{2,1,0:T(8,128)S(1)} %get-tuple-element.65), kind=kOutput, calls=%fused_computation.57 | convolution fusion | flops 485546688 | bytes 19819776 | tf_op jit(solution)/shard_map/bhts,bshd->bthd/dot_general | solution.py:113
  253.1 4.5 fusion.67
  277.1 4.8 all-to-all-start.3
  283.6 5.7 fusion.22
  295.7 7.0 fusion.43
  303.6 3.8 fusion.160
  310.2 5.4 all-to-all-start.2
  322.3 5.0 all-to-all-start.4
  337.8 3.8 fusion.87
  348.5 6.3 multiply_reduce_fusion.2
  364.4 4.5 copy.99
  368.9 12.5 %fusion.33 = bf16[8,12,64,197]{3,2,1,0:T(8,128)(2,1)} fusion(bf16[8,197,12,64]{1,3,2,0:T(8,128)(2,1)} %bitcast.249, f32[8,12,197,197]{2,3,1,0:T(8,128)} %get-tuple-element.66, f32[8,12,197]{2,1,0:T(8,128)S(1)} %copy-done.44), kind=kOutput, calls=%fused_computation.58 | convolution fusion | flops 485546688 | bytes 19819776 | tf_op jit(solution)/shard_map/bhts,bthd->bshd/dot_general | solution.py:278
  381.4 15.0 %multiply_reduce_fusion = (f32[8,12,197]{2,1,0:T(8,128)S(1)}, f32[8,12,197,197]{2,3,1,0:T(8,128)}) fusion(f32[8,12,197,197]{2,3,1,0:T(8,128)} %get-tuple-element.66, f32[8,12,197]{2,1,0:T(8,128)S(1)} %copy-done.44, bf16[8,197,12,64]{1,3,2,0:T(8,128)(2,1)} %bitcast.250, bf16[8,197,12,64]{1,3,2,0:T(8,128)(2,1)} %bitcast.247), kind=kOutput, calls=%fused_computation.6 | convolution fusion | flops 488043072 | bytes 34798080 | tf_op jit(solution)/shard_map/bthd,bshd->bhts/dot_general | solution.py:281
  396.5 18.3 %multiply_convert_fusion = bf16[8,12,197,197]{2,3,1,0:T(8,128)(2,1)} fusion(f32[8,12,197,197]{2,3,1,0:T(8,128)} %get-tuple-element.76, f32[8,12,197]{2,1,0:T(8,128)S(1)} %get-tuple-element.75, f32[8,12,197,197]{2,3,1,0:T(8,128)} %get-tuple-element.66, f32[8,12,197]{2,1,0:T(8,128)S(1)} %copy-done.44), kind=kLoop, calls=%fused_computation.5 | loop fusion | flops 14902656 | bytes 37407936 | tf_op jit(solution)/shard_map/convert_element_type | solution.py:286
  414.8 9.8 %multiply_convert_fusion.1 = bf16[8,12,64,197]{3,2,1,0:T(8,128)(2,1)} fusion(bf16[8,197,12,64]{1,3,2,0:T(8,128)(2,1)} %bitcast.238, bf16[8,12,197,197]{2,3,1,0:T(8,128)(2,1)} %multiply_convert_fusion), kind=kOutput, calls=%fused_computation.23 | convolution fusion | flops 479305728 | bytes 12292800 | tf_op jit(solution)/shard_map/bhts,bthd->bshd/dot_general | solution.py:292
  424.6 7.6 multiply_convert_fusion.2
  434.3 4.5 copy.105
  438.8 4.5 copy.103
  443.3 4.5 copy.104
  447.8 15.4 %all-reduce = bf16[128,16]{0,1:T(8,128)(2,1)S(1)} all-reduce(bf16[128,16]{0,1:T(8,128)(2,1)S(1)} %fusion.97), channel_id=7, replica_groups=mesh['replica'=4,'shard'=8] {'shard'}, use_global_device_ids=true, to_apply=%region_27.28.clone | all-reduce | flops 2048 | bytes 8192
  466.9 4.5 fusion.52
  474.6 6.5 fusion.24
  481.1 10.8 %fusion.25 = f32[8,197,768]{2,1,0:T(8,128)} fusion(bf16[768,2304]{1,0:T(8,128)(2,1)} %all-gather.5.cloned.1.call-done, bf16[8,197,768]{2,1,0:T(8,128)(2,1)} %copy.105, bf16[8,197,768]{2,1,0:T(8,128)(2,1)} %copy.104, bf16[8,197,768]{2,1,0:T(8,128)(2,1)} %copy.103), kind=kOutput, calls=%fused_computation.51 | convolution fusion | flops 5599162368 | bytes 15642624 | tf_op jit(solution)/shard_map/btk,dk->btd/dot_general | solution.py:31
  491.9 6.7 reduce-scatter.14.cloned.1.call-done
  498.6 63.2 %reduce-scatter.12.cloned.1.call-done = bf16[128,96]{0,1:T(8,128)(2,1)} async-done(((bf16[128,768]{0,1:T(8,128)(2,1)}), bf16[128,96]{0,1:T(8,128)(2,1)}) %reduce-scatter.12.cloned.1.call-update) | async-done | bytes 24592 | tf_op jit(solution)/shard_map/reduce_scatter | solution.py:321
  561.8 63.8 %reduce-scatter.10.cloned.1.call-done = bf16[96,128]{1,0:T(8,128)(2,1)} async-done(((bf16[768,128]{1,0:T(8,128)(2,1)}), bf16[96,128]{1,0:T(8,128)(2,1)}) %reduce-scatter.10.cloned.1.call-update) | async-done | bytes 24592 | tf_op jit(solution)/shard_map/reduce_scatter | solution.py:312
  625.6 63.8 %reduce-scatter.6.cloned.1.call-done = bf16[96,128]{1,0:T(8,128)(2,1)} async-done(((bf16[768,128]{1,0:T(8,128)(2,1)}), bf16[96,128]{1,0:T(8,128)(2,1)}) %reduce-scatter.6.cloned.1.call-update) | async-done | bytes 24592 | tf_op jit(solution)/shard_map/reduce_scatter | solution.py:309
  689.5 7.0 fusion.15
  696.5 58.2 %reduce-scatter.8.cloned.1.call-done = bf16[128,288]{0,1:T(8,128)(2,1)} async-done(((bf16[128,2304]{0,1:T(8,128)(2,1)}), bf16[128,288]{0,1:T(8,128)(2,1)}) %reduce-scatter.8.cloned.1.call-update) | async-done | bytes 73744 | tf_op jit(solution)/shard_map/reduce_scatter | solution.py:318
  754.7 4.8 multiply_convert_fusion.3
  763.3 3.9 fusion.36
  767.4 4.7 add_add_fusion.2
  775.8 13.8 %all-reduce.6.cloned.1.call-done = (bf16[96,128]{1,0:T(8,128)(2,1)}, bf16[96,128]{1,0:T(8,128)(2,1)}, bf16[128,96]{0,1:T(8,128)(2,1)}, bf16[96,128]{1,0:T(8,128)(2,1)}, bf16[128,2]{0,1:T(2,128)(2,1)}) async-done(((bf16[96,128]{1,0:T(8,128)(2,1)}, bf16[96,128]{1,0:T(8,128)(2,1)}, bf16[128,96]{0,1:T(8,128)(2,1)}, bf16[96,128]{1,0:T(8,128)(2,1)}, bf16[128,2]{0,1:T(2,128)(2,1)}), (bf16[96,128]{1,0:T(8,128)(2,1)}, ...) | async-done | bytes 98832 | tf_op jit(solution)/shard_map/psum | solution.py:329
  796.3 80.8 %all-reduce.8.cloned.1.call-done = (bf16[128,288]{0,1:T(8,128)(2,1)}, bf16[2,768,128]{2,1,0:T(8,128)(2,1)}, bf16[2,128,3072]{2,1,0:T(8,128)(2,1)}, bf16[2,3072,128]{2,1,0:T(8,128)(2,1)}, bf16[2,128,768]{2,1,0:T(8,128)(2,1)}) async-done(((bf16[128,288]{0,1:T(8,128)(2,1)}, bf16[2,768,128]{2,1,0:T(8,128)(2,1)}, bf16[2,128,3072]{2,1,0:T(8,128)(2,1)}, bf16[2,3072,128]{2,1,0:T(8,128)(2,1)}, ...) | async-done | bytes 4005904 | tf_op jit(solution)/shard_map/psum | solution.py:332
  (296 shorter events, 112.4 us)
Async XLA Ops:
  7.2 285.1 %copy-start = (bf16[2,3072,128]{2,1,0:T(8,128)(2,1)S(1)}, bf16[2,3072,128]{2,1,0:T(8,128)(2,1)}, u32[]{:S(2)}) copy-start(bf16[2,3072,128]{2,1,0:T(8,128)(2,1)} %param.36) | copy-start | bytes 4718596
  7.2 13.5 %copy-start.76 = (bf16[96,16]{0,1:T(8,128)(2,1)S(1)}, bf16[96,16]{0,1:T(8,128)(2,1)}, u32[]{:S(2)}) copy-start(bf16[96,16]{0,1:T(8,128)(2,1)} %param.25) | copy-start | bytes 9220
  7.2 38.0 %copy-start.64 = (bf16[96,128]{1,0:T(8,128)(2,1)S(1)}, bf16[96,128]{1,0:T(8,128)(2,1)}, u32[]{:S(2)}) copy-start(bf16[96,128]{1,0:T(8,128)(2,1)} %param.26) | copy-start | bytes 73732
  7.2 63.3 %copy-start.65 = (bf16[96,128]{1,0:T(8,128)(2,1)S(1)}, bf16[96,128]{1,0:T(8,128)(2,1)}, u32[]{:S(2)}) copy-start(bf16[96,128]{1,0:T(8,128)(2,1)} %param.28) | copy-start | bytes 73732
  7.2 88.2 %copy-start.66 = (bf16[128,96]{0,1:T(8,128)(2,1)S(1)}, bf16[128,96]{0,1:T(8,128)(2,1)}, u32[]{:S(2)}) copy-start(bf16[128,96]{0,1:T(8,128)(2,1)} %param.29) | copy-start | bytes 73732
  7.2 113.1 %copy-start.67 = (bf16[96,128]{1,0:T(8,128)(2,1)S(1)}, bf16[96,128]{1,0:T(8,128)(2,1)}, u32[]{:S(2)}) copy-start(bf16[96,128]{1,0:T(8,128)(2,1)} %param.30) | copy-start | bytes 73732
  7.2 137.6 %copy-start.57 = (bf16[128,288]{0,1:T(8,128)(2,1)S(1)}, bf16[128,288]{0,1:T(8,128)(2,1)}, u32[]{:S(2)}) copy-start(bf16[128,288]{0,1:T(8,128)(2,1)} %param.27) | copy-start | bytes 221188
  7.3 183.4 %all-gather.5.cloned.1.call-start = ((), (), s32[]{:S(2)}) async-start(), calls=%async_computation.10 | async-start | bytes 3981312 | tf_op jit(solution)/shard_map/all_gather | solution.py:74
  9.2 181.3 %all-to-all-start.1 = ((s32[8,8,2]{0,2,1:T(2,128)}), s32[8,8,2]{0,2,1:T(2,128)S(1)}, u32[]{:S(2)}, u32[]{:S(2)}) async-start(s32[8,8,2]{0,2,1:T(2,128)} %broadcast_in_dim.10), calls=%async_computation.1 | async-start | bytes 16384 | tf_op jit(solution)/shard_map/all_to_all | solution.py:132
  15.6 237.5 %all-gather.7.cloned.1.call-start = ((), (), s32[]{:S(2)}) async-start(), calls=%async_computation.11 | async-start | bytes 1327104 | tf_op jit(solution)/shard_map/all_gather | solution.py:75
  16.4 275.9 %copy-start.74 = (s32[128]{0:T(128)}, s32[128]{0:T(128)S(1)}, u32[]{:S(2)}) copy-start(s32[128]{0:T(128)S(1)} %fusion.145) | copy-start | bytes 1540
  17.2 254.0 %copy-start.72 = (f32[8]{0:T(128)}, f32[8]{0:T(128)S(1)}, u32[]{:S(2)}) copy-start(f32[8]{0:T(128)S(1)} %compare_convert_fusion.1) | copy-start | bytes 100
  17.2 152.7 %copy-start.78 = (s32[8]{0:T(128)S(1)}, s32[8]{0:T(128)}, u32[]{:S(2)}) copy-start(s32[8]{0:T(128)} %param.20) | copy-start | bytes 100
  19.7 171.0 %copy-start.41 = (f32[8,197]{1,0:T(8,128)}, f32[8,197]{1,0:T(8,128)S(1)}, u32[]{:S(2)}) copy-start(f32[8,197]{1,0:T(8,128)S(1)} %broadcast_multiply_fusion.1) | copy-start | bytes 18916
  20.7 151.6 %copy-start.53 = (f32[8,197]{1,0:T(8,128)}, f32[8,197]{1,0:T(8,128)S(1)}, u32[]{:S(2)}) copy-start(f32[8,197]{1,0:T(8,128)S(1)} %fusion.13) | copy-start | bytes 18916
  20.7 170.0 %copy-start.58 = (f32[8,197]{1,0:T(8,128)}, f32[8,197]{1,0:T(8,128)S(1)}, u32[]{:S(2)}) copy-start(f32[8,197]{1,0:T(8,128)S(1)} %fusion.139) | copy-start | bytes 18916
  70.5 101.8 %copy-start.29 = (bf16[768,128]{1,0:T(8,128)(2,1)}, bf16[768,128]{1,0:T(8,128)(2,1)S(1)}, u32[]{:S(2)}) copy-start(bf16[768,128]{1,0:T(8,128)(2,1)S(1)} %all_gather.37) | copy-start | bytes 589828
  95.5 154.9 %copy-start.21 = (bf16[768,128]{1,0:T(8,128)(2,1)}, bf16[768,128]{1,0:T(8,128)(2,1)S(1)}, u32[]{:S(2)}) copy-start(bf16[768,128]{1,0:T(8,128)(2,1)S(1)} %all_gather.40) | copy-start | bytes 589828
  120.3 137.3 %copy-start.31 = (bf16[128,768]{0,1:T(8,128)(2,1)}, bf16[128,768]{0,1:T(8,128)(2,1)S(1)}, u32[]{:S(2)}) copy-start(bf16[128,768]{0,1:T(8,128)(2,1)S(1)} %all_gather.41) | copy-start | bytes 589828
  144.9 117.2 %copy-start.27 = (bf16[768,128]{1,0:T(8,128)(2,1)}, bf16[768,128]{1,0:T(8,128)(2,1)S(1)}, u32[]{:S(2)}) copy-start(bf16[768,128]{1,0:T(8,128)(2,1)S(1)} %all_gather.43) | copy-start | bytes 589828
  169.9 33.6 %copy-start.19 = (bf16[128,2304]{0,1:T(8,128)(2,1)}, bf16[128,2304]{0,1:T(8,128)(2,1)S(1)}, u32[]{:S(2)}) copy-start(bf16[128,2304]{0,1:T(8,128)(2,1)S(1)} %all_gather.38) | copy-start | bytes 1769476
  170.7 18.6 %copy-start.81 = (u32[32]{0:T(128)S(1)}, u32[32]{0:T(128)}, u32[]{:S(2)}) copy-start(u32[32]{0:T(128)} %constant.80) | copy-start | bytes 388
  172.3 31.3 %copy-start.33 = (bf16[8,197,128]{2,1,0:T(8,128)(2,1)}, bf16[8,197,128]{2,1,0:T(8,128)(2,1)S(1)}, u32[]{:S(2)}) copy-start(bf16[8,197,128]{2,1,0:T(8,128)(2,1)S(1)} %fusion.62) | copy-start | bytes 1210372
  189.1 73.8 %copy-start.70 = (bf16[8,2,128]{2,1,0:T(2,128)(2,1)}, bf16[8,2,128]{2,1,0:T(2,128)(2,1)S(1)}, u32[]{:S(2)}) copy-start(bf16[8,2,128]{2,1,0:T(2,128)(2,1)S(1)} %all-gather.1) | copy-start | bytes 12292
  189.2 71.1 %copy-start.39 = (bf16[768,16,1]{0,1,2:T(8,128)(2,1)}, bf16[768,16,1]{0,1,2:T(8,128)(2,1)S(1)}, u32[]{:S(2)}) copy-start(bf16[768,16,1]{0,1,2:T(8,128)(2,1)S(1)} %reshape.260) | copy-start | bytes 73732
  190.6 101.6 %copy-start.68 = (s32[64,2]{0,1:T(2,128)}, s32[64,2]{0,1:T(2,128)S(1)}, u32[]{:S(2)}) copy-start(s32[64,2]{0,1:T(2,128)S(1)} %eq.32) | copy-start | bytes 1540
  240.6 9.7 %copy-start.43 = (f32[8,12,197]{2,1,0:T(8,128)}, f32[8,12,197]{2,1,0:T(8,128)S(1)}, u32[]{:S(2)}) copy-start(f32[8,12,197]{2,1,0:T(8,128)S(1)} %get-tuple-element.65) | copy-start | bytes 226948
  267.0 16.2 %copy-start.14 = (bf16[2,128,3072]{2,1,0:T(8,128)(2,1)S(1)}, bf16[2,128,3072]{2,1,0:T(8,128)(2,1)}, u32[]{:S(2)}) copy-start(bf16[2,128,3072]{2,1,0:T(8,128)(2,1)} %param.35) | copy-start | bytes 4718596
  267.0 10.1 %all-to-all-start = ((bf16[8,16,768]{2,0,1:T(8,128)(2,1)}), bf16[8,16,768]{2,0,1:T(8,128)(2,1)S(1)}, u32[]{:S(2)}, u32[]{:S(2)}) async-start(bf16[8,16,768]{2,0,1:T(8,128)(2,1)} %copy.89), calls=%async_computation | async-start | bytes 393216 | tf_op jit(solution)/shard_map/all_to_all | solution.py:131
  271.3 10.7 %copy-start.51 = (f32[8,197]{1,0:T(8,128)}, f32[8,197]{1,0:T(8,128)S(1)}, u32[]{:S(2)}) copy-start(f32[8,197]{1,0:T(8,128)S(1)} %get-tuple-element.71) | copy-start | bytes 18916
  277.1 16.4 %all-to-all-start.3 = ((bf16[8,16,768]{2,0,1:T(8,128)(2,1)}), bf16[8,16,768]{2,0,1:T(8,128)(2,1)}, u32[]{:S(2)}, u32[]{:S(2)}) async-start(bf16[8,16,768]{2,0,1:T(8,128)(2,1)} %copy.95), calls=%async_computation.3 | async-start | bytes 393216 | tf_op jit(solution)/shard_map/all_to_all | solution.py:199
  293.5 10.0 %slice-start.2 = ((s8[9437184]{0:T(1024)(128)(4,1)}), s8[4194304]{0:T(1024)(128)(4,1)S(1)}, s32[]{:S(2)}) async-start(s8[9437184]{0:T(1024)(128)(4,1)} %bitcast.230), calls=%async_computation.21 | async-start | bytes 8388608
  309.1 10.7 %copy-start.46 = (bf16[64,2,128]{2,0,1:T(8,128)(2,1)S(1)}, bf16[64,2,128]{2,0,1:T(8,128)(2,1)}, u32[]{:S(2)}) copy-start(bf16[64,2,128]{2,0,1:T(8,128)(2,1)} %copy-done.45) | copy-start | bytes 98308
  310.2 12.1 %all-to-all-start.2 = ((bf16[64,2,768]{2,1,0:T(2,128)(2,1)}), bf16[64,2,768]{2,1,0:T(2,128)(2,1)S(1)}, u32[]{:S(2)}, u32[]{:S(2)}) async-start(bf16[64,2,768]{2,1,0:T(2,128)(2,1)} %copy.92), calls=%async_computation.2 | async-start | bytes 393216 | tf_op jit(solution)/shard_map/all_to_all | solution.py:166
  319.8 9.0 %copy-start.73 = (f32[8]{0:T(128)S(1)}, f32[8]{0:T(128)}, u32[]{:S(2)}) copy-start(f32[8]{0:T(128)} %copy-done.72) | copy-start | bytes 100
  322.3 11.6 %all-to-all-start.4 = ((bf16[64,2,768]{2,1,0:T(2,128)(2,1)}), bf16[64,2,768]{2,1,0:T(2,128)(2,1)S(1)}, u32[]{:S(2)}, u32[]{:S(2)}) async-start(bf16[64,2,768]{2,1,0:T(2,128)(2,1)} %copy.97), calls=%async_computation.4 | async-start | bytes 393216 | tf_op jit(solution)/shard_map/all_to_all | solution.py:249
  327.3 171.3 %reduce-scatter.14.cloned.1.call-start = ((), (), s32[]{:S(2)}) async-start(), calls=%async_computation.16 | async-start | bytes 221184 | tf_op jit(solution)/shard_map/reduce_scatter | solution.py:315
  331.4 13.5 %copy-start.62 = (f32[8,197,16]{1,2,0:T(8,128)}, f32[8,197,16]{1,2,0:T(8,128)S(1)}, u32[]{:S(2)}) copy-start(f32[8,197,16]{1,2,0:T(8,128)S(1)} %fusion.99) | copy-start | bytes 302596
  396.5 165.4 %reduce-scatter.12.cloned.1.call-start = ((), (), s32[]{:S(2)}) async-start(), calls=%async_computation.15 | async-start | bytes 221184 | tf_op jit(solution)/shard_map/reduce_scatter | solution.py:321
  414.8 9.8 %copy-start.10 = (bf16[8,197,768]{1,2,0:T(8,128)(2,1)S(1)}, bf16[8,197,768]{1,2,0:T(8,128)(2,1)}, u32[]{:S(2)}) copy-start(bf16[8,197,768]{1,2,0:T(8,128)(2,1)} %copy.84) | copy-start | bytes 7262212
  434.0 191.6 %reduce-scatter.10.cloned.1.call-start = ((), (), s32[]{:S(2)}) async-start(), calls=%async_computation.14 | async-start | bytes 221184 | tf_op jit(solution)/shard_map/reduce_scatter | solution.py:312
  447.8 19.0 %copy-start.20 = (bf16[128,2304]{0,1:T(8,128)(2,1)S(1)}, bf16[128,2304]{0,1:T(8,128)(2,1)}, u32[]{:S(2)}) copy-start(bf16[128,2304]{0,1:T(8,128)(2,1)} %copy-done.19) | copy-start | bytes 1769476
  466.8 222.6 %reduce-scatter.6.cloned.1.call-start = ((), (), s32[]{:S(2)}) async-start(), calls=%async_computation.12 | async-start | bytes 221184 | tf_op jit(solution)/shard_map/reduce_scatter | solution.py:309
  474.5 280.1 %reduce-scatter.8.cloned.1.call-start = ((), (), s32[]{:S(2)}) async-start(), calls=%async_computation.13 | async-start | bytes 663552 | tf_op jit(solution)/shard_map/reduce_scatter | solution.py:318
  481.1 208.4 %copy-start.30 = (bf16[768,128]{1,0:T(8,128)(2,1)S(1)}, bf16[768,128]{1,0:T(8,128)(2,1)}, u32[]{:S(2)}) copy-start(bf16[768,128]{1,0:T(8,128)(2,1)} %copy-done.29) | copy-start | bytes 589828
  481.1 308.5 %all-reduce.6.cloned.1.call-start = ((), (), s32[]{:S(2)}) async-start(), calls=%async_computation.17 | async-start | bytes 197632 | tf_op jit(solution)/shard_map/psum | solution.py:329
  689.5 187.6 %all-reduce.8.cloned.1.call-start = ((), (), s32[]{:S(2)}) async-start(), calls=%async_computation.18 | async-start | bytes 8011776 | tf_op jit(solution)/shard_map/psum | solution.py:332
  754.7 12.6 %slice-start.5 = ((s8[4915200]{0:T(1024)(128)(4,1)}), s8[720896]{0:T(1024)(128)(4,1)S(1)}, s32[]{:S(2)}) async-start(s8[4915200]{0:T(1024)(128)(4,1)} %bitcast.232), calls=%async_computation.24 | async-start | bytes 1441792
  (58 other events, 260.8 us)
Sparse Core Ops, SparseCore 0:
  10.3 69.8 all-gather.4
  82.4 40.4 all-gather.6
  396.6 101.9 reduce-scatter.13
  501.7 60.0 reduce-scatter.11
  565.5 60.0 reduce-scatter.9
  629.3 60.0 reduce-scatter.5
  693.3 61.2 reduce-scatter.7
  758.1 31.4 all-reduce.5
  792.3 84.6 all-reduce.7
where the time goes:
time: 899 us; the launch traced here: 893 us
  waiting for transfers between devices  356 us (40%)
  matrix products  207 us (23%)
  blocking collectives  181 us (20%)
  local copies, waits for them, and re-layouts  54.4 us (6%)
  other arithmetic  52.5 us (6%)
  starting transfers between devices  25.7 us (3%)
  between operations  16.7 us (2%)
    psum x1, waiting for transfers between devices, per_device(): lax.psum(owned[3].astype(jnp.bfloat16), 'replica').astype(jnp.float32)  80.8 us
    reduce_scatter x1, waiting for transfers between devices, per_device(): lax.psum_scatter(grad_out_a.astype(jnp.bfloat16), 'shard', scatter_dimens...  63.8 us
    reduce_scatter x1, waiting for transfers between devices, per_device(): lax.psum_scatter(grad_qkv_a.astype(jnp.bfloat16), 'shard', scatter_dimens...  63.8 us
    reduce_scatter x1, waiting for transfers between devices, per_device(): lax.psum_scatter(grad_out_b.astype(jnp.bfloat16), 'shard', scatter_dimens...  63.2 us
    reduce_scatter x1, waiting for transfers between devices, per_device(): lax.psum_scatter(grad_qkv_b.astype(jnp.bfloat16), 'shard', scatter_dimens...  58.2 us
    dot_general x9, matrix products, project_back(): jnp.einsum('btk,dk->btd', left, right, preferred_element_type=jnp.float32)  37.5 us
    dot_general x9, matrix products, project(): jnp.einsum('btd,dk->btk', left, right, preferred_element_type=jnp.float32)  30.7 us
    all_gather x1, blocking collectives, per_device(): lax.all_gather(shared[3], 'shard', axis=0, tiled=True)  25.3 us
  transfers between devices with their start and end apart: 14, of which 10 were waited for; matrix products, arithmetic and copies ran while one was open for 23% of the time, Pallas kernels for 0%

commit v1 on v0

v1 whole, which is shorter than its diff:
```python
import functools

import jax
import jax.numpy as jnp
from jax import lax
from jax.experimental import pallas as pl
from jax.experimental.pallas import tpu as pltpu
from jax.sharding import PartitionSpec as P

HEADS = 12
RANK = 16
LANES = 128
HEAD_DIM = 64
GROUP = 256
F32 = jnp.float32
BF16 = jnp.bfloat16
NN = (((1,), (0,)), ((), ()))
NT = (((1,), (1,)), ((), ()))
TN = (((0,), (0,)), ((), ()))
NEG = -1e30
VMEM_LIMIT = 56 * 1024 * 1024
GELU_C = 0.7978845608028654
GELU_A = 0.044715


def dot(left, right, dims=NN):
    return lax.dot_general(left, right, dims, preferred_element_type=F32)


def params(*axes):
    return pltpu.CompilerParams(
        dimension_semantics=axes or None, vmem_limit_bytes=VMEM_LIMIT
    )


def cost(flops, moved, exps=0):
    return pl.CostEstimate(flops=int(flops), bytes_accessed=int(moved), transcendentals=int(exps))


def normalise(rows):
    centre = rows - jnp.mean(rows, axis=-1, keepdims=True)
    spread = jnp.mean(centre * centre, axis=-1, keepdims=True)
    scale = lax.rsqrt(spread + 1e-06)
    return centre * scale, scale


def normalise_back(unit, scale, upstream):
    inner = jnp.mean(upstream * unit, axis=-1, keepdims=True)
    return scale * (upstream - jnp.mean(upstream, axis=-1, keepdims=True) - unit * inner)


def rank_row(index):
    lane = lax.broadcasted_iota(jnp.int32, (1, LANES), 1) // RANK
    return (lane == index).astype(F32)


def zero_tail(rows, n_tok):
    total = rows.shape[0]
    cut = n_tok // 16 * 16
    if n_tok == total:
        return rows
    row = lax.broadcasted_iota(jnp.int32, (total - cut, rows.shape[1]), 0) + cut
    tail = jnp.where(row < n_tok, rows[cut:].astype(F32), 0.0).astype(rows.dtype)
    return jnp.concatenate([rows[:cut], tail], axis=0)


def mask_tail(scores, n_tok):
    total = scores.shape[0]
    cut = n_tok // 16 * 16
    if n_tok == total:
        return scores
    row = lax.broadcasted_iota(jnp.int32, (total - cut, scores.shape[1]), 0) + cut
    tail = jnp.where(row < n_tok, scores[cut:], NEG)
    return jnp.concatenate([scores[:cut], tail], axis=0)


def pad_rows(scratch, rows, n_tok):
    total = scratch.shape[0]
    scratch[n_tok // 8 * 8 :, :] = jnp.zeros((total - n_tok // 8 * 8, scratch.shape[1]), F32)
    scratch[0:n_tok, :] = rows.astype(F32)
    return scratch[...]


def assemble(place, chunks, wall, sems):
    part = wall.shape[1] // 4
    copies = []
    for step in range(4):
        column = pl.multiple_of((place ^ step) * part, LANES)
        copies.append(
            pltpu.make_async_copy(chunks[step], wall.at[:, pl.ds(column, part)], sems.at[step])
        )
    for copy in copies:
        copy.start()
    for copy in copies:
        copy.wait()


def norm_kernel(n_tok, image_ref, out_ref, pad_ref):
    unit, _ = normalise(pad_rows(pad_ref, image_ref[0], n_tok))
    out_ref[0] = unit.astype(BF16)


def head_mask(value):
    lane = lax.broadcasted_iota(jnp.int32, (1, LANES), 1)
    low = jnp.where(lane < HEAD_DIM, value, 0.0).astype(BF16)
    high = jnp.where(lane < HEAD_DIM, 0.0, value).astype(BF16)
    return low, high


def attention_forward(qkv, n_tok):
    masks = head_mask(0.125)
    value_t = qkv[:, 2 * GROUP :].T
    outs = []
    for pair in range(GROUP // LANES):
        q_pair = qkv[:, pair * LANES : (pair + 1) * LANES]
        k_pair = qkv[:, GROUP + pair * LANES : GROUP + (pair + 1) * LANES]
        for side in range(2):
            scores = mask_tail(dot(k_pair * masks[side], q_pair, NT), n_tok)
            top = jnp.max(scores, axis=0, keepdims=True)
            powers = jnp.exp(scores - top)
            total = jnp.sum(powers, axis=0, keepdims=True)
            head = 2 * pair + side
            mixed = dot(value_t[head * HEAD_DIM : (head + 1) * HEAD_DIM], powers.astype(BF16))
            outs.append((mixed * (1.0 / total)).astype(BF16))
    return zero_tail(jnp.concatenate(outs, axis=0).T, n_tok)


def first_attention_kernel(
    n_tok, shards, place_ref, index_ref, h1_ref, c0, c1, c2, c3,
    qkv_ref, att_ref, uq_ref, a_ref, bt_ref, ao_ref, ra_ref, wall, sems,
):
    image = pl.program_id(0)
    width = wall.shape[0]

    @pl.when(image == 0)
    def _():
        assemble(place_ref[0], (c0, c1, c2, c3), wall, sems)
        a_ref[...] = wall[:, width : width + LANES]
        ao_ref[...] = wall[:, width + 4 * LANES : width + 5 * LANES]
        ra_ref[...] = wall[:, width + 5 * LANES : width + 6 * LANES]
        rows = width // shards
        for shard in range(shards):
            for part in range(3):
                bt_ref[(shard * 3 + part) * rows : (shard * 3 + part + 1) * rows, :] = wall[
                    shard * rows : (shard + 1) * rows,
                    width + (1 + part) * LANES : width + (2 + part) * LANES,
                ]

    h1 = h1_ref[0]
    selector = rank_row(index_ref[image])
    uq = (dot(h1, a_ref[...]).astype(BF16).astype(F32) * selector).astype(BF16)
    uq_ref[0] = uq
    qkv = project_group(0, h1, uq, wall, bt_ref)
    qkv_ref[0] = qkv
    att_ref[0] = attention_forward(qkv, n_tok)


def group_rows(group, width, bt_ref):
    return jnp.concatenate(
        [bt_ref[part * width + group * GROUP : part * width + (group + 1) * GROUP, :] for part in range(3)],
        axis=0,
    )


def project_group(group, h1, uq, wall, bt_ref):
    width = wall.shape[0]
    second = group_rows(group, width, bt_ref)
    return (dot(h1, wall[:, : 3 * GROUP]) + dot(uq, second, NT)).astype(BF16)


def next_attention_kernel(
    n_tok, group, extra, place_ref, h1_ref, uq_ref, bt_ref, c0, c1, c2, c3, *rest
):
    qkv_ref, att_ref = rest[:2]
    wall, sems = rest[-2:]
    image = pl.program_id(0)

    @pl.when(image == 0)
    def _():
        assemble(place_ref[0], (c0, c1, c2, c3), wall, sems)
        for position in range(extra):
            column = 3 * GROUP + position * LANES
            rest[2 + position][...] = wall[:, column : column + LANES]

    qkv = project_group(group, h1_ref[0], uq_ref[0], wall, bt_ref)
    qkv_ref[0] = qkv
    att_ref[0] = attention_forward(qkv, n_tok)


def route_kernel(
    n_tok, n_exp, place_ref, index_ref, count_ref, image_ref, cot_ref, att0, att1, att2,
    ao_ref, bo_ref, ra_ref, wr_ref, rb_ref, c0, c1, c2, c3,
    x2_ref, uo_ref, ur_ref, disp_ref, comb_ref, sg_ref, wrt_ref, wall, pad_a, pad_b, sems,
):
    image = pl.program_id(0)
    width = wall.shape[0]

    @pl.when(image == 0)
    def _():
        assemble(place_ref[0], (c0, c1, c2, c3), wall, sems)
        wrt_ref[...] = wr_ref[...].astype(F32).T[:n_exp].astype(BF16)

    selector = rank_row(index_ref[image])
    living = (image < count_ref[0]).astype(F32)
    att = jnp.concatenate([att0[0], att1[0], att2[0]], axis=1)
    uo = (dot(att, ao_ref[...]).astype(BF16).astype(F32) * selector).astype(BF16)
    uo_ref[0] = uo
    x2 = pad_rows(pad_a, image_ref[0], n_tok) + dot(att, wall[:, :width]) + dot(uo, bo_ref[...], NT)
    x2_ref[0] = x2
    h2 = normalise(x2)[0].astype(BF16)
    ur = (dot(h2, ra_ref[...]).astype(BF16).astype(F32) * selector).astype(BF16)
    ur_ref[0] = ur
    logits = dot(wrt_ref[...], h2, NT) + dot(rb_ref[...], ur, NT)
    token = lax.broadcasted_iota(jnp.int32, logits.shape, 1)
    alive = token < n_tok
    over_tokens = jnp.where(alive, logits, NEG)
    powers = jnp.exp(over_tokens - jnp.max(over_tokens, axis=1, keepdims=True))
    disp = powers / jnp.sum(powers, axis=1, keepdims=True)
    powers = jnp.exp(logits - jnp.max(logits, axis=0, keepdims=True))
    comb = jnp.where(alive, powers / jnp.sum(powers, axis=0, keepdims=True), 0.0)
    disp_ref[0] = disp
    comb_ref[0] = comb
    upstream = (pad_rows(pad_b, cot_ref[0], n_tok) * living).astype(BF16)
    sg_ref[0, :, :width] = dot(disp.astype(BF16), h2).astype(BF16)
    sg_ref[0, :, width : 2 * width] = dot(comb.astype(BF16), upstream).astype(BF16)
    sg_ref[0, :, 2 * width :] = jnp.broadcast_to(selector, (n_exp, LANES)).astype(BF16)


def gelu_both(pre):
    square = pre * pre
    half = jnp.tanh(GELU_C * pre * (1.0 + GELU_A * square))
    both = 0.5 * (1.0 + half)
    slope = both + 0.5 * pre * (1.0 - half * half) * (GELU_C * (1.0 + 3.0 * GELU_A * square))
    return pre * both, slope


def expert_kernel(
    sg_ref, wu_ref, wd_ref, ua_ref, ub_ref, da_ref, db_ref, out_ref,
    u1_ref, gu2_ref, acc_y, acc_s, acc_u2, acc_gu1,
):
    step = pl.program_id(1)
    width = wu_ref.shape[1]
    selector = sg_ref[0, :, 2 * width :].astype(F32)

    @pl.when(step == 0)
    def _():
        u1_ref[...] = (
            dot(sg_ref[0, :, :width], ua_ref[0]).astype(BF16).astype(F32) * selector
        ).astype(BF16)
        gu2_ref[...] = (dot(sg_ref[0, :, width : 2 * width], db_ref[0], NT) * selector).astype(BF16)
        acc_y[...] = jnp.zeros_like(acc_y)
        acc_s[...] = jnp.zeros_like(acc_s)
        acc_u2[...] = jnp.zeros_like(acc_u2)
        acc_gu1[...] = jnp.zeros_like(acc_gu1)

    pre = dot(sg_ref[0, :, :width], wu_ref[0]) + dot(u1_ref[...], ub_ref[0])
    ghid = dot(sg_ref[0, :, width : 2 * width], wd_ref[0], NT) + dot(gu2_ref[...], da_ref[0], NT)
    hidden, slope = gelu_both(pre)
    hidden = hidden.astype(BF16)
    gpre = (slope * ghid).astype(BF16)
    acc_y[...] += dot(hidden, wd_ref[0])
    acc_u2[...] += dot(hidden, da_ref[0])
    acc_s[...] += dot(gpre, wu_ref[0], NT)
    acc_gu1[...] += dot(gpre, ub_ref[0], NT)

    @pl.when(step == pl.num_programs(1) - 1)
    def _():
        u2 = (acc_u2[...].astype(BF16).astype(F32) * selector).astype(BF16)
        gu1 = (acc_gu1[...] * selector).astype(BF16)
        out_ref[0, :, :width] = (acc_y[...] + dot(u2, db_ref[0])).astype(BF16)
        out_ref[0, :, width:] = (acc_s[...] + dot(gu1, ua_ref[0], NT)).astype(BF16)


def expert_grad_kernel(
    sg_ref, wu_ref, wd_ref, ua_ref, ub_ref, da_ref, db_ref,
    gua_ref, gub_ref, gda_ref, gdb_ref, u1_ref, gu2_ref, acc_u2, acc_gu1,
):
    step = pl.program_id(1)
    width = wu_ref.shape[1]
    selector = sg_ref[0, :, 2 * width :].astype(F32)

    @pl.when(step == 0)
    def _():
        u1_ref[...] = (
            dot(sg_ref[0, :, :width], ua_ref[0]).astype(BF16).astype(F32) * selector
        ).astype(BF16)
        gu2_ref[...] = (dot(sg_ref[0, :, width : 2 * width], db_ref[0], NT) * selector).astype(BF16)
        acc_u2[...] = jnp.zeros_like(acc_u2)
        acc_gu1[...] = jnp.zeros_like(acc_gu1)

    pre = dot(sg_ref[0, :, :width], wu_ref[0]) + dot(u1_ref[...], ub_ref[0])
    ghid = dot(sg_ref[0, :, width : 2 * width], wd_ref[0], NT) + dot(gu2_ref[...], da_ref[0], NT)
    hidden, slope = gelu_both(pre)
    hidden = hidden.astype(BF16)
    gpre = (slope * ghid).astype(BF16)
    gub_ref[0] = dot(u1_ref[...], gpre, TN)
    gda_ref[0] = dot(hidden, gu2_ref[...], TN)
    acc_u2[...] += dot(hidden, da_ref[0])
    acc_gu1[...] += dot(gpre, ub_ref[0], NT)

    @pl.when(step == pl.num_programs(1) - 1)
    def _():
        u2 = (acc_u2[...].astype(BF16).astype(F32) * selector).astype(BF16)
        gu1 = (acc_gu1[...] * selector).astype(BF16)
        gdb_ref[0] = dot(u2, sg_ref[0, :, width : 2 * width], TN)
        gua_ref[0] = dot(sg_ref[0, :, :width], gu1, TN)


def route_back_kernel(
    n_tok, n_exp, place_ref, index_ref, count_ref, cot_ref, x2_ref, uo_ref, ur_ref, disp_ref,
    comb_ref, att0, att1, att2, ret_ref, ao_ref, bo_ref, ra_ref, wrt_ref, rb_ref, c0, c1, c2, c3,
    block_ref, gx2_ref, gatt_ref, goa_ref, gob_ref, gra_ref, grb_ref,
    wall, pad_b, acc_oa, acc_ob, acc_ra, acc_rb, sems,
):
    image = pl.program_id(0)
    width = wall.shape[0]

    @pl.when(image == 0)
    def _():
        assemble(place_ref[0], (c0, c1, c2, c3), wall, sems)
        acc_oa[...] = jnp.zeros_like(acc_oa)
        acc_ob[...] = jnp.zeros_like(acc_ob)
        acc_ra[...] = jnp.zeros_like(acc_ra)
        acc_rb[...] = jnp.zeros_like(acc_rb)

    selector = rank_row(index_ref[image])
    living = (image < count_ref[0]).astype(F32)
    upstream = pad_rows(pad_b, cot_ref[0], n_tok) * living
    upstream_low = upstream.astype(BF16)
    x2 = x2_ref[0]
    disp, comb = disp_ref[0], comb_ref[0]
    yexp, gslot = ret_ref[0, :, :width], ret_ref[0, :, width:]
    mixed = dot(comb.T.astype(BF16), yexp)
    block_ref[0] = (living * (x2 + mixed)).astype(BF16)[:n_tok]
    unit, scale = normalise(x2)
    h2 = unit.astype(BF16)
    gcomb = dot(yexp, upstream_low, NT)
    gdisp = dot(gslot, h2, NT)
    glog = (
        disp * (gdisp - jnp.sum(gdisp * disp, axis=1, keepdims=True))
        + comb * (gcomb - jnp.sum(gcomb * comb, axis=0, keepdims=True))
    ).astype(BF16)
    acc_rb[...] += dot(glog, ur_ref[0])
    pair = jnp.concatenate([disp, glog.astype(F32)], axis=0).T.astype(BF16)
    gur = (dot(pair[:, n_exp:], rb_ref[...]) * selector).astype(BF16)
    acc_ra[...] += dot(gur, h2, TN)
    below = jnp.concatenate([gslot, wrt_ref[...]], axis=0)
    gh2 = dot(pair, below) + dot(gur, ra_ref[...], NT)
    gx2 = upstream + normalise_back(unit, scale, gh2)
    gx2_ref[0] = gx2
    gbr = gx2.astype(BF16)
    acc_ob[...] += dot(uo_ref[0], gbr, TN)
    guo = (dot(gbr, bo_ref[...]) * selector).astype(BF16)
    att = jnp.concatenate([att0[0], att1[0], att2[0]], axis=1)
    acc_oa[...] += dot(guo, att, TN)
    gatt_ref[0] = (dot(gbr, wall[:, :width], NT) + dot(guo, ao_ref[...], NT)).astype(BF16)

    @pl.when(image == pl.num_programs(0) - 1)
    def _():
        goa_ref[...] = acc_oa[...].T.astype(BF16)
        gob_ref[...] = acc_ob[...].T.astype(BF16)
        gra_ref[...] = acc_ra[...].T.astype(BF16)
        grb_ref[...] = acc_rb[...].astype(BF16)


def attention_backward(qkv, gatt, n_tok):
    masks = head_mask(0.125)
    keep = head_mask(1.0)
    key_t = qkv[:, GROUP : 2 * GROUP].T
    lane = lax.broadcasted_iota(jnp.int32, (1, LANES), 1)
    gq_parts, gk_parts, gv_parts = [], [], []
    for pair in range(GROUP // LANES):
        span = slice(pair * LANES, (pair + 1) * LANES)
        q_pair, ga_pair = qkv[:, span], gatt[:, span]
        k_pair = qkv[:, GROUP + pair * LANES : GROUP + (pair + 1) * LANES]
        v_pair = qkv[:, 2 * GROUP + pair * LANES : 2 * GROUP + (pair + 1) * LANES]
        gks, gvs = [], []
        for side in range(2):
            scores = mask_tail(dot(k_pair * masks[side], q_pair, NT), n_tok)
            top = jnp.max(scores, axis=0, keepdims=True)
            powers = jnp.exp(scores - top)
            probs = powers * (1.0 / jnp.sum(powers, axis=0, keepdims=True))
            gvs.append(dot(probs.astype(BF16), ga_pair))
            gprobs = dot(v_pair * keep[side], ga_pair, NT)
            inner = jnp.sum(gprobs * probs, axis=0, keepdims=True)
            gscores = (probs * (gprobs - inner)).astype(BF16)
            gks.append(dot(gscores, q_pair))
            head = 2 * pair + side
            gq_parts.append(
                (dot(key_t[head * HEAD_DIM : (head + 1) * HEAD_DIM], gscores) * 0.125).astype(BF16)
            )
        gk_parts.append((jnp.where(lane < HEAD_DIM, gks[0], gks[1]) * 0.125).astype(BF16))
        gv_parts.append(jnp.where(lane < HEAD_DIM, gvs[0], gvs[1]).astype(BF16))
    gq = jnp.concatenate(gq_parts, axis=0).T
    return jnp.concatenate([gq] + gk_parts + gv_parts, axis=1)


def attention_back_kernel(n_tok, group, last, *refs):
    refs = list(refs)
    index_ref = refs.pop(0) if last else None
    qkv_ref, gatt_ref, uq_ref, bt_ref = refs[:4]
    refs = refs[4:]
    before_ref = refs.pop(0) if group else None
    h1_ref = refs.pop(0) if last else None
    gqkv_ref, guq_ref, gb_ref = refs[:3]
    refs = refs[3:]
    ga_ref = refs.pop(0) if last else None
    acc_b = refs.pop(0)
    acc_a = refs.pop(0) if last else None
    image = pl.program_id(0)
    width = bt_ref.shape[0] // 3

    @pl.when(image == 0)
    def _():
        acc_b[...] = jnp.zeros_like(acc_b)
        if last:
            acc_a[...] = jnp.zeros_like(acc_a)

    gqkv = attention_backward(qkv_ref[0], gatt_ref[0], n_tok)
    gqkv_ref[0] = gqkv
    acc_b[...] += dot(uq_ref[0], gqkv, TN)
    guq = dot(gqkv, group_rows(group, width, bt_ref))
    if group:
        guq = guq + before_ref[0]
    if last:
        guq = (guq * rank_row(index_ref[image])).astype(BF16)
        acc_a[...] += dot(guq, h1_ref[0], TN)
    guq_ref[0] = guq

    @pl.when(image == pl.num_programs(0) - 1)
    def _():
        gb_ref[...] = acc_b[...].T.astype(BF16)
        if last:
            ga_ref[...] = acc_a[...].T.astype(BF16)


def input_grad_kernel(
    n_tok, groups, place_ref, image_ref, gx2_ref, guq_ref, a_ref, *refs
):
    gqkv = refs[:groups]
    chunks = refs[groups : groups + 4 * groups]
    out_ref = refs[5 * groups]
    walls = refs[5 * groups + 1 : 6 * groups + 1]
    pad_a, sems = refs[6 * groups + 1 :]
    image = pl.program_id(0)

    @pl.when(image == 0)
    def _():
        for group in range(groups):
            assemble(
                place_ref[0], chunks[4 * group : 4 * group + 4], walls[group], sems.at[group]
            )

    gh1 = dot(guq_ref[0], a_ref[...], NT)
    for group in range(groups):
        gh1 = gh1 + dot(gqkv[group][0], walls[group][:, : 3 * GROUP], NT)
    unit, scale = normalise(pad_rows(pad_a, image_ref[0], n_tok))
    out_ref[0] = (gx2_ref[0] + normalise_back(unit, scale, gh1))[:n_tok]


ANY = pl.BlockSpec(memory_space=pl.ANY)


def whole(shape):
    return pl.BlockSpec(shape, lambda *_: (0,) * len(shape))


def per_image(*shape):
    return pl.BlockSpec((1,) + shape, lambda i, *_: (i,) + (0,) * len(shape))


def call(kernel, scalars, grid, inputs, outputs, scratch, flops, exps=0):
    arrays = [array for array, _ in inputs]
    shapes = [jax.ShapeDtypeStruct(shape, dtype) for shape, dtype, _ in outputs]
    moved = sum(array.size * array.dtype.itemsize for array in arrays) + sum(
        shape.size * shape.dtype.itemsize for shape in shapes
    )
    return pl.pallas_call(
        kernel,
        out_shape=shapes,
        grid_spec=pltpu.PrefetchScalarGridSpec(
            num_scalar_prefetch=len(scalars),
            grid=grid,
            in_specs=[spec for _, spec in inputs],
            out_specs=[spec for _, _, spec in outputs],
            scratch_shapes=scratch,
        ),
        compiler_params=params(*(("arbitrary",) * len(grid))),
        cost_estimate=cost(flops, moved, exps),
    )(*scalars, *arrays)


def norm_call(images, total):
    n_img, n_tok, width = images.shape
    return call(
        functools.partial(norm_kernel, n_tok), (), (n_img,),
        [(images, per_image(n_tok, width))],
        [((n_img, total, width), BF16, per_image(total, width))],
        [pltpu.VMEM((total, width), F32)],
        8 * images.size,
    )[0]


def attention_flops(n_img, total, width, parts):
    return n_img * total * (2 * width * 3 * GROUP + parts * 8 * total * HEAD_DIM)


def first_attention_call(place, index, h1, chunks, n_tok, shards):
    n_img, total, width = h1.shape
    columns = 4 * chunks[0].shape[1]
    return call(
        functools.partial(first_attention_kernel, n_tok, shards), (place, index), (n_img,),
        [(h1, per_image(total, width))] + [(chunk, ANY) for chunk in chunks],
        [
            ((n_img, total, 3 * GROUP), BF16, per_image(total, 3 * GROUP)),
            ((n_img, total, GROUP), BF16, per_image(total, GROUP)),
            ((n_img, total, LANES), BF16, per_image(total, LANES)),
            ((width, LANES), BF16, whole((width, LANES))),
            ((3 * width, LANES), BF16, whole((3 * width, LANES))),
            ((width, LANES), BF16, whole((width, LANES))),
            ((width, LANES), BF16, whole((width, LANES))),
        ],
        [pltpu.VMEM((width, columns), BF16), pltpu.SemaphoreType.DMA((4,))],
        attention_flops(n_img, total, width, 2), n_img * total * total * 4,
    )


def next_attention_call(place, h1, uq, bt, chunks, n_tok, group, extra):
    n_img, total, width = h1.shape
    columns = 4 * chunks[0].shape[1]
    return call(
        functools.partial(next_attention_kernel, n_tok, group, extra), (place,), (n_img,),
        [
            (h1, per_image(total, width)),
            (uq, per_image(total, LANES)),
            (bt, whole(bt.shape)),
        ]
        + [(chunk, ANY) for chunk in chunks],
        [
            ((n_img, total, 3 * GROUP), BF16, per_image(total, 3 * GROUP)),
            ((n_img, total, GROUP), BF16, per_image(total, GROUP)),
        ]
        + [((width, LANES), BF16, whole((width, LANES)))] * extra,
        [pltpu.VMEM((width, columns), BF16), pltpu.SemaphoreType.DMA((4,))],
        attention_flops(n_img, total, width, 2), n_img * total * total * 4,
    )


def route_call(place, index, count, images, cotangent, atts, banks, chunks, n_exp, total):
    n_img, n_tok, width = images.shape
    return call(
        functools.partial(route_kernel, n_tok, n_exp), (place, index, count), (n_img,),
        [(images, per_image(n_tok, width)), (cotangent, per_image(n_tok, width))]
        + [(att, per_image(total, GROUP)) for att in atts]
        + [(bank, whole(bank.shape)) for bank in banks]
        + [(chunk, ANY) for chunk in chunks],
        [
            ((n_img, total, width), F32, per_image(total, width)),
            ((n_img, total, LANES), BF16, per_image(total, LANES)),
            ((n_img, total, LANES), BF16, per_image(total, LANES)),
            ((n_img, n_exp, total), F32, per_image(n_exp, total)),
            ((n_img, n_exp, total), F32, per_image(n_exp, total)),
            ((n_img, n_exp, 2 * width + LANES), BF16, per_image(n_exp, 2 * width + LANES)),
            ((n_exp, width), BF16, whole((n_exp, width))),
        ],
        [
            pltpu.VMEM((width, 4 * chunks[0].shape[1]), BF16),
            pltpu.VMEM((total, width), F32),
            pltpu.VMEM((total, width), F32),
            pltpu.SemaphoreType.DMA((4,)),
        ],
        n_img * total * 2 * width * (width + 3 * LANES), n_img * total * 2 * n_exp,
    )


def hidden_tile(hidden, limit):
    tile = hidden
    while tile > limit:
        tile //= 2
    return tile


def expert_specs(rows, width, tile):
    return (
        pl.BlockSpec((1, rows, 2 * width + LANES), lambda e, f: (e, 0, 0)),
        pl.BlockSpec((1, width, tile), lambda e, f: (e, 0, f)),
        pl.BlockSpec((1, tile, width), lambda e, f: (e, f, 0)),
        pl.BlockSpec((1, width, LANES), lambda e, f: (e, 0, 0)),
        pl.BlockSpec((1, LANES, tile), lambda e, f: (e, 0, f)),
        pl.BlockSpec((1, tile, LANES), lambda e, f: (e, f, 0)),
        pl.BlockSpec((1, LANES, width), lambda e, f: (e, 0, 0)),
    )


def expert_call(sg, weights):
    n_loc, rows, _ = sg.shape
    width, hidden = weights[0].shape[1:]
    tile = hidden_tile(hidden, 768)
    return call(
        expert_kernel, (), (n_loc, hidden // tile),
        list(zip((sg,) + weights, expert_specs(rows, width, tile))),
        [((n_loc, rows, 2 * width), BF16, pl.BlockSpec((1, rows, 2 * width), lambda e, f: (e, 0, 0)))],
        [
            pltpu.VMEM((rows, LANES), BF16),
            pltpu.VMEM((rows, LANES), BF16),
            pltpu.VMEM((rows, width), F32),
            pltpu.VMEM((rows, width), F32),
            pltpu.VMEM((rows, LANES), F32),
            pltpu.VMEM((rows, LANES), F32),
        ],
        n_loc * rows * 8 * width * hidden, n_loc * rows * hidden,
    )[0]


def expert_grad_call(sg, weights):
    n_loc, rows, _ = sg.shape
    width, hidden = weights[0].shape[1:]
    tile = hidden_tile(hidden, 768 if rows <= 512 else 384)
    return call(
        expert_grad_kernel, (), (n_loc, hidden // tile),
        list(zip((sg,) + weights, expert_specs(rows, width, tile))),
        [
            ((n_loc, width, LANES), F32, pl.BlockSpec((1, width, LANES), lambda e, f: (e, 0, 0))),
            ((n_loc, LANES, hidden), F32, pl.BlockSpec((1, LANES, tile), lambda e, f: (e, 0, f))),
            ((n_loc, hidden, LANES), F32, pl.BlockSpec((1, tile, LANES), lambda e, f: (e, f, 0))),
            ((n_loc, LANES, width), F32, pl.BlockSpec((1, LANES, width), lambda e, f: (e, 0, 0))),
        ],
        [
            pltpu.VMEM((rows, LANES), BF16),
            pltpu.VMEM((rows, LANES), BF16),
            pltpu.VMEM((rows, LANES), F32),
            pltpu.VMEM((rows, LANES), F32),
        ],
        n_loc * rows * 4 * width * hidden, n_loc * rows * hidden,
    )


def route_back_call(
    place, index, count, cotangent, x2, uo, ur, disp, comb, atts, ret, banks, chunks
):
    n_img, n_tok, width = cotangent.shape
    total, n_exp = x2.shape[1], disp.shape[1]
    return call(
        functools.partial(route_back_kernel, n_tok, n_exp), (place, index, count), (n_img,),
        [
            (cotangent, per_image(n_tok, width)),
            (x2, per_image(total, width)),
            (uo, per_image(total, LANES)),
            (ur, per_image(total, LANES)),
            (disp, per_image(n_exp, total)),
            (comb, per_image(n_exp, total)),
        ]
        + [(att, per_image(total, GROUP)) for att in atts]
        + [(ret, per_image(n_exp, 2 * width))]
        + [(bank, whole(bank.shape)) for bank in banks]
        + [(chunk, ANY) for chunk in chunks],
        [
            ((n_img, n_tok, width), BF16, per_image(n_tok, width)),
            ((n_img, total, width), F32, per_image(total, width)),
            ((n_img, total, width), BF16, per_image(total, width)),
            ((width, LANES), BF16, whole((width, LANES))),
            ((width, LANES), BF16, whole((width, LANES))),
            ((width, LANES), BF16, whole((width, LANES))),
            ((n_exp, LANES), BF16, whole((n_exp, LANES))),
        ],
        [
            pltpu.VMEM((width, 4 * chunks[0].shape[1]), BF16),
            pltpu.VMEM((total, width), F32),
            pltpu.VMEM((LANES, width), F32),
            pltpu.VMEM((LANES, width), F32),
            pltpu.VMEM((LANES, width), F32),
            pltpu.VMEM((n_exp, LANES), F32),
            pltpu.SemaphoreType.DMA((4,)),
        ],
        n_img * total * 2 * width * (width + 6 * LANES),
    )


def attention_back_call(index, qkv, gatt, uq, bt, before, h1, n_tok, group):
    n_img, total, _ = qkv.shape
    width = bt.shape[0] // 3
    last = h1 is not None
    inputs = [
        (qkv, per_image(total, 3 * GROUP)),
        (gatt, pl.BlockSpec((1, total, GROUP), lambda i, *_: (i, 0, group))),
        (uq, per_image(total, LANES)),
        (bt, whole(bt.shape)),
    ]
    outputs = [
        ((n_img, total, 3 * GROUP), BF16, per_image(total, 3 * GROUP)),
        ((n_img, total, LANES), BF16 if last else F32, per_image(total, LANES)),
        ((3 * GROUP, LANES), BF16, whole((3 * GROUP, LANES))),
    ]
    scratch = [pltpu.VMEM((LANES, 3 * GROUP), F32)]
    if group:
        inputs.append((before, per_image(total, LANES)))
    if last:
        inputs.append((h1, per_image(total, width)))
        outputs.append(((width, LANES), BF16, whole((width, LANES))))
        scratch.append(pltpu.VMEM((LANES, width), F32))
    return call(
        functools.partial(attention_back_kernel, n_tok, group, last),
        (index,) if last else (), (n_img,), inputs, outputs, scratch,
        attention_flops(n_img, total, LANES, 5), n_img * total * total * 4,
    )


def input_grad_call(place, images, gx2, guq, bank_a, gqkvs, packs):
    n_img, n_tok, width = images.shape
    total = gx2.shape[1]
    groups = len(gqkvs)
    return call(
        functools.partial(input_grad_kernel, n_tok, groups), (place,), (n_img,),
        [
            (images, per_image(n_tok, width)),
            (gx2, per_image(total, width)),
            (guq, per_image(total, LANES)),
            (bank_a, whole(bank_a.shape)),
        ]
        + [(gqkv, per_image(total, 3 * GROUP)) for gqkv in gqkvs]
        + [(chunk, ANY) for pack in packs for chunk in pack],
        [((n_img, n_tok, width), F32, per_image(n_tok, width))],
        [pltpu.VMEM((width, 4 * pack[0].shape[1]), BF16) for pack in packs]
        + [pltpu.VMEM((total, width), F32), pltpu.SemaphoreType.DMA((groups, 4))],
        n_img * total * 2 * width * (3 * width + LANES),
    )[0]


def swap(array, axis, size, bit):
    return lax.ppermute(array, axis, [(i, i ^ bit) for i in range(size)])


def gather_pack(pack, shards, replicas, quarter):
    rows, columns = pack.shape
    part = columns // 4
    mine = lax.dynamic_slice(pack, (0, quarter * part), (rows, part))
    spread = jnp.broadcast_to(mine[None], (shards, rows, part))
    own = lax.all_to_all(spread, "shard", split_axis=0, concat_axis=0, tiled=True)
    own = own.reshape(shards * rows, part)
    over_y = swap(own, "replica", replicas, 2)
    return own, swap(own, "replica", replicas, 1), over_y, swap(over_y, "replica", replicas, 1)


def reduce_pack(pack, replicas):
    where = lax.axis_index("replica")
    bits = []
    bit = 1
    while bit < replicas:
        half = pack.shape[1] // 2
        side = (where // bit) % 2
        keep = lax.dynamic_slice_in_dim(pack, side * half, half, axis=1)
        give = lax.dynamic_slice_in_dim(pack, (1 - side) * half, half, axis=1)
        got = swap(give, "replica", replicas, bit)
        pack = (keep.astype(F32) + got.astype(F32)).astype(BF16)
        bits.append(bit)
        bit *= 2
    landed = lax.all_to_all(pack, "shard", split_axis=0, concat_axis=0, tiled=True)
    total = jnp.sum(landed.astype(F32), axis=0).astype(BF16)
    for bit in reversed(bits):
        got = swap(total, "replica", replicas, bit)
        side = (where // bit) % 2
        total = jnp.where(
            side == 0,
            jnp.concatenate([total, got], axis=0),
            jnp.concatenate([got, total], axis=0),
        )
    return total


def per_device(
    replicas,
    shards,
    images,
    image_adapter_index,
    device_image_count,
    cotangent,
    query_key_value_weight,
    frozen_output_weight,
    frozen_dispatch_weight,
    query_key_value_first,
    query_key_value_second,
    output_adapter_first,
    output_adapter_second,
    dispatch_adapter_first,
    dispatch_adapter_second,
    frozen_up_weight,
    frozen_down_weight,
    up_adapter_first,
    up_adapter_second,
    down_adapter_first,
    down_adapter_second,
):
    n_img, n_tok, width = images.shape
    total = -(-n_tok // 16) * 16
    rows = width // shards
    n_loc = frozen_up_weight.shape[0]
    n_exp = n_loc * shards
    groups = width // GROUP
    quarter = lax.axis_index("replica") % 4
    place = quarter.astype(jnp.int32).reshape(1)

    def qkv_columns(group):
        return [
            query_key_value_weight[:, part * width + group * GROUP : part * width + (group + 1) * GROUP]
            for part in range(3)
        ]

    second_t = query_key_value_second.T.reshape(3, rows, LANES)
    route_block = jnp.concatenate(
        [
            frozen_dispatch_weight,
            jnp.zeros((rows, 64 - n_exp), BF16),
            jnp.pad(dispatch_adapter_second.T.reshape(16, n_loc * 8), ((0, rows - 16), (0, 0))),
            jnp.zeros((rows, 64 - n_loc * 8), BF16),
        ],
        axis=1,
    )
    empty = jnp.zeros((rows, LANES), BF16)
    packs = [
        qkv_columns(0)
        + [query_key_value_first, second_t[0], second_t[1], second_t[2], output_adapter_first, dispatch_adapter_first],
        qkv_columns(1) + [output_adapter_second.T, route_block],
        qkv_columns(2) + [empty, empty],
        [frozen_output_weight, empty, empty],
    ]
    packs = [jnp.concatenate(pack, axis=1) for pack in packs]
    packs = [gather_pack(pack, shards, replicas, quarter) for pack in packs]

    h1 = norm_call(images, total)
    qkv0, att0, uq, bank_a, bank_bt, bank_ao, bank_ra = first_attention_call(
        place, image_adapter_index, h1, packs[0], n_tok, shards
    )
    qkv1, att1, bank_bo, bank_wr = next_attention_call(place, h1, uq, bank_bt, packs[1], n_tok, 1, 2)
    qkv2, att2 = next_attention_call(place, h1, uq, bank_bt, packs[2], n_tok, 2, 0)
    atts = (att0, att1, att2)
    bank_rb = bank_wr.reshape(shards, rows, LANES)[:, :16, 64 : 64 + n_loc * 8].reshape(n_exp, LANES)
    x2, uo, ur, disp, comb, sg, bank_wrt = route_call(
        place, image_adapter_index, device_image_count, images, cotangent, atts,
        (bank_ao, bank_bo, bank_ra, bank_wr, bank_rb), packs[3], n_exp, total,
    )

    sent = sg.reshape(n_img, shards, n_loc, -1).transpose(1, 2, 0, 3)
    landed = lax.all_to_all(sent, "shard", split_axis=0, concat_axis=0, tiled=True)
    landed = landed.transpose(1, 0, 2, 3).reshape(n_loc, shards * n_img, -1)
    weights = (
        frozen_up_weight, frozen_down_weight, up_adapter_first, up_adapter_second,
        down_adapter_first, down_adapter_second,
    )
    ret = expert_call(landed, weights)
    every = landed
    bit = replicas // 2
    while bit:
        every = jnp.concatenate([every, swap(every, "replica", replicas, bit)], axis=1)
        bit //= 2
    back = ret.reshape(n_loc, shards, n_img, 2 * width).transpose(1, 0, 2, 3)
    back = lax.all_to_all(back, "shard", split_axis=0, concat_axis=0, tiled=True)
    back = back.transpose(2, 0, 1, 3).reshape(n_img, n_exp, 2 * width)
    grad_up_a, grad_up_b, grad_down_a, grad_down_b = expert_grad_call(every, weights)

    block_out, gx2, gatt, goa, gob, gra, grb = route_back_call(
        place, image_adapter_index, device_image_count, cotangent, x2, uo, ur, disp, comb, atts, back,
        (bank_ao, bank_bo, bank_ra, bank_wrt, bank_rb), packs[3],
    )
    fill = -(3 * rows + n_loc) % (8 * replicas)
    out_pack = jnp.concatenate(
        [
            goa.reshape(shards, rows, LANES),
            gob.reshape(shards, rows, LANES),
            gra.reshape(shards, rows, LANES),
            grb.reshape(shards, n_loc, LANES),
            jnp.zeros((shards, fill, LANES), BF16),
        ],
        axis=1,
    )
    out_sum = reduce_pack(out_pack, replicas).astype(F32)

    gqkv0, guq, gb0 = attention_back_call(None, qkv0, gatt, uq, bank_bt, None, None, n_tok, 0)
    gqkv1, guq, gb1 = attention_back_call(None, qkv1, gatt, uq, bank_bt, guq, None, n_tok, 1)
    gqkv2, guq, gb2, gqa = attention_back_call(
        image_adapter_index, qkv2, gatt, uq, bank_bt, guq, h1, n_tok, 2
    )
    gbt = jnp.concatenate(
        [gb[part * GROUP : (part + 1) * GROUP] for part in range(3) for gb in (gb0, gb1, gb2)], axis=0
    )
    qkv_pack = jnp.concatenate(
        [gbt.reshape(shards, 3 * rows, LANES), gqa.reshape(shards, rows, LANES)], axis=1
    )
    qkv_sum = reduce_pack(qkv_pack, replicas).astype(F32)
    input_grad = input_grad_call(
        place, images, gx2, guq, bank_a, (gqkv0, gqkv1, gqkv2), packs[:3]
    )
    return (
        block_out,
        input_grad,
        qkv_sum[3 * rows :],
        qkv_sum[: 3 * rows].T,
        out_sum[:rows],
        out_sum[rows : 2 * rows].T,
        out_sum[2 * rows : 3 * rows],
        out_sum[3 * rows : 3 * rows + n_loc].T,
        grad_up_a,
        grad_up_b,
        grad_down_a,
        grad_down_b,
    )


def solution(mesh):
    images = P(("replica", "shard"), None, None)
    each = P(("replica", "shard"))
    by_row, by_column, by_expert = P("shard", None), P(None, "shard"), P("shard", None, None)
    in_specs = (
        (images, each, each, images)
        + (by_row, by_row, by_row)
        + (by_row, by_column) * 3
        + (by_expert,) * 6
    )
    out_specs = (images, images) + (by_row, by_column) * 3 + (by_expert,) * 4
    return jax.shard_map(
        functools.partial(per_device, mesh.shape["replica"], mesh.shape["shard"]),
        mesh=mesh,
        in_specs=in_specs,
        out_specs=out_specs,
        check_vma=False,
    )
```

time: 899 us -> 411 us (0.46)
  waiting for transfers between devices: 356 us -> 61.8 us
  Pallas kernels: 0 us -> 220 us
  matrix products: 207 us -> 0 us
  blocking collectives: 181 us -> 17.5 us
  other arithmetic: 52.5 us -> 6.2 us
  starting transfers between devices: 25.7 us -> 59.9 us
  between operations: 16.7 us -> 1.81 us
  local copies, waits for them, and re-layouts: 54.4 us -> 41.1 us
    reduce_scatter x5 -> x0, waiting for transfers between devices: 256 us -> none  [the longest x1 63.8 us: per_device(): lax.psum_scatter(grad_out_a.astype(jnp.bfloat16), 'shard', scatter_dimens...]
    pallas_call x0 -> x12, Pallas kernels: none -> 220 us  [call(): pl.pallas_call(kernel, out_shape=shapes, grid_spec=pltpu.PrefetchScalarGr...]
    dot_general x50 -> x0, matrix products: 190 us -> none  [the longest x9 37.5 us: project_back(): jnp.einsum('btk,dk->btd', left, right, preferred_element_type=jnp.float32)]
    all_gather x7 -> x0, blocking collectives: 166 us -> none  [the longest x1 25.3 us: per_device(): lax.all_gather(shared[3], 'shard', axis=0, tiled=True)]
    psum x2 -> x0, waiting for transfers between devices: 94.6 us -> none  [the longest x1 80.8 us: per_device(): lax.psum(owned[3].astype(jnp.bfloat16), 'replica').astype(jnp.float32)]
    convert_element_type x15 -> x6, other arithmetic: 36.7 us -> 1.8 us  [the longest x4 1.77 us: reduce_pack(): pack = (keep.astype(F32) + got.astype(F32)).astype(BF16)]
    all_to_all x5 -> x7, waiting for transfers between devices: 4 us -> 35.9 us  [the longest x4 33.3 us: gather_pack(): lax.all_to_all(spread, 'shard', split_axis=0, concat_axis=0, tiled=True)]
    ppermute x0 -> x22, waiting for transfers between devices: none -> 26 us  [swap(): return lax.ppermute(array, axis, [(i, i ^ bit) for i in range(size)])]
  transfers between devices with their start and end apart: 14 -> 29, of which waited for: 10 -> 11; matrix products, arithmetic and copies ran while one was open for 23% -> 7% of each run, Pallas kernels for 0% -> 45%
where the time goes in v1:
time: 411 us; the launch traced here: 408 us
  Pallas kernels  220 us (54%)
  waiting for transfers between devices  61.8 us (15%)
  starting transfers between devices  59.9 us (15%)
  local copies, waits for them, and re-layouts  41.1 us (10%)
  blocking collectives  17.5 us (4%)
  other arithmetic  6.2 us (2%)
    pallas_call x12, Pallas kernels, call(): pl.pallas_call(kernel, out_shape=shapes, grid_spec=pltpu.PrefetchScalarGr...  220 us
    all_to_all x4, waiting for transfers between devices, gather_pack(): lax.all_to_all(spread, 'shard', split_axis=0, concat_axis=0, tiled=True)  33.3 us
    ppermute x22, waiting for transfers between devices, swap(): return lax.ppermute(array, axis, [(i, i ^ bit) for i in range(size)])  26 us
    ppermute x22, starting transfers between devices, swap(): return lax.ppermute(array, axis, [(i, i ^ bit) for i in range(size)])  23.8 us
    all_to_all x4, starting transfers between devices, gather_pack(): lax.all_to_all(spread, 'shard', split_axis=0, concat_axis=0, tiled=True)  23.5 us
    unnamed x58, local copies, waits for them, and re-layouts  20.3 us
    all_to_all x1, blocking collectives, per_device(): lax.all_to_all(sent, 'shard', split_axis=0, concat_axis=0, tiled=True)  17.5 us
    all_to_all x2, starting transfers between devices, reduce_pack(): lax.all_to_all(pack, 'shard', split_axis=0, concat_axis=0, tiled=True)  8.58 us
  transfers between devices with their start and end apart: 29, of which 11 were waited for; matrix products, arithmetic and copies ran while one was open for 7% of the time, Pallas kernels for 45%

profile of v1, /device:TPU:1, one launch (start us, length us, event | category | flops | bytes accessed | tf_op | source)
XLA Modules:
  0.0 408.3 jit_solution(10539644866144785862)
XLA Ops:
  2.3 1.6 fusion.7
  7.1 6.4 %all-to-all-start.1 = ((bf16[8,96,256]{2,1,0:T(8,128)(2,1)}), bf16[8,96,256]{2,1,0:T(8,128)(2,1)S(1)}, u32[]{:S(2)}, u32[]{:S(2)}) async-start(bf16[8,96,256]{2,1,0:T(8,128)(2,1)} %broadcast_in_dim.11), calls=%async_computation.1 | async-start | bytes 786432 | tf_op jit(solution)/shard_map/all_to_all | solution.py:738
  13.7 8.9 %all-to-all-done.1 = bf16[8,96,256]{2,1,0:T(8,128)(2,1)S(1)} async-done(((bf16[8,96,256]{2,1,0:T(8,128)(2,1)}), bf16[8,96,256]{2,1,0:T(8,128)(2,1)S(1)}, u32[]{:S(2)}, u32[]{:S(2)}) %all-to-all-start.1) | async-done | bytes 393248 | tf_op jit(solution)/shard_map/all_to_all | solution.py:738
  23.5 6.1 %all-to-all-start = ((bf16[8,96,384]{2,1,0:T(8,128)(2,1)}), bf16[8,96,384]{2,1,0:T(8,128)(2,1)S(1)}, u32[]{:S(2)}, u32[]{:S(2)}) async-start(bf16[8,96,384]{2,1,0:T(8,128)(2,1)} %broadcast_in_dim.10), calls=%async_computation | async-start | bytes 1179648 | tf_op jit(solution)/shard_map/all_to_all | solution.py:738
  30.5 13.6 %all-to-all-done = bf16[8,96,384]{2,1,0:T(8,128)(2,1)S(1)} async-done(((bf16[8,96,384]{2,1,0:T(8,128)(2,1)}), bf16[8,96,384]{2,1,0:T(8,128)(2,1)S(1)}, u32[]{:S(2)}, u32[]{:S(2)}) %all-to-all-start) | async-done | bytes 589856 | tf_op jit(solution)/shard_map/all_to_all | solution.py:738
  45.0 5.2 %all-to-all-start.2 = ((bf16[8,96,256]{2,1,0:T(8,128)(2,1)}), bf16[8,96,256]{2,1,0:T(8,128)(2,1)}, u32[]{:S(2)}, u32[]{:S(2)}) async-start(bf16[8,96,256]{2,1,0:T(8,128)(2,1)} %broadcast_in_dim.12), calls=%async_computation.2 | async-start | bytes 786432 | tf_op jit(solution)/shard_map/all_to_all | solution.py:738
  50.1 1.2 collective-permute-start.1
  52.2 7.0 %all-to-all-done.2 = bf16[8,96,256]{2,1,0:T(8,128)(2,1)} async-done(((bf16[8,96,256]{2,1,0:T(8,128)(2,1)}), bf16[8,96,256]{2,1,0:T(8,128)(2,1)}, u32[]{:S(2)}, u32[]{:S(2)}) %all-to-all-start.2) | async-done | bytes 393248 | tf_op jit(solution)/shard_map/all_to_all | solution.py:738
  59.9 5.9 %all-to-all-start.3 = ((bf16[8,96,256]{2,1,0:T(8,128)(2,1)}), bf16[8,96,256]{2,1,0:T(8,128)(2,1)}, u32[]{:S(2)}, u32[]{:S(2)}) async-start(bf16[8,96,256]{2,1,0:T(8,128)(2,1)} %broadcast_in_dim.13), calls=%async_computation.3 | async-start | bytes 786432 | tf_op jit(solution)/shard_map/all_to_all | solution.py:738
  65.8 2.1 collective-permute-start
  70.4 3.8 all-to-all-done.3
  74.2 4.2 %collective-permute-done.4.c2.refs_9_ = bf16[768,256]{1,0:T(8,128)(2,1)} collective-permute-done((bf16[768,256]{1,0:T(8,128)(2,1)S(1)}, bf16[768,256]{1,0:T(8,128)(2,1)}, u32[]{:S(2)}, u32[]{:S(2)}) %collective-permute-start.4) | collective-permute-done | bytes 393248 | tf_op jit(solution)/shard_map/ppermute | solution.py:730
  79.6 7.2 %collective-permute-done.7.c2.refs_13_ = bf16[768,256]{1,0:T(8,128)(2,1)} collective-permute-done((bf16[768,256]{1,0:T(8,128)(2,1)}, bf16[768,256]{1,0:T(8,128)(2,1)}, u32[]{:S(2)}, u32[]{:S(2)}) %collective-permute-start.7) | collective-permute-done | bytes 393248 | tf_op jit(solution)/shard_map/ppermute | solution.py:730
  86.7 2.1 collective-permute-start.5
  89.5 1.9 copy.49.cot_ref
  91.5 1.9 copy.43.image_ref
  93.4 6.7 %shard_map.274.h1_ref.refs_6_ = bf16[8,208,768]{2,1,0:T(8,128)(2,1)} custom-call(bf16[8,197,768]{2,1,0:T(8,128)(2,1)} %copy.43.image_ref), custom_call_target="tpu_custom_call" | custom-call | flops 9682944 | bytes 4976640 | tf_op jit(solution)/shard_map/pallas_call | solution.py:478
  100.6 15.9 %shard_map.275 = (bf16[8,208,768]{2,1,0:T(8,128)(2,1)}, bf16[8,208,256]{2,1,0:T(8,128)(2,1)}, bf16[8,208,128]{2,1,0:T(8,128)(2,1)}, bf16[768,128]{1,0:T(8,128)(2...) custom-call(s32[1]{0:T(128)} %bitcast.place_ref, s32[8]{0:T(128)} %refs_0_.1, ...), custom_call_target="tpu_custom_call" | custom-call | flops 2317352960 | bytes 9928704 | tf_op jit(solution)/shard_map/pallas_call | solution.py:478
  117.8 15.5 %shard_map.276 = (bf16[8,208,768]{2,1,0:T(8,128)(2,1)}, bf16[8,208,256]{2,1,0:T(8,128)(2,1)}, bf16[768,128]{1,0:T(8,128)(2,1)}, bf16[768,128]{1,0:T(8,128)(2,1)}) custom-call(s32[1]{0:T(128)} %bitcast.place_ref, bf16[8,208,768]{2,1,0:T(8,128)(2,1)} %shard_map.274.h1_ref.refs_6_, bf16[8,208,128]{2,1,0:T(8,128)(2,1)} %get-tuple-element.54.uq_ref.refs_2_.refs_3_, ...), custom_call_target="tpu_custom_call" | custom-call | flops 2317352960 | bytes 8945664 | tf_op jit(solution)/shard_map/pallas_call | solution.py:478
  136.4 15.5 %shard_map.277 = (bf16[8,208,768]{2,1,0:T(8,128)(2,1)}, bf16[8,208,256]{2,1,0:T(8,128)(2,1)}) custom-call(s32[1]{0:T(128)} %bitcast.place_ref, bf16[8,208,768]{2,1,0:T(8,128)(2,1)} %shard_map.274.h1_ref.refs_6_, bf16[8,208,128]{2,1,0:T(8,128)(2,1)} %get-tuple-element.54.uq_ref.refs_2_.refs_3_, bf16[2304,128]{1,0:T(8,128)(2,1)} %get-tuple-element.55.bt_ref.refs_3_.refs_4_, ...), custom_call_target="tpu_custom_call" | custom-call | flops 2317352960 | bytes 8552448 | tf_op jit(solution)/shard_map/pallas_call | solution.py:478
  152.9 19.2 %shard_map.278 = (f32[8,208,768]{2,1,0:T(8,128)}, bf16[8,208,128]{2,1,0:T(8,128)(2,1)}, bf16[8,208,128]{2,1,0:T(8,128)(2,1)}, f32[8,16,208]{2,1,0:T(8,128)}, f32...) custom-call(s32[1]{0:T(128)} %bitcast.place_ref, s32[8]{0:T(128)} %refs_0_.1, ...), custom_call_target="tpu_custom_call" | custom-call | flops 2944401408 | bytes 16388096 | tf_op jit(solution)/shard_map/pallas_call | solution.py:478
  173.2 17.5 %all_to_all.40 = bf16[8,2,8,1664]{3,2,1,0:T(8,128)(2,1)S(1)} all-to-all(bf16[8,2,8,1664]{3,2,1,0:T(8,128)(2,1)S(1)} %bitcast.40), channel_id=1, replica_groups=mesh['replica'=4,'shard'=8] {'shard'}, dimensions={0} | all-to-all | bytes 851968 | tf_op jit(solution)/shard_map/all_to_all | solution.py:843
  191.5 16.0 %shard_map.279 = bf16[2,64,1536]{2,1,0:T(8,128)(2,1)} custom-call(bf16[2,64,1664]{2,1,0:T(8,128)(2,1)} %copy_bitcast_fusion.sg_ref, bf16[2,768,3072]{2,1,0:T(8,128)(2,1)} %wu_ref.3, bf16[2,3072,768]{2,1,0:T(8,128)(2,1)} %wd_ref.3, bf16[2,768,128]{2,1,0:T(8,128)(2,1)} %ua_ref.3, bf16[2,128,3072]{2,1,0:T(8,128)(2,1)} %ub_ref.3, bf16[2,3072,128]{2,1,0:T(8,128)(2,1)} %da_ref.3, ...), custom_call_target="tpu_custom_call" | custom-call | flops 2415919104 | bytes 23625728 | tf_op jit(solution)/shard_map/pallas_call | solution.py:478
  207.5 2.2 copy.56
  209.7 4.0 all-to-all-start.5
  213.7 1.3 collective-permute-start.20
  215.0 9.0 %collective-permute-done.20 = bf16[2,64,1664]{2,1,0:T(8,128)(2,1)S(1)} collective-permute-done((bf16[2,64,1664]{2,1,0:T(8,128)(2,1)S(1)}, bf16[2,64,1664]{2,1,0:T(8,128)(2,1)S(1)}, u32[]{:S(2)}, u32[]{:S(2)}) %collective-permute-start.20) | collective-permute-done | bytes 426016 | tf_op jit(solution)/shard_map/ppermute | solution.py:730
  224.1 2.0 collective-permute-start.21
  227.3 26.7 %shard_map.280 = (bf16[8,197,768]{2,1,0:T(8,128)(2,1)}, f32[8,208,768]{2,1,0:T(8,128)}, bf16[8,208,768]{2,1,0:T(8,128)(2,1)}, bf16[768,128]{1,0:T(8,128)(2,1)}, ...) custom-call(s32[1]{0:T(128)} %bitcast.place_ref, s32[8]{0:T(128)} %refs_0_.1, ...), custom_call_target="tpu_custom_call" | custom-call | flops 3925868544 | bytes 24420352 | tf_op jit(solution)/shard_map/pallas_call | solution.py:478
  254.0 20.5 %shard_map.281 = (bf16[8,208,768]{2,1,0:T(8,128)(2,1)}, f32[8,208,128]{2,1,0:T(8,128)}, bf16[768,128]{1,0:T(8,128)(2,1)}) custom-call(bf16[8,208,768]{2,1,0:T(8,128)(2,1)} %get-tuple-element.74.refs_0_, bf16[8,208,768]{2,1,0:T(8,128)(2,1)} %get-tuple-element.72.refs_1_.refs_2_, bf16[8,208,128]{2,1,0:T(8,128)(2,1)} %get-tuple-element.54.uq_ref.refs_2_.refs_3_, ...), custom_call_target="tpu_custom_call" | custom-call | flops 1213202432 | bytes 9732096 | tf_op jit(solution)/shard_map/pallas_call | solution.py:478
  275.4 20.6 %shard_map.282 = (bf16[8,208,768]{2,1,0:T(8,128)(2,1)}, f32[8,208,128]{2,1,0:T(8,128)}, bf16[768,128]{1,0:T(8,128)(2,1)}) custom-call(bf16[8,208,768]{2,1,0:T(8,128)(2,1)} %get-tuple-element.73.refs_0_, bf16[8,208,768]{2,1,0:T(8,128)(2,1)} %get-tuple-element.72.refs_1_.refs_2_, bf16[8,208,128]{2,1,0:T(8,128)(2,1)} %get-tuple-element.54.uq_ref.refs_2_.refs_3_, ...), custom_call_target="tpu_custom_call" | custom-call | flops 1213202432 | bytes 10584064 | tf_op jit(solution)/shard_map/pallas_call | solution.py:478
  296.0 22.4 %shard_map.283 = (bf16[8,208,768]{2,1,0:T(8,128)(2,1)}, bf16[8,208,128]{2,1,0:T(8,128)(2,1)}, bf16[768,128]{1,0:T(8,128)(2,1)}, bf16[768,128]{1,0:T(8,128)(2,1)}) custom-call(s32[8]{0:T(128)} %refs_0_.1, bf16[8,208,768]{2,1,0:T(8,128)(2,1)} %get-tuple-element.71.refs_1_, bf16[8,208,768]{2,1,0:T(8,128)(2,1)} %get-tuple-element.72.refs_1_.refs_2_, ...), custom_call_target="tpu_custom_call" | custom-call | flops 1213202432 | bytes 12910592 | tf_op jit(solution)/shard_map/pallas_call | solution.py:478
  323.2 3.2 concatenate.62
  326.5 19.6 %shard_map.284 = f32[8,197,768]{2,1,0:T(8,128)} custom-call(s32[1]{0:T(128)} %bitcast.place_ref, bf16[8,197,768]{2,1,0:T(8,128)(2,1)} %copy.43.image_ref, f32[8,208,768]{2,1,0:T(8,128)} %get-tuple-element.70.gx2_ref, bf16[8,208,128]{2,1,0:T(8,128)(2,1)} %get-tuple-element.77.guq_ref, bf16[768,128]{1,0:T(8,128)(2,1)} %get-tuple-element.78.a_ref, ...), custom_call_target="tpu_custom_call" | custom-call | flops 6215958528 | bytes 26169344 | tf_op jit(solution)/shard_map/pallas_call | solution.py:478
  346.1 1.9 copy.51
  347.9 6.2 %copy.52 = f32[8,197,768]{2,0,1:T(8,128)} copy(f32[8,197,768]{2,1,0:T(8,128)} %shard_map.284) | data formatting | bytes 9682944
  354.3 1.3 collective-permute-start.17
  355.8 3.8 collective-permute-done.17
  360.4 5.2 %all-to-all-start.7 = ((bf16[8,80,128]{2,1,0:T(8,128)(2,1)}), bf16[8,80,128]{2,1,0:T(8,128)(2,1)S(1)}, u32[]{:S(2)}, u32[]{:S(2)}) async-start(bf16[8,80,128]{2,1,0:T(8,128)(2,1)} %add_convert_fusion.3), calls=%async_computation.7 | async-start | bytes 327680 | tf_op jit(solution)/shard_map/all_to_all | solution.py:757
  365.6 1.3 collective-permute-start.13
  366.9 2.5 pad_maximum_fusion.sg_ref
  369.4 2.6 all-to-all-done.7
  372.0 1.3 collective-permute-start.18
  374.1 3.4 all-to-all-start.6
  377.5 3.1 collective-permute-start.19
  380.6 21.4 %shard_map.285 = (f32[2,768,128]{2,1,0:T(8,128)}, f32[2,128,3072]{2,1,0:T(8,128)}, f32[2,3072,128]{2,1,0:T(8,128)}, f32[2,128,768]{2,1,0:T(8,128)}) custom-call(bf16[2,256,1664]{2,1,0:T(8,128)(2,1)} %pad_maximum_fusion.sg_ref, bf16[2,768,3072]{2,1,0:T(8,128)(2,1)} %wu_ref.3, bf16[2,3072,768]{2,1,0:T(8,128)(2,1)} %wd_ref.3, bf16[2,768,128]{2,1,0:T(8,128)(2,1)} %ua_ref.3, ...), custom_call_target="tpu_custom_call" | custom-call | flops 4831838208 | bytes 32374784 | tf_op jit(solution)/shard_map/pallas_call | solution.py:478
  403.4 1.4 collective-permute-done.14
  404.8 1.3 collective-permute-start.15
  (127 shorter events, 33.0 us)
Async XLA Ops:
  0.6 12.8 %copy-start.13 = (bf16[96,128]{1,0:T(8,128)(2,1)S(1)}, bf16[96,128]{1,0:T(8,128)(2,1)}, u32[]{:S(2)}) copy-start(bf16[96,128]{1,0:T(8,128)(2,1)} %param.26) | copy-start | bytes 73732
  0.7 12.9 %copy-start.12 = (bf16[128,288]{0,1:T(8,128)(2,1)S(1)}, bf16[128,288]{0,1:T(8,128)(2,1)}, u32[]{:S(2)}) copy-start(bf16[128,288]{0,1:T(8,128)(2,1)} %param.27) | copy-start | bytes 221188
  0.7 12.9 %copy-start.14 = (bf16[96,128]{1,0:T(8,128)(2,1)S(1)}, bf16[96,128]{1,0:T(8,128)(2,1)}, u32[]{:S(2)}) copy-start(bf16[96,128]{1,0:T(8,128)(2,1)} %param.28) | copy-start | bytes 73732
  0.7 12.9 %copy-start.15 = (bf16[96,128]{1,0:T(8,128)(2,1)S(1)}, bf16[96,128]{1,0:T(8,128)(2,1)}, u32[]{:S(2)}) copy-start(bf16[96,128]{1,0:T(8,128)(2,1)} %param.30) | copy-start | bytes 73732
  7.1 15.5 %all-to-all-start.1 = ((bf16[8,96,256]{2,1,0:T(8,128)(2,1)}), bf16[8,96,256]{2,1,0:T(8,128)(2,1)S(1)}, u32[]{:S(2)}, u32[]{:S(2)}) async-start(bf16[8,96,256]{2,1,0:T(8,128)(2,1)} %broadcast_in_dim.11), calls=%async_computation.1 | async-start | bytes 786432 | tf_op jit(solution)/shard_map/all_to_all | solution.py:738
  13.5 76.0 %copy-start.2 = (bf16[8,197,768]{2,0,1:T(8,128)(2,1)S(1)}, bf16[8,197,768]{2,0,1:T(8,128)(2,1)}, u32[]{:S(2)}) copy-start(bf16[8,197,768]{2,0,1:T(8,128)(2,1)} %param.22) | copy-start | bytes 7262212
  22.6 68.9 %copy-start.5 = (bf16[8,96,256]{2,1,0:T(8,128)(2,1)}, bf16[8,96,256]{2,1,0:T(8,128)(2,1)S(1)}, u32[]{:S(2)}) copy-start(bf16[8,96,256]{2,1,0:T(8,128)(2,1)S(1)} %all-to-all-done.1) | copy-start | bytes 1179652
  23.5 20.6 %all-to-all-start = ((bf16[8,96,384]{2,1,0:T(8,128)(2,1)}), bf16[8,96,384]{2,1,0:T(8,128)(2,1)S(1)}, u32[]{:S(2)}, u32[]{:S(2)}) async-start(bf16[8,96,384]{2,1,0:T(8,128)(2,1)} %broadcast_in_dim.10), calls=%async_computation | async-start | bytes 1179648 | tf_op jit(solution)/shard_map/all_to_all | solution.py:738
  44.1 47.3 %copy-start.4 = (bf16[8,96,384]{2,1,0:T(8,128)(2,1)}, bf16[8,96,384]{2,1,0:T(8,128)(2,1)S(1)}, u32[]{:S(2)}) copy-start(bf16[8,96,384]{2,1,0:T(8,128)(2,1)S(1)} %all-to-all-done) | copy-start | bytes 1769476
  45.0 14.2 %all-to-all-start.2 = ((bf16[8,96,256]{2,1,0:T(8,128)(2,1)}), bf16[8,96,256]{2,1,0:T(8,128)(2,1)}, u32[]{:S(2)}, u32[]{:S(2)}) async-start(bf16[8,96,256]{2,1,0:T(8,128)(2,1)} %broadcast_in_dim.12), calls=%async_computation.2 | async-start | bytes 786432 | tf_op jit(solution)/shard_map/all_to_all | solution.py:738
  50.1 17.7 %collective-permute-start.1 = (bf16[768,384]{1,0:T(8,128)(2,1)S(1)}, bf16[768,384]{1,0:T(8,128)(2,1)}, u32[]{:S(2)}, u32[]{:S(2)}) collective-permute-start(bf16[768,384]{1,0:T(8,128)(2,1)S(1)} %bitcast.36), channel_id=1, source_target_pairs={{0,16},{8,24},{16,0},{24,8},{1,17},{9,25},{17,1},{25,9},{2,18},{10... | collective-permute-start | bytes 1769480 | tf_op jit(solution)/shard_map/ppermute | solution.py:730
  59.9 14.2 %all-to-all-start.3 = ((bf16[8,96,256]{2,1,0:T(8,128)(2,1)}), bf16[8,96,256]{2,1,0:T(8,128)(2,1)}, u32[]{:S(2)}, u32[]{:S(2)}) async-start(bf16[8,96,256]{2,1,0:T(8,128)(2,1)} %broadcast_in_dim.13), calls=%async_computation.3 | async-start | bytes 786432 | tf_op jit(solution)/shard_map/all_to_all | solution.py:738
  65.8 34.3 %collective-permute-start = (bf16[768,384]{1,0:T(8,128)(2,1)S(1)}, bf16[768,384]{1,0:T(8,128)(2,1)}, u32[]{:S(2)}, u32[]{:S(2)}) collective-permute-start(bf16[768,384]{1,0:T(8,128)(2,1)S(1)} %bitcast.37), channel_id=1, source_target_pairs={{0,8},{8,0},{16,24},{24,16},{1,9},{9,1},{17,25},{25,17},{2,10},{10... | collective-permute-start | bytes 1769480 | tf_op jit(solution)/shard_map/ppermute | solution.py:730
  67.9 32.2 %collective-permute-start.2 = (bf16[768,384]{1,0:T(8,128)(2,1)}, bf16[768,384]{1,0:T(8,128)(2,1)}, u32[]{:S(2)}, u32[]{:S(2)}) collective-permute-start(bf16[768,384]{1,0:T(8,128)(2,1)} %collective-permute-done.1.c2.refs_5_), channel_id=1, source_target_pairs={{0,8},{8,0},{16,24},{24,16},{1,9},{9,1},{17,25},{25,17},{2,10},{10... | collective-permute-start | bytes 1769480 | tf_op jit(solution)/shard_map/ppermute | solution.py:730
  68.0 10.4 %collective-permute-start.4 = (bf16[768,256]{1,0:T(8,128)(2,1)S(1)}, bf16[768,256]{1,0:T(8,128)(2,1)}, u32[]{:S(2)}, u32[]{:S(2)}) collective-permute-start(bf16[768,256]{1,0:T(8,128)(2,1)S(1)} %bitcast.42), channel_id=1, source_target_pairs={{0,16},{8,24},{16,0},{24,8},{1,17},{9,25},{17,1},{25,9},{2,18},{10... | collective-permute-start | bytes 1179656 | tf_op jit(solution)/shard_map/ppermute | solution.py:730
  69.2 17.6 %collective-permute-start.7 = (bf16[768,256]{1,0:T(8,128)(2,1)}, bf16[768,256]{1,0:T(8,128)(2,1)}, u32[]{:S(2)}, u32[]{:S(2)}) collective-permute-start(bf16[768,256]{1,0:T(8,128)(2,1)} %bitcast.6.c0.refs_11_), channel_id=1, source_target_pairs={{0,16},{8,24},{16,0},{24,8},{1,17},{9,25},{17,1},{25,9},{2,18},{10... | collective-permute-start | bytes 1179656 | tf_op jit(solution)/shard_map/ppermute | solution.py:730
  69.4 47.1 %collective-permute-start.3 = (bf16[768,256]{1,0:T(8,128)(2,1)S(1)}, bf16[768,256]{1,0:T(8,128)(2,1)}, u32[]{:S(2)}, u32[]{:S(2)}) collective-permute-start(bf16[768,256]{1,0:T(8,128)(2,1)S(1)} %bitcast.43), channel_id=1, source_target_pairs={{0,8},{8,0},{16,24},{24,16},{1,9},{9,1},{17,25},{25,17},{2,10},{10... | collective-permute-start | bytes 1179656 | tf_op jit(solution)/shard_map/ppermute | solution.py:730
  74.2 17.3 %copy-start.3 = (bf16[8,197,768]{2,0,1:T(8,128)(2,1)S(1)}, bf16[8,197,768]{2,0,1:T(8,128)(2,1)}, u32[]{:S(2)}) copy-start(bf16[8,197,768]{2,0,1:T(8,128)(2,1)} %param.19) | copy-start | bytes 7262212
  78.3 38.3 %collective-permute-start.10 = (bf16[768,256]{1,0:T(8,128)(2,1)}, bf16[768,256]{1,0:T(8,128)(2,1)}, u32[]{:S(2)}, u32[]{:S(2)}) collective-permute-start(bf16[768,256]{1,0:T(8,128)(2,1)} %bitcast.8.c0), channel_id=1, source_target_pairs={{0,16},{8,24},{16,0},{24,8},{1,17},{9,25},{17,1},{25,9},{2,18},{10... | collective-permute-start | bytes 1179656 | tf_op jit(solution)/shard_map/ppermute | solution.py:730
  86.7 30.3 %collective-permute-start.5 = (bf16[768,256]{1,0:T(8,128)(2,1)}, bf16[768,256]{1,0:T(8,128)(2,1)S(1)}, u32[]{:S(2)}, u32[]{:S(2)}) collective-permute-start(bf16[768,256]{1,0:T(8,128)(2,1)} %collective-permute-done.4.c2.refs_9_), channel_id=1, source_target_pairs={{0,8},{8,0},{16,24},{24,16},{1,9},{9,1},{17,25},{25,17},{2,10},{10... | collective-permute-start | bytes 1179656 | tf_op jit(solution)/shard_map/ppermute | solution.py:730
  100.1 34.8 %collective-permute-start.6 = (bf16[768,256]{1,0:T(8,128)(2,1)}, bf16[768,256]{1,0:T(8,128)(2,1)S(1)}, u32[]{:S(2)}, u32[]{:S(2)}) collective-permute-start(bf16[768,256]{1,0:T(8,128)(2,1)} %bitcast.6.c0.refs_11_), channel_id=1, source_target_pairs={{0,8},{8,0},{16,24},{24,16},{1,9},{9,1},{17,25},{25,17},{2,10},{10... | collective-permute-start | bytes 1179656 | tf_op jit(solution)/shard_map/ppermute | solution.py:730
  100.1 34.8 %collective-permute-start.8 = (bf16[768,256]{1,0:T(8,128)(2,1)}, bf16[768,256]{1,0:T(8,128)(2,1)S(1)}, u32[]{:S(2)}, u32[]{:S(2)}) collective-permute-start(bf16[768,256]{1,0:T(8,128)(2,1)} %collective-permute-done.7.c2.refs_13_), channel_id=1, source_target_pairs={{0,8},{8,0},{16,24},{24,16},{1,9},{9,1},{17,25},{25,17},{2,10},{10... | collective-permute-start | bytes 1179656 | tf_op jit(solution)/shard_map/ppermute | solution.py:730
  116.5 35.5 %collective-permute-start.9 = (bf16[768,256]{1,0:T(8,128)(2,1)}, bf16[768,256]{1,0:T(8,128)(2,1)S(1)}, u32[]{:S(2)}, u32[]{:S(2)}) collective-permute-start(bf16[768,256]{1,0:T(8,128)(2,1)} %bitcast.8.c0), channel_id=1, source_target_pairs={{0,8},{8,0},{16,24},{24,16},{1,9},{9,1},{17,25},{25,17},{2,10},{10... | collective-permute-start | bytes 1179656 | tf_op jit(solution)/shard_map/ppermute | solution.py:730
  116.6 35.4 %collective-permute-start.11 = (bf16[768,256]{1,0:T(8,128)(2,1)}, bf16[768,256]{1,0:T(8,128)(2,1)S(1)}, u32[]{:S(2)}, u32[]{:S(2)}) collective-permute-start(bf16[768,256]{1,0:T(8,128)(2,1)} %collective-permute-done.10.c2), channel_id=1, source_target_pairs={{0,8},{8,0},{16,24},{24,16},{1,9},{9,1},{17,25},{25,17},{2,10},{10... | collective-permute-start | bytes 1179656 | tf_op jit(solution)/shard_map/ppermute | solution.py:730
  117.1 0.8 copy-start.7
  134.9 0.8 copy-start.8
  135.6 0.8 copy-start.9
  152.0 0.8 copy-start.17
  152.0 0.9 copy-start.18
  191.5 22.2 %copy-start = (bf16[2,64,1664]{2,1,0:T(8,128)(2,1)S(1)}, bf16[2,64,1664]{2,1,0:T(8,128)(2,1)}, u32[]{:S(2)}) copy-start(bf16[2,64,1664]{2,1,0:T(8,128)(2,1)} %copy_bitcast_fusion.sg_ref) | copy-start | bytes 1277956
  209.7 16.5 %all-to-all-start.5 = ((bf16[8,2,8,1536]{3,1,2,0:T(2,128)(2,1)}), bf16[8,2,8,1536]{3,1,2,0:T(2,128)(2,1)S(1)}, u32[]{:S(2)}, u32[]{:S(2)}) async-start(bf16[8,2,8,1536]{3,1,2,0:T(2,128)(2,1)} %bitcast.33), calls=%async_computation.5 | async-start | bytes 786432 | tf_op jit(solution)/shard_map/all_to_all | solution.py:856
  213.7 10.3 %collective-permute-start.20 = (bf16[2,64,1664]{2,1,0:T(8,128)(2,1)S(1)}, bf16[2,64,1664]{2,1,0:T(8,128)(2,1)S(1)}, u32[]{:S(2)}, u32[]{:S(2)}) collective-permute-start(bf16[2,64,1664]{2,1,0:T(8,128)(2,1)S(1)} %copy-done), channel_id=1, source_target_pairs={{0,16},{8,24},{16,0},{24,8},{1,17},{9,25},{17,1},{25,9},{2,18},{10... | collective-permute-start | bytes 1277960 | tf_op jit(solution)/shard_map/ppermute | solution.py:730
  224.1 142.8 %collective-permute-start.21 = (bf16[2,128,1664]{2,1,0:T(8,128)(2,1)S(1)}, bf16[2,128,1664]{2,1,0:T(8,128)(2,1)}, u32[]{:S(2)}, u32[]{:S(2)}) collective-permute-start(bf16[2,128,1664]{2,1,0:T(8,128)(2,1)S(1)} %pad_maximum_fusion.1), channel_id=1, source_target_pairs={{0,8},{8,0},{16,24},{24,16},{1,9},{9,1},{17,25},{25,17},{2,10},{10... | collective-permute-start | bytes 2555912 | tf_op jit(solution)/shard_map/ppermute | solution.py:730
  296.0 22.4 %copy-start.11 = (bf16[768,128]{1,0:T(8,128)(2,1)S(1)}, bf16[768,128]{1,0:T(8,128)(2,1)}, u32[]{:S(2)}) copy-start(bf16[768,128]{1,0:T(8,128)(2,1)} %get-tuple-element.83) | copy-start | bytes 589828
  296.0 23.3 %copy-start.10 = (bf16[768,128]{1,0:T(8,128)(2,1)S(1)}, bf16[768,128]{1,0:T(8,128)(2,1)}, u32[]{:S(2)}) copy-start(bf16[768,128]{1,0:T(8,128)(2,1)} %get-tuple-element.82) | copy-start | bytes 589828
  296.0 27.1 %copy-start.16 = (bf16[16,128]{1,0:T(8,128)(2,1)S(1)}, bf16[16,128]{1,0:T(8,128)(2,1)}, u32[]{:S(2)}) copy-start(bf16[16,128]{1,0:T(8,128)(2,1)} %get-tuple-element.89) | copy-start | bytes 12292
  322.0 33.6 %collective-permute-start.12 = (bf16[8,192,128]{2,1,0:T(8,128)(2,1)}, bf16[8,192,128]{2,1,0:T(8,128)(2,1)S(1)}, u32[]{:S(2)}, u32[]{:S(2)}) collective-permute-start(bf16[8,192,128]{2,1,0:T(8,128)(2,1)} %fusion), channel_id=1, source_target_pairs={{0,8},{8,0},{16,24},{24,16},{1,9},{9,1},{17,25},{25,17},{2,10},{10... | collective-permute-start | bytes 1179656 | tf_op jit(solution)/shard_map/ppermute | solution.py:730
  326.4 27.8 %collective-permute-start.16 = (bf16[8,160,128]{2,1,0:T(8,128)(2,1)S(1)}, bf16[8,160,128]{2,1,0:T(8,128)(2,1)S(1)}, u32[]{:S(2)}, u32[]{:S(2)}) collective-permute-start(bf16[8,160,128]{2,1,0:T(8,128)(2,1)S(1)} %constant_dynamic-slice_fusion.1), channel_id=1, source_target_pairs={{0,8},{8,0},{16,24},{24,16},{1,9},{9,1},{17,25},{25,17},{2,10},{10... | collective-permute-start | bytes 983048 | tf_op jit(solution)/shard_map/ppermute | solution.py:730
  326.5 19.6 %copy-start.1 = (bf16[8,197,768]{2,1,0:T(8,128)(2,1)S(1)}, bf16[8,197,768]{2,1,0:T(8,128)(2,1)}, u32[]{:S(2)}) copy-start(bf16[8,197,768]{2,1,0:T(8,128)(2,1)} %get-tuple-element.106) | copy-start | bytes 7262212
  347.9 7.7 %copy-start.6 = (bf16[768,128]{1,0:T(8,128)(2,1)S(1)}, bf16[768,128]{1,0:T(8,128)(2,1)}, u32[]{:S(2)}) copy-start(bf16[768,128]{1,0:T(8,128)(2,1)} %get-tuple-element.85) | copy-start | bytes 589828
  354.3 5.4 %collective-permute-start.17 = (bf16[8,80,128]{2,1,0:T(8,128)(2,1)S(1)}, bf16[8,80,128]{2,1,0:T(8,128)(2,1)S(1)}, u32[]{:S(2)}, u32[]{:S(2)}) collective-permute-start(bf16[8,80,128]{2,1,0:T(8,128)(2,1)S(1)} %constant_dynamic-slice_fusion), channel_id=1, source_target_pairs={{0,16},{8,24},{16,0},{24,8},{1,17},{9,25},{17,1},{25,9},{2,18},{10... | collective-permute-start | bytes 491528 | tf_op jit(solution)/shard_map/ppermute | solution.py:730
  360.4 11.6 %all-to-all-start.7 = ((bf16[8,80,128]{2,1,0:T(8,128)(2,1)}), bf16[8,80,128]{2,1,0:T(8,128)(2,1)S(1)}, u32[]{:S(2)}, u32[]{:S(2)}) async-start(bf16[8,80,128]{2,1,0:T(8,128)(2,1)} %add_convert_fusion.3), calls=%async_computation.7 | async-start | bytes 327680 | tf_op jit(solution)/shard_map/all_to_all | solution.py:757
  365.6 7.7 %collective-permute-start.13 = (bf16[8,96,128]{2,1,0:T(8,128)(2,1)S(1)}, bf16[8,96,128]{2,1,0:T(8,128)(2,1)S(1)}, u32[]{:S(2)}, u32[]{:S(2)}) collective-permute-start(bf16[8,96,128]{2,1,0:T(8,128)(2,1)S(1)} %constant_dynamic-slice_fusion.2), channel_id=1, source_target_pairs={{0,16},{8,24},{16,0},{24,8},{1,17},{9,25},{17,1},{25,9},{2,18},{10... | collective-permute-start | bytes 589832 | tf_op jit(solution)/shard_map/ppermute | solution.py:730
  372.0 5.5 %collective-permute-start.18 = (bf16[80,128]{1,0:T(8,128)(2,1)S(1)}, bf16[80,128]{1,0:T(8,128)(2,1)S(1)}, u32[]{:S(2)}, u32[]{:S(2)}) collective-permute-start(bf16[80,128]{1,0:T(8,128)(2,1)S(1)} %reduce_sum.25), channel_id=1, source_target_pairs={{0,16},{8,24},{16,0},{24,8},{1,17},{9,25},{17,1},{25,9},{2,18},{10... | collective-permute-start | bytes 61448 | tf_op jit(solution)/shard_map/ppermute | solution.py:730
  374.1 27.9 %all-to-all-start.6 = ((bf16[8,96,128]{2,1,0:T(8,128)(2,1)}), bf16[8,96,128]{2,1,0:T(8,128)(2,1)S(1)}, u32[]{:S(2)}, u32[]{:S(2)}) async-start(bf16[8,96,128]{2,1,0:T(8,128)(2,1)} %add_convert_fusion.2), calls=%async_computation.6 | async-start | bytes 393216 | tf_op jit(solution)/shard_map/all_to_all | solution.py:757
  377.5 24.5 %collective-permute-start.19 = (bf16[160,128]{1,0:T(8,128)(2,1)S(1)}, bf16[160,128]{1,0:T(8,128)(2,1)S(1)}, u32[]{:S(2)}, u32[]{:S(2)}) collective-permute-start(bf16[160,128]{1,0:T(8,128)(2,1)S(1)} %maximum_select_fusion.3), channel_id=1, source_target_pairs={{0,8},{8,0},{16,24},{24,16},{1,9},{9,1},{17,25},{25,17},{2,10},{10... | collective-permute-start | bytes 122888 | tf_op jit(solution)/shard_map/ppermute | solution.py:730
  402.0 2.7 collective-permute-start.14
  404.8 2.1 collective-permute-start.15

commit v2 on v1

v2 whole, which is shorter than its diff:
```python
import functools

import jax
import jax.numpy as jnp
from jax import lax
from jax.experimental import pallas as pl
from jax.experimental.pallas import tpu as pltpu
from jax.sharding import PartitionSpec as P

HEADS = 12
RANK = 16
LANES = 128
HEAD_DIM = 64
GROUP = 256
F32 = jnp.float32
BF16 = jnp.bfloat16
NN = (((1,), (0,)), ((), ()))
NT = (((1,), (1,)), ((), ()))
TN = (((0,), (0,)), ((), ()))
NEG = -1e30
VMEM_LIMIT = 56 * 1024 * 1024
GELU_C = 0.7978845608028654
GELU_A = 0.044715
IMAGES_FORWARD = 2
IMAGES_BACK = 2
IMAGES_ROUTE = 2
IMAGES_LAST = 2


def dot(left, right, dims=NN):
    return lax.dot_general(left, right, dims, preferred_element_type=F32)


def params(*axes):
    return pltpu.CompilerParams(
        dimension_semantics=axes or None, vmem_limit_bytes=VMEM_LIMIT
    )


def cost(flops, moved, exps=0):
    return pl.CostEstimate(flops=int(flops), bytes_accessed=int(moved), transcendentals=int(exps))


def normalise(rows):
    centre = rows - jnp.mean(rows, axis=-1, keepdims=True)
    spread = jnp.mean(centre * centre, axis=-1, keepdims=True)
    scale = lax.rsqrt(spread + 1e-06)
    return centre * scale, scale


def normalise_back(unit, scale, upstream):
    inner = jnp.mean(upstream * unit, axis=-1, keepdims=True)
    return scale * (upstream - jnp.mean(upstream, axis=-1, keepdims=True) - unit * inner)


def rank_row(index):
    lane = lax.broadcasted_iota(jnp.int32, (1, LANES), 1) // RANK
    return (lane == index).astype(F32)


def zero_tail(rows, n_tok):
    total = rows.shape[0]
    cut = n_tok // 16 * 16
    if n_tok == total:
        return rows
    row = lax.broadcasted_iota(jnp.int32, (total - cut, rows.shape[1]), 0) + cut
    tail = jnp.where(row < n_tok, rows[cut:].astype(F32), 0.0).astype(rows.dtype)
    return jnp.concatenate([rows[:cut], tail], axis=0)


def mask_tail(scores, n_tok):
    total = scores.shape[0]
    cut = n_tok // 16 * 16
    if n_tok == total:
        return scores
    row = lax.broadcasted_iota(jnp.int32, (total - cut, scores.shape[1]), 0) + cut
    tail = jnp.where(row < n_tok, scores[cut:], NEG)
    return jnp.concatenate([scores[:cut], tail], axis=0)


def pad_rows(scratch, ref):
    n_img, n_tok, width = ref.shape
    total = scratch.shape[0] // n_img
    cut = n_tok // 8 * 8
    for slot in range(n_img):
        base = slot * total
        scratch[base + cut : base + total, :] = jnp.zeros((total - cut, width), F32)
        scratch[base : base + n_tok, :] = ref[slot].astype(F32)
    return scratch[...]


def select_rows(rows, index_ref, first, n_img):
    total = rows.shape[0] // n_img
    return jnp.concatenate(
        [
            (rows[i * total : (i + 1) * total] * rank_row(index_ref[first + i])).astype(BF16)
            for i in range(n_img)
        ],
        axis=0,
    )


def flat(ref):
    return ref[...].reshape(ref.shape[0] * ref.shape[1], ref.shape[2])


def assemble(place, chunks, starts, wall, sems):
    pieces = len(chunks)
    part = wall.shape[1] // pieces
    copies = []
    for step in range(pieces):
        column = pl.multiple_of(((place % pieces) ^ step) * part, LANES)
        copies.append(
            pltpu.make_async_copy(
                chunks[step].at[:, pl.ds(starts[step], part)], wall.at[:, pl.ds(column, part)], sems.at[step]
            )
        )
    for copy in copies:
        copy.start()
    for copy in copies:
        copy.wait()


def norm_kernel(image_ref, _, out_ref, pad_ref):
    unit, _ = normalise(pad_rows(pad_ref, image_ref))
    out_ref[...] = unit.astype(BF16).reshape(out_ref.shape)


def pack_kernel(place_ref, qkv_ref, a_ref, b_ref, ao_ref, ra_ref, out_ref, pack):
    shards, rows, part = out_ref.shape
    width = qkv_ref.shape[1] // 3
    for piece in range(3):
        pack[:, piece * GROUP : (piece + 1) * GROUP] = qkv_ref[:, piece * width : piece * width + GROUP]
        column = width + (1 + piece) * LANES
        pack[:, column : column + LANES] = b_ref[piece * rows : (piece + 1) * rows, :]
    pack[:, width : width + LANES] = a_ref[...]
    pack[:, width + 4 * LANES : width + 5 * LANES] = ao_ref[...]
    pack[:, width + 5 * LANES : width + 6 * LANES] = ra_ref[...]
    mine = pack[:, pl.ds(pl.multiple_of(place_ref[0] * part, LANES), part)]
    for shard in range(shards):
        out_ref[shard] = mine


def head_mask(value):
    lane = lax.broadcasted_iota(jnp.int32, (1, LANES), 1)
    low = jnp.where(lane < HEAD_DIM, value, 0.0).astype(BF16)
    high = jnp.where(lane < HEAD_DIM, 0.0, value).astype(BF16)
    return low, high


def attention_forward(qkv, n_tok, prob_ref, slot):
    masks = head_mask(0.125)
    value_t = qkv[:, 2 * GROUP :].T
    outs = []
    for pair in range(GROUP // LANES):
        q_pair = qkv[:, pair * LANES : (pair + 1) * LANES]
        k_pair = qkv[:, GROUP + pair * LANES : GROUP + (pair + 1) * LANES]
        both = dot(jnp.concatenate([k_pair * masks[0], k_pair * masks[1]], axis=0), q_pair, NT)
        for side in range(2):
            total = k_pair.shape[0]
            scores = mask_tail(both[side * total : (side + 1) * total], n_tok)
            powers = jnp.exp(scores - jnp.max(scores, axis=0, keepdims=True))
            probs = (powers * (1.0 / jnp.sum(powers, axis=0, keepdims=True))).astype(BF16)
            head = 2 * pair + side
            prob_ref[slot, head] = probs
            outs.append(dot(value_t[head * HEAD_DIM : (head + 1) * HEAD_DIM], probs).astype(BF16))
    return zero_tail(jnp.concatenate(outs, axis=0).T, n_tok)


def first_attention_kernel(
    n_tok, shards, starts, place_ref, index_ref, h1_ref, *rest,
):
    chunks, rest = rest[: len(starts)], rest[len(starts) :]
    qkv_ref, att_ref, prob_ref, uq_ref, a_ref, bt_ref, ao_ref, ra_ref, wall, sems = rest
    step = pl.program_id(0)
    n_img, total, width = h1_ref.shape

    @pl.when(step == 0)
    def _():
        assemble(place_ref[0], chunks, starts, wall, sems)
        a_ref[...] = wall[:, width : width + LANES]
        ao_ref[...] = wall[:, width + 4 * LANES : width + 5 * LANES]
        ra_ref[...] = wall[:, width + 5 * LANES : width + 6 * LANES]
        rows = width // shards
        for shard in range(shards):
            for part in range(3):
                bt_ref[(shard * 3 + part) * rows : (shard * 3 + part + 1) * rows, :] = wall[
                    shard * rows : (shard + 1) * rows,
                    width + (1 + part) * LANES : width + (2 + part) * LANES,
                ]

    h1 = flat(h1_ref)
    low = dot(h1, a_ref[...]).astype(BF16).astype(F32)
    uq = select_rows(low, index_ref, step * n_img, n_img)
    uq_ref[...] = uq.reshape(uq_ref.shape)
    attend_group(0, n_tok, h1, uq, wall, bt_ref, qkv_ref, att_ref, prob_ref)


def group_rows(group, width, bt_ref):
    return jnp.concatenate(
        [bt_ref[part * width + group * GROUP : part * width + (group + 1) * GROUP, :] for part in range(3)],
        axis=0,
    )


def attend_group(group, n_tok, h1, uq, wall, bt_ref, qkv_ref, att_ref, prob_ref):
    n_img, total, _ = att_ref.shape
    second = group_rows(group, wall.shape[0], bt_ref)
    qkv = (dot(h1, wall[:, : 3 * GROUP]) + dot(uq, second, NT)).astype(BF16)
    qkv_ref[...] = qkv.reshape(qkv_ref.shape)
    for slot in range(n_img):
        att_ref[slot] = attention_forward(
            qkv[slot * total : (slot + 1) * total], n_tok, prob_ref, slot
        )


def next_attention_kernel(
    n_tok, group, extra, starts, place_ref, h1_ref, uq_ref, bt_ref, *rest
):
    chunks, rest = rest[: len(starts)], rest[len(starts) :]
    qkv_ref, att_ref, prob_ref = rest[:3]
    wall, sems = rest[-2:]

    @pl.when(pl.program_id(0) == 0)
    def _():
        assemble(place_ref[0], chunks, starts, wall, sems)
        for position in range(extra):
            column = 3 * GROUP + position * LANES
            rest[3 + position][...] = wall[:, column : column + LANES]

    attend_group(
        group, n_tok, flat(h1_ref), flat(uq_ref), wall, bt_ref, qkv_ref, att_ref, prob_ref,
    )


def route_kernel(
    n_exp, starts, place_ref, index_ref, count_ref, image_ref, cot_ref, att0, att1, att2,
    ao_ref, bo_ref, ra_ref, wr_ref, rb_ref, *rest,
):
    chunks, rest = rest[: len(starts)], rest[len(starts) :]
    x2_ref, uo_ref, ur_ref, disp_ref, comb_ref, sg_ref, wrt_ref, wall, pad_a, pad_b, sems = rest
    n_img, n_tok, width = image_ref.shape
    first = pl.program_id(0) * n_img
    total = x2_ref.shape[1]

    @pl.when(first == 0)
    def _():
        assemble(place_ref[0], chunks, starts, wall, sems)
        wrt_ref[...] = wr_ref[...].astype(F32).T[:n_exp].astype(BF16)

    att = jnp.concatenate([flat(att0), flat(att1), flat(att2)], axis=1)
    uo = select_rows(dot(att, ao_ref[...]).astype(BF16).astype(F32), index_ref, first, n_img)
    uo_ref[...] = uo.reshape(uo_ref.shape)
    x2 = pad_rows(pad_a, image_ref) + dot(att, wall[:, :width]) + dot(uo, bo_ref[...], NT)
    x2_ref[...] = x2.reshape(x2_ref.shape)
    h2 = normalise(x2)[0].astype(BF16)
    ur = select_rows(dot(h2, ra_ref[...]).astype(BF16).astype(F32), index_ref, first, n_img)
    ur_ref[...] = ur.reshape(ur_ref.shape)
    cot = pad_rows(pad_b, cot_ref)
    for slot in range(n_img):
        rows = slice(slot * total, (slot + 1) * total)
        living = (first + slot < count_ref[0]).astype(F32)
        logits = dot(wrt_ref[...], h2[rows], NT) + dot(rb_ref[...], ur[rows], NT)
        alive = lax.broadcasted_iota(jnp.int32, logits.shape, 1) < n_tok
        over_tokens = jnp.where(alive, logits, NEG)
        powers = jnp.exp(over_tokens - jnp.max(over_tokens, axis=1, keepdims=True))
        disp = powers / jnp.sum(powers, axis=1, keepdims=True)
        powers = jnp.exp(logits - jnp.max(logits, axis=0, keepdims=True))
        comb = jnp.where(alive, powers / jnp.sum(powers, axis=0, keepdims=True), 0.0)
        disp_ref[slot] = disp
        comb_ref[slot] = comb
        upstream = (cot[rows] * living).astype(BF16)
        sg_ref[slot, :, :width] = dot(disp.astype(BF16), h2[rows]).astype(BF16)
        sg_ref[slot, :, width : 2 * width] = dot(comb.astype(BF16), upstream).astype(BF16)
        selector = rank_row(index_ref[first + slot])
        sg_ref[slot, :, 2 * width :] = jnp.broadcast_to(selector, (n_exp, LANES)).astype(BF16)


def gelu_both(pre):
    square = pre * pre
    half = jnp.tanh(GELU_C * pre * (1.0 + GELU_A * square))
    both = 0.5 * (1.0 + half)
    slope = both + 0.5 * pre * (1.0 - half * half) * (GELU_C * (1.0 + 3.0 * GELU_A * square))
    return pre * both, slope


def expert_tile(slots, gy, u1, gu2, wu_ref, wd_ref, ub_ref, da_ref):
    pre = dot(slots, wu_ref[0]) + dot(u1, ub_ref[0])
    ghid = (dot(wd_ref[0], gy, NT) + dot(da_ref[0], gu2, NT)).T
    hidden, slope = gelu_both(pre)
    return hidden.astype(BF16), (slope * ghid).astype(BF16)


def expert_kernel(
    sg_ref, wu_ref, wd_ref, ua_ref, ub_ref, da_ref, db_ref, out_ref,
    u1_ref, gu2_ref, acc_y, acc_s, acc_u2, acc_gu1,
):
    step = pl.program_id(1)
    width = wu_ref.shape[1]
    selector = sg_ref[0, :, 2 * width :].astype(F32)

    @pl.when(step == 0)
    def _():
        u1_ref[...] = (
            dot(sg_ref[0, :, :width], ua_ref[0]).astype(BF16).astype(F32) * selector
        ).astype(BF16)
        gu2_ref[...] = (dot(sg_ref[0, :, width : 2 * width], db_ref[0], NT) * selector).astype(BF16)
        acc_y[...] = jnp.zeros_like(acc_y)
        acc_s[...] = jnp.zeros_like(acc_s)
        acc_u2[...] = jnp.zeros_like(acc_u2)
        acc_gu1[...] = jnp.zeros_like(acc_gu1)

    hidden, gpre = expert_tile(
        sg_ref[0, :, :width], sg_ref[0, :, width : 2 * width], u1_ref[...], gu2_ref[...],
        wu_ref, wd_ref, ub_ref, da_ref,
    )
    acc_y[...] += dot(hidden, wd_ref[0])
    acc_u2[...] += dot(hidden, da_ref[0])
    acc_s[...] += dot(wu_ref[0], gpre, NT)
    acc_gu1[...] += dot(ub_ref[0], gpre, NT)

    @pl.when(step == pl.num_programs(1) - 1)
    def _():
        u2 = (acc_u2[...].astype(BF16).astype(F32) * selector).astype(BF16)
        gu1 = (acc_gu1[...].T * selector).astype(BF16)
        out_ref[0, :, :width] = (acc_y[...] + dot(u2, db_ref[0])).astype(BF16)
        out_ref[0, :, width:] = (acc_s[...].T + dot(gu1, ua_ref[0], NT)).astype(BF16)


def expert_grad_kernel(
    sg_ref, wu_ref, wd_ref, ua_ref, ub_ref, da_ref, db_ref,
    gua_ref, gub_ref, gda_ref, gdb_ref, u1_ref, gu2_ref, u1t_ref, gu2t_ref, acc_u2, acc_gu1,
):
    step = pl.program_id(1)
    width = wu_ref.shape[1]
    selector = sg_ref[0, :, 2 * width :].astype(F32)

    @pl.when(step == 0)
    def _():
        u1 = dot(sg_ref[0, :, :width], ua_ref[0]).astype(BF16).astype(F32) * selector
        gu2 = dot(sg_ref[0, :, width : 2 * width], db_ref[0], NT) * selector
        u1_ref[...] = u1.astype(BF16)
        gu2_ref[...] = gu2.astype(BF16)
        u1t_ref[...] = u1.T.astype(BF16)
        gu2t_ref[...] = gu2.T.astype(BF16)
        acc_u2[...] = jnp.zeros_like(acc_u2)
        acc_gu1[...] = jnp.zeros_like(acc_gu1)

    hidden, gpre = expert_tile(
        sg_ref[0, :, :width], sg_ref[0, :, width : 2 * width], u1_ref[...], gu2_ref[...],
        wu_ref, wd_ref, ub_ref, da_ref,
    )
    gub_ref[0] = dot(u1t_ref[...], gpre)
    gda_ref[0] = dot(gu2t_ref[...], hidden).T
    acc_u2[...] += dot(hidden, da_ref[0])
    acc_gu1[...] += dot(ub_ref[0], gpre, NT)

    @pl.when(step == pl.num_programs(1) - 1)
    def _():
        u2 = acc_u2[...].astype(BF16).astype(F32) * selector
        gu1 = (acc_gu1[...] * selector.T).astype(BF16)
        gdb_ref[0] = dot(u2.T.astype(BF16), sg_ref[0, :, width : 2 * width])
        gua_ref[0] = dot(gu1, sg_ref[0, :, :width]).T


def route_back_kernel(
    n_exp, starts, place_ref, index_ref, count_ref, cot_ref, x2_ref, uo_ref, ur_ref, disp_ref,
    comb_ref, att0, att1, att2, ret_ref, ao_ref, bo_ref, ra_ref, wrt_ref, rb_ref, *rest,
):
    chunks, rest = rest[: len(starts)], rest[len(starts) :]
    block_ref, gx2_ref, gatt_ref, pack_ref, *rest = rest
    wall, pad_b, acc_oa, acc_ob, acc_ra, acc_rb, sems = rest
    n_img, n_tok, width = cot_ref.shape
    first = pl.program_id(0) * n_img
    total = x2_ref.shape[1]

    @pl.when(first == 0)
    def _():
        assemble(place_ref[0], chunks, starts, wall, sems)
        acc_oa[...] = jnp.zeros_like(acc_oa)
        acc_ob[...] = jnp.zeros_like(acc_ob)
        acc_ra[...] = jnp.zeros_like(acc_ra)
        acc_rb[...] = jnp.zeros_like(acc_rb)

    cot = pad_rows(pad_b, cot_ref)
    x2 = flat(x2_ref)
    unit, scale = normalise(x2)
    h2 = unit.astype(BF16)
    pairs, belows, upstreams = [], [], []
    for slot in range(n_img):
        rows = slice(slot * total, (slot + 1) * total)
        living = (first + slot < count_ref[0]).astype(F32)
        upstream = cot[rows] * living
        upstreams.append(upstream)
        disp, comb = disp_ref[slot], comb_ref[slot]
        yexp, gslot = ret_ref[slot, :, :width], ret_ref[slot, :, width:]
        gcomb = dot(yexp, upstream.astype(BF16), NT)
        gdisp = dot(gslot, h2[rows], NT)
        glog = (
            disp * (gdisp - jnp.sum(gdisp * disp, axis=1, keepdims=True))
            + comb * (gcomb - jnp.sum(gcomb * comb, axis=0, keepdims=True))
        )
        acc_rb[...] += dot(glog.astype(BF16), ur_ref[slot])
        three = jnp.concatenate([disp, glog, comb], axis=0).T.astype(BF16)
        mixed = dot(three[:, 2 * n_exp :], yexp)
        block_ref[slot] = (living * (x2[rows] + mixed)).astype(BF16)[:n_tok]
        pairs.append(three[:, : 2 * n_exp])
        belows.append(jnp.concatenate([gslot, wrt_ref[...]], axis=0))
    glog_rows = jnp.concatenate([pair[:, n_exp:] for pair in pairs], axis=0)
    gur = select_rows(dot(glog_rows, rb_ref[...]), index_ref, first, n_img)
    acc_ra[...] += dot(gur, h2, TN)
    gh2 = dot(gur, ra_ref[...], NT) + jnp.concatenate(
        [dot(pair, below) for pair, below in zip(pairs, belows)], axis=0
    )
    gx2 = jnp.concatenate(upstreams, axis=0) + normalise_back(unit, scale, gh2)
    gx2_ref[...] = gx2.reshape(gx2_ref.shape)
    gbr = gx2.astype(BF16)
    acc_ob[...] += dot(flat(uo_ref), gbr, TN)
    guo = select_rows(dot(gbr, bo_ref[...]), index_ref, first, n_img)
    att = jnp.concatenate([flat(att0), flat(att1), flat(att2)], axis=1)
    acc_oa[...] += dot(guo, att, TN)
    gatt = (dot(gbr, wall[:, :width], NT) + dot(guo, ao_ref[...], NT)).astype(BF16)
    gatt_ref[...] = gatt.reshape(gatt_ref.shape)

    @pl.when(pl.program_id(0) == pl.num_programs(0) - 1)
    def _():
        shards = pack_ref.shape[0]
        rows = width // shards
        n_loc = n_exp // shards
        for position, acc in enumerate((acc_oa, acc_ob, acc_ra)):
            summed = acc[...].T.astype(BF16)
            for shard in range(shards):
                pack_ref[shard, position * rows : (position + 1) * rows, :] = summed[
                    shard * rows : (shard + 1) * rows
                ]
        tail = pack_ref.shape[1] - 3 * rows
        for shard in range(shards):
            last = jnp.concatenate(
                [acc_rb[shard * n_loc : (shard + 1) * n_loc, :], jnp.zeros((tail - n_loc, LANES), F32)],
                axis=0,
            )
            pack_ref[shard, 3 * rows :, :] = last.astype(BF16)


def attention_backward(qkv, gatt, prob_ref, slot):
    keep = head_mask(1.0)
    key_t = qkv[:, GROUP : 2 * GROUP].T
    total = qkv.shape[0]
    lane = lax.broadcasted_iota(jnp.int32, (1, LANES), 1)
    gq_parts, gk_parts, gv_parts = [], [], []
    for pair in range(GROUP // LANES):
        span = slice(pair * LANES, (pair + 1) * LANES)
        q_pair, ga_pair = qkv[:, span], gatt[:, span]
        v_pair = qkv[:, 2 * GROUP + pair * LANES : 2 * GROUP + (pair + 1) * LANES]
        lows = [prob_ref[slot, 2 * pair], prob_ref[slot, 2 * pair + 1]]
        gv = dot(jnp.concatenate(lows, axis=0), ga_pair)
        gprobs = dot(jnp.concatenate([v_pair * keep[0], v_pair * keep[1]], axis=0), ga_pair, NT)
        gscores = []
        for side in range(2):
            probs = lows[side].astype(F32)
            gprob = gprobs[side * total : (side + 1) * total]
            inner = jnp.sum(gprob * probs, axis=0, keepdims=True)
            gscores.append((probs * (gprob - inner)).astype(BF16))
            head = 2 * pair + side
            gq_parts.append(
                (dot(key_t[head * HEAD_DIM : (head + 1) * HEAD_DIM], gscores[side]) * 0.125).astype(BF16)
            )
        gk = dot(jnp.concatenate(gscores, axis=0), q_pair)
        gk_parts.append((jnp.where(lane < HEAD_DIM, gk[:total], gk[total:]) * 0.125).astype(BF16))
        gv_parts.append(jnp.where(lane < HEAD_DIM, gv[:total], gv[total:]).astype(BF16))
    gq = jnp.concatenate(gq_parts, axis=0).T
    return jnp.concatenate([gq] + gk_parts + gv_parts, axis=1)


def attention_back_kernel(group, last, *refs):
    refs = list(refs)
    index_ref = refs.pop(0) if last else None
    qkv_ref, gatt_ref, prob_ref, uq_ref, bt_ref = refs[:5]
    refs = refs[5:]
    before_ref = refs.pop(0) if group else None
    h1_ref = refs.pop(0) if last else None
    befores = [refs.pop(0) for _ in range(group)] if last else ()
    gqkv_ref, guq_ref, gb_ref = refs[:3]
    refs = refs[3:]
    acc_b = refs.pop(0)
    acc_a = refs.pop(0) if last else None
    step = pl.program_id(0)
    width = bt_ref.shape[0] // 3
    n_img, total, _ = qkv_ref.shape

    @pl.when(step == 0)
    def _():
        acc_b[...] = jnp.zeros_like(acc_b)
        if last:
            acc_a[...] = jnp.zeros_like(acc_a)

    parts = [attention_backward(qkv_ref[i], gatt_ref[i], prob_ref, i) for i in range(n_img)]
    for i in range(n_img):
        gqkv_ref[i] = parts[i]
    gqkv = jnp.concatenate(parts, axis=0)
    acc_b[...] += dot(flat(uq_ref), gqkv, TN)
    guq = dot(gqkv, group_rows(group, width, bt_ref))
    if group:
        guq = guq + flat(before_ref)
    if last:
        guq = select_rows(guq, index_ref, step * n_img, n_img)
        acc_a[...] += dot(guq, flat(h1_ref), TN)
    guq_ref[...] = guq.reshape(guq_ref.shape)

    @pl.when(step == pl.num_programs(0) - 1)
    def _():
        summed = acc_b[...].T.astype(BF16)
        if not last:
            gb_ref[...] = summed
            return
        shards = gb_ref.shape[0]
        rows = width // shards
        own = acc_a[...].T.astype(BF16)
        for shard in range(shards):
            gb_ref[shard, 3 * rows :, :] = own[shard * rows : (shard + 1) * rows]
        sources = [before[...] for before in befores] + [summed]
        for part in range(3):
            for source in range(group + 1):
                start = part * width + source * GROUP
                place = start
                while place < start + GROUP:
                    shard, offset = divmod(place, 3 * rows)
                    length = min(start + GROUP - place, 3 * rows - offset)
                    take = part * GROUP + place - start
                    gb_ref[shard, offset : offset + length, :] = sources[source][take : take + length]
                    place += length


def input_grad_kernel(starts, place_ref, image_ref, gx2_ref, guq_ref, a_ref, *refs):
    refs = list(refs)
    groups = len(starts)
    gqkv = [refs.pop(0) for _ in starts]
    chunks = [[refs.pop(0) for _ in start] for start in starts]
    out_ref = refs.pop(0)
    walls = [refs.pop(0) for _ in starts]
    pad_a, sems = refs
    n_img, n_tok, width = image_ref.shape
    step = pl.program_id(0)
    parts = width // LANES
    every = out_ref.shape[0] // (n_tok * parts)

    @pl.when(step == 0)
    def _():
        for group in range(groups):
            assemble(place_ref[0], chunks[group], starts[group], walls[group], sems.at[group])

    gh1 = dot(flat(guq_ref), a_ref[...], NT)
    for group in range(groups):
        gh1 = gh1 + dot(flat(gqkv[group]), walls[group][:, : 3 * GROUP], NT)
    unit, scale = normalise(pad_rows(pad_a, image_ref))
    total = gx2_ref.shape[1]
    result = flat(gx2_ref) + normalise_back(unit, scale, gh1)
    for slot in range(n_img):
        for part in range(parts):
            out_ref[pl.ds(part * every + step * n_img + slot, n_tok, stride=parts * every), :] = result[
                slot * total : slot * total + n_tok, part * LANES : (part + 1) * LANES
            ]


ANY = pl.BlockSpec(memory_space=pl.ANY)


def whole(shape):
    return pl.BlockSpec(shape, lambda *_: (0,) * len(shape))


def per_image(*shape, images=1):
    return pl.BlockSpec((images,) + shape, lambda i, *_: (i,) + (0,) * len(shape))


def several(images, limit):
    return max(n for n in range(1, limit + 1) if images % n == 0)


def call(kernel, scalars, grid, inputs, outputs, scratch, flops, exps=0, aliases=None):
    arrays = [array for array, _ in inputs]
    shapes = [jax.ShapeDtypeStruct(shape, dtype) for shape, dtype, _ in outputs]
    moved = sum(array.size * array.dtype.itemsize for array in arrays) + sum(
        shape.size * shape.dtype.itemsize for shape in shapes
    )
    return pl.pallas_call(
        kernel,
        out_shape=shapes,
        grid_spec=pltpu.PrefetchScalarGridSpec(
            num_scalar_prefetch=len(scalars),
            grid=grid,
            in_specs=[spec for _, spec in inputs],
            out_specs=[spec for _, _, spec in outputs],
            scratch_shapes=scratch,
        ),
        input_output_aliases=aliases or {},
        compiler_params=params(*(("arbitrary",) * len(grid))),
        cost_estimate=cost(flops, moved, exps),
    )(*scalars, *arrays)


def norm_call(images, cotangent, total):
    n_img, n_tok, width = images.shape
    each = several(n_img, 4)
    return call(
        norm_kernel, (), (n_img // each,),
        [(images, per_image(n_tok, width, images=each)), (cotangent, ANY)],
        [((n_img, total, width), BF16, per_image(total, width, images=each))],
        [pltpu.VMEM((each * total, width), F32)],
        8 * images.size,
    )[0]


def pack_call(place, weights, shards):
    rows, columns = weights[0].shape
    part = (columns // 3 + 6 * LANES) // 4
    return call(
        pack_kernel, (place,), (1,), [(weight, whole(weight.shape)) for weight in weights],
        [((shards, rows, part), BF16, whole((shards, rows, part)))],
        [pltpu.VMEM((rows, 4 * part), BF16)],
        rows * columns,
    )[0]


def attention_flops(n_img, total, width, parts):
    return n_img * total * (2 * width * 3 * GROUP + parts * 8 * total * HEAD_DIM)


def attention_outputs(n_img, total, each):
    return [
        ((n_img, total, 3 * GROUP), BF16, per_image(total, 3 * GROUP, images=each)),
        ((n_img, total, GROUP), BF16, per_image(total, GROUP, images=each)),
        (
            (n_img, GROUP // HEAD_DIM, total, total), BF16,
            per_image(GROUP // HEAD_DIM, total, total, images=each),
        ),
    ]


def first_attention_call(place, index, h1, pack, n_tok, shards):
    n_img, total, width = h1.shape
    chunks, starts, columns = pack
    each = several(n_img, IMAGES_FORWARD)
    return call(
        functools.partial(first_attention_kernel, n_tok, shards, starts), (place, index), (n_img // each,),
        [(h1, per_image(total, width, images=each))] + [(chunk, ANY) for chunk in chunks],
        attention_outputs(n_img, total, each)
        + [
            ((n_img, total, LANES), BF16, per_image(total, LANES, images=each)),
            ((width, LANES), BF16, whole((width, LANES))),
            ((3 * width, LANES), BF16, whole((3 * width, LANES))),
            ((width, LANES), BF16, whole((width, LANES))),
            ((width, LANES), BF16, whole((width, LANES))),
        ],
        [pltpu.VMEM((width, columns), BF16), pltpu.SemaphoreType.DMA((4,))],
        attention_flops(n_img, total, width, 2), n_img * total * total * 4,
    )


def next_attention_call(place, h1, uq, bt, pack, n_tok, group, extra):
    n_img, total, width = h1.shape
    chunks, starts, columns = pack
    each = several(n_img, IMAGES_FORWARD)
    return call(
        functools.partial(next_attention_kernel, n_tok, group, extra, starts), (place,), (n_img // each,),
        [
            (h1, per_image(total, width, images=each)),
            (uq, per_image(total, LANES, images=each)),
            (bt, whole(bt.shape)),
        ]
        + [(chunk, ANY) for chunk in chunks],
        attention_outputs(n_img, total, each)
        + [((width, LANES), BF16, whole((width, LANES)))] * extra,
        [pltpu.VMEM((width, columns), BF16), pltpu.SemaphoreType.DMA((4,))],
        attention_flops(n_img, total, width, 2), n_img * total * total * 4,
    )


def route_call(place, index, count, images, cotangent, atts, banks, pack, n_exp, total):
    n_img, n_tok, width = images.shape
    chunks, starts, columns = pack
    each = several(n_img, IMAGES_ROUTE)
    here = functools.partial(per_image, images=each)
    return call(
        functools.partial(route_kernel, n_exp, starts), (place, index, count), (n_img // each,),
        [(images, here(n_tok, width)), (cotangent, here(n_tok, width))]
        + [(att, here(total, GROUP)) for att in atts]
        + [(bank, whole(bank.shape)) for bank in banks]
        + [(chunk, ANY) for chunk in chunks],
        [
            ((n_img, total, width), F32, here(total, width)),
            ((n_img, total, LANES), BF16, here(total, LANES)),
            ((n_img, total, LANES), BF16, here(total, LANES)),
            ((n_img, n_exp, total), F32, here(n_exp, total)),
            ((n_img, n_exp, total), F32, here(n_exp, total)),
            ((n_img, n_exp, 2 * width + LANES), BF16, here(n_exp, 2 * width + LANES)),
            ((n_exp, width), BF16, whole((n_exp, width))),
        ],
        [
            pltpu.VMEM((width, columns), BF16),
            pltpu.VMEM((each * total, width), F32),
            pltpu.VMEM((each * total, width), F32),
            pltpu.SemaphoreType.DMA((4,)),
        ],
        n_img * total * 2 * width * (width + 3 * LANES), n_img * total * 2 * n_exp,
    )


def hidden_tile(hidden, limit):
    tile = hidden
    while tile > limit:
        tile //= 2
    return tile


def expert_specs(rows, width, tile, first=0):
    return (
        pl.BlockSpec((1, rows, 2 * width + LANES), lambda e, f: (e + first, 0, 0)),
        pl.BlockSpec((1, width, tile), lambda e, f: (e + first, 0, f)),
        pl.BlockSpec((1, tile, width), lambda e, f: (e + first, f, 0)),
        pl.BlockSpec((1, width, LANES), lambda e, f: (e + first, 0, 0)),
        pl.BlockSpec((1, LANES, tile), lambda e, f: (e + first, 0, f)),
        pl.BlockSpec((1, tile, LANES), lambda e, f: (e + first, f, 0)),
        pl.BlockSpec((1, LANES, width), lambda e, f: (e + first, 0, 0)),
    )


def expert_call(sg, weights):
    n_loc, rows, _ = sg.shape
    width, hidden = weights[0].shape[1:]
    tile = hidden_tile(hidden, 768)
    return call(
        expert_kernel, (), (n_loc, hidden // tile),
        list(zip((sg,) + weights, expert_specs(rows, width, tile))),
        [((n_loc, rows, 2 * width), BF16, pl.BlockSpec((1, rows, 2 * width), lambda e, f: (e, 0, 0)))],
        [
            pltpu.VMEM((rows, LANES), BF16),
            pltpu.VMEM((rows, LANES), BF16),
            pltpu.VMEM((rows, width), F32),
            pltpu.VMEM((width, rows), F32),
            pltpu.VMEM((rows, LANES), F32),
            pltpu.VMEM((LANES, rows), F32),
        ],
        n_loc * rows * 8 * width * hidden, n_loc * rows * hidden,
    )[0]


def expert_grad_call(sg, weights, first, before):
    n_loc, rows, _ = sg.shape
    width, hidden = weights[0].shape[1:]
    tile = hidden_tile(hidden, 768 if rows <= 512 else 384)
    kernel = expert_grad_kernel
    if before:
        kernel = lambda *refs: expert_grad_kernel(*refs[:7], *refs[11:])
    return call(
        kernel, (), (1, hidden // tile),
        list(zip((sg,) + weights, expert_specs(rows, width, tile, first)))
        + [(array, ANY) for array in before],
        [
            ((n_loc, width, LANES), F32, pl.BlockSpec((1, width, LANES), lambda e, f: (e + first, 0, 0))),
            ((n_loc, LANES, hidden), F32, pl.BlockSpec((1, LANES, tile), lambda e, f: (e + first, 0, f))),
            ((n_loc, hidden, LANES), F32, pl.BlockSpec((1, tile, LANES), lambda e, f: (e + first, f, 0))),
            ((n_loc, LANES, width), F32, pl.BlockSpec((1, LANES, width), lambda e, f: (e + first, 0, 0))),
        ],
        [
            pltpu.VMEM((rows, LANES), BF16),
            pltpu.VMEM((rows, LANES), BF16),
            pltpu.VMEM((LANES, rows), BF16),
            pltpu.VMEM((LANES, rows), BF16),
            pltpu.VMEM((rows, LANES), F32),
            pltpu.VMEM((LANES, rows), F32),
        ],
        rows * 4 * width * hidden, rows * hidden,
        {7 + i: i for i in range(4)} if before else {},
    )


def route_back_call(
    place, index, count, cotangent, x2, uo, ur, disp, comb, atts, ret, banks, pack, shards, replicas
):
    n_img, n_tok, width = cotangent.shape
    chunks, starts, columns = pack
    total, n_exp = x2.shape[1], disp.shape[1]
    rows = width // shards
    unit = 16 * replicas
    pack_rows = -(-(3 * rows + n_exp // shards) // unit) * unit
    each = several(n_img, IMAGES_ROUTE)
    here = functools.partial(per_image, images=each)
    return call(
        functools.partial(route_back_kernel, n_exp, starts), (place, index, count), (n_img // each,),
        [
            (cotangent, here(n_tok, width)),
            (x2, here(total, width)),
            (uo, here(total, LANES)),
            (ur, here(total, LANES)),
            (disp, here(n_exp, total)),
            (comb, here(n_exp, total)),
        ]
        + [(att, here(total, GROUP)) for att in atts]
        + [(ret, here(n_exp, 2 * width))]
        + [(bank, whole(bank.shape)) for bank in banks]
        + [(chunk, ANY) for chunk in chunks],
        [
            ((n_img, n_tok, width), BF16, here(n_tok, width)),
            ((n_img, total, width), F32, here(total, width)),
            ((n_img, total, width), BF16, here(total, width)),
            ((shards, pack_rows, LANES), BF16, whole((shards, pack_rows, LANES))),
        ],
        [
            pltpu.VMEM((width, columns), BF16),
            pltpu.VMEM((each * total, width), F32),
            pltpu.VMEM((LANES, width), F32),
            pltpu.VMEM((LANES, width), F32),
            pltpu.VMEM((LANES, width), F32),
            pltpu.VMEM((n_exp, LANES), F32),
            pltpu.SemaphoreType.DMA((4,)),
        ],
        n_img * total * 2 * width * (width + 6 * LANES),
    )


def attention_back_call(index, qkv, gatt, prob, uq, bt, before, h1, group, gbs=(), shards=1):
    n_img, total, _ = qkv.shape
    width = bt.shape[0] // 3
    last = h1 is not None
    each = several(n_img, IMAGES_BACK)
    inputs = [
        (qkv, per_image(total, 3 * GROUP, images=each)),
        (gatt, pl.BlockSpec((each, total, GROUP), lambda i, *_: (i, 0, group))),
        (prob, per_image(GROUP // HEAD_DIM, total, total, images=each)),
        (uq, per_image(total, LANES, images=each)),
        (bt, whole(bt.shape)),
    ]
    outputs = [
        ((n_img, total, 3 * GROUP), BF16, per_image(total, 3 * GROUP, images=each)),
        ((n_img, total, LANES), BF16 if last else F32, per_image(total, LANES, images=each)),
        ((3 * GROUP, LANES), BF16, whole((3 * GROUP, LANES))),
    ]
    scratch = [pltpu.VMEM((LANES, 3 * GROUP), F32)]
    if group:
        inputs.append((before, per_image(total, LANES, images=each)))
    if last:
        inputs.append((h1, per_image(total, width, images=each)))
        inputs.extend((gb, whole(gb.shape)) for gb in gbs)
        shape = (shards, 4 * width // shards, LANES)
        outputs[-1] = (shape, BF16, whole(shape))
        scratch.append(pltpu.VMEM((LANES, width), F32))
    return call(
        functools.partial(attention_back_kernel, group, last),
        (index,) if last else (), (n_img // each,), inputs, outputs, scratch,
        attention_flops(n_img, total, LANES, 5), n_img * total * total * 4,
    )


def input_grad_call(place, images, gx2, guq, bank_a, gqkvs, packs):
    n_img, n_tok, width = images.shape
    total = gx2.shape[1]
    groups = len(gqkvs)
    each = several(n_img, IMAGES_LAST)
    here = functools.partial(per_image, images=each)
    out = call(
        functools.partial(input_grad_kernel, tuple(pack[1] for pack in packs)), (place,), (n_img // each,),
        [
            (images, here(n_tok, width)),
            (gx2, here(total, width)),
            (guq, here(total, LANES)),
            (bank_a, whole(bank_a.shape)),
        ]
        + [(gqkv, here(total, 3 * GROUP)) for gqkv in gqkvs]
        + [(chunk, ANY) for pack in packs for chunk in pack[0]],
        [((images.size // LANES, LANES), F32, whole((images.size // LANES, LANES)))],
        [pltpu.VMEM((width, pack[2]), BF16) for pack in packs]
        + [pltpu.VMEM((each * total, width), F32), pltpu.SemaphoreType.DMA((groups, 4))],
        n_img * total * 2 * width * (3 * width + LANES),
    )[0]
    out = out.reshape(n_tok, width // LANES, n_img, LANES).transpose(2, 0, 1, 3)
    return out.reshape(n_img, n_tok, width)


def swap(array, axis, size, bit):
    return lax.ppermute(array, axis, [(i, i ^ bit) for i in range(size)])


def tie(*arrays):
    return lax.optimization_barrier(arrays)


def own_columns(pack, quarter, pieces):
    part = pack.shape[1] // pieces
    return lax.dynamic_slice(pack, (0, quarter % pieces * part), (pack.shape[0], part))


def spread(rows, shards):
    return jnp.broadcast_to(rows[None], (shards,) + rows.shape)


def over_shard(spread):
    own = lax.all_to_all(spread, "shard", split_axis=0, concat_axis=0, tiled=True)
    return own.reshape(-1, spread.shape[2])


def reduce_pack(pack, replicas):
    where = lax.axis_index("replica")
    bits = []
    bit = 1
    while bit < replicas:
        half = pack.shape[1] // 2
        side = (where // bit) % 2
        keep = lax.dynamic_slice_in_dim(pack, side * half, half, axis=1)
        give = lax.dynamic_slice_in_dim(pack, (1 - side) * half, half, axis=1)
        got = swap(give, "replica", replicas, bit)
        pack = (keep.astype(F32) + got.astype(F32)).astype(BF16)
        bits.append(bit)
        bit *= 2
    landed = lax.all_to_all(pack, "shard", split_axis=0, concat_axis=0, tiled=True)
    total = jnp.sum(landed.astype(F32), axis=0).astype(BF16)
    for bit in reversed(bits):
        got = swap(total, "replica", replicas, bit)
        side = (where // bit) % 2
        total = jnp.where(
            side == 0,
            jnp.concatenate([total, got], axis=0),
            jnp.concatenate([got, total], axis=0),
        )
    return total


def per_device(
    replicas,
    shards,
    images,
    image_adapter_index,
    device_image_count,
    cotangent,
    query_key_value_weight,
    frozen_output_weight,
    frozen_dispatch_weight,
    query_key_value_first,
    query_key_value_second,
    output_adapter_first,
    output_adapter_second,
    dispatch_adapter_first,
    dispatch_adapter_second,
    frozen_up_weight,
    frozen_down_weight,
    up_adapter_first,
    up_adapter_second,
    down_adapter_first,
    down_adapter_second,
):
    n_img, n_tok, width = images.shape
    total = -(-n_tok // 16) * 16
    rows = width // shards
    n_loc = frozen_up_weight.shape[0]
    n_exp = n_loc * shards
    groups = width // GROUP
    quarter = lax.axis_index("replica") % 4
    place = quarter.astype(jnp.int32).reshape(1)

    def qkv_columns(group):
        return [
            query_key_value_weight[:, part * width + group * GROUP : part * width + (group + 1) * GROUP]
            for part in range(3)
        ]

    route_block = jnp.concatenate(
        [
            frozen_dispatch_weight,
            jnp.zeros((rows, 64 - n_exp), BF16),
            jnp.pad(dispatch_adapter_second.T.reshape(16, n_loc * 8), ((0, rows - 16), (0, 0))),
            jnp.zeros((rows, 64 - n_loc * 8), BF16),
        ],
        axis=1,
    )
    empty = jnp.zeros((rows, LANES), BF16)
    packs = [
        (qkv_columns(1) + [output_adapter_second.T, route_block], 2),
        (qkv_columns(2) + [empty, empty], 4),
        ([frozen_output_weight, empty, empty], 4),
    ]
    spread0 = pack_call(
        place,
        (
            query_key_value_weight, query_key_value_first, query_key_value_second.T,
            output_adapter_first, dispatch_adapter_first,
        ),
        shards,
    )
    mine = [own_columns(jnp.concatenate(pack, axis=1), quarter, pieces) for pack, pieces in packs]
    near = functools.partial(swap, axis="replica", size=replicas, bit=1)
    far = functools.partial(swap, axis="replica", size=replicas, bit=2)

    own0 = over_shard(spread0)
    h1 = norm_call(images, cotangent, total)
    own0, h1, mine1, mine2 = tie(own0, h1, *mine[:2])
    own12 = over_shard(spread(jnp.concatenate([mine1, mine2], axis=1), shards))
    y0 = far(own0)
    chunks0 = (own0, near(own0), y0, near(y0))
    *chunks0, h1 = tie(*chunks0, h1)
    pack0 = (chunks0, (0,) * 4, 3 * GROUP + 6 * LANES)
    qkv0, att0, prob0, uq, bank_a, bank_bt, bank_ao, bank_ra = first_attention_call(
        place, image_adapter_index, h1, pack0, n_tok, shards
    )
    uq, own12, mine3 = tie(uq, own12, mine[2])
    first = mine1.shape[1]
    own1, own2 = own12[:, :first], own12[:, first:]
    pack1 = ((own12, near(own1)), (0, 0), 3 * GROUP + 2 * LANES)
    y2 = far(own2)
    own3 = over_shard(spread(mine3, shards))
    qkv1, att1, prob1, bank_bo, bank_wr = next_attention_call(
        place, h1, uq, bank_bt, pack1, n_tok, 1, 2
    )
    att1, uq, own2, y2, own3 = tie(att1, uq, own2, y2, own3)
    pack2 = ((own12, near(own2), y2, near(y2)), (first, 0, 0, 0), 3 * GROUP + 2 * LANES)
    y3 = far(own3)
    qkv2, att2, prob2 = next_attention_call(place, h1, uq, bank_bt, pack2, n_tok, 2, 0)
    att2, own3, y3 = tie(att2, own3, y3)
    pack3 = ((own3, near(own3), y3, near(y3)), (0,) * 4, width + 2 * LANES)
    packs = (pack0, pack1, pack2, pack3)
    atts = (att0, att1, att2)
    bank_rb = bank_wr.reshape(shards, rows, LANES)[:, :16, 64 : 64 + n_loc * 8].reshape(n_exp, LANES)
    x2, uo, ur, disp, comb, sg, bank_wrt = route_call(
        place, image_adapter_index, device_image_count, images, cotangent, atts,
        (bank_ao, bank_bo, bank_ra, bank_wr, bank_rb), packs[3], n_exp, total,
    )

    sent = sg.reshape(n_img, shards, n_loc, -1).transpose(1, 2, 0, 3)
    landed = lax.all_to_all(sent, "shard", split_axis=0, concat_axis=0, tiled=True)
    landed = landed.transpose(1, 0, 2, 3).reshape(n_loc, shards * n_img, -1)
    weights = (
        frozen_up_weight, frozen_down_weight, up_adapter_first, up_adapter_second,
        down_adapter_first, down_adapter_second,
    )
    ret = expert_call(landed, weights)
    over_y = [swap(landed, "replica", replicas, bit) for bit in range(2, replicas, 2)]
    ret, *over_y = tie(ret, *over_y)
    back = ret.reshape(n_loc, shards, n_img, 2 * width).transpose(1, 0, 2, 3)
    back = lax.all_to_all(back, "shard", split_axis=0, concat_axis=0, tiled=True)
    every = jnp.concatenate([landed] + over_y, axis=1)
    every = jnp.concatenate([every, swap(every, "replica", replicas, 1)], axis=1)
    grads = expert_grad_call(every, weights, 0, ())
    back, *grads = tie(back, *grads)
    back = back.transpose(2, 0, 1, 3).reshape(n_img, n_exp, 2 * width)

    block_out, gx2, gatt, out_pack = route_back_call(
        place, image_adapter_index, device_image_count, cotangent, x2, uo, ur, disp, comb, atts, back,
        (bank_ao, bank_bo, bank_ra, bank_wrt, bank_rb), packs[3], shards, replicas,
    )
    out_sum = reduce_pack(out_pack, replicas).astype(F32)

    gqkv0, guq, gb0 = attention_back_call(None, qkv0, gatt, prob0, uq, bank_bt, None, None, 0)
    gqkv1, guq, gb1 = attention_back_call(None, qkv1, gatt, prob1, uq, bank_bt, guq, None, 1)
    gqkv2, guq, qkv_pack = attention_back_call(
        image_adapter_index, qkv2, gatt, prob2, uq, bank_bt, guq, h1, 2, (gb0, gb1), shards
    )
    qkv_sum = reduce_pack(qkv_pack, replicas).astype(F32)
    input_grad = input_grad_call(
        place, images, gx2, guq, bank_a, (gqkv0, gqkv1, gqkv2), packs[:3]
    )
    for expert in range(1, n_loc):
        grads = expert_grad_call(every, weights, expert, tuple(grads))
    return (
        block_out,
        input_grad,
        qkv_sum[3 * rows :],
        qkv_sum[: 3 * rows].T,
        out_sum[:rows],
        out_sum[rows : 2 * rows].T,
        out_sum[2 * rows : 3 * rows],
        out_sum[3 * rows : 3 * rows + n_loc].T,
        *grads,
    )


def solution(mesh):
    images = P(("replica", "shard"), None, None)
    each = P(("replica", "shard"))
    by_row, by_column, by_expert = P("shard", None), P(None, "shard"), P("shard", None, None)
    in_specs = (
        (images, each, each, images)
        + (by_row, by_row, by_row)
        + (by_row, by_column) * 3
        + (by_expert,) * 6
    )
    out_specs = (images, images) + (by_row, by_column) * 3 + (by_expert,) * 4
    return jax.shard_map(
        functools.partial(per_device, mesh.shape["replica"], mesh.shape["shard"]),
        mesh=mesh,
        in_specs=in_specs,
        out_specs=out_specs,
        check_vma=False,
    )
```

time: 411 us -> 318 us (0.77)
  waiting for transfers between devices: 61.8 us -> 24.4 us
  Pallas kernels: 220 us -> 192 us
  local copies, waits for them, and re-layouts: 41.1 us -> 25.6 us
  starting transfers between devices: 59.9 us -> 49.6 us
    pallas_call x12 -> x14, Pallas kernels: 220 us -> 192 us  [call(): pl.pallas_call(kernel, out_shape=shapes, grid_spec=pltpu.PrefetchScalarGr...]
    all_to_all x4 -> x3, waiting for transfers between devices: 33.3 us -> 4.84 us  [over_shard(): lax.all_to_all(spread, 'shard', split_axis=0, concat_axis=0, tiled=True)]
    unnamed x58 -> x42, local copies, waits for them, and re-layouts: 20.3 us -> 10.3 us
    all_to_all x4 -> x3, starting transfers between devices: 23.5 us -> 16.8 us  [over_shard(): lax.all_to_all(spread, 'shard', split_axis=0, concat_axis=0, tiled=True)]
    ppermute x22 -> x20, waiting for transfers between devices: 26 us -> 19.5 us  [swap(): return lax.ppermute(array, axis, [(i, i ^ bit) for i in range(size)])]
    ppermute x22 -> x20, starting transfers between devices: 23.8 us -> 18.7 us  [swap(): return lax.ppermute(array, axis, [(i, i ^ bit) for i in range(size)])]
    concatenate x4 -> x1, local copies, waits for them, and re-layouts: 4.87 us -> 0.11 us  [per_device(): jnp.concatenate(pack, axis=1)]
  transfers between devices with their start and end apart: 29 -> 26, of which waited for: 11 -> 9; matrix products, arithmetic and copies ran while one was open for 7% -> 6% of each run, Pallas kernels for 45% -> 47%
where the time goes in v2:
time: 318 us; the launch traced here: 316 us
  Pallas kernels  192 us (60%)
  starting transfers between devices  49.6 us (16%)
  local copies, waits for them, and re-layouts  25.6 us (8%)
  waiting for transfers between devices  24.4 us (8%)
  blocking collectives  17.3 us (5%)
  other arithmetic  6.21 us (2%)
    pallas_call x14, Pallas kernels, call(): pl.pallas_call(kernel, out_shape=shapes, grid_spec=pltpu.PrefetchScalarGr...  192 us
    ppermute x20, waiting for transfers between devices, swap(): return lax.ppermute(array, axis, [(i, i ^ bit) for i in range(size)])  19.5 us
    ppermute x20, starting transfers between devices, swap(): return lax.ppermute(array, axis, [(i, i ^ bit) for i in range(size)])  18.7 us
    all_to_all x1, blocking collectives, per_device(): lax.all_to_all(sent, 'shard', split_axis=0, concat_axis=0, tiled=True)  17.3 us
    all_to_all x3, starting transfers between devices, over_shard(): lax.all_to_all(spread, 'shard', split_axis=0, concat_axis=0, tiled=True)  16.8 us
    all_to_all x2, starting transfers between devices, reduce_pack(): lax.all_to_all(pack, 'shard', split_axis=0, concat_axis=0, tiled=True)  10.3 us
    unnamed x42, local copies, waits for them, and re-layouts  10.3 us
  transfers between devices with their start and end apart: 26, of which 9 were waited for; matrix products, arithmetic and copies ran while one was open for 6% of the time, Pallas kernels for 47%

profile of v2, /device:TPU:1, one launch (start us, length us, event | category | flops | bytes accessed | tf_op | source)
XLA Modules:
  0.0 316.4 jit_solution(12854372226670643414)
XLA Ops:
  0.7 2.1 shard_map.274
  2.8 6.4 %all-to-all-start = ((bf16[8,96,384]{2,1,0:T(8,128)(2,1)}), bf16[8,96,384]{2,1,0:T(8,128)(2,1)S(1)}, u32[]{:S(2)}, u32[]{:S(2)}) async-start(bf16[8,96,384]{2,1,0:T(8,128)(2,1)} %shard_map.274), calls=%async_computation | async-start | bytes 1179648 | tf_op jit(solution)/shard_map/all_to_all | solution.py:898
  10.7 1.9 copy.48.image_ref
  12.9 2.0 copy.54._.cot_ref
  15.1 3.7 %shard_map.275.h1_ref.refs_7_ = bf16[8,208,768]{2,1,0:T(8,128)(2,1)} custom-call(bf16[8,197,768]{2,1,0:T(8,128)(2,1)} %copy.48.image_ref, bf16[8,197,768]{2,1,0:T(8,128)(2,1)} %copy.54._.cot_ref), custom_call_target="tpu_custom_call" | custom-call | flops 9682944 | bytes 7397376 | tf_op jit(solution)/shard_map/pallas_call | solution.py:586
  19.0 4.8 %all-to-all-done = bf16[8,96,384]{2,1,0:T(8,128)(2,1)S(1)} async-done(((bf16[8,96,384]{2,1,0:T(8,128)(2,1)}), bf16[8,96,384]{2,1,0:T(8,128)(2,1)S(1)}, u32[]{:S(2)}, u32[]{:S(2)}) %all-to-all-start) | async-done | bytes 589856 | tf_op jit(solution)/shard_map/all_to_all | solution.py:898
  23.8 1.2 broadcast_in_dim.4
  25.0 5.0 %all-to-all-start.1 = ((bf16[8,96,768]{2,1,0:T(8,128)(2,1)}), bf16[8,96,768]{2,1,0:T(8,128)(2,1)S(1)}, u32[]{:S(2)}, u32[]{:S(2)}) async-start(bf16[8,96,768]{2,1,0:T(8,128)(2,1)} %broadcast_in_dim.4), calls=%async_computation.1 | async-start | bytes 2359296 | tf_op jit(solution)/shard_map/all_to_all | solution.py:898
  30.0 1.2 collective-permute-start.1
  31.3 1.1 collective-permute-start
  32.4 11.7 %collective-permute-done.1.rest_2_.refs_5_ = bf16[768,384]{1,0:T(8,128)(2,1)S(1)} collective-permute-done((bf16[768,384]{1,0:T(8,128)(2,1)S(1)}, bf16[768,384]{1,0:T(8,128)(2,1)S(1)}, u32[]{:S(2)}, u32[]{:S(2)}) %collective-permute-start.1) | collective-permute-done | bytes 589856 | tf_op jit(solution)/shard_map/ppermute | solution.py:881
  44.1 1.7 collective-permute-start.2
  45.8 1.6 collective-permute-done.2.rest_3_.refs_6_
  48.2 17.3 %shard_map.276 = (bf16[8,208,768]{2,1,0:T(8,128)(2,1)}, bf16[8,208,256]{2,1,0:T(8,128)(2,1)}, bf16[8,4,208,208]{3,2,1,0:T(8,128)(2,1)}, bf16[8,208,128]{2,1,0:T(...) custom-call(s32[1]{0:T(128)} %bitcast.place_ref, ...), custom_call_target="tpu_custom_call" | custom-call | flops 2317352960 | bytes 12697600 | tf_op jit(solution)/shard_map/pallas_call | solution.py:586
  65.5 1.0 slice.51
  67.7 5.4 %all-to-all-start.2 = ((bf16[8,96,256]{2,1,0:T(8,128)(2,1)}), bf16[8,96,256]{2,1,0:T(8,128)(2,1)S(1)}, u32[]{:S(2)}, u32[]{:S(2)}) async-start(bf16[8,96,256]{2,1,0:T(8,128)(2,1)} %broadcast_in_dim.5), calls=%async_computation.2 | async-start | bytes 786432 | tf_op jit(solution)/shard_map/all_to_all | solution.py:898
  73.2 1.3 collective-permute-start.4
  75.4 13.2 %shard_map.277 = (bf16[8,208,768]{2,1,0:T(8,128)(2,1)}, bf16[8,208,256]{2,1,0:T(8,128)(2,1)}, bf16[8,4,208,208]{3,2,1,0:T(8,128)(2,1)}, bf16[768,128]{1,0:T(8,128)(2,1)}, bf16[768,128]{1,0:T(8,128)(2,1)}) custom-call(s32[1]{0:T(128)} %bitcast.place_ref, bf16[8,208,768]{2,1,0:T(8,128)(2,1)} %shard_map.275.h1_ref.refs_7_, ...), custom_call_target="tpu_custom_call" | custom-call | flops 2317352960 | bytes 12107776 | tf_op jit(solution)/shard_map/pallas_call | solution.py:586
  89.7 1.0 collective-permute-done.5.rest_1_.refs_10_
  92.3 13.3 %shard_map.278 = (bf16[8,208,768]{2,1,0:T(8,128)(2,1)}, bf16[8,208,256]{2,1,0:T(8,128)(2,1)}, bf16[8,4,208,208]{3,2,1,0:T(8,128)(2,1)}) custom-call(s32[1]{0:T(128)} %bitcast.place_ref, bf16[8,208,768]{2,1,0:T(8,128)(2,1)} %shard_map.275.h1_ref.refs_7_, bf16[8,208,128]{2,1,0:T(8,128)(2,1)} %get-tuple-element.100.uq_ref.refs_3_.refs_4_, ...), custom_call_target="tpu_custom_call" | custom-call | flops 2317352960 | bytes 12107776 | tf_op jit(solution)/shard_map/pallas_call | solution.py:586
  109.3 16.8 %shard_map.279 = (f32[8,208,768]{2,1,0:T(8,128)}, bf16[8,208,128]{2,1,0:T(8,128)(2,1)}, bf16[8,208,128]{2,1,0:T(8,128)(2,1)}, f32[8,16,208]{2,1,0:T(8,128)}, f32...) custom-call(s32[1]{0:T(128)} %bitcast.place_ref, s32[8]{0:T(128)} %refs_0_.1, ...), custom_call_target="tpu_custom_call" | custom-call | flops 2944401408 | bytes 16388096 | tf_op jit(solution)/shard_map/pallas_call | solution.py:586
  126.1 1.1 copy.57
  127.2 17.3 %all_to_all.35 = bf16[8,2,8,1664]{3,2,1,0:T(8,128)(2,1)S(1)} all-to-all(bf16[8,2,8,1664]{3,2,1,0:T(8,128)(2,1)S(1)} %bitcast.43), channel_id=1, replica_groups=mesh['replica'=4,'shard'=8] {'shard'}, dimensions={0} | all-to-all | bytes 851968 | tf_op jit(solution)/shard_map/all_to_all | solution.py:1028
  145.7 15.3 %shard_map.280 = bf16[2,64,1536]{2,1,0:T(8,128)(2,1)} custom-call(bf16[2,64,1664]{2,1,0:T(8,128)(2,1)} %copy_bitcast_fusion.sg_ref, bf16[2,768,3072]{2,1,0:T(8,128)(2,1)} %refs_1_.1, bf16[2,3072,768]{2,1,0:T(8,128)(2,1)} %refs_2_.1, bf16[2,768,128]{2,1,0:T(8,128)(2,1)} %refs_3_.1, bf16[2,128,3072]{2,1,0:T(8,128)(2,1)} %refs_4_.1, ...), custom_call_target="tpu_custom_call" | custom-call | flops 2415919104 | bytes 23625728 | tf_op jit(solution)/shard_map/pallas_call | solution.py:586
  161.0 1.1 pad_maximum_fusion.1
  162.0 2.2 collective-permute-start.11
  164.2 2.1 copy.60
  166.4 3.7 %all-to-all-start.4 = ((bf16[8,2,8,1536]{3,1,2,0:T(2,128)(2,1)}), bf16[8,2,8,1536]{3,1,2,0:T(2,128)(2,1)S(1)}, u32[]{:S(2)}, u32[]{:S(2)}) async-start(bf16[8,2,8,1536]{3,1,2,0:T(2,128)(2,1)} %bitcast.31), calls=%async_computation.4 | async-start | bytes 786432 | tf_op jit(solution)/shard_map/all_to_all | solution.py:1038
  170.1 2.3 pad_maximum_fusion.sg_ref.refs_0_
  172.4 12.7 %shard_map.281 = (f32[2,768,128]{2,1,0:T(8,128)}, f32[2,128,3072]{2,1,0:T(8,128)}, f32[2,3072,128]{2,1,0:T(8,128)}, f32[2,128,768]{2,1,0:T(8,128)}) custom-call(bf16[2,256,1664]{2,1,0:T(8,128)(2,1)} %pad_maximum_fusion.sg_ref.refs_0_, bf16[2,768,3072]{2,1,0:T(8,128)(2,1)} %refs_1_.1, bf16[2,3072,768]{2,1,0:T(8,128)(2,1)} %refs_2_.1, ...), custom_call_target="tpu_custom_call" | custom-call | flops 2415919104 | bytes 32374784 | tf_op jit(solution)/shard_map/pallas_call | solution.py:586
  186.3 24.0 %shard_map.282 = (bf16[8,197,768]{2,1,0:T(8,128)(2,1)}, f32[8,208,768]{2,1,0:T(8,128)}, bf16[8,208,768]{2,1,0:T(8,128)(2,1)}, bf16[8,320,128]{2,1,0:T(8,128)(2,1)}) custom-call(s32[1]{0:T(128)} %bitcast.place_ref, s32[8]{0:T(128)} %refs_0_.1, s32[1]{0:T(128)S(6)} %copy.65.count_ref, bf16[8,197,768]{2,1,0:T(8,128)(2,1)} %copy.54._.cot_ref, ...), custom_call_target="tpu_custom_call" | custom-call | flops 3925868544 | bytes 24481792 | tf_op jit(solution)/shard_map/pallas_call | solution.py:586
  211.4 12.5 %shard_map.283 = (bf16[8,208,768]{2,1,0:T(8,128)(2,1)}, f32[8,208,128]{2,1,0:T(8,128)}, bf16[768,128]{1,0:T(8,128)(2,1)}) custom-call(bf16[8,208,768]{2,1,0:T(8,128)(2,1)} %get-tuple-element.133.refs_0_, bf16[8,208,768]{2,1,0:T(8,128)(2,1)} %get-tuple-element.129.refs_1_.refs_2_, bf16[8,4,208,208]{3,2,1,0:T(8,128)(2,1)} %get-tuple-element.134.refs_2_, ...), custom_call_target="tpu_custom_call" | custom-call | flops 1213202432 | bytes 12500992 | tf_op jit(solution)/shard_map/pallas_call | solution.py:586
  224.0 12.7 %shard_map.284 = (bf16[8,208,768]{2,1,0:T(8,128)(2,1)}, f32[8,208,128]{2,1,0:T(8,128)}, bf16[768,128]{1,0:T(8,128)(2,1)}) custom-call(bf16[8,208,768]{2,1,0:T(8,128)(2,1)} %get-tuple-element.131.refs_0_, bf16[8,208,768]{2,1,0:T(8,128)(2,1)} %get-tuple-element.129.refs_1_.refs_2_, bf16[8,4,208,208]{3,2,1,0:T(8,128)(2,1)} %get-tuple-element.132.refs_2_, ...), custom_call_target="tpu_custom_call" | custom-call | flops 1213202432 | bytes 13352960 | tf_op jit(solution)/shard_map/pallas_call | solution.py:586
  236.6 15.5 %shard_map.285 = (bf16[8,208,768]{2,1,0:T(8,128)(2,1)}, bf16[8,208,128]{2,1,0:T(8,128)(2,1)}, bf16[8,384,128]{2,1,0:T(8,128)(2,1)}) custom-call(s32[8]{0:T(128)} %refs_0_.1, bf16[8,208,768]{2,1,0:T(8,128)(2,1)} %get-tuple-element.128.refs_1_, bf16[8,208,768]{2,1,0:T(8,128)(2,1)} %get-tuple-element.129.refs_1_.refs_2_, ...), custom_call_target="tpu_custom_call" | custom-call | flops 1213202432 | bytes 16465920 | tf_op jit(solution)/shard_map/pallas_call | solution.py:586
  252.2 1.0 constant_dynamic-slice_fusion.3
  253.9 1.1 collective-permute-start.17
  255.1 1.1 add_convert_fusion
  256.3 1.1 collective-permute-start.13
  257.3 2.4 collective-permute-done.17
  260.4 4.9 %all-to-all-start.6 = ((bf16[8,80,128]{2,1,0:T(8,128)(2,1)}), bf16[8,80,128]{2,1,0:T(8,128)(2,1)S(1)}, u32[]{:S(2)}, u32[]{:S(2)}) async-start(bf16[8,80,128]{2,1,0:T(8,128)(2,1)} %add_convert_fusion.3), calls=%async_computation.6 | async-start | bytes 327680 | tf_op jit(solution)/shard_map/all_to_all | solution.py:915
  265.3 19.7 %shard_map.286 = f32[9456,128]{1,0:T(8,128)} custom-call(s32[1]{0:T(128)} %bitcast.place_ref, bf16[8,197,768]{2,1,0:T(8,128)(2,1)} %copy.48.image_ref, f32[8,208,768]{2,1,0:T(8,128)} %get-tuple-element.127.gx2_ref, bf16[8,208,128]{2,1,0:T(8,128)(2,1)} %get-tuple-element.139.guq_ref, bf16[768,128]{1,0:T(8,128)(2,1)} %get-tuple-element.140.a_ref, ...), custom_call_target="tpu_custom_call" | custom-call | flops 6215958528 | bytes 27348992 | tf_op jit(solution)/shard_map/pallas_call | solution.py:586
  285.1 1.1 collective-permute-start.18
  286.9 5.4 %all-to-all-start.5 = ((bf16[8,96,128]{2,1,0:T(8,128)(2,1)}), bf16[8,96,128]{2,1,0:T(8,128)(2,1)S(1)}, u32[]{:S(2)}, u32[]{:S(2)}) async-start(bf16[8,96,128]{2,1,0:T(8,128)(2,1)} %add_convert_fusion.2), calls=%async_computation.5 | async-start | bytes 393216 | tf_op jit(solution)/shard_map/all_to_all | solution.py:915
  292.4 2.9 collective-permute-start.19
  295.3 12.8 %shard_map.287 = (f32[2,768,128]{2,1,0:T(8,128)}, f32[2,128,3072]{2,1,0:T(8,128)}, f32[2,3072,128]{2,1,0:T(8,128)}, f32[2,128,768]{2,1,0:T(8,128)}) custom-call(bf16[2,256,1664]{2,1,0:T(8,128)(2,1)} %pad_maximum_fusion.sg_ref.refs_0_, bf16[2,768,3072]{2,1,0:T(8,128)(2,1)} %refs_1_.1, ...), custom_call_target="tpu_custom_call", output_to_operand_aliasing={{0}: (7, {}), {1}: (8, {}), {2}: (9, {}), {3}: (10, {})} | custom-call | flops 2415919104 | bytes 40239104 | tf_op jit(solution)/shard_map/pallas_call | solution.py:586
  308.1 1.9 copy.56
  311.2 1.6 collective-permute-done.14
  312.8 1.4 collective-permute-start.15
  (103 shorter events, 20.0 us)
Async XLA Ops:
  0.6 10.0 %copy-start.2 = (bf16[8,197,768]{2,0,1:T(8,128)(2,1)S(1)}, bf16[8,197,768]{2,0,1:T(8,128)(2,1)}, u32[]{:S(2)}) copy-start(bf16[8,197,768]{2,0,1:T(8,128)(2,1)} %param.19) | copy-start | bytes 7262212
  2.8 21.0 %all-to-all-start = ((bf16[8,96,384]{2,1,0:T(8,128)(2,1)}), bf16[8,96,384]{2,1,0:T(8,128)(2,1)S(1)}, u32[]{:S(2)}, u32[]{:S(2)}) async-start(bf16[8,96,384]{2,1,0:T(8,128)(2,1)} %shard_map.274), calls=%async_computation | async-start | bytes 1179648 | tf_op jit(solution)/shard_map/all_to_all | solution.py:898
  10.7 2.3 copy-start.3
  12.9 2.0 copy-start.5
  12.9 2.0 copy-start.15
  18.8 27.0 %copy-start.14 = (bf16[96,768]{1,0:T(8,128)(2,1)S(1)}, bf16[96,768]{1,0:T(8,128)(2,1)}, u32[]{:S(2)}) copy-start(bf16[96,768]{1,0:T(8,128)(2,1)} %param.24) | copy-start | bytes 442372
  23.8 23.6 %copy-start.4 = (bf16[8,96,384]{2,1,0:T(8,128)(2,1)}, bf16[8,96,384]{2,1,0:T(8,128)(2,1)S(1)}, u32[]{:S(2)}) copy-start(bf16[8,96,384]{2,1,0:T(8,128)(2,1)S(1)} %all-to-all-done) | copy-start | bytes 1769476
  25.0 40.5 %all-to-all-start.1 = ((bf16[8,96,768]{2,1,0:T(8,128)(2,1)}), bf16[8,96,768]{2,1,0:T(8,128)(2,1)S(1)}, u32[]{:S(2)}, u32[]{:S(2)}) async-start(bf16[8,96,768]{2,1,0:T(8,128)(2,1)} %broadcast_in_dim.4), calls=%async_computation.1 | async-start | bytes 2359296 | tf_op jit(solution)/shard_map/all_to_all | solution.py:898
  30.0 14.0 %collective-permute-start.1 = (bf16[768,384]{1,0:T(8,128)(2,1)S(1)}, bf16[768,384]{1,0:T(8,128)(2,1)S(1)}, u32[]{:S(2)}, u32[]{:S(2)}) collective-permute-start(bf16[768,384]{1,0:T(8,128)(2,1)S(1)} %bitcast.39), channel_id=1, source_target_pairs={{0,16},{8,24},{16,0},{24,8},{1,17},{9,25},{17,1},{25,9},{2,18},{10... | collective-permute-start | bytes 1769480 | tf_op jit(solution)/shard_map/ppermute | solution.py:881
  31.3 14.5 %collective-permute-start = (bf16[768,384]{1,0:T(8,128)(2,1)S(1)}, bf16[768,384]{1,0:T(8,128)(2,1)S(1)}, u32[]{:S(2)}, u32[]{:S(2)}) collective-permute-start(bf16[768,384]{1,0:T(8,128)(2,1)S(1)} %bitcast.40), channel_id=1, source_target_pairs={{0,8},{8,0},{16,24},{24,16},{1,9},{9,1},{17,25},{25,17},{2,10},{10... | collective-permute-start | bytes 1769480 | tf_op jit(solution)/shard_map/ppermute | solution.py:881
  44.1 3.3 %copy-start.8 = (bf16[768,384]{1,0:T(8,128)(2,1)}, bf16[768,384]{1,0:T(8,128)(2,1)S(1)}, u32[]{:S(2)}) copy-start(bf16[768,384]{1,0:T(8,128)(2,1)S(1)} %collective-permute-done.1.rest_2_.refs_5_) | copy-start | bytes 1769476
  44.1 3.3 %collective-permute-start.2 = (bf16[768,384]{1,0:T(8,128)(2,1)S(1)}, bf16[768,384]{1,0:T(8,128)(2,1)S(1)}, u32[]{:S(2)}, u32[]{:S(2)}) collective-permute-start(bf16[768,384]{1,0:T(8,128)(2,1)S(1)} %collective-permute-done.1.rest_2_.refs_5_), channel_id=1, source_target_pairs={{0,8},{8,0},{16,24},{24,16},{1,9},{9,1},{17,25},{25,17},{2,10},{10... | collective-permute-start | bytes 1769480 | tf_op jit(solution)/shard_map/ppermute | solution.py:881
  45.8 1.6 copy-start.9
  47.4 0.8 copy-start.10
  65.5 9.0 %copy-start = (bf16[8,96,768]{2,1,0:T(8,128)(2,1)}, bf16[8,96,768]{2,1,0:T(8,128)(2,1)S(1)}, u32[]{:S(2)}) copy-start(bf16[8,96,768]{2,1,0:T(8,128)(2,1)S(1)} %all-to-all-done.1) | copy-start | bytes 3538948
  66.6 7.9 %collective-permute-start.3 = (bf16[768,512]{1,0:T(8,128)(2,1)}, bf16[768,512]{1,0:T(8,128)(2,1)S(1)}, u32[]{:S(2)}, u32[]{:S(2)}) collective-permute-start(bf16[768,512]{1,0:T(8,128)(2,1)} %slice.51), channel_id=1, source_target_pairs={{0,8},{8,0},{16,24},{24,16},{1,9},{9,1},{17,25},{25,17},{2,10},{10... | collective-permute-start | bytes 2359304 | tf_op jit(solution)/shard_map/ppermute | solution.py:881
  67.7 20.9 %all-to-all-start.2 = ((bf16[8,96,256]{2,1,0:T(8,128)(2,1)}), bf16[8,96,256]{2,1,0:T(8,128)(2,1)S(1)}, u32[]{:S(2)}, u32[]{:S(2)}) async-start(bf16[8,96,256]{2,1,0:T(8,128)(2,1)} %broadcast_in_dim.5), calls=%async_computation.2 | async-start | bytes 786432 | tf_op jit(solution)/shard_map/all_to_all | solution.py:898
  73.2 15.4 %collective-permute-start.4 = (bf16[768,256]{1,0:T(8,128)(2,1)S(1)}, bf16[768,256]{1,0:T(8,128)(2,1)}, u32[]{:S(2)}, u32[]{:S(2)}) collective-permute-start(bf16[768,256]{1,0:T(8,128)(2,1)S(1)} %slice.52), channel_id=1, source_target_pairs={{0,16},{8,24},{16,0},{24,8},{1,17},{9,25},{17,1},{25,9},{2,18},{10... | collective-permute-start | bytes 1179656 | tf_op jit(solution)/shard_map/ppermute | solution.py:881
  74.5 0.9 copy-start.6
  88.6 17.0 %copy-start.11 = (bf16[8,96,256]{2,1,0:T(8,128)(2,1)}, bf16[8,96,256]{2,1,0:T(8,128)(2,1)S(1)}, u32[]{:S(2)}) copy-start(bf16[8,96,256]{2,1,0:T(8,128)(2,1)S(1)} %all-to-all-done.2) | copy-start | bytes 1179652
  88.6 2.1 collective-permute-start.5
  89.4 2.1 collective-permute-start.6
  89.5 16.1 %collective-permute-start.7 = (bf16[768,256]{1,0:T(8,128)(2,1)S(1)}, bf16[768,256]{1,0:T(8,128)(2,1)S(1)}, u32[]{:S(2)}, u32[]{:S(2)}) collective-permute-start(bf16[768,256]{1,0:T(8,128)(2,1)S(1)} %bitcast.46), channel_id=1, source_target_pairs={{0,16},{8,24},{16,0},{24,8},{1,17},{9,25},{17,1},{25,9},{2,18},{10... | collective-permute-start | bytes 1179656 | tf_op jit(solution)/shard_map/ppermute | solution.py:881
  90.8 0.8 copy-start.12
  91.5 0.8 copy-start.13
  105.6 2.8 copy-start.16
  105.6 2.8 collective-permute-start.8
  106.1 2.3 collective-permute-start.9
  108.4 0.7 copy-start.17
  108.4 0.9 copy-start.18
  145.3 15.7 %collective-permute-start.10 = (bf16[2,64,1664]{2,1,0:T(8,128)(2,1)}, bf16[2,64,1664]{2,1,0:T(8,128)(2,1)S(1)}, u32[]{:S(2)}, u32[]{:S(2)}) collective-permute-start(bf16[2,64,1664]{2,1,0:T(8,128)(2,1)} %copy_bitcast_fusion.sg_ref), channel_id=1, source_target_pairs={{0,16},{8,24},{16,0},{24,8},{1,17},{9,25},{17,1},{25,9},{2,18},{10... | collective-permute-start | bytes 1277960 | tf_op jit(solution)/shard_map/ppermute | solution.py:881
  162.0 8.0 %collective-permute-start.11 = (bf16[2,128,1664]{2,1,0:T(8,128)(2,1)S(1)}, bf16[2,128,1664]{2,1,0:T(8,128)(2,1)S(1)}, u32[]{:S(2)}, u32[]{:S(2)}) collective-permute-start(bf16[2,128,1664]{2,1,0:T(8,128)(2,1)S(1)} %pad_maximum_fusion.1), channel_id=1, source_target_pairs={{0,8},{8,0},{16,24},{24,16},{1,9},{9,1},{17,25},{25,17},{2,10},{10... | collective-permute-start | bytes 2555912 | tf_op jit(solution)/shard_map/ppermute | solution.py:881
  166.4 18.8 %all-to-all-start.4 = ((bf16[8,2,8,1536]{3,1,2,0:T(2,128)(2,1)}), bf16[8,2,8,1536]{3,1,2,0:T(2,128)(2,1)S(1)}, u32[]{:S(2)}, u32[]{:S(2)}) async-start(bf16[8,2,8,1536]{3,1,2,0:T(2,128)(2,1)} %bitcast.31), calls=%async_computation.4 | async-start | bytes 786432 | tf_op jit(solution)/shard_map/all_to_all | solution.py:1038
  211.3 42.5 %collective-permute-start.16 = (bf16[8,160,128]{2,1,0:T(8,128)(2,1)S(1)}, bf16[8,160,128]{2,1,0:T(8,128)(2,1)S(1)}, u32[]{:S(2)}, u32[]{:S(2)}) collective-permute-start(bf16[8,160,128]{2,1,0:T(8,128)(2,1)S(1)} %constant_dynamic-slice_fusion.1), channel_id=1, source_target_pairs={{0,8},{8,0},{16,24},{24,16},{1,9},{9,1},{17,25},{25,17},{2,10},{10... | collective-permute-start | bytes 983048 | tf_op jit(solution)/shard_map/ppermute | solution.py:881
  236.6 17.2 %copy-start.7 = (bf16[8,320,128]{2,1,0:T(8,128)(2,1)S(1)}, bf16[8,320,128]{2,1,0:T(8,128)(2,1)}, u32[]{:S(2)}) copy-start(bf16[8,320,128]{2,1,0:T(8,128)(2,1)} %get-tuple-element.145) | copy-start | bytes 1966084
  253.2 1.9 collective-permute-start.12
  253.9 5.8 %collective-permute-start.17 = (bf16[8,80,128]{2,1,0:T(8,128)(2,1)S(1)}, bf16[8,80,128]{2,1,0:T(8,128)(2,1)S(1)}, u32[]{:S(2)}, u32[]{:S(2)}) collective-permute-start(bf16[8,80,128]{2,1,0:T(8,128)(2,1)S(1)} %constant_dynamic-slice_fusion), channel_id=1, source_target_pairs={{0,16},{8,24},{16,0},{24,8},{1,17},{9,25},{17,1},{25,9},{2,18},{10... | collective-permute-start | bytes 491528 | tf_op jit(solution)/shard_map/ppermute | solution.py:881
  256.3 29.9 %collective-permute-start.13 = (bf16[8,96,128]{2,1,0:T(8,128)(2,1)S(1)}, bf16[8,96,128]{2,1,0:T(8,128)(2,1)S(1)}, u32[]{:S(2)}, u32[]{:S(2)}) collective-permute-start(bf16[8,96,128]{2,1,0:T(8,128)(2,1)S(1)} %constant_dynamic-slice_fusion.2), channel_id=1, source_target_pairs={{0,16},{8,24},{16,0},{24,8},{1,17},{9,25},{17,1},{25,9},{2,18},{10... | collective-permute-start | bytes 589832 | tf_op jit(solution)/shard_map/ppermute | solution.py:881
  260.4 24.6 %all-to-all-start.6 = ((bf16[8,80,128]{2,1,0:T(8,128)(2,1)}), bf16[8,80,128]{2,1,0:T(8,128)(2,1)S(1)}, u32[]{:S(2)}, u32[]{:S(2)}) async-start(bf16[8,80,128]{2,1,0:T(8,128)(2,1)} %add_convert_fusion.3), calls=%async_computation.6 | async-start | bytes 327680 | tf_op jit(solution)/shard_map/all_to_all | solution.py:915
  285.1 7.3 %collective-permute-start.18 = (bf16[80,128]{1,0:T(8,128)(2,1)S(1)}, bf16[80,128]{1,0:T(8,128)(2,1)S(1)}, u32[]{:S(2)}, u32[]{:S(2)}) collective-permute-start(bf16[80,128]{1,0:T(8,128)(2,1)S(1)} %reduce_sum.25), channel_id=1, source_target_pairs={{0,16},{8,24},{16,0},{24,8},{1,17},{9,25},{17,1},{25,9},{2,18},{10... | collective-permute-start | bytes 61448 | tf_op jit(solution)/shard_map/ppermute | solution.py:881
  286.9 23.1 %all-to-all-start.5 = ((bf16[8,96,128]{2,1,0:T(8,128)(2,1)}), bf16[8,96,128]{2,1,0:T(8,128)(2,1)S(1)}, u32[]{:S(2)}, u32[]{:S(2)}) async-start(bf16[8,96,128]{2,1,0:T(8,128)(2,1)} %add_convert_fusion.2), calls=%async_computation.5 | async-start | bytes 393216 | tf_op jit(solution)/shard_map/all_to_all | solution.py:915
  292.4 15.7 %copy-start.1 = (bf16[8,197,768]{2,1,0:T(8,128)(2,1)S(1)}, bf16[8,197,768]{2,1,0:T(8,128)(2,1)}, u32[]{:S(2)}) copy-start(bf16[8,197,768]{2,1,0:T(8,128)(2,1)} %get-tuple-element.166) | copy-start | bytes 7262212
  292.4 17.6 %collective-permute-start.19 = (bf16[160,128]{1,0:T(8,128)(2,1)S(1)}, bf16[160,128]{1,0:T(8,128)(2,1)S(1)}, u32[]{:S(2)}, u32[]{:S(2)}) collective-permute-start(bf16[160,128]{1,0:T(8,128)(2,1)S(1)} %maximum_select_fusion.3), channel_id=1, source_target_pairs={{0,8},{8,0},{16,24},{24,16},{1,9},{9,1},{17,25},{25,17},{2,10},{10... | collective-permute-start | bytes 122888 | tf_op jit(solution)/shard_map/ppermute | solution.py:881
  310.0 2.7 collective-permute-start.14
  312.8 2.3 collective-permute-start.15

commit v3 on v2

--- a/solution.py
+++ b/solution.py
@@ -22,9 +22,10 @@
 GELU_C = 0.7978845608028654
 GELU_A = 0.044715
 IMAGES_FORWARD = 2
-IMAGES_BACK = 2
+IMAGES_BACK = 1
 IMAGES_ROUTE = 2
 IMAGES_LAST = 2
+STRIPS = 4
 
 
 def dot(left, right, dims=NN):
@@ -104,21 +105,21 @@
     return ref[...].reshape(ref.shape[0] * ref.shape[1], ref.shape[2])
 
 
-def assemble(place, chunks, starts, wall, sems):
-    pieces = len(chunks)
+def assemble(place_ref, chunks, layout, wall):
+    pieces, entries = layout
     part = wall.shape[1] // pieces
-    copies = []
-    for step in range(pieces):
-        column = pl.multiple_of(((place % pieces) ^ step) * part, LANES)
-        copies.append(
-            pltpu.make_async_copy(
-                chunks[step].at[:, pl.ds(starts[step], part)], wall.at[:, pl.ds(column, part)], sems.at[step]
-            )
-        )
-    for copy in copies:
-        copy.start()
-    for copy in copies:
-        copy.wait()
+    for chunk, (replica, neighbour, start) in zip(chunks, entries):
+        column = pl.multiple_of(((place_ref[0] % pieces) ^ replica) * part, LANES)
+        if neighbour is None:
+            wall[:, pl.ds(column, part)] = chunk[:, start : start + part]
+            continue
+        strips = STRIPS
+        rows = chunk.shape[0] // strips
+        for strip in range(strips):
+            row = pl.multiple_of((2 * strip + (place_ref[1] ^ neighbour)) * rows, 16)
+            wall[pl.ds(row, rows), pl.ds(column, part)] = chunk[
+                strip * rows : (strip + 1) * rows, start : start + part
+            ]
 
 
 def norm_kernel(image_ref, _, out_ref, pad_ref):
@@ -127,7 +128,7 @@
 
 
 def pack_kernel(place_ref, qkv_ref, a_ref, b_ref, ao_ref, ra_ref, out_ref, pack):
-    shards, rows, part = out_ref.shape
+    copies, rows, part = out_ref.shape
     width = qkv_ref.shape[1] // 3
     for piece in range(3):
         pack[:, piece * GROUP : (piece + 1) * GROUP] = qkv_ref[:, piece * width : piece * width + GROUP]
@@ -137,8 +138,8 @@
     pack[:, width + 4 * LANES : width + 5 * LANES] = ao_ref[...]
     pack[:, width + 5 * LANES : width + 6 * LANES] = ra_ref[...]
     mine = pack[:, pl.ds(pl.multiple_of(place_ref[0] * part, LANES), part)]
-    for shard in range(shards):
-        out_ref[shard] = mine
+    for copy in range(copies):
+        out_ref[copy] = mine
 
 
 def head_mask(value):
@@ -148,36 +149,48 @@
     return low, high
 
 
+def each_head(columns, value):
+    head = lax.broadcasted_iota(jnp.int32, (1, GROUP), 1) // HEAD_DIM
+    return jnp.concatenate(
+        [
+            columns * jnp.where(head == number, value, 0.0).astype(BF16)
+            for number in range(GROUP // HEAD_DIM)
+        ],
+        axis=0,
+    )
+
+
+def merge_pair(low, high):
+    lane = lax.broadcasted_iota(jnp.int32, (1, LANES), 1)
+    return jnp.where(lane < HEAD_DIM, low, high)
+
+
 def attention_forward(qkv, n_tok, prob_ref, slot):
-    masks = head_mask(0.125)
-    value_t = qkv[:, 2 * GROUP :].T
+    total = qkv.shape[0]
+    every = dot(each_head(qkv[:, GROUP : 2 * GROUP], 0.125), qkv[:, :GROUP], NT)
     outs = []
-    for pair in range(GROUP // LANES):
-        q_pair = qkv[:, pair * LANES : (pair + 1) * LANES]
-        k_pair = qkv[:, GROUP + pair * LANES : GROUP + (pair + 1) * LANES]
-        both = dot(jnp.concatenate([k_pair * masks[0], k_pair * masks[1]], axis=0), q_pair, NT)
-        for side in range(2):
-            total = k_pair.shape[0]
-            scores = mask_tail(both[side * total : (side + 1) * total], n_tok)
-            powers = jnp.exp(scores - jnp.max(scores, axis=0, keepdims=True))
-            probs = (powers * (1.0 / jnp.sum(powers, axis=0, keepdims=True))).astype(BF16)
-            head = 2 * pair + side
-            prob_ref[slot, head] = probs
-            outs.append(dot(value_t[head * HEAD_DIM : (head + 1) * HEAD_DIM], probs).astype(BF16))
-    return zero_tail(jnp.concatenate(outs, axis=0).T, n_tok)
+    for head in range(GROUP // HEAD_DIM):
+        scores = mask_tail(every[head * total : (head + 1) * total], n_tok)
+        powers = jnp.exp(scores - jnp.max(scores, axis=0, keepdims=True))
+        probs = (powers * (1.0 / jnp.sum(powers, axis=0, keepdims=True))).astype(BF16)
+        prob_ref[slot, head] = probs
+        column = 2 * GROUP + head // 2 * LANES
+        outs.append(dot(probs, qkv[:, column : column + LANES], TN))
+    pairs = [merge_pair(outs[head], outs[head + 1]) for head in range(0, len(outs), 2)]
+    return zero_tail(jnp.concatenate(pairs, axis=1).astype(BF16), n_tok)
 
 
 def first_attention_kernel(
-    n_tok, shards, starts, place_ref, index_ref, h1_ref, *rest,
+    n_tok, shards, layout, place_ref, index_ref, h1_ref, *rest,
 ):
-    chunks, rest = rest[: len(starts)], rest[len(starts) :]
-    qkv_ref, att_ref, prob_ref, uq_ref, a_ref, bt_ref, ao_ref, ra_ref, wall, sems = rest
+    chunks, rest = rest[: len(layout[1])], rest[len(layout[1]) :]
+    qkv_ref, att_ref, prob_ref, uq_ref, a_ref, bt_ref, ao_ref, ra_ref, wall = rest
     step = pl.program_id(0)
     n_img, total, width = h1_ref.shape
 
     @pl.when(step == 0)
     def _():
-        assemble(place_ref[0], chunks, starts, wall, sems)
+        assemble(place_ref, chunks, layout, wall)
         a_ref[...] = wall[:, width : width + LANES]
         ao_ref[...] = wall[:, width + 4 * LANES : width + 5 * LANES]
         ra_ref[...] = wall[:, width + 5 * LANES : width + 6 * LANES]
@@ -215,15 +228,15 @@
 
 
 def next_attention_kernel(
-    n_tok, group, extra, starts, place_ref, h1_ref, uq_ref, bt_ref, *rest
+    n_tok, group, extra, layout, place_ref, h1_ref, uq_ref, bt_ref, *rest
 ):
-    chunks, rest = rest[: len(starts)], rest[len(starts) :]
+    chunks, rest = rest[: len(layout[1])], rest[len(layout[1]) :]
     qkv_ref, att_ref, prob_ref = rest[:3]
-    wall, sems = rest[-2:]
+    wall = rest[-1]
 
     @pl.when(pl.program_id(0) == 0)
     def _():
-        assemble(place_ref[0], chunks, starts, wall, sems)
+        assemble(place_ref, chunks, layout, wall)
         for position in range(extra):
             column = 3 * GROUP + position * LANES
             rest[3 + position][...] = wall[:, column : column + LANES]
@@ -234,18 +247,18 @@
 
 
 def route_kernel(
-    n_exp, starts, place_ref, index_ref, count_ref, image_ref, cot_ref, att0, att1, att2,
+    n_exp, layout, place_ref, index_ref, count_ref, image_ref, cot_ref, att0, att1, att2,
     ao_ref, bo_ref, ra_ref, wr_ref, rb_ref, *rest,
 ):
-    chunks, rest = rest[: len(starts)], rest[len(starts) :]
-    x2_ref, uo_ref, ur_ref, disp_ref, comb_ref, sg_ref, wrt_ref, wall, pad_a, pad_b, sems = rest
+    chunks, rest = rest[: len(layout[1])], rest[len(layout[1]) :]
+    x2_ref, uo_ref, ur_ref, disp_ref, comb_ref, sg_ref, wrt_ref, wall, pad_a, pad_b = rest
     n_img, n_tok, width = image_ref.shape
     first = pl.program_id(0) * n_img
     total = x2_ref.shape[1]
 
     @pl.when(first == 0)
     def _():
-        assemble(place_ref[0], chunks, starts, wall, sems)
+        assemble(place_ref, chunks, layout, wall)
         wrt_ref[...] = wr_ref[...].astype(F32).T[:n_exp].astype(BF16)
 
     att = jnp.concatenate([flat(att0), flat(att1), flat(att2)], axis=1)
@@ -291,27 +304,35 @@
     return hidden.astype(BF16), (slope * ghid).astype(BF16)
 
 
+def gather_rows(part_refs, out_ref):
+    rows = part_refs[0].shape[0] * part_refs[0].shape[2]
+    for number, part_ref in enumerate(part_refs):
+        part = part_ref[:, 0].astype(F32).reshape(rows, part_ref.shape[3])
+        out_ref[number * rows : (number + 1) * rows, :] = part.astype(BF16)
+
+
 def expert_kernel(
-    sg_ref, wu_ref, wd_ref, ua_ref, ub_ref, da_ref, db_ref, out_ref,
-    u1_ref, gu2_ref, acc_y, acc_s, acc_u2, acc_gu1,
+    wu_ref, wd_ref, ua_ref, ub_ref, da_ref, db_ref, part_ref, out_ref,
+    sg_ref, u1_ref, gu2_ref, acc_y, acc_s, acc_u2, acc_gu1,
 ):
     step = pl.program_id(1)
     width = wu_ref.shape[1]
-    selector = sg_ref[0, :, 2 * width :].astype(F32)
 
     @pl.when(step == 0)
     def _():
+        gather_rows((part_ref,), sg_ref)
+        selector = sg_ref[:, 2 * width :].astype(F32)
         u1_ref[...] = (
-            dot(sg_ref[0, :, :width], ua_ref[0]).astype(BF16).astype(F32) * selector
+            dot(sg_ref[:, :width], ua_ref[0]).astype(BF16).astype(F32) * selector
         ).astype(BF16)
-        gu2_ref[...] = (dot(sg_ref[0, :, width : 2 * width], db_ref[0], NT) * selector).astype(BF16)
+        gu2_ref[...] = (dot(sg_ref[:, width : 2 * width], db_ref[0], NT) * selector).astype(BF16)
         acc_y[...] = jnp.zeros_like(acc_y)
         acc_s[...] = jnp.zeros_like(acc_s)
         acc_u2[...] = jnp.zeros_like(acc_u2)
         acc_gu1[...] = jnp.zeros_like(acc_gu1)
 
     hidden, gpre = expert_tile(
-        sg_ref[0, :, :width], sg_ref[0, :, width : 2 * width], u1_ref[...], gu2_ref[...],
+        sg_ref[:, :width], sg_ref[:, width : 2 * width], u1_ref[...], gu2_ref[...],
         wu_ref, wd_ref, ub_ref, da_ref,
     )
     acc_y[...] += dot(hidden, wd_ref[0])
@@ -321,24 +342,31 @@
 
     @pl.when(step == pl.num_programs(1) - 1)
     def _():
+        selector = sg_ref[:, 2 * width :].astype(F32)
         u2 = (acc_u2[...].astype(BF16).astype(F32) * selector).astype(BF16)
         gu1 = (acc_gu1[...].T * selector).astype(BF16)
-        out_ref[0, :, :width] = (acc_y[...] + dot(u2, db_ref[0])).astype(BF16)
-        out_ref[0, :, width:] = (acc_s[...].T + dot(gu1, ua_ref[0], NT)).astype(BF16)
+        shards, _, n_img, _ = out_ref.shape
+        result = acc_y[...] + dot(u2, db_ref[0])
+        out_ref[:, 0, :, :width] = result.reshape(shards, n_img, width).astype(BF16)
+        result = acc_s[...].T + dot(gu1, ua_ref[0], NT)
+        out_ref[:, 0, :, width:] = result.reshape(shards, n_img, width).astype(BF16)
 
 
 def expert_grad_kernel(
-    sg_ref, wu_ref, wd_ref, ua_ref, ub_ref, da_ref, db_ref,
-    gua_ref, gub_ref, gda_ref, gdb_ref, u1_ref, gu2_ref, u1t_ref, gu2t_ref, acc_u2, acc_gu1,
+    copies, wu_ref, wd_ref, ua_ref, ub_ref, da_ref, db_ref, *rest
 ):
+    part_refs = rest[:copies]
+    gua_ref, gub_ref, gda_ref, gdb_ref = rest[-11:-7]
+    sg_ref, u1_ref, gu2_ref, u1t_ref, gu2t_ref, acc_u2, acc_gu1 = rest[-7:]
     step = pl.program_id(1)
     width = wu_ref.shape[1]
-    selector = sg_ref[0, :, 2 * width :].astype(F32)
 
     @pl.when(step == 0)
     def _():
-        u1 = dot(sg_ref[0, :, :width], ua_ref[0]).astype(BF16).astype(F32) * selector
-        gu2 = dot(sg_ref[0, :, width : 2 * width], db_ref[0], NT) * selector
+        gather_rows(part_refs, sg_ref)
+        selector = sg_ref[:, 2 * width :].astype(F32)
+        u1 = dot(sg_ref[:, :width], ua_ref[0]).astype(BF16).astype(F32) * selector
+        gu2 = dot(sg_ref[:, width : 2 * width], db_ref[0], NT) * selector
         u1_ref[...] = u1.astype(BF16)
         gu2_ref[...] = gu2.astype(BF16)
         u1t_ref[...] = u1.T.astype(BF16)
@@ -347,7 +375,7 @@
         acc_gu1[...] = jnp.zeros_like(acc_gu1)
 
     hidden, gpre = expert_tile(
-        sg_ref[0, :, :width], sg_ref[0, :, width : 2 * width], u1_ref[...], gu2_ref[...],
+        sg_ref[:, :width], sg_ref[:, width : 2 * width], u1_ref[...], gu2_ref[...],
         wu_ref, wd_ref, ub_ref, da_ref,
     )
     gub_ref[0] = dot(u1t_ref[...], gpre)
@@ -357,26 +385,27 @@
 
     @pl.when(step == pl.num_programs(1) - 1)
     def _():
+        selector = sg_ref[:, 2 * width :].astype(F32)
         u2 = acc_u2[...].astype(BF16).astype(F32) * selector
         gu1 = (acc_gu1[...] * selector.T).astype(BF16)
-        gdb_ref[0] = dot(u2.T.astype(BF16), sg_ref[0, :, width : 2 * width])
-        gua_ref[0] = dot(gu1, sg_ref[0, :, :width]).T
+        gdb_ref[0] = dot(u2.T.astype(BF16), sg_ref[:, width : 2 * width])
+        gua_ref[0] = dot(gu1, sg_ref[:, :width]).T
 
 
 def route_back_kernel(
-    n_exp, starts, place_ref, index_ref, count_ref, cot_ref, x2_ref, uo_ref, ur_ref, disp_ref,
+    n_exp, layout, place_ref, index_ref, count_ref, cot_ref, x2_ref, uo_ref, ur_ref, disp_ref,
     comb_ref, att0, att1, att2, ret_ref, ao_ref, bo_ref, ra_ref, wrt_ref, rb_ref, *rest,
 ):
-    chunks, rest = rest[: len(starts)], rest[len(starts) :]
+    chunks, rest = rest[: len(layout[1])], rest[len(layout[1]) :]
     block_ref, gx2_ref, gatt_ref, pack_ref, *rest = rest
-    wall, pad_b, acc_oa, acc_ob, acc_ra, acc_rb, sems = rest
+    wall, pad_b, acc_oa, acc_ob, acc_ra, acc_rb = rest
     n_img, n_tok, width = cot_ref.shape
     first = pl.program_id(0) * n_img
     total = x2_ref.shape[1]
 
     @pl.when(first == 0)
     def _():
-        assemble(place_ref[0], chunks, starts, wall, sems)
+        assemble(place_ref, chunks, layout, wall)
         acc_oa[...] = jnp.zeros_like(acc_oa)
         acc_ob[...] = jnp.zeros_like(acc_ob)
         acc_ra[...] = jnp.zeros_like(acc_ra)
@@ -446,7 +475,6 @@
     keep = head_mask(1.0)
     key_t = qkv[:, GROUP : 2 * GROUP].T
     total = qkv.shape[0]
-    lane = lax.broadcasted_iota(jnp.int32, (1, LANES), 1)
     gq_parts, gk_parts, gv_parts = [], [], []
     for pair in range(GROUP // LANES):
         span = slice(pair * LANES, (pair + 1) * LANES)
@@ -466,79 +494,76 @@
                 (dot(key_t[head * HEAD_DIM : (head + 1) * HEAD_DIM], gscores[side]) * 0.125).astype(BF16)
             )
         gk = dot(jnp.concatenate(gscores, axis=0), q_pair)
-        gk_parts.append((jnp.where(lane < HEAD_DIM, gk[:total], gk[total:]) * 0.125).astype(BF16))
-        gv_parts.append(jnp.where(lane < HEAD_DIM, gv[:total], gv[total:]).astype(BF16))
+        gk_parts.append((merge_pair(gk[:total], gk[total:]) * 0.125).astype(BF16))
+        gv_parts.append(merge_pair(gv[:total], gv[total:]).astype(BF16))
     gq = jnp.concatenate(gq_parts, axis=0).T
     return jnp.concatenate([gq] + gk_parts + gv_parts, axis=1)
 
 
-def attention_back_kernel(group, last, *refs):
+def attention_back_kernel(groups, index_ref, *refs):
     refs = list(refs)
-    index_ref = refs.pop(0) if last else None
-    qkv_ref, gatt_ref, prob_ref, uq_ref, bt_ref = refs[:5]
+    qkv_refs = [refs.pop(0) for _ in range(groups)]
+    prob_refs = [refs.pop(0) for _ in range(groups)]
+    gatt_ref, uq_ref, h1_ref, bt_ref, others_ref = refs[:5]
     refs = refs[5:]
-    before_ref = refs.pop(0) if group else None
-    h1_ref = refs.pop(0) if last else None
-    befores = [refs.pop(0) for _ in range(group)] if last else ()
-    gqkv_ref, guq_ref, gb_ref = refs[:3]
-    refs = refs[3:]
-    acc_b = refs.pop(0)
-    acc_a = refs.pop(0) if last else None
+    gqkv_refs = [refs.pop(0) for _ in range(groups)]
+    guq_ref, pack_ref, acc_b, acc_a = refs
     step = pl.program_id(0)
-    width = bt_ref.shape[0] // 3
-    n_img, total, _ = qkv_ref.shape
+    n_img, total, width = h1_ref.shape
 
     @pl.when(step == 0)
     def _():
         acc_b[...] = jnp.zeros_like(acc_b)
-        if last:
-            acc_a[...] = jnp.zeros_like(acc_a)
-
-    parts = [attention_backward(qkv_ref[i], gatt_ref[i], prob_ref, i) for i in range(n_img)]
-    for i in range(n_img):
-        gqkv_ref[i] = parts[i]
-    gqkv = jnp.concatenate(parts, axis=0)
-    acc_b[...] += dot(flat(uq_ref), gqkv, TN)
-    guq = dot(gqkv, group_rows(group, width, bt_ref))
-    if group:
-        guq = guq + flat(before_ref)
-    if last:
-        guq = select_rows(guq, index_ref, step * n_img, n_img)
-        acc_a[...] += dot(guq, flat(h1_ref), TN)
+        acc_a[...] = jnp.zeros_like(acc_a)
+
+    uq_t = flat(uq_ref).T
+    guq = None
+    for group in range(groups):
+        parts = []
+        for i in range(n_img):
+            part = attention_backward(
+                qkv_refs[group][i], gatt_ref[i, :, group * GROUP : (group + 1) * GROUP],
+                prob_refs[group], i,
+            )
+            gqkv_refs[group][i] = part
+            parts.append(part)
+        gqkv = jnp.concatenate(parts, axis=0)
+        acc_b[:, group * 3 * GROUP : (group + 1) * 3 * GROUP] += dot(uq_t, gqkv)
+        part = dot(gqkv, group_rows(group, width, bt_ref))
+        guq = part if guq is None else guq + part
+    guq = select_rows(guq, index_ref, step * n_img, n_img)
+    acc_a[...] += dot(guq, flat(h1_ref), TN)
     guq_ref[...] = guq.reshape(guq_ref.shape)
 
     @pl.when(step == pl.num_programs(0) - 1)
     def _():
-        summed = acc_b[...].T.astype(BF16)
-        if not last:
-            gb_ref[...] = summed
-            return
-        shards = gb_ref.shape[0]
+        shards = pack_ref.shape[0]
         rows = width // shards
+        pack_ref[:, 4 * rows :, :] = others_ref[...]
         own = acc_a[...].T.astype(BF16)
         for shard in range(shards):
-            gb_ref[shard, 3 * rows :, :] = own[shard * rows : (shard + 1) * rows]
-        sources = [before[...] for before in befores] + [summed]
-        for part in range(3):
-            for source in range(group + 1):
-                start = part * width + source * GROUP
+            pack_ref[shard, 3 * rows : 4 * rows, :] = own[shard * rows : (shard + 1) * rows]
+        for group in range(groups):
+            summed = acc_b[:, group * 3 * GROUP : (group + 1) * 3 * GROUP].T.astype(BF16)
+            for part in range(3):
+                start = part * width + group * GROUP
                 place = start
                 while place < start + GROUP:
                     shard, offset = divmod(place, 3 * rows)
                     length = min(start + GROUP - place, 3 * rows - offset)
                     take = part * GROUP + place - start
-                    gb_ref[shard, offset : offset + length, :] = sources[source][take : take + length]
+                    pack_ref[shard, offset : offset + length, :] = summed[take : take + length]
                     place += length
 
 
-def input_grad_kernel(starts, place_ref, image_ref, gx2_ref, guq_ref, a_ref, *refs):
+def input_grad_kernel(layouts, place_ref, image_ref, gx2_ref, guq_ref, a_ref, *refs):
     refs = list(refs)
-    groups = len(starts)
-    gqkv = [refs.pop(0) for _ in starts]
-    chunks = [[refs.pop(0) for _ in start] for start in starts]
+    groups = len(layouts)
+    gqkv = [refs.pop(0) for _ in layouts]
+    chunks = [[refs.pop(0) for _ in layout[1]] for layout in layouts]
     out_ref = refs.pop(0)
-    walls = [refs.pop(0) for _ in starts]
-    pad_a, sems = refs
+    walls = [refs.pop(0) for _ in layouts]
+    pad_a = refs.pop(0)
     n_img, n_tok, width = image_ref.shape
     step = pl.program_id(0)
     parts = width // LANES
@@ -547,7 +572,7 @@
     @pl.when(step == 0)
     def _():
         for group in range(groups):
-            assemble(place_ref[0], chunks[group], starts[group], walls[group], sems.at[group])
+            assemble(place_ref, chunks[group], layouts[group], walls[group])
 
     gh1 = dot(flat(guq_ref), a_ref[...], NT)
     for group in range(groups):
@@ -567,6 +592,10 @@
 
 def whole(shape):
     return pl.BlockSpec(shape, lambda *_: (0,) * len(shape))
+
+
+def once(shape):
+    return pl.BlockSpec(shape, lambda *_: (0,) * len(shape), pipeline_mode=pl.Buffered(1))
 
 
 def per_image(*shape, images=1):
@@ -611,12 +640,12 @@
     )[0]
 
 
-def pack_call(place, weights, shards):
+def pack_call(place, weights, copies):
     rows, columns = weights[0].shape
     part = (columns // 3 + 6 * LANES) // 4
     return call(
         pack_kernel, (place,), (1,), [(weight, whole(weight.shape)) for weight in weights],
-        [((shards, rows, part), BF16, whole((shards, rows, part)))],
+        [((copies, rows, part), BF16, whole((copies, rows, part)))],
         [pltpu.VMEM((rows, 4 * part), BF16)],
         rows * columns,
     )[0]
@@ -639,11 +668,11 @@
 
 def first_attention_call(place, index, h1, pack, n_tok, shards):
     n_img, total, width = h1.shape
-    chunks, starts, columns = pack
+    chunks, layout, columns = pack
     each = several(n_img, IMAGES_FORWARD)
     return call(
-        functools.partial(first_attention_kernel, n_tok, shards, starts), (place, index), (n_img // each,),
-        [(h1, per_image(total, width, images=each))] + [(chunk, ANY) for chunk in chunks],
+        functools.partial(first_attention_kernel, n_tok, shards, layout), (place, index), (n_img // each,),
+        [(h1, per_image(total, width, images=each))] + [(chunk, once(chunk.shape)) for chunk in chunks],
         attention_outputs(n_img, total, each)
         + [
             ((n_img, total, LANES), BF16, per_image(total, LANES, images=each)),
@@ -652,41 +681,41 @@
             ((width, LANES), BF16, whole((width, LANES))),
             ((width, LANES), BF16, whole((width, LANES))),
         ],
-        [pltpu.VMEM((width, columns), BF16), pltpu.SemaphoreType.DMA((4,))],
+        [pltpu.VMEM((width, columns), BF16)],
         attention_flops(n_img, total, width, 2), n_img * total * total * 4,
     )
 
 
 def next_attention_call(place, h1, uq, bt, pack, n_tok, group, extra):
     n_img, total, width = h1.shape
-    chunks, starts, columns = pack
+    chunks, layout, columns = pack
     each = several(n_img, IMAGES_FORWARD)
     return call(
-        functools.partial(next_attention_kernel, n_tok, group, extra, starts), (place,), (n_img // each,),
+        functools.partial(next_attention_kernel, n_tok, group, extra, layout), (place,), (n_img // each,),
         [
             (h1, per_image(total, width, images=each)),
             (uq, per_image(total, LANES, images=each)),
             (bt, whole(bt.shape)),
         ]
-        + [(chunk, ANY) for chunk in chunks],
+        + [(chunk, once(chunk.shape)) for chunk in chunks],
         attention_outputs(n_img, total, each)
         + [((width, LANES), BF16, whole((width, LANES)))] * extra,
-        [pltpu.VMEM((width, columns), BF16), pltpu.SemaphoreType.DMA((4,))],
+        [pltpu.VMEM((width, columns), BF16)],
         attention_flops(n_img, total, width, 2), n_img * total * total * 4,
     )
 
 
 def route_call(place, index, count, images, cotangent, atts, banks, pack, n_exp, total):
     n_img, n_tok, width = images.shape
-    chunks, starts, columns = pack
+    chunks, layout, columns = pack
     each = several(n_img, IMAGES_ROUTE)
     here = functools.partial(per_image, images=each)
     return call(
-        functools.partial(route_kernel, n_exp, starts), (place, index, count), (n_img // each,),
+        functools.partial(route_kernel, n_exp, layout), (place, index, count), (n_img // each,),
         [(images, here(n_tok, width)), (cotangent, here(n_tok, width))]
         + [(att, here(total, GROUP)) for att in atts]
         + [(bank, whole(bank.shape)) for bank in banks]
-        + [(chunk, ANY) for chunk in chunks],
+        + [(chunk, once(chunk.shape)) for chunk in chunks],
         [
             ((n_img, total, width), F32, here(total, width)),
             ((n_img, total, LANES), BF16, here(total, LANES)),
@@ -700,7 +729,6 @@
             pltpu.VMEM((width, columns), BF16),
             pltpu.VMEM((each * total, width), F32),
             pltpu.VMEM((each * total, width), F32),
-            pltpu.SemaphoreType.DMA((4,)),
         ],
         n_img * total * 2 * width * (width + 3 * LANES), n_img * total * 2 * n_exp,
     )
@@ -713,9 +741,8 @@
     return tile
 
 
-def expert_specs(rows, width, tile, first=0):
+def expert_specs(width, tile, first=0):
     return (
-        pl.BlockSpec((1, rows, 2 * width + LANES), lambda e, f: (e + first, 0, 0)),
         pl.BlockSpec((1, width, tile), lambda e, f: (e + first, 0, f)),
         pl.BlockSpec((1, tile, width), lambda e, f: (e + first, f, 0)),
         pl.BlockSpec((1, width, LANES), lambda e, f: (e + first, 0, 0)),
@@ -725,15 +752,23 @@
     )
 
 
-def expert_call(sg, weights):
-    n_loc, rows, _ = sg.shape
+def expert_rows(shape, first=0):
+    shards, _, n_img, columns = shape
+    return pl.BlockSpec((shards, 1, n_img, columns), lambda e, f: (0, e + first, 0, 0))
+
+
+def expert_call(landed, weights):
+    shards, n_loc, n_img, columns = landed.shape
+    rows = shards * n_img
     width, hidden = weights[0].shape[1:]
-    tile = hidden_tile(hidden, 768)
+    tile = hidden_tile(hidden, 1536)
+    out = (shards, n_loc, n_img, 2 * width)
     return call(
         expert_kernel, (), (n_loc, hidden // tile),
-        list(zip((sg,) + weights, expert_specs(rows, width, tile))),
-        [((n_loc, rows, 2 * width), BF16, pl.BlockSpec((1, rows, 2 * width), lambda e, f: (e, 0, 0)))],
-        [
+        list(zip(weights, expert_specs(width, tile))) + [(landed, expert_rows(landed.shape))],
+        [(out, BF16, expert_rows(out))],
+        [
+            pltpu.VMEM((rows, columns), BF16),
             pltpu.VMEM((rows, LANES), BF16),
             pltpu.VMEM((rows, LANES), BF16),
             pltpu.VMEM((rows, width), F32),
@@ -745,16 +780,16 @@
     )[0]
 
 
-def expert_grad_call(sg, weights, first, before):
-    n_loc, rows, _ = sg.shape
+def expert_grad_call(every, weights, first, before):
+    shards, n_loc, n_img, columns = every[0].shape
+    rows = shards * n_img * len(every)
     width, hidden = weights[0].shape[1:]
     tile = hidden_tile(hidden, 768 if rows <= 512 else 384)
-    kernel = expert_grad_kernel
-    if before:
-        kernel = lambda *refs: expert_grad_kernel(*refs[:7], *refs[11:])
+    aliases = {len(weights) + len(every) + i: i for i in range(4)} if before else {}
     return call(
-        kernel, (), (1, hidden // tile),
-        list(zip((sg,) + weights, expert_specs(rows, width, tile, first)))
+        functools.partial(expert_grad_kernel, len(every)), (), (1, hidden // tile),
+        list(zip(weights, expert_specs(width, tile, first)))
+        + [(part, expert_rows(part.shape, first)) for part in every]
         + [(array, ANY) for array in before],
         [
             ((n_loc, width, LANES), F32, pl.BlockSpec((1, width, LANES), lambda e, f: (e + first, 0, 0))),
@@ -763,6 +798,7 @@
             ((n_loc, LANES, width), F32, pl.BlockSpec((1, LANES, width), lambda e, f: (e + first, 0, 0))),
         ],
         [
+            pltpu.VMEM((rows, columns), BF16),
             pltpu.VMEM((rows, LANES), BF16),
             pltpu.VMEM((rows, LANES), BF16),
             pltpu.VMEM((LANES, rows), BF16),
@@ -770,8 +806,7 @@
             pltpu.VMEM((rows, LANES), F32),
             pltpu.VMEM((LANES, rows), F32),
         ],
-        rows * 4 * width * hidden, rows * hidden,
-        {7 + i: i for i in range(4)} if before else {},
+        rows * 4 * width * hidden, rows * hidden, aliases,
     )
 
 
@@ -779,15 +814,15 @@
     place, index, count, cotangent, x2, uo, ur, disp, comb, atts, ret, banks, pack, shards, replicas
 ):
     n_img, n_tok, width = cotangent.shape
-    chunks, starts, columns = pack
+    chunks, layout, columns = pack
     total, n_exp = x2.shape[1], disp.shape[1]
     rows = width // shards
     unit = 16 * replicas
-    pack_rows = -(-(3 * rows + n_exp // shards) // unit) * unit
+    pack_rows = -(-(7 * rows + n_exp // shards) // unit) * unit - 4 * rows
     each = several(n_img, IMAGES_ROUTE)
     here = functools.partial(per_image, images=each)
     return call(
-        functools.partial(route_back_kernel, n_exp, starts), (place, index, count), (n_img // each,),
+        functools.partial(route_back_kernel, n_exp, layout), (place, index, count), (n_img // each,),
         [
             (cotangent, here(n_tok, width)),
             (x2, here(total, width)),
@@ -799,7 +834,7 @@
         + [(att, here(total, GROUP)) for att in atts]
         + [(ret, here(n_exp, 2 * width))]
         + [(bank, whole(bank.shape)) for bank in banks]
-        + [(chunk, ANY) for chunk in chunks],
+        + [(chunk, once(chunk.shape)) for chunk in chunks],
         [
             ((n_img, n_tok, width), BF16, here(n_tok, width)),
             ((n_img, total, width), F32, here(total, width)),
@@ -813,42 +848,33 @@
             pltpu.VMEM((LANES, width), F32),
             pltpu.VMEM((LANES, width), F32),
             pltpu.VMEM((n_exp, LANES), F32),
-            pltpu.SemaphoreType.DMA((4,)),
         ],
         n_img * total * 2 * width * (width + 6 * LANES),
     )
 
 
-def attention_back_call(index, qkv, gatt, prob, uq, bt, before, h1, group, gbs=(), shards=1):
-    n_img, total, _ = qkv.shape
-    width = bt.shape[0] // 3
-    last = h1 is not None
+def attention_back_call(index, qkvs, probs, gatt, uq, h1, bt, others):
+    n_img, total, width = h1.shape
+    groups = len(qkvs)
+    shards = others.shape[0]
     each = several(n_img, IMAGES_BACK)
-    inputs = [
-        (qkv, per_image(total, 3 * GROUP, images=each)),
-        (gatt, pl.BlockSpec((each, total, GROUP), lambda i, *_: (i, 0, group))),
-        (prob, per_image(GROUP // HEAD_DIM, total, total, images=each)),
-        (uq, per_image(total, LANES, images=each)),
-        (bt, whole(bt.shape)),
-    ]
-    outputs = [
-        ((n_img, total, 3 * GROUP), BF16, per_image(total, 3 * GROUP, images=each)),
-        ((n_img, total, LANES), BF16 if last else F32, per_image(total, LANES, images=each)),
-        ((3 * GROUP, LANES), BF16, whole((3 * GROUP, LANES))),
-    ]
-    scratch = [pltpu.VMEM((LANES, 3 * GROUP), F32)]
-    if group:
-        inputs.append((before, per_image(total, LANES, images=each)))
-    if last:
-        inputs.append((h1, per_image(total, width, images=each)))
-        inputs.extend((gb, whole(gb.shape)) for gb in gbs)
-        shape = (shards, 4 * width // shards, LANES)
-        outputs[-1] = (shape, BF16, whole(shape))
-        scratch.append(pltpu.VMEM((LANES, width), F32))
+    here = functools.partial(per_image, images=each)
+    pack = (shards, 4 * width // shards + others.shape[1], LANES)
     return call(
-        functools.partial(attention_back_kernel, group, last),
-        (index,) if last else (), (n_img // each,), inputs, outputs, scratch,
-        attention_flops(n_img, total, LANES, 5), n_img * total * total * 4,
+        functools.partial(attention_back_kernel, groups), (index,), (n_img // each,),
+        [(qkv, here(total, 3 * GROUP)) for qkv in qkvs]
+        + [(prob, here(GROUP // HEAD_DIM, total, total)) for prob in probs]
+        + [
+            (gatt, here(total, width)),
+            (uq, here(total, LANES)),
+            (h1, here(total, width)),
+            (bt, whole(bt.shape)),
+            (others, whole(others.shape)),
+        ],
+        [((n_img, total, 3 * GROUP), BF16, here(total, 3 * GROUP))] * groups
+        + [((n_img, total, LANES), BF16, here(total, LANES)), (pack, BF16, whole(pack))],
+        [pltpu.VMEM((LANES, 3 * width), F32), pltpu.VMEM((LANES, width), F32)],
+        groups * attention_flops(n_img, total, LANES, 5), groups * n_img * total * total * 4,
     )
 
 
@@ -867,10 +893,10 @@
             (bank_a, whole(bank_a.shape)),
         ]
         + [(gqkv, here(total, 3 * GROUP)) for gqkv in gqkvs]
-        + [(chunk, ANY) for pack in packs for chunk in pack[0]],
+        + [(chunk, once(chunk.shape)) for pack in packs for chunk in pack[0]],
         [((images.size // LANES, LANES), F32, whole((images.size // LANES, LANES)))],
         [pltpu.VMEM((width, pack[2]), BF16) for pack in packs]
-        + [pltpu.VMEM((each * total, width), F32), pltpu.SemaphoreType.DMA((groups, 4))],
+        + [pltpu.VMEM((each * total, width), F32)],
         n_img * total * 2 * width * (3 * width + LANES),
     )[0]
     out = out.reshape(n_tok, width // LANES, n_img, LANES).transpose(2, 0, 1, 3)
@@ -894,12 +920,14 @@
     return jnp.broadcast_to(rows[None], (shards,) + rows.shape)
 
 
-def over_shard(spread):
-    own = lax.all_to_all(spread, "shard", split_axis=0, concat_axis=0, tiled=True)
+def over_shard(spread, lines=None):
+    own = lax.all_to_all(
+        spread, "shard", split_axis=0, concat_axis=0, tiled=True, axis_index_groups=lines
+    )
     return own.reshape(-1, spread.shape[2])
 
 
-def reduce_pack(pack, replicas):
+def reduce_pack(pack, replicas, beside_swap, beside_spread):
     where = lax.axis_index("replica")
     bits = []
     bit = 1
@@ -909,10 +937,13 @@
         keep = lax.dynamic_slice_in_dim(pack, side * half, half, axis=1)
         give = lax.dynamic_slice_in_dim(pack, (1 - side) * half, half, axis=1)
         got = swap(give, "replica", replicas, bit)
+        if 2 * bit == replicas:
+            got, *swap_work = tie(got, *beside_swap())
         pack = (keep.astype(F32) + got.astype(F32)).astype(BF16)
         bits.append(bit)
         bit *= 2
     landed = lax.all_to_all(pack, "shard", split_axis=0, concat_axis=0, tiled=True)
+    landed, *spread_work = tie(landed, *beside_spread())
     total = jnp.sum(landed.astype(F32), axis=0).astype(BF16)
     for bit in reversed(bits):
         got = swap(total, "replica", replicas, bit)
@@ -922,7 +953,7 @@
             jnp.concatenate([total, got], axis=0),
             jnp.concatenate([got, total], axis=0),
         )
-    return total
+    return total, swap_work, spread_work
 
 
 def per_device(
@@ -955,7 +986,8 @@
     n_exp = n_loc * shards
     groups = width // GROUP
     quarter = lax.axis_index("replica") % 4
-    place = quarter.astype(jnp.int32).reshape(1)
+    place = jnp.stack([quarter, lax.axis_index("shard") % 2]).astype(jnp.int32)
+    by_axis = shards == 2 * STRIPS and replicas == 4
 
     def qkv_columns(group):
         return [
@@ -973,10 +1005,11 @@
         axis=1,
     )
     empty = jnp.zeros((rows, LANES), BF16)
+    empty = jnp.zeros((rows, 2 * LANES), BF16)
     packs = [
-        (qkv_columns(1) + [output_adapter_second.T, route_block], 2),
-        (qkv_columns(2) + [empty, empty], 4),
-        ([frozen_output_weight, empty, empty], 4),
+        (qkv_columns(1) + [output_adapter_second.T, route_block], 4),
+        (qkv_columns(2), 2),
+        ([frozen_output_weight, empty], 4),
     ]
     spread0 = pack_call(
         place,
@@ -984,38 +1017,49 @@
             query_key_value_weight, query_key_value_first, query_key_value_second.T,
             output_adapter_first, dispatch_adapter_first,
         ),
-        shards,
+        STRIPS if by_axis else shards,
     )
     mine = [own_columns(jnp.concatenate(pack, axis=1), quarter, pieces) for pack, pieces in packs]
     near = functools.partial(swap, axis="replica", size=replicas, bit=1)
     far = functools.partial(swap, axis="replica", size=replicas, bit=2)
-
-    own0 = over_shard(spread0)
+    beside = functools.partial(swap, axis="shard", size=shards, bit=1)
+
     h1 = norm_call(images, cotangent, total)
-    own0, h1, mine1, mine2 = tie(own0, h1, *mine[:2])
-    own12 = over_shard(spread(jnp.concatenate([mine1, mine2], axis=1), shards))
-    y0 = far(own0)
-    chunks0 = (own0, near(own0), y0, near(y0))
-    *chunks0, h1 = tie(*chunks0, h1)
-    pack0 = (chunks0, (0,) * 4, 3 * GROUP + 6 * LANES)
+    if by_axis:
+        lines = [[2 * strip + side for strip in range(STRIPS)] for side in range(2)]
+        own0 = over_shard(spread0, lines)
+        beside0, far0, h1, mine1 = tie(beside(own0), far(own0), h1, mine[0])
+        held = [(own0, 0, 0), (beside0, 0, 1), (far0, 2, 0)]
+        own1 = over_shard(spread(mine1, shards))
+        held.append((far(held[1][0]), 2, 1))
+    else:
+        own0 = over_shard(spread0)
+        own0, h1, mine1 = tie(own0, h1, mine[0])
+        held = [(own0, 0, None), (far(own0), 2, None)]
+        own1 = over_shard(spread(mine1, shards))
+    chunks0 = [chunk for chunk, _, _ in held] + [near(chunk) for chunk, _, _ in held]
+    layout0 = [(replica, side, 0) for _, replica, side in held]
+    layout0 += [(replica ^ 1, side, 0) for _, replica, side in held]
+    *chunks0, own1, mine2, mine3 = tie(*chunks0, own1, *mine[1:])
+    pack0 = (tuple(chunks0), (4, tuple(layout0)), 3 * GROUP + 6 * LANES)
+    far1 = far(own1)
+    own23 = over_shard(spread(jnp.concatenate([mine2, mine3], axis=1), shards))
     qkv0, att0, prob0, uq, bank_a, bank_bt, bank_ao, bank_ra = first_attention_call(
         place, image_adapter_index, h1, pack0, n_tok, shards
     )
-    uq, own12, mine3 = tie(uq, own12, mine[2])
-    first = mine1.shape[1]
-    own1, own2 = own12[:, :first], own12[:, first:]
-    pack1 = ((own12, near(own1)), (0, 0), 3 * GROUP + 2 * LANES)
-    y2 = far(own2)
-    own3 = over_shard(spread(mine3, shards))
+    uq, own1, far1 = tie(uq, own1, far1)
+    four = (4, ((0, None, 0), (1, None, 0), (2, None, 0), (3, None, 0)))
+    pack1 = ((own1, near(own1), far1, near(far1)), four, 3 * GROUP + 2 * LANES)
     qkv1, att1, prob1, bank_bo, bank_wr = next_attention_call(
         place, h1, uq, bank_bt, pack1, n_tok, 1, 2
     )
-    att1, uq, own2, y2, own3 = tie(att1, uq, own2, y2, own3)
-    pack2 = ((own12, near(own2), y2, near(y2)), (first, 0, 0, 0), 3 * GROUP + 2 * LANES)
-    y3 = far(own3)
+    att1, uq, own23 = tie(att1, uq, own23)
+    own2, own3 = own23[:, : mine2.shape[1]], own23[:, mine2.shape[1] :]
+    far3 = far(own3)
+    pack2 = ((own2, near(own2)), (2, ((0, None, 0), (1, None, 0))), 3 * GROUP)
     qkv2, att2, prob2 = next_attention_call(place, h1, uq, bank_bt, pack2, n_tok, 2, 0)
-    att2, own3, y3 = tie(att2, own3, y3)
-    pack3 = ((own3, near(own3), y3, near(y3)), (0,) * 4, width + 2 * LANES)
+    att2, own3, far3 = tie(att2, own3, far3)
+    pack3 = ((own3, near(own3), far3, near(far3)), four, width + 2 * LANES)
     packs = (pack0, pack1, pack2, pack3)
     atts = (att0, att1, att2)
     bank_rb = bank_wr.reshape(shards, rows, LANES)[:, :16, 64 : 64 + n_loc * 8].reshape(n_exp, LANES)
@@ -1026,18 +1070,17 @@
 
     sent = sg.reshape(n_img, shards, n_loc, -1).transpose(1, 2, 0, 3)
     landed = lax.all_to_all(sent, "shard", split_axis=0, concat_axis=0, tiled=True)
-    landed = landed.transpose(1, 0, 2, 3).reshape(n_loc, shards * n_img, -1)
     weights = (
         frozen_up_weight, frozen_down_weight, up_adapter_first, up_adapter_second,
         down_adapter_first, down_adapter_second,
     )
     ret = expert_call(landed, weights)
-    over_y = [swap(landed, "replica", replicas, bit) for bit in range(2, replicas, 2)]
-    ret, *over_y = tie(ret, *over_y)
-    back = ret.reshape(n_loc, shards, n_img, 2 * width).transpose(1, 0, 2, 3)
-    back = lax.all_to_all(back, "shard", split_axis=0, concat_axis=0, tiled=True)
-    every = jnp.concatenate([landed] + over_y, axis=1)
-    every = jnp.concatenate([every, swap(every, "replica", replicas, 1)], axis=1)
+    every = [landed]
+    for bit in range(2, replicas, 2):
+        every.append(swap(landed, "replica", replicas, bit))
+    ret, *every = tie(ret, *every)
+    back = lax.all_to_all(ret, "shard", split_axis=0, concat_axis=0, tiled=True)
+    every = every + [swap(part, "replica", replicas, 1) for part in every]
     grads = expert_grad_call(every, weights, 0, ())
     back, *grads = tie(back, *grads)
     back = back.transpose(2, 0, 1, 3).reshape(n_img, n_exp, 2 * width)
@@ -1046,28 +1089,31 @@
         place, image_adapter_index, device_image_count, cotangent, x2, uo, ur, disp, comb, atts, back,
         (bank_ao, bank_bo, bank_ra, bank_wrt, bank_rb), packs[3], shards, replicas,
     )
-    out_sum = reduce_pack(out_pack, replicas).astype(F32)
-
-    gqkv0, guq, gb0 = attention_back_call(None, qkv0, gatt, prob0, uq, bank_bt, None, None, 0)
-    gqkv1, guq, gb1 = attention_back_call(None, qkv1, gatt, prob1, uq, bank_bt, guq, None, 1)
-    gqkv2, guq, qkv_pack = attention_back_call(
-        image_adapter_index, qkv2, gatt, prob2, uq, bank_bt, guq, h1, 2, (gb0, gb1), shards
-    )
-    qkv_sum = reduce_pack(qkv_pack, replicas).astype(F32)
-    input_grad = input_grad_call(
-        place, images, gx2, guq, bank_a, (gqkv0, gqkv1, gqkv2), packs[:3]
-    )
-    for expert in range(1, n_loc):
-        grads = expert_grad_call(every, weights, expert, tuple(grads))
+    *gqkvs, guq, pack = attention_back_call(
+        image_adapter_index, (qkv0, qkv1, qkv2), (prob0, prob1, prob2), gatt, uq, h1, bank_bt, out_pack
+    )
+
+    def rest_of_experts():
+        done = tuple(grads)
+        for expert in range(1, n_loc):
+            done = expert_grad_call(every, weights, expert, tuple(done))
+        return done
+
+    summed, (input_grad,), grads = reduce_pack(
+        pack, replicas,
+        lambda: (input_grad_call(place, images, gx2, guq, bank_a, gqkvs, packs[:3]),),
+        rest_of_experts,
+    )
+    summed = summed.astype(F32)
     return (
         block_out,
         input_grad,
-        qkv_sum[3 * rows :],
-        qkv_sum[: 3 * rows].T,
-        out_sum[:rows],
-        out_sum[rows : 2 * rows].T,
-        out_sum[2 * rows : 3 * rows],
-        out_sum[3 * rows : 3 * rows + n_loc].T,
+        summed[3 * rows : 4 * rows],
+        summed[: 3 * rows].T,
+        summed[4 * rows : 5 * rows],
+        summed[5 * rows : 6 * rows].T,
+        summed[6 * rows : 7 * rows],
+        summed[7 * rows : 7 * rows + n_loc].T,
         *grads,
     )
 

time: 318 us -> 277 us (0.87)
  Pallas kernels: 192 us -> 173 us
  waiting for transfers between devices: 24.4 us -> 12.8 us
  local copies, waits for them, and re-layouts: 25.6 us -> 22 us
  other arithmetic: 6.21 us -> 2.91 us
    pallas_call x14 -> x12, Pallas kernels: 192 us -> 173 us  [call(): pl.pallas_call(kernel, out_shape=shapes, grid_spec=pltpu.PrefetchScalarGr...]
    ppermute x20 -> x21, waiting for transfers between devices: 19.5 us -> 11.9 us  [swap(): return lax.ppermute(array, axis, [(i, i ^ bit) for i in range(size)])]
    all_to_all x2 -> x1, starting transfers between devices: 10.3 us -> 5.98 us  [reduce_pack(): lax.all_to_all(pack, 'shard', split_axis=0, concat_axis=0, tiled=True)]
    reshape x3 -> x0, local copies, waits for them, and re-layouts: 4.02 us -> none  [the longest x1 2.15 us: per_device(): back = ret.reshape(n_loc, shards, n_img, 2 * width).transpose(1, 0, 2, 3)]
    all_to_all x4, waiting for transfers between devices: 4.84 us -> 0.89 us  [the longest x3 0.89 us: over_shard(): lax.all_to_all(spread, 'shard', split_axis=0, concat_axis=0, tiled=True,...]
    concatenate x3 -> x1, other arithmetic: 3.4 us -> 0.01 us  [per_device(): own23 = over_shard(spread(jnp.concatenate([mine2, mine3], axis=1), shards))]
    unnamed x42 -> x58, local copies, waits for them, and re-layouts: 10.3 us -> 12.3 us
    ppermute x20 -> x21, starting transfers between devices: 18.7 us -> 20.7 us  [swap(): return lax.ppermute(array, axis, [(i, i ^ bit) for i in range(size)])]
  transfers between devices with their start and end apart: 26 -> 26, of which waited for: 9 -> 11; matrix products, arithmetic and copies ran while one was open for 6% -> 4% of each run, Pallas kernels for 47% -> 35%
where the time goes in v3:
time: 277 us; the launch traced here: 276 us
  Pallas kernels  173 us (62%)
  starting transfers between devices  46.7 us (17%)
  local copies, waits for them, and re-layouts  22 us (8%)
  blocking collectives  17.3 us (6%)
  waiting for transfers between devices  12.8 us (5%)
  other arithmetic  2.91 us (1%)
    pallas_call x12, Pallas kernels, call(): pl.pallas_call(kernel, out_shape=shapes, grid_spec=pltpu.PrefetchScalarGr...  173 us
    ppermute x21, starting transfers between devices, swap(): return lax.ppermute(array, axis, [(i, i ^ bit) for i in range(size)])  20.7 us
    all_to_all x1, blocking collectives, per_device(): lax.all_to_all(sent, 'shard', split_axis=0, concat_axis=0, tiled=True)  17.3 us
    all_to_all x3, starting transfers between devices, over_shard(): lax.all_to_all(spread, 'shard', split_axis=0, concat_axis=0, tiled=True,...  16 us
    unnamed x58, local copies, waits for them, and re-layouts  12.3 us
    ppermute x21, waiting for transfers between devices, swap(): return lax.ppermute(array, axis, [(i, i ^ bit) for i in range(size)])  11.9 us
    all_to_all x1, starting transfers between devices, reduce_pack(): lax.all_to_all(pack, 'shard', split_axis=0, concat_axis=0, tiled=True)  5.98 us
  transfers between devices with their start and end apart: 26, of which 11 were waited for; matrix products, arithmetic and copies ran while one was open for 4% of the time, Pallas kernels for 35%

profile of v3, /device:TPU:1, one launch (start us, length us, event | category | flops | bytes accessed | tf_op | source)
XLA Modules:
  0.0 276.0 jit_solution(204953471734767909)
XLA Ops:
  1.2 2.5 shard_map.274
  3.7 5.4 %all-to-all-start = ((bf16[4,96,384]{2,1,0:T(8,128)(2,1)}), bf16[4,96,384]{2,1,0:T(8,128)(2,1)S(1)}, u32[]{:S(2)}, u32[]{:S(2)}) async-start(bf16[4,96,384]{2,1,0:T(8,128)(2,1)} %shard_map.274), calls=%async_computation | async-start | bytes 589824 | tf_op jit(solution)/shard_map/all_to_all | solution.py:924
  9.2 0.9 reshape.57
  10.8 3.6 %copy.38.image_ref = bf16[8,197,768]{2,1,0:T(8,128)(2,1)} copy(bf16[8,197,768]{2,0,1:T(8,128)(2,1)} %param.19) | data formatting | bytes 4841472 | tf_op args[0]
  14.4 1.9 copy.42._.cot_ref
  16.3 0.9 all-to-all-done
  17.2 1.2 collective-permute-start
  18.4 1.2 collective-permute-start.1
  19.8 3.8 %shard_map.275.h1_ref.refs_8_ = bf16[8,208,768]{2,1,0:T(8,128)(2,1)} custom-call(bf16[8,197,768]{2,1,0:T(8,128)(2,1)} %copy.38.image_ref, bf16[8,197,768]{2,1,0:T(8,128)(2,1)} %copy.42._.cot_ref), custom_call_target="tpu_custom_call" | custom-call | flops 9682944 | bytes 7397376 | tf_op jit(solution)/shard_map/pallas_call | solution.py:615
  24.3 0.8 broadcast_in_dim.4
  25.1 4.9 %all-to-all-start.1 = ((bf16[8,96,256]{2,1,0:T(8,128)(2,1)}), bf16[8,96,256]{2,1,0:T(8,128)(2,1)S(1)}, u32[]{:S(2)}, u32[]{:S(2)}) async-start(bf16[8,96,256]{2,1,0:T(8,128)(2,1)} %broadcast_in_dim.4), calls=%async_computation.1 | async-start | bytes 786432 | tf_op jit(solution)/shard_map/all_to_all | solution.py:924
  30.0 1.2 collective-permute-start.2
  31.2 3.0 %collective-permute-start.3 = (bf16[384,384]{1,0:T(8,128)(2,1)S(1)}, bf16[384,384]{1,0:T(8,128)(2,1)S(1)}, u32[]{:S(2)}, u32[]{:S(2)}) collective-permute-start(bf16[384,384]{1,0:T(8,128)(2,1)S(1)} %bitcast.37), channel_id=1, source_target_pairs={{0,8},{8,0},{16,24},{24,16},{1,9},{9,1},{17,25},{25,17},{2,10},{10... | collective-permute-start | bytes 884744 | tf_op jit(solution)/shard_map/ppermute | solution.py:907
  34.7 0.8 collective-permute-done.2.rest_3_.refs_6_
  35.6 3.8 %collective-permute-start.6 = (bf16[384,384]{1,0:T(8,128)(2,1)S(1)}, bf16[384,384]{1,0:T(8,128)(2,1)S(1)}, u32[]{:S(2)}, u32[]{:S(2)}) collective-permute-start(bf16[384,384]{1,0:T(8,128)(2,1)S(1)} %collective-permute-done.2.rest_3_.refs_6_), channel_id=1, source_target_pairs={{0,8},{8,0},{16,24},{24,16},{1,9},{9,1},{17,25},{25,17},{2,10},{10... | collective-permute-start | bytes 884744 | tf_op jit(solution)/shard_map/ppermute | solution.py:907
  39.6 1.1 collective-permute-done.6.rest_7_.refs_10_
  40.6 1.1 broadcast_in_dim.5
  41.8 5.7 %all-to-all-start.2 = ((bf16[8,96,640]{2,1,0:T(8,128)(2,1)}), bf16[8,96,640]{2,1,0:T(8,128)(2,1)S(1)}, u32[]{:S(2)}, u32[]{:S(2)}) async-start(bf16[8,96,640]{2,1,0:T(8,128)(2,1)} %broadcast_in_dim.5), calls=%async_computation.2 | async-start | bytes 1966080 | tf_op jit(solution)/shard_map/all_to_all | solution.py:924
  47.5 1.2 collective-permute-start.7
  48.7 14.8 %shard_map.276 = (bf16[8,208,768]{2,1,0:T(8,128)(2,1)}, bf16[8,208,256]{2,1,0:T(8,128)(2,1)}, bf16[8,4,208,208]{3,2,1,0:T(8,128)(2,1)}, bf16[8,208,128]{2,1,0:T(...) custom-call(s32[2]{0:T(128)} %pad_add_fusion.place_ref, ...), custom_call_target="tpu_custom_call" | custom-call | flops 2317352960 | bytes 12697600 | tf_op jit(solution)/shard_map/pallas_call | solution.py:615
  63.6 1.0 collective-permute-start.8
  64.7 1.3 collective-permute-done.8.rest_1_.refs_12_
  67.2 10.6 %shard_map.277 = (bf16[8,208,768]{2,1,0:T(8,128)(2,1)}, bf16[8,208,256]{2,1,0:T(8,128)(2,1)}, bf16[8,4,208,208]{3,2,1,0:T(8,128)(2,1)}, bf16[768,128]{1,0:T(8,128)(2,1)}, bf16[768,128]{1,0:T(8,128)(2,1)}) custom-call(s32[2]{0:T(128)} %pad_add_fusion.place_ref, bf16[8,208,768]{2,1,0:T(8,128)(2,1)} %shard_map.275.h1_ref.refs_8_, ...), custom_call_target="tpu_custom_call" | custom-call | flops 2317352960 | bytes 11714560 | tf_op jit(solution)/shard_map/pallas_call | solution.py:615
  78.7 1.3 collective-permute-done.10.rest_1_.refs_16_
  80.8 10.3 %shard_map.278 = (bf16[8,208,768]{2,1,0:T(8,128)(2,1)}, bf16[8,208,256]{2,1,0:T(8,128)(2,1)}, bf16[8,4,208,208]{3,2,1,0:T(8,128)(2,1)}) custom-call(s32[2]{0:T(128)} %pad_add_fusion.place_ref, bf16[8,208,768]{2,1,0:T(8,128)(2,1)} %shard_map.275.h1_ref.refs_8_, bf16[8,208,128]{2,1,0:T(8,128)(2,1)} %get-tuple-element.114.uq_ref.refs_7_, ...), custom_call_target="tpu_custom_call" | custom-call | flops 2317352960 | bytes 10928128 | tf_op jit(solution)/shard_map/pallas_call | solution.py:615
  92.3 0.8 slice.60
  94.7 15.8 %shard_map.279 = (f32[8,208,768]{2,1,0:T(8,128)}, bf16[8,208,128]{2,1,0:T(8,128)(2,1)}, bf16[8,208,128]{2,1,0:T(8,128)(2,1)}, f32[8,16,208]{2,1,0:T(8,128)}, f32...) custom-call(s32[2]{0:T(128)} %pad_add_fusion.place_ref, s32[8]{0:T(128)} %index_ref.7, ...), custom_call_target="tpu_custom_call" | custom-call | flops 2944401408 | bytes 16388096 | tf_op jit(solution)/shard_map/pallas_call | solution.py:615
  110.5 1.1 copy.40
  111.6 17.3 %all_to_all.30.part_ref.rest_0_ = bf16[8,2,8,1664]{3,2,1,0:T(8,128)(2,1)S(1)} all-to-all(bf16[8,2,8,1664]{3,2,1,0:T(8,128)(2,1)S(1)} %bitcast.29), channel_id=1, replica_groups=mesh['replica'=4,'shard'=8] {'shard'}, dimensions={0} | all-to-all | bytes 851968 | tf_op jit(solution)/shard_map/all_to_all | solution.py:1072
  129.7 14.8 %shard_map.280 = bf16[8,2,8,1536]{3,2,1,0:T(8,128)(2,1)} custom-call(bf16[2,768,3072]{2,1,0:T(8,128)(2,1)} %wu_ref.5, bf16[2,3072,768]{2,1,0:T(8,128)(2,1)} %wd_ref.5, bf16[2,768,128]{2,1,0:T(8,128)(2,1)} %ua_ref.5, bf16[2,128,3072]{2,1,0:T(8,128)(2,1)} %ub_ref.5, bf16[2,3072,128]{2,1,0:T(8,128)(2,1)} %da_ref.5, bf16[2,128,768]{2,1,0:T(8,128)(2,1)} %db_ref.5, ...), custom_call_target="tpu_custom_call" | custom-call | flops 2415919104 | bytes 23625728 | tf_op jit(solution)/shard_map/pallas_call | solution.py:615
  144.4 4.0 %all-to-all-start.4 = ((bf16[8,2,8,1536]{3,2,1,0:T(8,128)(2,1)}), bf16[8,2,8,1536]{3,2,1,0:T(8,128)(2,1)S(1)}, u32[]{:S(2)}, u32[]{:S(2)}) async-start(bf16[8,2,8,1536]{3,2,1,0:T(8,128)(2,1)} %shard_map.280), calls=%async_computation.4 | async-start | bytes 786432 | tf_op jit(solution)/shard_map/all_to_all | solution.py:1082
  148.4 1.5 collective-permute-start.15
  150.1 1.5 collective-permute-done.15.rest_2_
  153.1 12.8 %shard_map.281 = (f32[2,768,128]{2,1,0:T(8,128)}, f32[2,128,3072]{2,1,0:T(8,128)}, f32[2,3072,128]{2,1,0:T(8,128)}, f32[2,128,768]{2,1,0:T(8,128)}) custom-call(bf16[2,768,3072]{2,1,0:T(8,128)(2,1)} %wu_ref.5, bf16[2,3072,768]{2,1,0:T(8,128)(2,1)} %wd_ref.5, bf16[2,768,128]{2,1,0:T(8,128)(2,1)} %ua_ref.5, bf16[2,128,3072]{2,1,0:T(8,128)(2,1)} %ub_ref.5, ...), custom_call_target="tpu_custom_call" | custom-call | flops 2415919104 | bytes 32374784 | tf_op jit(solution)/shard_map/pallas_call | solution.py:615
  165.9 0.9 copy.45.ret_ref
  166.8 23.3 %shard_map.282 = (bf16[8,197,768]{2,1,0:T(8,128)(2,1)}, f32[8,208,768]{2,1,0:T(8,128)}, bf16[8,208,768]{2,1,0:T(8,128)(2,1)}, bf16[8,320,128]{2,1,0:T(8,128)(2,1)}) custom-call(s32[2]{0:T(128)} %pad_add_fusion.place_ref, s32[8]{0:T(128)} %index_ref.7, s32[1]{0:T(128)S(6)} %copy.50.count_ref, bf16[8,197,768]{2,1,0:T(8,128)(2,1)} %copy.42._.cot_ref, ...), custom_call_target="tpu_custom_call" | custom-call | flops 3925868544 | bytes 24481792 | tf_op jit(solution)/shard_map/pallas_call | solution.py:615
  190.1 33.2 %shard_map.283 = (bf16[8,208,768]{2,1,0:T(8,128)(2,1)}, bf16[8,208,768]{2,1,0:T(8,128)(2,1)}, bf16[8,208,768]{2,1,0:T(8,128)(2,1)}, bf16[8,208,128]{2,1,0:T(8,128)(2,1)}, bf16[8,704,128]{2,1,0:T(8,128)(2,1)}) custom-call(s32[8]{0:T(128)} %index_ref.7, bf16[8,208,768]{2,1,0:T(8,128)(2,1)} %get-tuple-element.140.refs_0_, ...), custom_call_target="tpu_custom_call" | custom-call | flops 3639607296 | bytes 32292864 | tf_op jit(solution)/shard_map/pallas_call | solution.py:615
  223.3 1.2 constant_dynamic-slice_fusion.1
  224.9 1.8 collective-permute-done.17
  226.7 1.3 add_convert_fusion
  228.1 1.0 collective-permute-start.18
  229.1 18.1 %shard_map.284 = f32[9456,128]{1,0:T(8,128)} custom-call(s32[2]{0:T(128)} %pad_add_fusion.place_ref, bf16[8,197,768]{2,1,0:T(8,128)(2,1)} %copy.38.image_ref, f32[8,208,768]{2,1,0:T(8,128)} %get-tuple-element.149.gx2_ref, bf16[8,208,128]{2,1,0:T(8,128)(2,1)} %get-tuple-element.150.guq_ref, bf16[768,128]{1,0:T(8,128)(2,1)} %get-tuple-element.151.a_ref, ...), custom_call_target="tpu_custom_call" | custom-call | flops 6215958528 | bytes 25776128 | tf_op jit(solution)/shard_map/pallas_call | solution.py:615
  247.2 0.8 add_convert_fusion.1
  248.0 6.0 %all-to-all-start.5 = ((bf16[8,176,128]{2,1,0:T(8,128)(2,1)}), bf16[8,176,128]{2,1,0:T(8,128)(2,1)S(1)}, u32[]{:S(2)}, u32[]{:S(2)}) async-start(bf16[8,176,128]{2,1,0:T(8,128)(2,1)} %add_convert_fusion.1), calls=%async_computation.5 | async-start | bytes 720896 | tf_op jit(solution)/shard_map/all_to_all | solution.py:945
  254.0 13.0 %shard_map.285 = (f32[2,768,128]{2,1,0:T(8,128)}, f32[2,128,3072]{2,1,0:T(8,128)}, f32[2,3072,128]{2,1,0:T(8,128)}, f32[2,128,768]{2,1,0:T(8,128)}) custom-call(bf16[2,768,3072]{2,1,0:T(8,128)(2,1)} %wu_ref.5, bf16[2,3072,768]{2,1,0:T(8,128)(2,1)} %wd_ref.5, ...), custom_call_target="tpu_custom_call", output_to_operand_aliasing={{0}: (10, {}), {1}: (11, {}), {2}: (12, {}), {3}: (13, {})} | custom-call | flops 2415919104 | bytes 40239104 | tf_op jit(solution)/shard_map/pallas_call | solution.py:615
  267.6 2.4 collective-permute-done.19
  270.0 2.2 collective-permute-start.20
  272.2 1.9 copy.44
  (103 shorter events, 13.4 us)
Async XLA Ops:
  3.7 13.5 %all-to-all-start = ((bf16[4,96,384]{2,1,0:T(8,128)(2,1)}), bf16[4,96,384]{2,1,0:T(8,128)(2,1)S(1)}, u32[]{:S(2)}, u32[]{:S(2)}) async-start(bf16[4,96,384]{2,1,0:T(8,128)(2,1)} %shard_map.274), calls=%async_computation | async-start | bytes 589824 | tf_op jit(solution)/shard_map/all_to_all | solution.py:924
  9.2 5.3 %copy-start.2 = (bf16[8,197,768]{2,0,1:T(8,128)(2,1)S(1)}, bf16[8,197,768]{2,0,1:T(8,128)(2,1)}, u32[]{:S(2)}) copy-start(bf16[8,197,768]{2,0,1:T(8,128)(2,1)} %param.22) | copy-start | bytes 7262212
  14.4 5.2 %copy-start.8 = (bf16[96,2304]{1,0:T(8,128)(2,1)S(1)}, bf16[96,2304]{1,0:T(8,128)(2,1)}, u32[]{:S(2)}) copy-start(bf16[96,2304]{1,0:T(8,128)(2,1)} %qkv_ref.1) | copy-start | bytes 1327108
  14.4 5.3 %copy-start.23 = (bf16[128,96]{0,1:T(8,128)(2,1)S(1)}, bf16[128,96]{0,1:T(8,128)(2,1)}, u32[]{:S(2)}) copy-start(bf16[128,96]{0,1:T(8,128)(2,1)} %param.29) | copy-start | bytes 73732
  17.2 14.0 %copy-start.9 = (bf16[4,96,384]{2,1,0:T(8,128)(2,1)}, bf16[4,96,384]{2,1,0:T(8,128)(2,1)S(1)}, u32[]{:S(2)}) copy-start(bf16[4,96,384]{2,1,0:T(8,128)(2,1)S(1)} %all-to-all-done) | copy-start | bytes 884740
  17.2 6.4 %collective-permute-start = (bf16[384,384]{1,0:T(8,128)(2,1)S(1)}, bf16[384,384]{1,0:T(8,128)(2,1)S(1)}, u32[]{:S(2)}, u32[]{:S(2)}) collective-permute-start(bf16[384,384]{1,0:T(8,128)(2,1)S(1)} %bitcast.35), channel_id=1, source_target_pairs={{0,1},{1,0},{2,3},{3,2},{4,5},{5,4},{6,7},{7,6},{8,9},{9,8},{10,11... | collective-permute-start | bytes 884744 | tf_op jit(solution)/shard_map/ppermute | solution.py:907
  18.4 5.9 %collective-permute-start.1 = (bf16[384,384]{1,0:T(8,128)(2,1)S(1)}, bf16[384,384]{1,0:T(8,128)(2,1)S(1)}, u32[]{:S(2)}, u32[]{:S(2)}) collective-permute-start(bf16[384,384]{1,0:T(8,128)(2,1)S(1)} %bitcast.36), channel_id=1, source_target_pairs={{0,16},{8,24},{16,0},{24,8},{1,17},{9,25},{17,1},{25,9},{2,18},{10... | collective-permute-start | bytes 884744 | tf_op jit(solution)/shard_map/ppermute | solution.py:907
  19.8 19.6 %copy-start.22 = (bf16[96,768]{1,0:T(8,128)(2,1)S(1)}, bf16[96,768]{1,0:T(8,128)(2,1)}, u32[]{:S(2)}) copy-start(bf16[96,768]{1,0:T(8,128)(2,1)} %param.24) | copy-start | bytes 442372
  23.6 25.1 %copy-start.15 = (bf16[384,384]{1,0:T(8,128)(2,1)}, bf16[384,384]{1,0:T(8,128)(2,1)S(1)}, u32[]{:S(2)}) copy-start(bf16[384,384]{1,0:T(8,128)(2,1)S(1)} %collective-permute-done.rest_1_.refs_4_) | copy-start | bytes 884740
  24.3 24.4 %copy-start.16 = (bf16[384,384]{1,0:T(8,128)(2,1)}, bf16[384,384]{1,0:T(8,128)(2,1)S(1)}, u32[]{:S(2)}) copy-start(bf16[384,384]{1,0:T(8,128)(2,1)S(1)} %collective-permute-done.1.rest_2_.refs_5_) | copy-start | bytes 884740
  25.1 15.5 %all-to-all-start.1 = ((bf16[8,96,256]{2,1,0:T(8,128)(2,1)}), bf16[8,96,256]{2,1,0:T(8,128)(2,1)S(1)}, u32[]{:S(2)}, u32[]{:S(2)}) async-start(bf16[8,96,256]{2,1,0:T(8,128)(2,1)} %broadcast_in_dim.4), calls=%async_computation.1 | async-start | bytes 786432 | tf_op jit(solution)/shard_map/all_to_all | solution.py:924
  30.0 5.6 %collective-permute-start.2 = (bf16[384,384]{1,0:T(8,128)(2,1)S(1)}, bf16[384,384]{1,0:T(8,128)(2,1)S(1)}, u32[]{:S(2)}, u32[]{:S(2)}) collective-permute-start(bf16[384,384]{1,0:T(8,128)(2,1)S(1)} %collective-permute-done.rest_1_.refs_4_), channel_id=1, source_target_pairs={{0,16},{8,24},{16,0},{24,8},{1,17},{9,25},{17,1},{25,9},{2,18},{10... | collective-permute-start | bytes 884744 | tf_op jit(solution)/shard_map/ppermute | solution.py:907
  31.2 8.3 %collective-permute-start.3 = (bf16[384,384]{1,0:T(8,128)(2,1)S(1)}, bf16[384,384]{1,0:T(8,128)(2,1)S(1)}, u32[]{:S(2)}, u32[]{:S(2)}) collective-permute-start(bf16[384,384]{1,0:T(8,128)(2,1)S(1)} %bitcast.37), channel_id=1, source_target_pairs={{0,8},{8,0},{16,24},{24,16},{1,9},{9,1},{17,25},{25,17},{2,10},{10... | collective-permute-start | bytes 884744 | tf_op jit(solution)/shard_map/ppermute | solution.py:907
  34.2 5.3 %collective-permute-start.4 = (bf16[384,384]{1,0:T(8,128)(2,1)S(1)}, bf16[384,384]{1,0:T(8,128)(2,1)S(1)}, u32[]{:S(2)}, u32[]{:S(2)}) collective-permute-start(bf16[384,384]{1,0:T(8,128)(2,1)S(1)} %collective-permute-done.rest_1_.refs_4_), channel_id=1, source_target_pairs={{0,8},{8,0},{16,24},{24,16},{1,9},{9,1},{17,25},{25,17},{2,10},{10... | collective-permute-start | bytes 884744 | tf_op jit(solution)/shard_map/ppermute | solution.py:907
  34.2 5.3 %collective-permute-start.5 = (bf16[384,384]{1,0:T(8,128)(2,1)S(1)}, bf16[384,384]{1,0:T(8,128)(2,1)S(1)}, u32[]{:S(2)}, u32[]{:S(2)}) collective-permute-start(bf16[384,384]{1,0:T(8,128)(2,1)S(1)} %collective-permute-done.1.rest_2_.refs_5_), channel_id=1, source_target_pairs={{0,8},{8,0},{16,24},{24,16},{1,9},{9,1},{17,25},{25,17},{2,10},{10... | collective-permute-start | bytes 884744 | tf_op jit(solution)/shard_map/ppermute | solution.py:907
  35.6 13.2 %copy-start.17 = (bf16[384,384]{1,0:T(8,128)(2,1)}, bf16[384,384]{1,0:T(8,128)(2,1)S(1)}, u32[]{:S(2)}) copy-start(bf16[384,384]{1,0:T(8,128)(2,1)S(1)} %collective-permute-done.2.rest_3_.refs_6_) | copy-start | bytes 884740
  35.6 5.1 %collective-permute-start.6 = (bf16[384,384]{1,0:T(8,128)(2,1)S(1)}, bf16[384,384]{1,0:T(8,128)(2,1)S(1)}, u32[]{:S(2)}, u32[]{:S(2)}) collective-permute-start(bf16[384,384]{1,0:T(8,128)(2,1)S(1)} %collective-permute-done.2.rest_3_.refs_6_), channel_id=1, source_target_pairs={{0,8},{8,0},{16,24},{24,16},{1,9},{9,1},{17,25},{25,17},{2,10},{10... | collective-permute-start | bytes 884744 | tf_op jit(solution)/shard_map/ppermute | solution.py:907
  39.5 9.2 %copy-start.18 = (bf16[384,384]{1,0:T(8,128)(2,1)}, bf16[384,384]{1,0:T(8,128)(2,1)S(1)}, u32[]{:S(2)}) copy-start(bf16[384,384]{1,0:T(8,128)(2,1)S(1)} %collective-permute-done.3.rest_4_.refs_7_) | copy-start | bytes 884740
  39.5 9.2 %copy-start.19 = (bf16[384,384]{1,0:T(8,128)(2,1)}, bf16[384,384]{1,0:T(8,128)(2,1)S(1)}, u32[]{:S(2)}) copy-start(bf16[384,384]{1,0:T(8,128)(2,1)S(1)} %collective-permute-done.4.rest_5_.refs_8_) | copy-start | bytes 884740
  39.5 2.2 copy-start.20
  40.6 1.1 copy-start.21
  40.6 22.9 %copy-start.7 = (bf16[8,96,256]{2,1,0:T(8,128)(2,1)}, bf16[8,96,256]{2,1,0:T(8,128)(2,1)S(1)}, u32[]{:S(2)}) copy-start(bf16[8,96,256]{2,1,0:T(8,128)(2,1)S(1)} %all-to-all-done.1) | copy-start | bytes 1179652
  41.8 36.0 %all-to-all-start.2 = ((bf16[8,96,640]{2,1,0:T(8,128)(2,1)}), bf16[8,96,640]{2,1,0:T(8,128)(2,1)S(1)}, u32[]{:S(2)}, u32[]{:S(2)}) async-start(bf16[8,96,640]{2,1,0:T(8,128)(2,1)} %broadcast_in_dim.5), calls=%async_computation.2 | async-start | bytes 1966080 | tf_op jit(solution)/shard_map/all_to_all | solution.py:924
  47.5 16.1 %collective-permute-start.7 = (bf16[768,256]{1,0:T(8,128)(2,1)S(1)}, bf16[768,256]{1,0:T(8,128)(2,1)S(1)}, u32[]{:S(2)}, u32[]{:S(2)}) collective-permute-start(bf16[768,256]{1,0:T(8,128)(2,1)S(1)} %bitcast.31), channel_id=1, source_target_pairs={{0,16},{8,24},{16,0},{24,8},{1,17},{9,25},{17,1},{25,9},{2,18},{10... | collective-permute-start | bytes 1179656 | tf_op jit(solution)/shard_map/ppermute | solution.py:907
  63.6 2.9 %copy-start.12 = (bf16[768,256]{1,0:T(8,128)(2,1)}, bf16[768,256]{1,0:T(8,128)(2,1)S(1)}, u32[]{:S(2)}) copy-start(bf16[768,256]{1,0:T(8,128)(2,1)S(1)} %collective-permute-done.7.rest_2_.refs_13_) | copy-start | bytes 1179652
  63.6 2.3 collective-permute-start.8
  64.6 1.9 collective-permute-start.9
  77.9 2.1 copy-start.3
  77.9 2.1 collective-permute-start.10
  78.4 15.5 %copy-start.11 = (bf16[768,256]{1,0:T(8,128)(2,1)}, bf16[768,256]{1,0:T(8,128)(2,1)S(1)}, u32[]{:S(2)}) copy-start(bf16[768,256]{1,0:T(8,128)(2,1)S(1)} %slice.52.rest_0_) | copy-start | bytes 1179652
  78.4 12.7 %collective-permute-start.11 = (bf16[768,256]{1,0:T(8,128)(2,1)S(1)}, bf16[768,256]{1,0:T(8,128)(2,1)S(1)}, u32[]{:S(2)}, u32[]{:S(2)}) collective-permute-start(bf16[768,256]{1,0:T(8,128)(2,1)S(1)} %slice.52.rest_0_), channel_id=1, source_target_pairs={{0,16},{8,24},{16,0},{24,8},{1,17},{9,25},{17,1},{25,9},{2,18},{10... | collective-permute-start | bytes 1179656 | tf_op jit(solution)/shard_map/ppermute | solution.py:907
  80.0 0.8 copy-start.10
  91.1 2.8 %copy-start.24 = (bf16[768,256]{1,0:T(8,128)(2,1)}, bf16[768,256]{1,0:T(8,128)(2,1)S(1)}, u32[]{:S(2)}) copy-start(bf16[768,256]{1,0:T(8,128)(2,1)S(1)} %collective-permute-done.11.rest_2_) | copy-start | bytes 1179652
  91.1 2.8 %collective-permute-start.12 = (bf16[768,256]{1,0:T(8,128)(2,1)S(1)}, bf16[768,256]{1,0:T(8,128)(2,1)S(1)}, u32[]{:S(2)}, u32[]{:S(2)}) collective-permute-start(bf16[768,256]{1,0:T(8,128)(2,1)S(1)} %slice.52.rest_0_), channel_id=1, source_target_pairs={{0,8},{8,0},{16,24},{24,16},{1,9},{9,1},{17,25},{25,17},{2,10},{10... | collective-permute-start | bytes 1179656 | tf_op jit(solution)/shard_map/ppermute | solution.py:907
  91.5 2.3 collective-permute-start.13
  93.8 0.8 copy-start.25
  93.8 0.9 copy-start.26
  128.9 15.5 %collective-permute-start.14 = (bf16[8,2,8,1664]{3,2,1,0:T(8,128)(2,1)S(1)}, bf16[8,2,8,1664]{3,2,1,0:T(8,128)(2,1)S(1)}, u32[]{:S(2)}, u32[]{:S(2)}) collective-permute-start(bf16[8,2,8,1664]{3,2,1,0:T(8,128)(2,1)S(1)} %all_to_all.30.part_ref.rest_0_), channel_id=1, source_target_pairs={{0,16},{8,24},{16,0},{24,8},{1,17},{9,25},{17,1},{25,9},{2,18},{10... | collective-permute-start | bytes 1277960 | tf_op jit(solution)/shard_map/ppermute | solution.py:907
  144.4 7.6 %copy-start.4 = (bf16[8,2,8,1664]{3,2,1,0:T(8,128)(2,1)}, bf16[8,2,8,1664]{3,2,1,0:T(8,128)(2,1)S(1)}, u32[]{:S(2)}) copy-start(bf16[8,2,8,1664]{3,2,1,0:T(8,128)(2,1)S(1)} %collective-permute-done.14.rest_1_) | copy-start | bytes 1277956
  144.4 21.5 %all-to-all-start.4 = ((bf16[8,2,8,1536]{3,2,1,0:T(8,128)(2,1)}), bf16[8,2,8,1536]{3,2,1,0:T(8,128)(2,1)S(1)}, u32[]{:S(2)}, u32[]{:S(2)}) async-start(bf16[8,2,8,1536]{3,2,1,0:T(8,128)(2,1)} %shard_map.280), calls=%async_computation.4 | async-start | bytes 786432 | tf_op jit(solution)/shard_map/all_to_all | solution.py:1082
  148.4 3.1 %collective-permute-start.15 = (bf16[8,2,8,1664]{3,2,1,0:T(8,128)(2,1)}, bf16[8,2,8,1664]{3,2,1,0:T(8,128)(2,1)S(1)}, u32[]{:S(2)}, u32[]{:S(2)}) collective-permute-start(bf16[8,2,8,1664]{3,2,1,0:T(8,128)(2,1)} %copy-done), channel_id=1, source_target_pairs={{0,8},{8,0},{16,24},{24,16},{1,9},{9,1},{17,25},{25,17},{2,10},{10... | collective-permute-start | bytes 1277960 | tf_op jit(solution)/shard_map/ppermute | solution.py:907
  150.0 2.0 collective-permute-start.16
  224.5 2.3 collective-permute-start.17
  228.1 19.1 %collective-permute-start.18 = (bf16[8,176,128]{2,1,0:T(8,128)(2,1)S(1)}, bf16[8,176,128]{2,1,0:T(8,128)(2,1)S(1)}, u32[]{:S(2)}, u32[]{:S(2)}) collective-permute-start(bf16[8,176,128]{2,1,0:T(8,128)(2,1)S(1)} %constant_dynamic-slice_fusion), channel_id=1, source_target_pairs={{0,16},{8,24},{16,0},{24,8},{1,17},{9,25},{17,1},{25,9},{2,18},{10... | collective-permute-start | bytes 1081352 | tf_op jit(solution)/shard_map/ppermute | solution.py:907
  248.0 18.9 %all-to-all-start.5 = ((bf16[8,176,128]{2,1,0:T(8,128)(2,1)}), bf16[8,176,128]{2,1,0:T(8,128)(2,1)S(1)}, u32[]{:S(2)}, u32[]{:S(2)}) async-start(bf16[8,176,128]{2,1,0:T(8,128)(2,1)} %add_convert_fusion.1), calls=%async_computation.5 | async-start | bytes 720896 | tf_op jit(solution)/shard_map/all_to_all | solution.py:945
  254.0 18.2 %copy-start.1 = (bf16[8,197,768]{2,1,0:T(8,128)(2,1)S(1)}, bf16[8,197,768]{2,1,0:T(8,128)(2,1)}, u32[]{:S(2)}) copy-start(bf16[8,197,768]{2,1,0:T(8,128)(2,1)} %get-tuple-element.170) | copy-start | bytes 7262212
  267.0 3.0 %collective-permute-start.19 = (bf16[176,128]{1,0:T(8,128)(2,1)S(1)}, bf16[176,128]{1,0:T(8,128)(2,1)S(1)}, u32[]{:S(2)}, u32[]{:S(2)}) collective-permute-start(bf16[176,128]{1,0:T(8,128)(2,1)S(1)} %reduce_sum.12), channel_id=1, source_target_pairs={{0,16},{8,24},{16,0},{24,8},{1,17},{9,25},{17,1},{25,9},{2,18},{10... | collective-permute-start | bytes 135176 | tf_op jit(solution)/shard_map/ppermute | solution.py:907
  270.0 4.0 %collective-permute-start.20 = (bf16[352,128]{1,0:T(8,128)(2,1)S(1)}, bf16[352,128]{1,0:T(8,128)(2,1)S(1)}, u32[]{:S(2)}, u32[]{:S(2)}) collective-permute-start(bf16[352,128]{1,0:T(8,128)(2,1)S(1)} %maximum_select_fusion.1), channel_id=1, source_target_pairs={{0,8},{8,0},{16,24},{24,16},{1,9},{9,1},{17,25},{25,17},{2,10},{10... | collective-permute-start | bytes 270344 | tf_op jit(solution)/shard_map/ppermute | solution.py:907
  (5 other events, 3.8 us)

commit v4 on v3

--- a/solution.py
+++ b/solution.py
@@ -22,7 +22,7 @@
 GELU_C = 0.7978845608028654
 GELU_A = 0.044715
 IMAGES_FORWARD = 2
-IMAGES_BACK = 1
+IMAGES_BACK = 2
 IMAGES_ROUTE = 2
 IMAGES_LAST = 2
 STRIPS = 4
@@ -142,6 +142,35 @@
         out_ref[copy] = mine
 
 
+def later_pack_kernel(
+    place_ref, qkv_ref, bo_ref, wr_ref, wo_ref, rb_ref, first_ref, second_ref, pack1, pack2, pack3
+):
+    shards, rows, part = first_ref.shape
+    width = wo_ref.shape[1]
+    for piece in range(3):
+        for group, pack in ((1, pack1), (2, pack2)):
+            start = piece * width + group * GROUP
+            pack[:, piece * GROUP : (piece + 1) * GROUP] = qkv_ref[:, start : start + GROUP]
+    pack1[:, width : width + LANES] = bo_ref[...]
+    n_exp, n_loc = wr_ref.shape[0], rb_ref.shape[0]
+    route = jnp.concatenate([wr_ref[...].astype(F32), jnp.zeros((LANES - n_exp, rows), F32)], axis=0)
+    pack1[:, width + LANES :] = route.T.astype(BF16)
+    pack3[:, :width] = wo_ref[...]
+    second = jnp.concatenate([rb_ref[...].astype(F32), jnp.zeros((rows - n_loc, LANES), F32)], axis=0)
+    pack3[:, width : width + LANES] = second.astype(BF16)
+    pack3[:, width + LANES :] = jnp.zeros((rows, LANES), BF16)
+    half = pack2.shape[1] // 2
+
+    def own(pack, pieces, size):
+        return pack[:, pl.ds(pl.multiple_of(place_ref[0] % pieces * size, LANES), size)]
+
+    one, two, three = own(pack1, 4, part), own(pack2, 2, half), own(pack3, 4, part)
+    for shard in range(shards):
+        first_ref[shard] = one
+        second_ref[shard, :, :half] = two
+        second_ref[shard, :, half:] = three
+
+
 def head_mask(value):
     lane = lax.broadcasted_iota(jnp.int32, (1, LANES), 1)
     low = jnp.where(lane < HEAD_DIM, value, 0.0).astype(BF16)
@@ -247,11 +276,13 @@
 
 
 def route_kernel(
-    n_exp, layout, place_ref, index_ref, count_ref, image_ref, cot_ref, att0, att1, att2,
-    ao_ref, bo_ref, ra_ref, wr_ref, rb_ref, *rest,
+    n_exp, shards, layout, place_ref, index_ref, count_ref, image_ref, cot_ref, att0, att1, att2,
+    ao_ref, bo_ref, ra_ref, wr_ref, *rest,
 ):
     chunks, rest = rest[: len(layout[1])], rest[len(layout[1]) :]
-    x2_ref, uo_ref, ur_ref, disp_ref, comb_ref, sg_ref, wrt_ref, wall, pad_a, pad_b = rest
+    x2_ref, uo_ref, ur_ref, disp_ref, comb_ref, sg_ref, wrt_ref, rb_ref, *rest = rest
+    wall, rb_f, pad_a, pad_b, sent_ref = rest
+    every = sg_ref.shape[2]
     n_img, n_tok, width = image_ref.shape
     first = pl.program_id(0) * n_img
     total = x2_ref.shape[1]
@@ -260,6 +291,12 @@
     def _():
         assemble(place_ref, chunks, layout, wall)
         wrt_ref[...] = wr_ref[...].astype(F32).T[:n_exp].astype(BF16)
+        n_loc, rows = n_exp // shards, width // shards
+        for shard in range(shards):
+            rb_f[shard * n_loc : (shard + 1) * n_loc, :] = wall[
+                shard * rows : shard * rows + 8, width : width + LANES
+            ].astype(F32)[:n_loc]
+        rb_ref[...] = rb_f[...].astype(BF16)
 
     att = jnp.concatenate([flat(att0), flat(att1), flat(att2)], axis=1)
     uo = select_rows(dot(att, ao_ref[...]).astype(BF16).astype(F32), index_ref, first, n_img)
@@ -283,10 +320,24 @@
         disp_ref[slot] = disp
         comb_ref[slot] = comb
         upstream = (cot[rows] * living).astype(BF16)
-        sg_ref[slot, :, :width] = dot(disp.astype(BF16), h2[rows]).astype(BF16)
-        sg_ref[slot, :, width : 2 * width] = dot(comb.astype(BF16), upstream).astype(BF16)
-        selector = rank_row(index_ref[first + slot])
-        sg_ref[slot, :, 2 * width :] = jnp.broadcast_to(selector, (n_exp, LANES)).astype(BF16)
+        sent = jnp.concatenate(
+            [
+                dot(disp.astype(BF16), h2[rows]),
+                dot(comb.astype(BF16), upstream),
+                jnp.broadcast_to(rank_row(index_ref[first + slot]), (n_exp, LANES)),
+            ],
+            axis=1,
+        )
+        for block in range(sent.shape[1] // LANES):
+            start = block * n_exp * every + first + slot
+            sent_ref[pl.ds(start, n_exp, stride=every), :] = sent[:, block * LANES : (block + 1) * LANES]
+
+    @pl.when(pl.program_id(0) == pl.num_programs(0) - 1)
+    def _():
+        for block in range(sg_ref.shape[3] // LANES):
+            span = slice(block * LANES, (block + 1) * LANES)
+            piece = sent_ref[block * n_exp * every : (block + 1) * n_exp * every, :]
+            sg_ref[:, :, :, span] = piece.reshape(sg_ref.shape[:3] + (LANES,)).astype(BF16)
 
 
 def gelu_both(pre):
@@ -312,7 +363,7 @@
 
 
 def expert_kernel(
-    wu_ref, wd_ref, ua_ref, ub_ref, da_ref, db_ref, part_ref, out_ref,
+    wu_ref, wd_ref, ua_ref, ub_ref, da_ref, db_ref, part_ref, out_ref, hidden_ref, gpre_ref, low_ref,
     sg_ref, u1_ref, gu2_ref, acc_y, acc_s, acc_u2, acc_gu1,
 ):
     step = pl.program_id(1)
@@ -335,6 +386,8 @@
         sg_ref[:, :width], sg_ref[:, width : 2 * width], u1_ref[...], gu2_ref[...],
         wu_ref, wd_ref, ub_ref, da_ref,
     )
+    hidden_ref[0] = hidden
+    gpre_ref[0] = gpre
     acc_y[...] += dot(hidden, wd_ref[0])
     acc_u2[...] += dot(hidden, da_ref[0])
     acc_s[...] += dot(wu_ref[0], gpre, NT)
@@ -350,62 +403,70 @@
         out_ref[:, 0, :, :width] = result.reshape(shards, n_img, width).astype(BF16)
         result = acc_s[...].T + dot(gu1, ua_ref[0], NT)
         out_ref[:, 0, :, width:] = result.reshape(shards, n_img, width).astype(BF16)
-
-
-def expert_grad_kernel(
-    copies, wu_ref, wd_ref, ua_ref, ub_ref, da_ref, db_ref, *rest
-):
-    part_refs = rest[:copies]
-    gua_ref, gub_ref, gda_ref, gdb_ref = rest[-11:-7]
-    sg_ref, u1_ref, gu2_ref, u1t_ref, gu2t_ref, acc_u2, acc_gu1 = rest[-7:]
-    step = pl.program_id(1)
-    width = wu_ref.shape[1]
-
-    @pl.when(step == 0)
+        for place, low in enumerate((u1_ref[...], u2, gu1, gu2_ref[...])):
+            low_ref[0, :, place * LANES : (place + 1) * LANES] = low
+
+
+def expert_grad_kernel(copies, *refs):
+    refs = list(refs)
+    part_refs, hidden_refs, gpre_refs, low_refs = (
+        [refs.pop(0) for _ in range(copies)] for _ in range(4)
+    )
+    gua_ref, gub_ref, gda_ref, gdb_ref, sg_ref, low_t, rows_ref = refs
+    rows = hidden_refs[0].shape[1]
+    width = gua_ref.shape[1]
+
+    @pl.when(pl.program_id(1) == 0)
     def _():
         gather_rows(part_refs, sg_ref)
-        selector = sg_ref[:, 2 * width :].astype(F32)
-        u1 = dot(sg_ref[:, :width], ua_ref[0]).astype(BF16).astype(F32) * selector
-        gu2 = dot(sg_ref[:, width : 2 * width], db_ref[0], NT) * selector
-        u1_ref[...] = u1.astype(BF16)
-        gu2_ref[...] = gu2.astype(BF16)
-        u1t_ref[...] = u1.T.astype(BF16)
-        gu2t_ref[...] = gu2.T.astype(BF16)
-        acc_u2[...] = jnp.zeros_like(acc_u2)
-        acc_gu1[...] = jnp.zeros_like(acc_gu1)
-
-    hidden, gpre = expert_tile(
-        sg_ref[:, :width], sg_ref[:, width : 2 * width], u1_ref[...], gu2_ref[...],
-        wu_ref, wd_ref, ub_ref, da_ref,
-    )
-    gub_ref[0] = dot(u1t_ref[...], gpre)
-    gda_ref[0] = dot(gu2t_ref[...], hidden).T
-    acc_u2[...] += dot(hidden, da_ref[0])
-    acc_gu1[...] += dot(ub_ref[0], gpre, NT)
-
-    @pl.when(step == pl.num_programs(1) - 1)
-    def _():
-        selector = sg_ref[:, 2 * width :].astype(F32)
-        u2 = acc_u2[...].astype(BF16).astype(F32) * selector
-        gu1 = (acc_gu1[...] * selector.T).astype(BF16)
-        gdb_ref[0] = dot(u2.T.astype(BF16), sg_ref[:, width : 2 * width])
-        gua_ref[0] = dot(gu1, sg_ref[:, :width]).T
+        low = jnp.concatenate([ref[0] for ref in low_refs], axis=0)
+        low_t[...] = low.astype(F32).T.astype(BF16)
+        u2_t, gu1_t = low_t[LANES : 2 * LANES, :], low_t[2 * LANES : 3 * LANES, :]
+        gdb_ref[0] = dot(u2_t, sg_ref[:, width : 2 * width])
+        gua_ref[0] = dot(gu1_t, sg_ref[:, :width]).T
+
+    for number in range(copies):
+        rows_ref[number * rows : (number + 1) * rows, :] = gpre_refs[number][0]
+    gub_ref[0] = dot(low_t[:LANES, :], rows_ref[...])
+    for number in range(copies):
+        rows_ref[number * rows : (number + 1) * rows, :] = hidden_refs[number][0]
+    gda_ref[0] = dot(low_t[3 * LANES :, :], rows_ref[...]).T
+
+
+def turn_kernel(layouts, place_ref, ao_ref, ra_ref, *refs):
+    refs = list(refs)
+    chunks = [[refs.pop(0) for _ in layout[1]] for layout in layouts]
+    qkv_ref, out_ref, route_ref = refs[:3]
+    walls = refs[3:]
+    for chunk, layout, wall in zip(chunks, layouts, walls):
+        assemble(place_ref, chunk, layout, wall)
+    width = walls[0].shape[0]
+    for group, wall in enumerate(walls[:-1]):
+        qkv_ref[group * 3 * GROUP : (group + 1) * 3 * GROUP, :] = wall[:, : 3 * GROUP].T
+    qkv_ref[3 * width :, :] = walls[0][:, 3 * GROUP : 3 * GROUP + LANES].T
+    out_ref[:width, :] = walls[-1][:, :width].T
+    out_ref[width:, :] = ao_ref[...].T
+    route_ref[...] = ra_ref[...].T
 
 
 def route_back_kernel(
-    n_exp, layout, place_ref, index_ref, count_ref, cot_ref, x2_ref, uo_ref, ur_ref, disp_ref,
-    comb_ref, att0, att1, att2, ret_ref, ao_ref, bo_ref, ra_ref, wrt_ref, rb_ref, *rest,
+    n_exp, index_ref, count_ref, cot_ref, x2_ref, uo_ref, ur_ref, disp_ref, comb_ref,
+    att0, att1, att2, ret_ref, bo_ref, wrt_ref, rb_ref, out_ref, route_ref,
+    block_ref, gx2_ref, gatt_ref, pack_ref, pad_b, back_ref, acc_oa, acc_ob, acc_ra, acc_rb,
 ):
-    chunks, rest = rest[: len(layout[1])], rest[len(layout[1]) :]
-    block_ref, gx2_ref, gatt_ref, pack_ref, *rest = rest
-    wall, pad_b, acc_oa, acc_ob, acc_ra, acc_rb = rest
     n_img, n_tok, width = cot_ref.shape
     first = pl.program_id(0) * n_img
     total = x2_ref.shape[1]
 
+    every = ret_ref.shape[2]
+
     @pl.when(first == 0)
     def _():
-        assemble(place_ref, chunks, layout, wall)
+        for block in range(2 * width // LANES):
+            piece = ret_ref[:, :, :, block * LANES : (block + 1) * LANES].astype(F32)
+            back_ref[block * n_exp * every : (block + 1) * n_exp * every, :] = piece.reshape(
+                n_exp * every, LANES
+            )
         acc_oa[...] = jnp.zeros_like(acc_oa)
         acc_ob[...] = jnp.zeros_like(acc_ob)
         acc_ra[...] = jnp.zeros_like(acc_ra)
@@ -422,7 +483,12 @@
         upstream = cot[rows] * living
         upstreams.append(upstream)
         disp, comb = disp_ref[slot], comb_ref[slot]
-        yexp, gslot = ret_ref[slot, :, :width], ret_ref[slot, :, width:]
+        blocks = [
+            back_ref[pl.ds(block * n_exp * every + first + slot, n_exp, stride=every), :]
+            for block in range(2 * width // LANES)
+        ]
+        back = jnp.concatenate(blocks, axis=1).astype(BF16)
+        yexp, gslot = back[:, :width], back[:, width:]
         gcomb = dot(yexp, upstream.astype(BF16), NT)
         gdisp = dot(gslot, h2[rows], NT)
         glog = (
@@ -438,17 +504,17 @@
     glog_rows = jnp.concatenate([pair[:, n_exp:] for pair in pairs], axis=0)
     gur = select_rows(dot(glog_rows, rb_ref[...]), index_ref, first, n_img)
     acc_ra[...] += dot(gur, h2, TN)
-    gh2 = dot(gur, ra_ref[...], NT) + jnp.concatenate(
+    gh2 = dot(gur, route_ref[...]) + jnp.concatenate(
         [dot(pair, below) for pair, below in zip(pairs, belows)], axis=0
     )
     gx2 = jnp.concatenate(upstreams, axis=0) + normalise_back(unit, scale, gh2)
-    gx2_ref[...] = gx2.reshape(gx2_ref.shape)
     gbr = gx2.astype(BF16)
+    gx2_ref[...] = gbr.reshape(gx2_ref.shape)
     acc_ob[...] += dot(flat(uo_ref), gbr, TN)
     guo = select_rows(dot(gbr, bo_ref[...]), index_ref, first, n_img)
     att = jnp.concatenate([flat(att0), flat(att1), flat(att2)], axis=1)
     acc_oa[...] += dot(guo, att, TN)
-    gatt = (dot(gbr, wall[:, :width], NT) + dot(guo, ao_ref[...], NT)).astype(BF16)
+    gatt = dot(jnp.concatenate([gbr, guo], axis=1), out_ref[...]).astype(BF16)
     gatt_ref[...] = gatt.reshape(gatt_ref.shape)
 
     @pl.when(pl.program_id(0) == pl.num_programs(0) - 1)
@@ -500,14 +566,14 @@
     return jnp.concatenate([gq] + gk_parts + gv_parts, axis=1)
 
 
-def attention_back_kernel(groups, index_ref, *refs):
+def attention_back_kernel(groups, place_ref, index_ref, *refs):
     refs = list(refs)
     qkv_refs = [refs.pop(0) for _ in range(groups)]
     prob_refs = [refs.pop(0) for _ in range(groups)]
     gatt_ref, uq_ref, h1_ref, bt_ref, others_ref = refs[:5]
     refs = refs[5:]
     gqkv_refs = [refs.pop(0) for _ in range(groups)]
-    guq_ref, pack_ref, acc_b, acc_a = refs
+    guq_ref, keep_ref, give_ref, pack_ref, acc_b, acc_a = refs
     step = pl.program_id(0)
     n_img, total, width = h1_ref.shape
 
@@ -554,32 +620,22 @@
                     take = part * GROUP + place - start
                     pack_ref[shard, offset : offset + length, :] = summed[take : take + length]
                     place += length
-
-
-def input_grad_kernel(layouts, place_ref, image_ref, gx2_ref, guq_ref, a_ref, *refs):
-    refs = list(refs)
-    groups = len(layouts)
-    gqkv = [refs.pop(0) for _ in layouts]
-    chunks = [[refs.pop(0) for _ in layout[1]] for layout in layouts]
-    out_ref = refs.pop(0)
-    walls = [refs.pop(0) for _ in layouts]
-    pad_a = refs.pop(0)
+        half = keep_ref.shape[1]
+        side = place_ref[2] % 2
+        keep_ref[...] = pack_ref[:, pl.ds(pl.multiple_of(side * half, 16), half), :]
+        give_ref[...] = pack_ref[:, pl.ds(pl.multiple_of((1 - side) * half, 16), half), :]
+
+
+def input_grad_kernel(image_ref, gx2_ref, guq_ref, turned_ref, *refs):
+    *gqkv, out_ref, pad_a = refs
     n_img, n_tok, width = image_ref.shape
     step = pl.program_id(0)
     parts = width // LANES
     every = out_ref.shape[0] // (n_tok * parts)
-
-    @pl.when(step == 0)
-    def _():
-        for group in range(groups):
-            assemble(place_ref, chunks[group], layouts[group], walls[group])
-
-    gh1 = dot(flat(guq_ref), a_ref[...], NT)
-    for group in range(groups):
-        gh1 = gh1 + dot(flat(gqkv[group]), walls[group][:, : 3 * GROUP], NT)
+    total = gx2_ref.shape[1]
+    gh1 = dot(jnp.concatenate([flat(ref) for ref in gqkv] + [flat(guq_ref)], axis=1), turned_ref[...])
     unit, scale = normalise(pad_rows(pad_a, image_ref))
-    total = gx2_ref.shape[1]
-    result = flat(gx2_ref) + normalise_back(unit, scale, gh1)
+    result = flat(gx2_ref).astype(F32) + normalise_back(unit, scale, gh1)
     for slot in range(n_img):
         for part in range(parts):
             out_ref[pl.ds(part * every + step * n_img + slot, n_tok, stride=parts * every), :] = result[
@@ -651,6 +707,20 @@
     )[0]
 
 
+def later_pack_call(place, weights, shards):
+    rows, width = weights[3].shape
+    part, half = (width + 2 * LANES) // 4, width // 2
+    return call(
+        later_pack_kernel, (place,), (1,), [(weight, whole(weight.shape)) for weight in weights],
+        [
+            ((shards, rows, part), BF16, whole((shards, rows, part))),
+            ((shards, rows, half + part), BF16, whole((shards, rows, half + part))),
+        ],
+        [pltpu.VMEM((rows, columns), BF16) for columns in (4 * part, 2 * half, 4 * part)],
+        rows * width,
+    )
+
+
 def attention_flops(n_img, total, width, parts):
     return n_img * total * (2 * width * 3 * GROUP + parts * 8 * total * HEAD_DIM)
 
@@ -705,13 +775,14 @@
     )
 
 
-def route_call(place, index, count, images, cotangent, atts, banks, pack, n_exp, total):
+def route_call(place, index, count, images, cotangent, atts, banks, pack, n_exp, total, shards):
     n_img, n_tok, width = images.shape
     chunks, layout, columns = pack
     each = several(n_img, IMAGES_ROUTE)
     here = functools.partial(per_image, images=each)
+    sent = (shards, n_exp // shards, n_img, 2 * width + LANES)
     return call(
-        functools.partial(route_kernel, n_exp, layout), (place, index, count), (n_img // each,),
+        functools.partial(route_kernel, n_exp, shards, layout), (place, index, count), (n_img // each,),
         [(images, here(n_tok, width)), (cotangent, here(n_tok, width))]
         + [(att, here(total, GROUP)) for att in atts]
         + [(bank, whole(bank.shape)) for bank in banks]
@@ -722,13 +793,16 @@
             ((n_img, total, LANES), BF16, here(total, LANES)),
             ((n_img, n_exp, total), F32, here(n_exp, total)),
             ((n_img, n_exp, total), F32, here(n_exp, total)),
-            ((n_img, n_exp, 2 * width + LANES), BF16, here(n_exp, 2 * width + LANES)),
+            (sent, BF16, whole(sent)),
             ((n_exp, width), BF16, whole((n_exp, width))),
+            ((n_exp, LANES), BF16, whole((n_exp, LANES))),
         ],
         [
             pltpu.VMEM((width, columns), BF16),
+            pltpu.VMEM((n_exp, LANES), F32),
             pltpu.VMEM((each * total, width), F32),
             pltpu.VMEM((each * total, width), F32),
+            pltpu.VMEM(((2 * width // LANES + 1) * n_exp * n_img, LANES), F32),
         ],
         n_img * total * 2 * width * (width + 3 * LANES), n_img * total * 2 * n_exp,
     )
@@ -763,10 +837,19 @@
     width, hidden = weights[0].shape[1:]
     tile = hidden_tile(hidden, 1536)
     out = (shards, n_loc, n_img, 2 * width)
+    tiled = pl.BlockSpec((1, rows, tile), lambda e, f: (e, 0, f))
     return call(
         expert_kernel, (), (n_loc, hidden // tile),
         list(zip(weights, expert_specs(width, tile))) + [(landed, expert_rows(landed.shape))],
-        [(out, BF16, expert_rows(out))],
+        [
+            (out, BF16, expert_rows(out)),
+            ((n_loc, rows, hidden), BF16, tiled),
+            ((n_loc, rows, hidden), BF16, tiled),
+            (
+                (n_loc, rows, 4 * LANES), BF16,
+                pl.BlockSpec((1, rows, 4 * LANES), lambda e, f: (e, 0, 0)),
+            ),
+        ],
         [
             pltpu.VMEM((rows, columns), BF16),
             pltpu.VMEM((rows, LANES), BF16),
@@ -777,44 +860,41 @@
             pltpu.VMEM((LANES, rows), F32),
         ],
         n_loc * rows * 8 * width * hidden, n_loc * rows * hidden,
-    )[0]
-
-
-def expert_grad_call(every, weights, first, before):
-    shards, n_loc, n_img, columns = every[0].shape
-    rows = shards * n_img * len(every)
-    width, hidden = weights[0].shape[1:]
-    tile = hidden_tile(hidden, 768 if rows <= 512 else 384)
-    aliases = {len(weights) + len(every) + i: i for i in range(4)} if before else {}
+    )
+
+
+def expert_grad_call(every, width):
+    parts, hiddens, gpres, lows = zip(*every)
+    shards, n_loc, n_img, columns = parts[0].shape
+    rows, hidden = hiddens[0].shape[1:]
+    total = rows * len(every)
+    tile = hidden_tile(hidden, 1536 if total <= 512 else 384)
+    tiled = pl.BlockSpec((1, rows, tile), lambda e, f: (e, 0, f))
+    low = pl.BlockSpec((1, rows, 4 * LANES), lambda e, f: (e, 0, 0))
     return call(
-        functools.partial(expert_grad_kernel, len(every)), (), (1, hidden // tile),
-        list(zip(weights, expert_specs(width, tile, first)))
-        + [(part, expert_rows(part.shape, first)) for part in every]
-        + [(array, ANY) for array in before],
-        [
-            ((n_loc, width, LANES), F32, pl.BlockSpec((1, width, LANES), lambda e, f: (e + first, 0, 0))),
-            ((n_loc, LANES, hidden), F32, pl.BlockSpec((1, LANES, tile), lambda e, f: (e + first, 0, f))),
-            ((n_loc, hidden, LANES), F32, pl.BlockSpec((1, tile, LANES), lambda e, f: (e + first, f, 0))),
-            ((n_loc, LANES, width), F32, pl.BlockSpec((1, LANES, width), lambda e, f: (e + first, 0, 0))),
-        ],
-        [
-            pltpu.VMEM((rows, columns), BF16),
-            pltpu.VMEM((rows, LANES), BF16),
-            pltpu.VMEM((rows, LANES), BF16),
-            pltpu.VMEM((LANES, rows), BF16),
-            pltpu.VMEM((LANES, rows), BF16),
-            pltpu.VMEM((rows, LANES), F32),
-            pltpu.VMEM((LANES, rows), F32),
-        ],
-        rows * 4 * width * hidden, rows * hidden, aliases,
+        functools.partial(expert_grad_kernel, len(every)), (), (n_loc, hidden // tile),
+        [(part, expert_rows(part.shape)) for part in parts]
+        + [(array, tiled) for array in hiddens + gpres]
+        + [(array, low) for array in lows],
+        [
+            ((n_loc, width, LANES), F32, pl.BlockSpec((1, width, LANES), lambda e, f: (e, 0, 0))),
+            ((n_loc, LANES, hidden), F32, pl.BlockSpec((1, LANES, tile), lambda e, f: (e, 0, f))),
+            ((n_loc, hidden, LANES), F32, pl.BlockSpec((1, tile, LANES), lambda e, f: (e, f, 0))),
+            ((n_loc, LANES, width), F32, pl.BlockSpec((1, LANES, width), lambda e, f: (e, 0, 0))),
+        ],
+        [
+            pltpu.VMEM((total, columns), BF16),
+            pltpu.VMEM((4 * LANES, total), BF16),
+            pltpu.VMEM((total, tile), BF16),
+        ],
+        4 * n_loc * total * LANES * hidden,
     )
 
 
 def route_back_call(
-    place, index, count, cotangent, x2, uo, ur, disp, comb, atts, ret, banks, pack, shards, replicas
+    index, count, cotangent, x2, uo, ur, disp, comb, atts, ret, banks, shards, replicas
 ):
     n_img, n_tok, width = cotangent.shape
-    chunks, layout, columns = pack
     total, n_exp = x2.shape[1], disp.shape[1]
     rows = width // shards
     unit = 16 * replicas
@@ -822,7 +902,7 @@
     each = several(n_img, IMAGES_ROUTE)
     here = functools.partial(per_image, images=each)
     return call(
-        functools.partial(route_back_kernel, n_exp, layout), (place, index, count), (n_img // each,),
+        functools.partial(route_back_kernel, n_exp), (index, count), (n_img // each,),
         [
             (cotangent, here(n_tok, width)),
             (x2, here(total, width)),
@@ -832,18 +912,17 @@
             (comb, here(n_exp, total)),
         ]
         + [(att, here(total, GROUP)) for att in atts]
-        + [(ret, here(n_exp, 2 * width))]
-        + [(bank, whole(bank.shape)) for bank in banks]
-        + [(chunk, once(chunk.shape)) for chunk in chunks],
+        + [(ret, once(ret.shape))]
+        + [(bank, once(bank.shape)) for bank in banks],
         [
             ((n_img, n_tok, width), BF16, here(n_tok, width)),
-            ((n_img, total, width), F32, here(total, width)),
+            ((n_img, total, width), BF16, here(total, width)),
             ((n_img, total, width), BF16, here(total, width)),
             ((shards, pack_rows, LANES), BF16, whole((shards, pack_rows, LANES))),
         ],
         [
-            pltpu.VMEM((width, columns), BF16),
             pltpu.VMEM((each * total, width), F32),
+            pltpu.VMEM((2 * width // LANES * n_exp * n_img, LANES), F32),
             pltpu.VMEM((LANES, width), F32),
             pltpu.VMEM((LANES, width), F32),
             pltpu.VMEM((LANES, width), F32),
@@ -853,15 +932,16 @@
     )
 
 
-def attention_back_call(index, qkvs, probs, gatt, uq, h1, bt, others):
+def attention_back_call(place, index, qkvs, probs, gatt, uq, h1, bt, others):
     n_img, total, width = h1.shape
     groups = len(qkvs)
     shards = others.shape[0]
     each = several(n_img, IMAGES_BACK)
     here = functools.partial(per_image, images=each)
     pack = (shards, 4 * width // shards + others.shape[1], LANES)
+    half = (shards, pack[1] // 2, LANES)
     return call(
-        functools.partial(attention_back_kernel, groups), (index,), (n_img // each,),
+        functools.partial(attention_back_kernel, groups), (place, index), (n_img // each,),
         [(qkv, here(total, 3 * GROUP)) for qkv in qkvs]
         + [(prob, here(GROUP // HEAD_DIM, total, total)) for prob in probs]
         + [
@@ -872,52 +952,58 @@
             (others, whole(others.shape)),
         ],
         [((n_img, total, 3 * GROUP), BF16, here(total, 3 * GROUP))] * groups
-        + [((n_img, total, LANES), BF16, here(total, LANES)), (pack, BF16, whole(pack))],
-        [pltpu.VMEM((LANES, 3 * width), F32), pltpu.VMEM((LANES, width), F32)],
+        + [((n_img, total, LANES), BF16, here(total, LANES))]
+        + [(half, BF16, whole(half))] * 2,
+        [
+            pltpu.VMEM(pack, BF16),
+            pltpu.VMEM((LANES, 3 * width), F32),
+            pltpu.VMEM((LANES, width), F32),
+        ],
         groups * attention_flops(n_img, total, LANES, 5), groups * n_img * total * total * 4,
     )
 
 
-def input_grad_call(place, images, gx2, guq, bank_a, gqkvs, packs):
+def input_grad_call(images, gx2, guq, gqkvs, turned):
     n_img, n_tok, width = images.shape
     total = gx2.shape[1]
-    groups = len(gqkvs)
     each = several(n_img, IMAGES_LAST)
     here = functools.partial(per_image, images=each)
     out = call(
-        functools.partial(input_grad_kernel, tuple(pack[1] for pack in packs)), (place,), (n_img // each,),
+        input_grad_kernel, (), (n_img // each,),
         [
             (images, here(n_tok, width)),
             (gx2, here(total, width)),
             (guq, here(total, LANES)),
-            (bank_a, whole(bank_a.shape)),
+            (turned, once(turned.shape)),
         ]
-        + [(gqkv, here(total, 3 * GROUP)) for gqkv in gqkvs]
-        + [(chunk, once(chunk.shape)) for pack in packs for chunk in pack[0]],
+        + [(gqkv, here(total, 3 * GROUP)) for gqkv in gqkvs],
         [((images.size // LANES, LANES), F32, whole((images.size // LANES, LANES)))],
-        [pltpu.VMEM((width, pack[2]), BF16) for pack in packs]
-        + [pltpu.VMEM((each * total, width), F32)],
+        [pltpu.VMEM((each * total, width), F32)],
         n_img * total * 2 * width * (3 * width + LANES),
     )[0]
     out = out.reshape(n_tok, width // LANES, n_img, LANES).transpose(2, 0, 1, 3)
     return out.reshape(n_img, n_tok, width)
 
 
+def turn_call(place, bank_ao, bank_ra, packs):
+    width = bank_ao.shape[0]
+    shapes = [(3 * width + LANES, width), (width + LANES, width), (LANES, width)]
+    return call(
+        functools.partial(turn_kernel, tuple(pack[1] for pack in packs)), (place,), (1,),
+        [(bank, once(bank.shape)) for bank in (bank_ao, bank_ra)]
+        + [(chunk, once(chunk.shape)) for pack in packs for chunk in pack[0]],
+        [(shape, BF16, once(shape)) for shape in shapes],
+        [pltpu.VMEM((width, pack[2]), BF16) for pack in packs],
+        8 * width * width,
+    )
+
+
 def swap(array, axis, size, bit):
     return lax.ppermute(array, axis, [(i, i ^ bit) for i in range(size)])
 
 
 def tie(*arrays):
     return lax.optimization_barrier(arrays)
-
-
-def own_columns(pack, quarter, pieces):
-    part = pack.shape[1] // pieces
-    return lax.dynamic_slice(pack, (0, quarter % pieces * part), (pack.shape[0], part))
-
-
-def spread(rows, shards):
-    return jnp.broadcast_to(rows[None], (shards,) + rows.shape)
 
 
 def over_shard(spread, lines=None):
@@ -927,23 +1013,27 @@
     return own.reshape(-1, spread.shape[2])
 
 
-def reduce_pack(pack, replicas, beside_swap, beside_spread):
+def reduce_pack(keep, give, replicas, beside_first, beside_swap, beside_spread):
     where = lax.axis_index("replica")
     bits = []
     bit = 1
+    first_work = swap_work = ()
     while bit < replicas:
-        half = pack.shape[1] // 2
-        side = (where // bit) % 2
-        keep = lax.dynamic_slice_in_dim(pack, side * half, half, axis=1)
-        give = lax.dynamic_slice_in_dim(pack, (1 - side) * half, half, axis=1)
         got = swap(give, "replica", replicas, bit)
+        if bit == 1:
+            got, *first_work = tie(got, *beside_first())
         if 2 * bit == replicas:
             got, *swap_work = tie(got, *beside_swap())
         pack = (keep.astype(F32) + got.astype(F32)).astype(BF16)
         bits.append(bit)
         bit *= 2
+        if bit < replicas:
+            half = pack.shape[1] // 2
+            side = (where // bit) % 2
+            keep = lax.dynamic_slice_in_dim(pack, side * half, half, axis=1)
+            give = lax.dynamic_slice_in_dim(pack, (1 - side) * half, half, axis=1)
     landed = lax.all_to_all(pack, "shard", split_axis=0, concat_axis=0, tiled=True)
-    landed, *spread_work = tie(landed, *beside_spread())
+    landed, *spread_work = tie(landed, *beside_spread(*first_work))
     total = jnp.sum(landed.astype(F32), axis=0).astype(BF16)
     for bit in reversed(bits):
         got = swap(total, "replica", replicas, bit)
@@ -953,7 +1043,7 @@
             jnp.concatenate([total, got], axis=0),
             jnp.concatenate([got, total], axis=0),
         )
-    return total, swap_work, spread_work
+    return total, first_work, swap_work, spread_work
 
 
 def per_device(
@@ -986,31 +1076,11 @@
     n_exp = n_loc * shards
     groups = width // GROUP
     quarter = lax.axis_index("replica") % 4
-    place = jnp.stack([quarter, lax.axis_index("shard") % 2]).astype(jnp.int32)
+    place = jnp.stack(
+        [quarter, lax.axis_index("shard") % 2, lax.axis_index("replica")]
+    ).astype(jnp.int32)
     by_axis = shards == 2 * STRIPS and replicas == 4
 
-    def qkv_columns(group):
-        return [
-            query_key_value_weight[:, part * width + group * GROUP : part * width + (group + 1) * GROUP]
-            for part in range(3)
-        ]
-
-    route_block = jnp.concatenate(
-        [
-            frozen_dispatch_weight,
-            jnp.zeros((rows, 64 - n_exp), BF16),
-            jnp.pad(dispatch_adapter_second.T.reshape(16, n_loc * 8), ((0, rows - 16), (0, 0))),
-            jnp.zeros((rows, 64 - n_loc * 8), BF16),
-        ],
-        axis=1,
-    )
-    empty = jnp.zeros((rows, LANES), BF16)
-    empty = jnp.zeros((rows, 2 * LANES), BF16)
-    packs = [
-        (qkv_columns(1) + [output_adapter_second.T, route_block], 4),
-        (qkv_columns(2), 2),
-        ([frozen_output_weight, empty], 4),
-    ]
     spread0 = pack_call(
         place,
         (
@@ -1019,7 +1089,14 @@
         ),
         STRIPS if by_axis else shards,
     )
-    mine = [own_columns(jnp.concatenate(pack, axis=1), quarter, pieces) for pack, pieces in packs]
+    spread1, spread23 = later_pack_call(
+        place,
+        (
+            query_key_value_weight, output_adapter_second.T, frozen_dispatch_weight.T,
+            frozen_output_weight, dispatch_adapter_second.T,
+        ),
+        shards,
+    )
     near = functools.partial(swap, axis="replica", size=replicas, bit=1)
     far = functools.partial(swap, axis="replica", size=replicas, bit=2)
     beside = functools.partial(swap, axis="shard", size=shards, bit=1)
@@ -1027,23 +1104,23 @@
     h1 = norm_call(images, cotangent, total)
     if by_axis:
         lines = [[2 * strip + side for strip in range(STRIPS)] for side in range(2)]
-        own0 = over_shard(spread0, lines)
-        beside0, far0, h1, mine1 = tie(beside(own0), far(own0), h1, mine[0])
+        own0, spread1, spread23 = tie(over_shard(spread0, lines), spread1, spread23)
+        beside0, far0, h1, spread1 = tie(beside(own0), far(own0), h1, spread1)
         held = [(own0, 0, 0), (beside0, 0, 1), (far0, 2, 0)]
-        own1 = over_shard(spread(mine1, shards))
+        own1 = over_shard(spread1)
         held.append((far(held[1][0]), 2, 1))
     else:
         own0 = over_shard(spread0)
-        own0, h1, mine1 = tie(own0, h1, mine[0])
+        own0, h1, spread1 = tie(own0, h1, spread1)
         held = [(own0, 0, None), (far(own0), 2, None)]
-        own1 = over_shard(spread(mine1, shards))
+        own1 = over_shard(spread1)
     chunks0 = [chunk for chunk, _, _ in held] + [near(chunk) for chunk, _, _ in held]
     layout0 = [(replica, side, 0) for _, replica, side in held]
     layout0 += [(replica ^ 1, side, 0) for _, replica, side in held]
-    *chunks0, own1, mine2, mine3 = tie(*chunks0, own1, *mine[1:])
+    *chunks0, own1, spread23 = tie(*chunks0, own1, spread23)
     pack0 = (tuple(chunks0), (4, tuple(layout0)), 3 * GROUP + 6 * LANES)
     far1 = far(own1)
-    own23 = over_shard(spread(jnp.concatenate([mine2, mine3], axis=1), shards))
+    own23 = over_shard(spread23)
     qkv0, att0, prob0, uq, bank_a, bank_bt, bank_ao, bank_ra = first_attention_call(
         place, image_adapter_index, h1, pack0, n_tok, shards
     )
@@ -1054,7 +1131,7 @@
         place, h1, uq, bank_bt, pack1, n_tok, 1, 2
     )
     att1, uq, own23 = tie(att1, uq, own23)
-    own2, own3 = own23[:, : mine2.shape[1]], own23[:, mine2.shape[1] :]
+    own2, own3 = own23[:, : width // 2], own23[:, width // 2 :]
     far3 = far(own3)
     pack2 = ((own2, near(own2)), (2, ((0, None, 0), (1, None, 0))), 3 * GROUP)
     qkv2, att2, prob2 = next_attention_call(place, h1, uq, bank_bt, pack2, n_tok, 2, 0)
@@ -1062,48 +1139,49 @@
     pack3 = ((own3, near(own3), far3, near(far3)), four, width + 2 * LANES)
     packs = (pack0, pack1, pack2, pack3)
     atts = (att0, att1, att2)
-    bank_rb = bank_wr.reshape(shards, rows, LANES)[:, :16, 64 : 64 + n_loc * 8].reshape(n_exp, LANES)
-    x2, uo, ur, disp, comb, sg, bank_wrt = route_call(
+    x2, uo, ur, disp, comb, sg, bank_wrt, bank_rb = route_call(
         place, image_adapter_index, device_image_count, images, cotangent, atts,
-        (bank_ao, bank_bo, bank_ra, bank_wr, bank_rb), packs[3], n_exp, total,
-    )
-
-    sent = sg.reshape(n_img, shards, n_loc, -1).transpose(1, 2, 0, 3)
-    landed = lax.all_to_all(sent, "shard", split_axis=0, concat_axis=0, tiled=True)
+        (bank_ao, bank_bo, bank_ra, bank_wr), packs[3], n_exp, total, shards,
+    )
+
+    landed = lax.all_to_all(sg, "shard", split_axis=0, concat_axis=0, tiled=True)
+    landed, *turned = tie(landed, *turn_call(place, bank_ao, bank_ra, packs))
+    turned_qkv, turned_out, turned_route = turned
     weights = (
         frozen_up_weight, frozen_down_weight, up_adapter_first, up_adapter_second,
         down_adapter_first, down_adapter_second,
     )
-    ret = expert_call(landed, weights)
-    every = [landed]
-    for bit in range(2, replicas, 2):
-        every.append(swap(landed, "replica", replicas, bit))
-    ret, *every = tie(ret, *every)
+    far_landed = [swap(landed, "replica", replicas, bit) for bit in range(2, replicas, 2)]
+    ret, *kept = expert_call(landed, weights)
+    ret, *far_landed = tie(ret, *far_landed)
     back = lax.all_to_all(ret, "shard", split_axis=0, concat_axis=0, tiled=True)
-    every = every + [swap(part, "replica", replicas, 1) for part in every]
-    grads = expert_grad_call(every, weights, 0, ())
-    back, *grads = tie(back, *grads)
-    back = back.transpose(2, 0, 1, 3).reshape(n_img, n_exp, 2 * width)
+    every = [(landed, *kept)]
+    for number, bit in enumerate(range(2, replicas, 2)):
+        far_kept = [swap(array, "replica", replicas, bit) for array in kept]
+        every.append((far_landed[number], *far_kept))
 
     block_out, gx2, gatt, out_pack = route_back_call(
-        place, image_adapter_index, device_image_count, cotangent, x2, uo, ur, disp, comb, atts, back,
-        (bank_ao, bank_bo, bank_ra, bank_wrt, bank_rb), packs[3], shards, replicas,
-    )
-    *gqkvs, guq, pack = attention_back_call(
-        image_adapter_index, (qkv0, qkv1, qkv2), (prob0, prob1, prob2), gatt, uq, h1, bank_bt, out_pack
-    )
-
-    def rest_of_experts():
-        done = tuple(grads)
-        for expert in range(1, n_loc):
-            done = expert_grad_call(every, weights, expert, tuple(done))
-        return done
-
-    summed, (input_grad,), grads = reduce_pack(
-        pack, replicas,
-        lambda: (input_grad_call(place, images, gx2, guq, bank_a, gqkvs, packs[:3]),),
-        rest_of_experts,
-    )
+        image_adapter_index, device_image_count, cotangent, x2, uo, ur, disp, comb, atts, back,
+        (bank_bo, bank_wrt, bank_rb, turned_out, turned_route), shards, replicas,
+    )
+    gatt, *lows = tie(gatt, *[row[3] for row in every])
+    held = [array for row, low in zip(every, lows) for array in (*row[:3], low)]
+    *gqkvs, guq, keep, give = attention_back_call(
+        place, image_adapter_index, (qkv0, qkv1, qkv2), (prob0, prob1, prob2), gatt, uq, h1, bank_bt, out_pack
+    )
+
+    def expert_grads(block, *arrays):
+        arrays = list(arrays) + [swap(array, "replica", replicas, 1) for array in arrays]
+        rows_of = [tuple(arrays[place : place + 4]) for place in range(0, len(arrays), 4)]
+        return expert_grad_call(rows_of, width)
+
+    summed, (block_out, *_), (input_grad,), grads = reduce_pack(
+        keep, give, replicas,
+        lambda: (block_out.transpose(1, 0, 2), *held),
+        lambda: (input_grad_call(images, gx2, guq, gqkvs, turned_qkv),),
+        expert_grads,
+    )
+    block_out = block_out.transpose(1, 0, 2)
     summed = summed.astype(F32)
     return (
         block_out,

time: 277 us -> 266 us (0.960)
  blocking collectives: 17.3 us -> 0 us
  waiting for transfers between devices: 12.8 us -> 27.7 us
  Pallas kernels: 173 us -> 162 us
  starting transfers between devices: 46.7 us -> 55.8 us
  local copies, waits for them, and re-layouts: 22 us -> 14.7 us
    all_to_all x1 -> x0, blocking collectives: 17.3 us -> none  [per_device(): lax.all_to_all(sent, 'shard', split_axis=0, concat_axis=0, tiled=True)]
    pallas_call x12 -> x13, Pallas kernels: 173 us -> 162 us  [call(): pl.pallas_call(kernel, out_shape=shapes, grid_spec=pltpu.PrefetchScalarGr...]
    ppermute x21 -> x30, starting transfers between devices: 20.7 us -> 27.8 us  [swap(): return lax.ppermute(array, axis, [(i, i ^ bit) for i in range(size)])]
    all_to_all x1, waiting for transfers between devices: 0.01 us -> 6.8 us  [per_device(): back = lax.all_to_all(ret, 'shard', split_axis=0, concat_axis=0, tiled=True)]
    all_to_all x0 -> x1, starting transfers between devices: none -> 5.72 us  [per_device(): lax.all_to_all(sg, 'shard', split_axis=0, concat_axis=0, tiled=True)]
    all_to_all x0 -> x1, waiting for transfers between devices: none -> 4.19 us  [per_device(): lax.all_to_all(sg, 'shard', split_axis=0, concat_axis=0, tiled=True)]
    all_to_all x3, waiting for transfers between devices: 0.89 us -> 5.08 us  [over_shard(): lax.all_to_all(spread, 'shard', split_axis=0, concat_axis=0, tiled=True,...]
    unnamed x58 -> x61, local copies, waits for them, and re-layouts: 12.3 us -> 12.7 us
  transfers between devices with their start and end apart: 26 -> 36, of which waited for: 11 -> 13; matrix products, arithmetic and copies ran while one was open for 4% -> 3% of each run, Pallas kernels for 35% -> 54%
where the time goes in v4:
time: 266 us; the launch traced here: 265 us
  Pallas kernels  162 us (61%)
  starting transfers between devices  55.8 us (21%)
  waiting for transfers between devices  27.7 us (10%)
  local copies, waits for them, and re-layouts  14.7 us (6%)
  other arithmetic  2.82 us (1%)
    pallas_call x13, Pallas kernels, call(): pl.pallas_call(kernel, out_shape=shapes, grid_spec=pltpu.PrefetchScalarGr...  162 us
    ppermute x30, starting transfers between devices, swap(): return lax.ppermute(array, axis, [(i, i ^ bit) for i in range(size)])  27.8 us
    all_to_all x3, starting transfers between devices, over_shard(): lax.all_to_all(spread, 'shard', split_axis=0, concat_axis=0, tiled=True,...  14.5 us
    unnamed x61, local copies, waits for them, and re-layouts  12.7 us
    ppermute x30, waiting for transfers between devices, swap(): return lax.ppermute(array, axis, [(i, i ^ bit) for i in range(size)])  11.7 us
    all_to_all x1, waiting for transfers between devices, per_device(): back = lax.all_to_all(ret, 'shard', split_axis=0, concat_axis=0, tiled=True)  6.8 us
    all_to_all x1, starting transfers between devices, per_device(): lax.all_to_all(sg, 'shard', split_axis=0, concat_axis=0, tiled=True)  5.72 us
  transfers between devices with their start and end apart: 36, of which 13 were waited for; matrix products, arithmetic and copies ran while one was open for 3% of the time, Pallas kernels for 54%

profile of v4, /device:TPU:1, one launch (start us, length us, event | category | flops | bytes accessed | tf_op | source)
XLA Modules:
  0.0 264.6 jit_solution(7190590367849873816)
XLA Ops:
  1.3 2.5 shard_map.274
  3.7 5.4 %all-to-all-start = ((bf16[4,96,384]{2,1,0:T(8,128)(2,1)}), bf16[4,96,384]{2,1,0:T(8,128)(2,1)S(1)}, u32[]{:S(2)}, u32[]{:S(2)}) async-start(bf16[4,96,384]{2,1,0:T(8,128)(2,1)} %shard_map.274), calls=%async_computation | async-start | bytes 589824 | tf_op jit(solution)/shard_map/all_to_all | solution.py:1010
  9.2 3.0 %shard_map.275 = (bf16[8,96,256]{2,1,0:T(8,128)(2,1)}, bf16[8,96,640]{2,1,0:T(8,128)(2,1)}) custom-call(s32[3]{0:T(128)} %pad_add_fusion.place_ref, bf16[96,2304]{1,0:T(8,128)(2,1)} %qkv_ref.3, bf16[96,128]{1,0:T(8,128)(2,1)} %bitcast.35, bf16[16,96]{1,0:T(8,128)(2,1)} %bitcast.36, bf16[96,768]{1,0:T(8,128)(2,1)} %wo_ref.1, bf16[2,128]{1,0:T(2,128)(2,1)} %bitcast.37), custom_call_target="tpu_custom_call" | custom-call | flops 73728 | bytes 1994240 | tf_op jit(solution)/shard_map/pallas_call | solution.py:671
  12.1 5.1 %all-to-all-done = bf16[4,96,384]{2,1,0:T(8,128)(2,1)S(1)} async-done(((bf16[4,96,384]{2,1,0:T(8,128)(2,1)}), bf16[4,96,384]{2,1,0:T(8,128)(2,1)S(1)}, u32[]{:S(2)}, u32[]{:S(2)}) %all-to-all-start) | async-done | bytes 294944 | tf_op jit(solution)/shard_map/all_to_all | solution.py:1010
  17.2 1.2 collective-permute-start
  18.4 1.2 collective-permute-start.1
  19.7 3.6 %copy.31.image_ref = bf16[8,197,768]{2,1,0:T(8,128)(2,1)} copy(bf16[8,197,768]{2,0,1:T(8,128)(2,1)} %param.19) | data formatting | bytes 4841472 | tf_op args[0]
  23.2 1.9 copy.32._.cot_ref
  25.1 3.7 %shard_map.276.h1_ref.refs_8_ = bf16[8,208,768]{2,1,0:T(8,128)(2,1)} custom-call(bf16[8,197,768]{2,1,0:T(8,128)(2,1)} %copy.31.image_ref, bf16[8,197,768]{2,1,0:T(8,128)(2,1)} %copy.32._.cot_ref), custom_call_target="tpu_custom_call" | custom-call | flops 9682944 | bytes 7397376 | tf_op jit(solution)/shard_map/pallas_call | solution.py:671
  28.8 3.5 %all-to-all-start.1 = ((bf16[8,96,256]{2,1,0:T(8,128)(2,1)}), bf16[8,96,256]{2,1,0:T(8,128)(2,1)S(1)}, u32[]{:S(2)}, u32[]{:S(2)}) async-start(bf16[8,96,256]{2,1,0:T(8,128)(2,1)} %get-tuple-element.117), calls=%async_computation.1 | async-start | bytes 786432 | tf_op jit(solution)/shard_map/all_to_all | solution.py:1010
  32.6 3.4 %collective-permute-start.3 = (bf16[384,384]{1,0:T(8,128)(2,1)S(1)}, bf16[384,384]{1,0:T(8,128)(2,1)S(1)}, u32[]{:S(2)}, u32[]{:S(2)}) collective-permute-start(bf16[384,384]{1,0:T(8,128)(2,1)S(1)} %bitcast.31), channel_id=1, source_target_pairs={{0,8},{8,0},{16,24},{24,16},{1,9},{9,1},{17,25},{25,17},{2,10},{10... | collective-permute-start | bytes 884744 | tf_op jit(solution)/shard_map/ppermute | solution.py:1002
  36.5 1.5 collective-permute-done.2.rest_3_.refs_3_
  38.0 4.2 %collective-permute-start.6 = (bf16[384,384]{1,0:T(8,128)(2,1)S(1)}, bf16[384,384]{1,0:T(8,128)(2,1)S(1)}, u32[]{:S(2)}, u32[]{:S(2)}) collective-permute-start(bf16[384,384]{1,0:T(8,128)(2,1)S(1)} %collective-permute-done.2.rest_3_.refs_3_), channel_id=1, source_target_pairs={{0,8},{8,0},{16,24},{24,16},{1,9},{9,1},{17,25},{25,17},{2,10},{10... | collective-permute-start | bytes 884744 | tf_op jit(solution)/shard_map/ppermute | solution.py:1002
  42.2 1.2 collective-permute-done.6.rest_7_.refs_7_
  44.1 5.6 %all-to-all-start.2 = ((bf16[8,96,640]{2,1,0:T(8,128)(2,1)}), bf16[8,96,640]{2,1,0:T(8,128)(2,1)S(1)}, u32[]{:S(2)}, u32[]{:S(2)}) async-start(bf16[8,96,640]{2,1,0:T(8,128)(2,1)} %get-tuple-element.136), calls=%async_computation.2 | async-start | bytes 1966080 | tf_op jit(solution)/shard_map/all_to_all | solution.py:1010
  49.9 14.8 %shard_map.277 = (bf16[8,208,768]{2,1,0:T(8,128)(2,1)}, bf16[8,208,256]{2,1,0:T(8,128)(2,1)}, bf16[8,4,208,208]{3,2,1,0:T(8,128)(2,1)}, bf16[8,208,128]{2,1,0:T(...) custom-call(s32[3]{0:T(128)} %pad_add_fusion.place_ref, ...), custom_call_target="tpu_custom_call" | custom-call | flops 2317352960 | bytes 12697600 | tf_op jit(solution)/shard_map/pallas_call | solution.py:671
  64.8 1.0 collective-permute-start.8
  65.9 1.3 collective-permute-done.8.rest_1_.refs_9_
  68.4 10.6 %shard_map.278 = (bf16[8,208,768]{2,1,0:T(8,128)(2,1)}, bf16[8,208,256]{2,1,0:T(8,128)(2,1)}, bf16[8,4,208,208]{3,2,1,0:T(8,128)(2,1)}, bf16[768,128]{1,0:T(8,128)(2,1)}, bf16[768,128]{1,0:T(8,128)(2,1)}) custom-call(s32[3]{0:T(128)} %pad_add_fusion.place_ref, bf16[8,208,768]{2,1,0:T(8,128)(2,1)} %shard_map.276.h1_ref.refs_8_, ...), custom_call_target="tpu_custom_call" | custom-call | flops 2317352960 | bytes 11714560 | tf_op jit(solution)/shard_map/pallas_call | solution.py:671
  79.6 1.3 collective-permute-start.11
  81.2 0.8 copy-done.8
  82.0 10.2 %shard_map.279 = (bf16[8,208,768]{2,1,0:T(8,128)(2,1)}, bf16[8,208,256]{2,1,0:T(8,128)(2,1)}, bf16[8,4,208,208]{3,2,1,0:T(8,128)(2,1)}) custom-call(s32[3]{0:T(128)} %pad_add_fusion.place_ref, bf16[8,208,768]{2,1,0:T(8,128)(2,1)} %shard_map.276.h1_ref.refs_8_, bf16[8,208,128]{2,1,0:T(8,128)(2,1)} %get-tuple-element.137.uq_ref.refs_7_, ...), custom_call_target="tpu_custom_call" | custom-call | flops 2317352960 | bytes 10928128 | tf_op jit(solution)/shard_map/pallas_call | solution.py:671
  95.4 16.3 %shard_map.280 = (f32[8,208,768]{2,1,0:T(8,128)}, bf16[8,208,128]{2,1,0:T(8,128)(2,1)}, bf16[8,208,128]{2,1,0:T(8,128)(2,1)}, f32[8,16,208]{2,1,0:T(8,128)}, f32...) custom-call(s32[3]{0:T(128)} %pad_add_fusion.place_ref, ...), custom_call_target="tpu_custom_call" | custom-call | flops 2944401408 | bytes 16388096 | tf_op jit(solution)/shard_map/pallas_call | solution.py:671
  111.8 5.7 %all-to-all-start.3 = ((bf16[8,2,8,1664]{3,2,1,0:T(8,128)(2,1)}), bf16[8,2,8,1664]{3,2,1,0:T(8,128)(2,1)S(1)}, u32[]{:S(2)}, u32[]{:S(2)}) async-start(bf16[8,2,8,1664]{3,2,1,0:T(8,128)(2,1)} %get-tuple-element.158), calls=%async_computation.3 | async-start | bytes 851968 | tf_op jit(solution)/shard_map/all_to_all | solution.py:1147
  117.5 7.6 %shard_map.281 = (bf16[2432,768]{1,0:T(8,128)(2,1)}, bf16[896,768]{1,0:T(8,128)(2,1)}, bf16[128,768]{1,0:T(8,128)(2,1)}) custom-call(s32[3]{0:T(128)} %pad_add_fusion.place_ref, bf16[768,128]{1,0:T(8,128)(2,1)} %get-tuple-element.147.ao_ref, bf16[768,128]{1,0:T(8,128)(2,1)} %get-tuple-element.149.ra_ref, bf16[384,384]{1,0:T(8,128)(2,1)} %bitcast.33, ...), custom_call_target="tpu_custom_call" | custom-call | flops 4718592 | bytes 12386304 | tf_op jit(solution)/shard_map/pallas_call | solution.py:671
  125.1 4.2 %all-to-all-done.3.part_ref.refs_0_ = bf16[8,2,8,1664]{3,2,1,0:T(8,128)(2,1)S(1)} async-done(((bf16[8,2,8,1664]{3,2,1,0:T(8,128)(2,1)}), bf16[8,2,8,1664]{3,2,1,0:T(8,128)(2,1)S(1)}, u32[]{:S(2)}, u32[]{:S(2)}) %all-to-all-start.3) | async-done | bytes 426016 | tf_op jit(solution)/shard_map/all_to_all | solution.py:1147
  129.3 1.3 collective-permute-start.14
  130.6 14.9 %shard_map.282 = (bf16[8,2,8,1536]{3,2,1,0:T(8,128)(2,1)}, bf16[2,64,3072]{2,1,0:T(8,128)(2,1)}, bf16[2,64,3072]{2,1,0:T(8,128)(2,1)}, bf16[2,64,512]{2,1,0:T(8,128)(2,1)}) custom-call(bf16[2,768,3072]{2,1,0:T(8,128)(2,1)} %wu_ref.1, bf16[2,3072,768]{2,1,0:T(8,128)(2,1)} %wd_ref.1, bf16[2,768,128]{2,1,0:T(8,128)(2,1)} %ua_ref.1, ...), custom_call_target="tpu_custom_call" | custom-call | flops 2415919104 | bytes 25329664 | tf_op jit(solution)/shard_map/pallas_call | solution.py:671
  145.5 0.7 copy-done.9
  146.2 4.4 %all-to-all-start.4 = ((bf16[8,2,8,1536]{3,2,1,0:T(8,128)(2,1)}), bf16[8,2,8,1536]{3,2,1,0:T(8,128)(2,1)S(1)}, u32[]{:S(2)}, u32[]{:S(2)}) async-start(bf16[8,2,8,1536]{3,2,1,0:T(8,128)(2,1)} %get-tuple-element.164), calls=%async_computation.4 | async-start | bytes 786432 | tf_op jit(solution)/shard_map/all_to_all | solution.py:1157
  150.6 0.7 collective-permute-start.15
  152.1 0.7 collective-permute-start.18
  152.8 6.8 %all-to-all-done.4.ret_ref = bf16[8,2,8,1536]{3,2,1,0:T(8,128)(2,1)S(1)} async-done(((bf16[8,2,8,1536]{3,2,1,0:T(8,128)(2,1)}), bf16[8,2,8,1536]{3,2,1,0:T(8,128)(2,1)S(1)}, u32[]{:S(2)}, u32[]{:S(2)}) %all-to-all-start.4) | async-done | bytes 393248 | tf_op jit(solution)/shard_map/all_to_all | solution.py:1157
  159.6 0.7 copy-done.17
  160.3 22.7 %shard_map.283 = (bf16[8,197,768]{2,1,0:T(8,128)(2,1)}, bf16[8,208,768]{2,1,0:T(8,128)(2,1)}, bf16[8,208,768]{2,1,0:T(8,128)(2,1)}, bf16[8,320,128]{2,1,0:T(8,128)(2,1)}) custom-call(s32[8]{0:T(128)} %index_ref.7, s32[1]{0:T(128)S(6)} %copy.38.count_ref, bf16[8,197,768]{2,1,0:T(8,128)(2,1)} %copy.32._.cot_ref, f32[8,208,768]{2,1,0:T(8,128)} %get-tuple-element.153.x2_ref, ...), custom_call_target="tpu_custom_call" | custom-call | flops 3925868544 | bytes 21532672 | tf_op jit(solution)/shard_map/pallas_call | solution.py:671
  183.0 31.6 %shard_map.284 = (bf16[8,208,768]{2,1,0:T(8,128)(2,1)}, bf16[8,208,768]{2,1,0:T(8,128)(2,1)}, bf16[8,208,768]{2,1,0:T(8,128)(2,1)}, bf16[8,208,128]{2,1,0:T(8,12...) custom-call(s32[3]{0:T(128)} %pad_add_fusion.place_ref, s32[8]{0:T(128)} %index_ref.7, ...), custom_call_target="tpu_custom_call" | custom-call | flops 3639607296 | bytes 32292864 | tf_op jit(solution)/shard_map/pallas_call | solution.py:671
  214.6 3.8 %collective-permute-start.16 = (bf16[8,352,128]{2,1,0:T(8,128)(2,1)}, bf16[8,352,128]{2,1,0:T(8,128)(2,1)S(1)}, u32[]{:S(2)}, u32[]{:S(2)}) collective-permute-start(bf16[8,352,128]{2,1,0:T(8,128)(2,1)} %get-tuple-element.173), channel_id=1, source_target_pairs={{0,8},{8,0},{16,24},{24,16},{1,9},{9,1},{17,25},{25,17},{2,10},{10... | collective-permute-start | bytes 2162696 | tf_op jit(solution)/shard_map/ppermute | solution.py:1002
  218.4 2.0 collective-permute-done.16
  220.4 1.3 add_convert_fusion
  223.7 15.6 %shard_map.285 = f32[9456,128]{1,0:T(8,128)} custom-call(bf16[8,197,768]{2,1,0:T(8,128)(2,1)} %copy.31.image_ref, bf16[8,208,768]{2,1,0:T(8,128)(2,1)} %get-tuple-element.183.gx2_ref, bf16[8,208,128]{2,1,0:T(8,128)(2,1)} %get-tuple-element.184.guq_ref, bf16[2432,768]{1,0:T(8,128)(2,1)} %get-tuple-element.185.turned_ref, ...), custom_call_target="tpu_custom_call" | custom-call | flops 6215958528 | bytes 21647360 | tf_op jit(solution)/shard_map/pallas_call | solution.py:671
  240.3 0.8 add_convert_fusion.1
  241.2 3.4 %all-to-all-start.5 = ((bf16[8,176,128]{2,1,0:T(8,128)(2,1)}), bf16[8,176,128]{2,1,0:T(8,128)(2,1)S(1)}, u32[]{:S(2)}, u32[]{:S(2)}) async-start(bf16[8,176,128]{2,1,0:T(8,128)(2,1)} %add_convert_fusion.1), calls=%async_computation.5 | async-start | bytes 720896 | tf_op jit(solution)/shard_map/all_to_all | solution.py:1035
  245.1 1.6 collective-permute-done.21.refs_3_
  247.5 8.4 %shard_map.286 = (f32[2,768,128]{2,1,0:T(8,128)}, f32[2,128,3072]{2,1,0:T(8,128)}, f32[2,3072,128]{2,1,0:T(8,128)}, f32[2,128,768]{2,1,0:T(8,128)}) custom-call(bf16[8,2,8,1664]{3,2,1,0:T(8,128)(2,1)} %copy-done, bf16[8,2,8,1664]{3,2,1,0:T(8,128)(2,1)} %copy-done.9, bf16[8,2,8,1664]{3,2,1,0:T(8,128)(2,1)} %collective-permute-done.20.refs_2_, ...), custom_call_target="tpu_custom_call" | custom-call | flops 805306368 | bytes 16384000 | tf_op jit(solution)/shard_map/pallas_call | solution.py:671
  255.9 0.8 collective-permute-start.28
  256.8 2.1 collective-permute-done.28
  258.9 1.8 collective-permute-start.29
  260.7 1.9 copy.37
  (110 shorter events, 14.0 us)
Async XLA Ops:
  3.7 13.5 %all-to-all-start = ((bf16[4,96,384]{2,1,0:T(8,128)(2,1)}), bf16[4,96,384]{2,1,0:T(8,128)(2,1)S(1)}, u32[]{:S(2)}, u32[]{:S(2)}) async-start(bf16[4,96,384]{2,1,0:T(8,128)(2,1)} %shard_map.274), calls=%async_computation | async-start | bytes 589824 | tf_op jit(solution)/shard_map/all_to_all | solution.py:1010
  12.1 11.1 %copy-start.3 = (bf16[8,197,768]{2,0,1:T(8,128)(2,1)S(1)}, bf16[8,197,768]{2,0,1:T(8,128)(2,1)}, u32[]{:S(2)}) copy-start(bf16[8,197,768]{2,0,1:T(8,128)(2,1)} %param.22) | copy-start | bytes 7262212
  17.2 15.4 %copy-start.7 = (bf16[4,96,384]{2,1,0:T(8,128)(2,1)}, bf16[4,96,384]{2,1,0:T(8,128)(2,1)S(1)}, u32[]{:S(2)}) copy-start(bf16[4,96,384]{2,1,0:T(8,128)(2,1)S(1)} %all-to-all-done) | copy-start | bytes 884740
  17.2 11.6 %collective-permute-start = (bf16[384,384]{1,0:T(8,128)(2,1)S(1)}, bf16[384,384]{1,0:T(8,128)(2,1)S(1)}, u32[]{:S(2)}, u32[]{:S(2)}) collective-permute-start(bf16[384,384]{1,0:T(8,128)(2,1)S(1)} %bitcast.29), channel_id=1, source_target_pairs={{0,1},{1,0},{2,3},{3,2},{4,5},{5,4},{6,7},{7,6},{8,9},{9,8},{10,11... | collective-permute-start | bytes 884744 | tf_op jit(solution)/shard_map/ppermute | solution.py:1002
  18.4 10.4 %collective-permute-start.1 = (bf16[384,384]{1,0:T(8,128)(2,1)S(1)}, bf16[384,384]{1,0:T(8,128)(2,1)S(1)}, u32[]{:S(2)}, u32[]{:S(2)}) collective-permute-start(bf16[384,384]{1,0:T(8,128)(2,1)S(1)} %bitcast.30), channel_id=1, source_target_pairs={{0,16},{8,24},{16,0},{24,8},{1,17},{9,25},{17,1},{25,9},{2,18},{10... | collective-permute-start | bytes 884744 | tf_op jit(solution)/shard_map/ppermute | solution.py:1002
  28.8 21.1 %copy-start.18 = (bf16[384,384]{1,0:T(8,128)(2,1)}, bf16[384,384]{1,0:T(8,128)(2,1)S(1)}, u32[]{:S(2)}) copy-start(bf16[384,384]{1,0:T(8,128)(2,1)S(1)} %collective-permute-done.rest_1_.refs_1_) | copy-start | bytes 884740
  28.8 21.1 %copy-start.19 = (bf16[384,384]{1,0:T(8,128)(2,1)}, bf16[384,384]{1,0:T(8,128)(2,1)S(1)}, u32[]{:S(2)}) copy-start(bf16[384,384]{1,0:T(8,128)(2,1)S(1)} %collective-permute-done.1.rest_2_.refs_2_) | copy-start | bytes 884740
  28.8 14.6 %all-to-all-start.1 = ((bf16[8,96,256]{2,1,0:T(8,128)(2,1)}), bf16[8,96,256]{2,1,0:T(8,128)(2,1)S(1)}, u32[]{:S(2)}, u32[]{:S(2)}) async-start(bf16[8,96,256]{2,1,0:T(8,128)(2,1)} %get-tuple-element.117), calls=%async_computation.1 | async-start | bytes 786432 | tf_op jit(solution)/shard_map/all_to_all | solution.py:1010
  32.3 5.6 %collective-permute-start.2 = (bf16[384,384]{1,0:T(8,128)(2,1)S(1)}, bf16[384,384]{1,0:T(8,128)(2,1)S(1)}, u32[]{:S(2)}, u32[]{:S(2)}) collective-permute-start(bf16[384,384]{1,0:T(8,128)(2,1)S(1)} %collective-permute-done.rest_1_.refs_1_), channel_id=1, source_target_pairs={{0,16},{8,24},{16,0},{24,8},{1,17},{9,25},{17,1},{25,9},{2,18},{10... | collective-permute-start | bytes 884744 | tf_op jit(solution)/shard_map/ppermute | solution.py:1002
  32.6 9.6 %collective-permute-start.3 = (bf16[384,384]{1,0:T(8,128)(2,1)S(1)}, bf16[384,384]{1,0:T(8,128)(2,1)S(1)}, u32[]{:S(2)}, u32[]{:S(2)}) collective-permute-start(bf16[384,384]{1,0:T(8,128)(2,1)S(1)} %bitcast.31), channel_id=1, source_target_pairs={{0,8},{8,0},{16,24},{24,16},{1,9},{9,1},{17,25},{25,17},{2,10},{10... | collective-permute-start | bytes 884744 | tf_op jit(solution)/shard_map/ppermute | solution.py:1002
  36.0 6.2 %collective-permute-start.4 = (bf16[384,384]{1,0:T(8,128)(2,1)S(1)}, bf16[384,384]{1,0:T(8,128)(2,1)S(1)}, u32[]{:S(2)}, u32[]{:S(2)}) collective-permute-start(bf16[384,384]{1,0:T(8,128)(2,1)S(1)} %collective-permute-done.rest_1_.refs_1_), channel_id=1, source_target_pairs={{0,8},{8,0},{16,24},{24,16},{1,9},{9,1},{17,25},{25,17},{2,10},{10... | collective-permute-start | bytes 884744 | tf_op jit(solution)/shard_map/ppermute | solution.py:1002
  36.0 6.2 %collective-permute-start.5 = (bf16[384,384]{1,0:T(8,128)(2,1)S(1)}, bf16[384,384]{1,0:T(8,128)(2,1)S(1)}, u32[]{:S(2)}, u32[]{:S(2)}) collective-permute-start(bf16[384,384]{1,0:T(8,128)(2,1)S(1)} %collective-permute-done.1.rest_2_.refs_2_), channel_id=1, source_target_pairs={{0,8},{8,0},{16,24},{24,16},{1,9},{9,1},{17,25},{25,17},{2,10},{10... | collective-permute-start | bytes 884744 | tf_op jit(solution)/shard_map/ppermute | solution.py:1002
  37.9 12.0 %copy-start.20 = (bf16[384,384]{1,0:T(8,128)(2,1)}, bf16[384,384]{1,0:T(8,128)(2,1)S(1)}, u32[]{:S(2)}) copy-start(bf16[384,384]{1,0:T(8,128)(2,1)S(1)} %collective-permute-done.2.rest_3_.refs_3_) | copy-start | bytes 884740
  38.0 5.5 %collective-permute-start.6 = (bf16[384,384]{1,0:T(8,128)(2,1)S(1)}, bf16[384,384]{1,0:T(8,128)(2,1)S(1)}, u32[]{:S(2)}, u32[]{:S(2)}) collective-permute-start(bf16[384,384]{1,0:T(8,128)(2,1)S(1)} %collective-permute-done.2.rest_3_.refs_3_), channel_id=1, source_target_pairs={{0,8},{8,0},{16,24},{24,16},{1,9},{9,1},{17,25},{25,17},{2,10},{10... | collective-permute-start | bytes 884744 | tf_op jit(solution)/shard_map/ppermute | solution.py:1002
  42.2 7.7 %copy-start.21 = (bf16[384,384]{1,0:T(8,128)(2,1)}, bf16[384,384]{1,0:T(8,128)(2,1)S(1)}, u32[]{:S(2)}) copy-start(bf16[384,384]{1,0:T(8,128)(2,1)S(1)} %collective-permute-done.3.rest_4_.refs_4_) | copy-start | bytes 884740
  43.4 21.4 %copy-start.5 = (bf16[8,96,256]{2,1,0:T(8,128)(2,1)}, bf16[8,96,256]{2,1,0:T(8,128)(2,1)S(1)}, u32[]{:S(2)}) copy-start(bf16[8,96,256]{2,1,0:T(8,128)(2,1)S(1)} %all-to-all-done.1) | copy-start | bytes 1179652
  44.1 35.0 %all-to-all-start.2 = ((bf16[8,96,640]{2,1,0:T(8,128)(2,1)}), bf16[8,96,640]{2,1,0:T(8,128)(2,1)S(1)}, u32[]{:S(2)}, u32[]{:S(2)}) async-start(bf16[8,96,640]{2,1,0:T(8,128)(2,1)} %get-tuple-element.136), calls=%async_computation.2 | async-start | bytes 1966080 | tf_op jit(solution)/shard_map/all_to_all | solution.py:1010
  49.7 15.1 %collective-permute-start.7 = (bf16[768,256]{1,0:T(8,128)(2,1)S(1)}, bf16[768,256]{1,0:T(8,128)(2,1)S(1)}, u32[]{:S(2)}, u32[]{:S(2)}) collective-permute-start(bf16[768,256]{1,0:T(8,128)(2,1)S(1)} %bitcast.25), channel_id=1, source_target_pairs={{0,16},{8,24},{16,0},{24,8},{1,17},{9,25},{17,1},{25,9},{2,18},{10... | collective-permute-start | bytes 1179656 | tf_op jit(solution)/shard_map/ppermute | solution.py:1002
  64.8 2.3 collective-permute-start.8
  65.8 1.9 collective-permute-start.9
  79.1 2.1 collective-permute-start.10
  79.6 12.7 %copy-start.6 = (bf16[768,256]{1,0:T(8,128)(2,1)}, bf16[768,256]{1,0:T(8,128)(2,1)S(1)}, u32[]{:S(2)}) copy-start(bf16[768,256]{1,0:T(8,128)(2,1)S(1)} %slice.25.rest_0_.refs_14_) | copy-start | bytes 1179652
  79.6 12.7 %collective-permute-start.11 = (bf16[768,256]{1,0:T(8,128)(2,1)S(1)}, bf16[768,256]{1,0:T(8,128)(2,1)S(1)}, u32[]{:S(2)}, u32[]{:S(2)}) collective-permute-start(bf16[768,256]{1,0:T(8,128)(2,1)S(1)} %slice.25.rest_0_.refs_14_), channel_id=1, source_target_pairs={{0,16},{8,24},{16,0},{24,8},{1,17},{9,25},{17,1},{25,9},{2,18},{10... | collective-permute-start | bytes 1179656 | tf_op jit(solution)/shard_map/ppermute | solution.py:1002
  92.3 1.8 collective-permute-start.12
  92.7 1.9 collective-permute-start.13
  111.8 17.5 %all-to-all-start.3 = ((bf16[8,2,8,1664]{3,2,1,0:T(8,128)(2,1)}), bf16[8,2,8,1664]{3,2,1,0:T(8,128)(2,1)S(1)}, u32[]{:S(2)}, u32[]{:S(2)}) async-start(bf16[8,2,8,1664]{3,2,1,0:T(8,128)(2,1)} %get-tuple-element.158), calls=%async_computation.3 | async-start | bytes 851968 | tf_op jit(solution)/shard_map/all_to_all | solution.py:1147
  129.3 16.2 %collective-permute-start.14 = (bf16[8,2,8,1664]{3,2,1,0:T(8,128)(2,1)S(1)}, bf16[8,2,8,1664]{3,2,1,0:T(8,128)(2,1)S(1)}, u32[]{:S(2)}, u32[]{:S(2)}) collective-permute-start(bf16[8,2,8,1664]{3,2,1,0:T(8,128)(2,1)S(1)} %all-to-all-done.3.part_ref.refs_0_), channel_id=1, source_target_pairs={{0,16},{8,24},{16,0},{24,8},{1,17},{9,25},{17,1},{25,9},{2,18},{10... | collective-permute-start | bytes 1277960 | tf_op jit(solution)/shard_map/ppermute | solution.py:1002
  146.2 13.4 %all-to-all-start.4 = ((bf16[8,2,8,1536]{3,2,1,0:T(8,128)(2,1)}), bf16[8,2,8,1536]{3,2,1,0:T(8,128)(2,1)S(1)}, u32[]{:S(2)}, u32[]{:S(2)}) async-start(bf16[8,2,8,1536]{3,2,1,0:T(8,128)(2,1)} %get-tuple-element.164), calls=%async_computation.4 | async-start | bytes 786432 | tf_op jit(solution)/shard_map/all_to_all | solution.py:1157
  150.6 32.4 %collective-permute-start.15 = (bf16[2,64,512]{2,1,0:T(8,128)(2,1)}, bf16[2,64,512]{2,1,0:T(8,128)(2,1)S(1)}, u32[]{:S(2)}, u32[]{:S(2)}) collective-permute-start(bf16[2,64,512]{2,1,0:T(8,128)(2,1)} %get-tuple-element.197.refs_12_), channel_id=1, source_target_pairs={{0,16},{8,24},{16,0},{24,8},{1,17},{9,25},{17,1},{25,9},{2,18},{10... | collective-permute-start | bytes 393224 | tf_op jit(solution)/shard_map/ppermute | solution.py:1002
  151.3 67.1 %collective-permute-start.17 = (bf16[2,64,3072]{2,1,0:T(8,128)(2,1)}, bf16[2,64,3072]{2,1,0:T(8,128)(2,1)}, u32[]{:S(2)}, u32[]{:S(2)}) collective-permute-start(bf16[2,64,3072]{2,1,0:T(8,128)(2,1)} %get-tuple-element.193.refs_4_), channel_id=1, source_target_pairs={{0,16},{8,24},{16,0},{24,8},{1,17},{9,25},{17,1},{25,9},{2,18},{10... | collective-permute-start | bytes 2359304 | tf_op jit(solution)/shard_map/ppermute | solution.py:1002
  152.1 66.4 %collective-permute-start.18 = (bf16[2,64,3072]{2,1,0:T(8,128)(2,1)}, bf16[2,64,3072]{2,1,0:T(8,128)(2,1)}, u32[]{:S(2)}, u32[]{:S(2)}) collective-permute-start(bf16[2,64,3072]{2,1,0:T(8,128)(2,1)} %get-tuple-element.195.refs_8_), channel_id=1, source_target_pairs={{0,16},{8,24},{16,0},{24,8},{1,17},{9,25},{17,1},{25,9},{2,18},{10... | collective-permute-start | bytes 2359304 | tf_op jit(solution)/shard_map/ppermute | solution.py:1002
  183.0 40.2 %copy-start.26 = (bf16[2,64,512]{2,1,0:T(8,128)(2,1)}, bf16[2,64,512]{2,1,0:T(8,128)(2,1)S(1)}, u32[]{:S(2)}) copy-start(bf16[2,64,512]{2,1,0:T(8,128)(2,1)S(1)} %collective-permute-done.15.refs_13_) | copy-start | bytes 393220
  214.6 7.9 %copy-start.1 = (bf16[8,2,8,1664]{3,2,1,0:T(8,128)(2,1)S(1)}, bf16[8,2,8,1664]{3,2,1,0:T(8,128)(2,1)}, u32[]{:S(2)}) copy-start(bf16[8,2,8,1664]{3,2,1,0:T(8,128)(2,1)} %copy-done) | copy-start | bytes 1277956
  214.6 8.5 %copy-start.25 = (bf16[2,64,512]{2,1,0:T(8,128)(2,1)S(1)}, bf16[2,64,512]{2,1,0:T(8,128)(2,1)}, u32[]{:S(2)}) copy-start(bf16[2,64,512]{2,1,0:T(8,128)(2,1)} %get-tuple-element.197.refs_12_) | copy-start | bytes 393220
  214.6 5.8 %collective-permute-start.16 = (bf16[8,352,128]{2,1,0:T(8,128)(2,1)}, bf16[8,352,128]{2,1,0:T(8,128)(2,1)S(1)}, u32[]{:S(2)}, u32[]{:S(2)}) collective-permute-start(bf16[8,352,128]{2,1,0:T(8,128)(2,1)} %get-tuple-element.173), channel_id=1, source_target_pairs={{0,8},{8,0},{16,24},{24,16},{1,9},{9,1},{17,25},{25,17},{2,10},{10... | collective-permute-start | bytes 2162696 | tf_op jit(solution)/shard_map/ppermute | solution.py:1002
  221.8 17.8 %collective-permute-start.19 = (bf16[8,176,128]{2,1,0:T(8,128)(2,1)S(1)}, bf16[8,176,128]{2,1,0:T(8,128)(2,1)S(1)}, u32[]{:S(2)}, u32[]{:S(2)}) collective-permute-start(bf16[8,176,128]{2,1,0:T(8,128)(2,1)S(1)} %constant_dynamic-slice_fusion), channel_id=1, source_target_pairs={{0,16},{8,24},{16,0},{24,8},{1,17},{9,25},{17,1},{25,9},{2,18},{10... | collective-permute-start | bytes 1081352 | tf_op jit(solution)/shard_map/ppermute | solution.py:1002
  222.5 22.1 %collective-permute-start.20 = (bf16[8,2,8,1664]{3,2,1,0:T(8,128)(2,1)S(1)}, bf16[8,2,8,1664]{3,2,1,0:T(8,128)(2,1)}, u32[]{:S(2)}, u32[]{:S(2)}) collective-permute-start(bf16[8,2,8,1664]{3,2,1,0:T(8,128)(2,1)S(1)} %copy-done.1), channel_id=1, source_target_pairs={{0,8},{8,0},{16,24},{24,16},{1,9},{9,1},{17,25},{25,17},{2,10},{10... | collective-permute-start | bytes 1277960 | tf_op jit(solution)/shard_map/ppermute | solution.py:1002
  223.2 16.6 %collective-permute-start.26 = (bf16[2,64,512]{2,1,0:T(8,128)(2,1)S(1)}, bf16[2,64,512]{2,1,0:T(8,128)(2,1)S(1)}, u32[]{:S(2)}, u32[]{:S(2)}) collective-permute-start(bf16[2,64,512]{2,1,0:T(8,128)(2,1)S(1)} %copy-done.25), channel_id=1, source_target_pairs={{0,8},{8,0},{16,24},{24,16},{1,9},{9,1},{17,25},{25,17},{2,10},{10... | collective-permute-start | bytes 393224 | tf_op jit(solution)/shard_map/ppermute | solution.py:1002
  223.2 16.8 %collective-permute-start.27 = (bf16[2,64,512]{2,1,0:T(8,128)(2,1)S(1)}, bf16[2,64,512]{2,1,0:T(8,128)(2,1)S(1)}, u32[]{:S(2)}, u32[]{:S(2)}) collective-permute-start(bf16[2,64,512]{2,1,0:T(8,128)(2,1)S(1)} %collective-permute-done.15.refs_13_), channel_id=1, source_target_pairs={{0,8},{8,0},{16,24},{24,16},{1,9},{9,1},{17,25},{25,17},{2,10},{10... | collective-permute-start | bytes 393224 | tf_op jit(solution)/shard_map/ppermute | solution.py:1002
  239.3 7.4 %collective-permute-start.22 = (bf16[2,64,3072]{2,1,0:T(8,128)(2,1)}, bf16[2,64,3072]{2,1,0:T(8,128)(2,1)}, u32[]{:S(2)}, u32[]{:S(2)}) collective-permute-start(bf16[2,64,3072]{2,1,0:T(8,128)(2,1)} %get-tuple-element.193.refs_4_), channel_id=1, source_target_pairs={{0,8},{8,0},{16,24},{24,16},{1,9},{9,1},{17,25},{25,17},{2,10},{10... | collective-permute-start | bytes 2359304 | tf_op jit(solution)/shard_map/ppermute | solution.py:1002
  239.5 7.2 %collective-permute-start.23 = (bf16[2,64,3072]{2,1,0:T(8,128)(2,1)}, bf16[2,64,3072]{2,1,0:T(8,128)(2,1)}, u32[]{:S(2)}, u32[]{:S(2)}) collective-permute-start(bf16[2,64,3072]{2,1,0:T(8,128)(2,1)} %collective-permute-done.17.refs_5_), channel_id=1, source_target_pairs={{0,8},{8,0},{16,24},{24,16},{1,9},{9,1},{17,25},{25,17},{2,10},{10... | collective-permute-start | bytes 2359304 | tf_op jit(solution)/shard_map/ppermute | solution.py:1002
  239.8 6.9 %collective-permute-start.24 = (bf16[2,64,3072]{2,1,0:T(8,128)(2,1)}, bf16[2,64,3072]{2,1,0:T(8,128)(2,1)}, u32[]{:S(2)}, u32[]{:S(2)}) collective-permute-start(bf16[2,64,3072]{2,1,0:T(8,128)(2,1)} %get-tuple-element.195.refs_8_), channel_id=1, source_target_pairs={{0,8},{8,0},{16,24},{24,16},{1,9},{9,1},{17,25},{25,17},{2,10},{10... | collective-permute-start | bytes 2359304 | tf_op jit(solution)/shard_map/ppermute | solution.py:1002
  240.1 6.7 %collective-permute-start.25 = (bf16[2,64,3072]{2,1,0:T(8,128)(2,1)}, bf16[2,64,3072]{2,1,0:T(8,128)(2,1)}, u32[]{:S(2)}, u32[]{:S(2)}) collective-permute-start(bf16[2,64,3072]{2,1,0:T(8,128)(2,1)} %collective-permute-done.18.refs_9_), channel_id=1, source_target_pairs={{0,8},{8,0},{16,24},{24,16},{1,9},{9,1},{17,25},{25,17},{2,10},{10... | collective-permute-start | bytes 2359304 | tf_op jit(solution)/shard_map/ppermute | solution.py:1002
  241.2 14.7 %all-to-all-start.5 = ((bf16[8,176,128]{2,1,0:T(8,128)(2,1)}), bf16[8,176,128]{2,1,0:T(8,128)(2,1)S(1)}, u32[]{:S(2)}, u32[]{:S(2)}) async-start(bf16[8,176,128]{2,1,0:T(8,128)(2,1)} %add_convert_fusion.1), calls=%async_computation.5 | async-start | bytes 720896 | tf_op jit(solution)/shard_map/all_to_all | solution.py:1035
  244.6 16.1 %copy-start.2 = (bf16[8,197,768]{2,1,0:T(8,128)(2,1)S(1)}, bf16[8,197,768]{2,1,0:T(8,128)(2,1)}, u32[]{:S(2)}) copy-start(bf16[8,197,768]{2,1,0:T(8,128)(2,1)} %get-tuple-element.174) | copy-start | bytes 7262212
  244.6 2.1 collective-permute-start.21
  255.9 3.0 %collective-permute-start.28 = (bf16[176,128]{1,0:T(8,128)(2,1)S(1)}, bf16[176,128]{1,0:T(8,128)(2,1)S(1)}, u32[]{:S(2)}, u32[]{:S(2)}) collective-permute-start(bf16[176,128]{1,0:T(8,128)(2,1)S(1)} %reduce_sum.12), channel_id=1, source_target_pairs={{0,16},{8,24},{16,0},{24,8},{1,17},{9,25},{17,1},{25,9},{2,18},{10... | collective-permute-start | bytes 135176 | tf_op jit(solution)/shard_map/ppermute | solution.py:1002
  258.9 3.7 %collective-permute-start.29 = (bf16[352,128]{1,0:T(8,128)(2,1)S(1)}, bf16[352,128]{1,0:T(8,128)(2,1)S(1)}, u32[]{:S(2)}, u32[]{:S(2)}) collective-permute-start(bf16[352,128]{1,0:T(8,128)(2,1)S(1)} %maximum_select_fusion.1), channel_id=1, source_target_pairs={{0,8},{8,0},{16,24},{24,16},{1,9},{9,1},{17,25},{25,17},{2,10},{10... | collective-permute-start | bytes 270344 | tf_op jit(solution)/shard_map/ppermute | solution.py:1002
  (17 other events, 26.8 us)

commit v5 on v4

--- a/solution.py
+++ b/solution.py
@@ -127,48 +127,52 @@
     out_ref[...] = unit.astype(BF16).reshape(out_ref.shape)
 
 
-def pack_kernel(place_ref, qkv_ref, a_ref, b_ref, ao_ref, ra_ref, out_ref, pack):
-    copies, rows, part = out_ref.shape
+def group_columns(pack, qkv_ref, group):
     width = qkv_ref.shape[1] // 3
     for piece in range(3):
-        pack[:, piece * GROUP : (piece + 1) * GROUP] = qkv_ref[:, piece * width : piece * width + GROUP]
+        start = piece * width + group * GROUP
+        pack[:, piece * GROUP : (piece + 1) * GROUP] = qkv_ref[:, start : start + GROUP]
+
+
+def own_part(place_ref, pack, pieces):
+    part = pack.shape[1] // pieces
+    return pack[:, pl.ds(pl.multiple_of(place_ref[0] % pieces * part, LANES), part)]
+
+
+def pack_kernel(
+    place_ref, qkv_ref, a_ref, b_ref, ao_ref, ra_ref, bo_ref, wr_ref, out_ref, pack0, pack1
+):
+    copies, rows, _ = out_ref.shape
+    width = qkv_ref.shape[1] // 3
+    group_columns(pack0, qkv_ref, 0)
+    for piece in range(3):
         column = width + (1 + piece) * LANES
-        pack[:, column : column + LANES] = b_ref[piece * rows : (piece + 1) * rows, :]
-    pack[:, width : width + LANES] = a_ref[...]
-    pack[:, width + 4 * LANES : width + 5 * LANES] = ao_ref[...]
-    pack[:, width + 5 * LANES : width + 6 * LANES] = ra_ref[...]
-    mine = pack[:, pl.ds(pl.multiple_of(place_ref[0] * part, LANES), part)]
+        pack0[:, column : column + LANES] = b_ref[piece * rows : (piece + 1) * rows, :]
+    pack0[:, width : width + LANES] = a_ref[...]
+    pack0[:, width + 4 * LANES : width + 5 * LANES] = ao_ref[...]
+    pack0[:, width + 5 * LANES : width + 6 * LANES] = ra_ref[...]
+    group_columns(pack1, qkv_ref, 1)
+    pack1[:, width : width + LANES] = bo_ref[...]
+    n_exp = wr_ref.shape[0]
+    route = jnp.concatenate([wr_ref[...].astype(F32), jnp.zeros((LANES - n_exp, rows), F32)], axis=0)
+    pack1[:, width + LANES :] = route.T.astype(BF16)
+    mine = jnp.concatenate([own_part(place_ref, pack0, 4), own_part(place_ref, pack1, 4)], axis=1)
     for copy in range(copies):
         out_ref[copy] = mine
 
 
-def later_pack_kernel(
-    place_ref, qkv_ref, bo_ref, wr_ref, wo_ref, rb_ref, first_ref, second_ref, pack1, pack2, pack3
-):
-    shards, rows, part = first_ref.shape
+def later_pack_kernel(place_ref, qkv_ref, wo_ref, rb_ref, out_ref, pack2, pack3):
+    shards, rows, _ = out_ref.shape
     width = wo_ref.shape[1]
-    for piece in range(3):
-        for group, pack in ((1, pack1), (2, pack2)):
-            start = piece * width + group * GROUP
-            pack[:, piece * GROUP : (piece + 1) * GROUP] = qkv_ref[:, start : start + GROUP]
-    pack1[:, width : width + LANES] = bo_ref[...]
-    n_exp, n_loc = wr_ref.shape[0], rb_ref.shape[0]
-    route = jnp.concatenate([wr_ref[...].astype(F32), jnp.zeros((LANES - n_exp, rows), F32)], axis=0)
-    pack1[:, width + LANES :] = route.T.astype(BF16)
+    group_columns(pack2, qkv_ref, 2)
     pack3[:, :width] = wo_ref[...]
+    n_loc = rb_ref.shape[0]
     second = jnp.concatenate([rb_ref[...].astype(F32), jnp.zeros((rows - n_loc, LANES), F32)], axis=0)
     pack3[:, width : width + LANES] = second.astype(BF16)
     pack3[:, width + LANES :] = jnp.zeros((rows, LANES), BF16)
-    half = pack2.shape[1] // 2
-
-    def own(pack, pieces, size):
-        return pack[:, pl.ds(pl.multiple_of(place_ref[0] % pieces * size, LANES), size)]
-
-    one, two, three = own(pack1, 4, part), own(pack2, 2, half), own(pack3, 4, part)
+    mine = jnp.concatenate([own_part(place_ref, pack2, 2), own_part(place_ref, pack3, 4)], axis=1)
     for shard in range(shards):
-        first_ref[shard] = one
-        second_ref[shard, :, :half] = two
-        second_ref[shard, :, half:] = three
+        out_ref[shard] = mine
 
 
 def head_mask(value):
@@ -232,10 +236,11 @@
                 ]
 
     h1 = flat(h1_ref)
-    low = dot(h1, a_ref[...]).astype(BF16).astype(F32)
+    both = dot(h1, wall[:, : 3 * GROUP + LANES])
+    low = both[:, 3 * GROUP :].astype(BF16).astype(F32)
     uq = select_rows(low, index_ref, step * n_img, n_img)
     uq_ref[...] = uq.reshape(uq_ref.shape)
-    attend_group(0, n_tok, h1, uq, wall, bt_ref, qkv_ref, att_ref, prob_ref)
+    attend_group(0, n_tok, both[:, : 3 * GROUP], uq, bt_ref, qkv_ref, att_ref, prob_ref)
 
 
 def group_rows(group, width, bt_ref):
@@ -245,10 +250,10 @@
     )
 
 
-def attend_group(group, n_tok, h1, uq, wall, bt_ref, qkv_ref, att_ref, prob_ref):
+def attend_group(group, n_tok, base, uq, bt_ref, qkv_ref, att_ref, prob_ref):
     n_img, total, _ = att_ref.shape
-    second = group_rows(group, wall.shape[0], bt_ref)
-    qkv = (dot(h1, wall[:, : 3 * GROUP]) + dot(uq, second, NT)).astype(BF16)
+    second = group_rows(group, bt_ref.shape[0] // 3, bt_ref)
+    qkv = (base + dot(uq, second, NT)).astype(BF16)
     qkv_ref[...] = qkv.reshape(qkv_ref.shape)
     for slot in range(n_img):
         att_ref[slot] = attention_forward(
@@ -271,7 +276,7 @@
             rest[3 + position][...] = wall[:, column : column + LANES]
 
     attend_group(
-        group, n_tok, flat(h1_ref), flat(uq_ref), wall, bt_ref, qkv_ref, att_ref, prob_ref,
+        group, n_tok, dot(flat(h1_ref), wall[:, : 3 * GROUP]), flat(uq_ref), bt_ref, qkv_ref, att_ref, prob_ref,
     )
 
 
@@ -281,7 +286,7 @@
 ):
     chunks, rest = rest[: len(layout[1])], rest[len(layout[1]) :]
     x2_ref, uo_ref, ur_ref, disp_ref, comb_ref, sg_ref, wrt_ref, rb_ref, *rest = rest
-    wall, rb_f, pad_a, pad_b, sent_ref = rest
+    wall, rb_f, pair_ref, pad_a, pad_b, sent_ref = rest
     every = sg_ref.shape[2]
     n_img, n_tok, width = image_ref.shape
     first = pl.program_id(0) * n_img
@@ -297,20 +302,26 @@
                 shard * rows : shard * rows + 8, width : width + LANES
             ].astype(F32)[:n_loc]
         rb_ref[...] = rb_f[...].astype(BF16)
+        wall[:, width : width + LANES] = ao_ref[...]
+        pair_ref[:, :LANES] = ra_ref[...]
+        pair_ref[:, LANES:] = wr_ref[...]
 
     att = jnp.concatenate([flat(att0), flat(att1), flat(att2)], axis=1)
-    uo = select_rows(dot(att, ao_ref[...]).astype(BF16).astype(F32), index_ref, first, n_img)
+    both = dot(att, wall[:, : width + LANES])
+    uo = select_rows(both[:, width:].astype(BF16).astype(F32), index_ref, first, n_img)
     uo_ref[...] = uo.reshape(uo_ref.shape)
-    x2 = pad_rows(pad_a, image_ref) + dot(att, wall[:, :width]) + dot(uo, bo_ref[...], NT)
+    x2 = pad_rows(pad_a, image_ref) + both[:, :width] + dot(uo, bo_ref[...], NT)
     x2_ref[...] = x2.reshape(x2_ref.shape)
     h2 = normalise(x2)[0].astype(BF16)
-    ur = select_rows(dot(h2, ra_ref[...]).astype(BF16).astype(F32), index_ref, first, n_img)
+    both = dot(h2, pair_ref[...])
+    ur = select_rows(both[:, :LANES].astype(BF16).astype(F32), index_ref, first, n_img)
+    base = both[:, LANES:]
     ur_ref[...] = ur.reshape(ur_ref.shape)
     cot = pad_rows(pad_b, cot_ref)
     for slot in range(n_img):
         rows = slice(slot * total, (slot + 1) * total)
         living = (first + slot < count_ref[0]).astype(F32)
-        logits = dot(wrt_ref[...], h2[rows], NT) + dot(rb_ref[...], ur[rows], NT)
+        logits = base[rows].T[:n_exp] + dot(rb_ref[...], ur[rows], NT)
         alive = lax.broadcasted_iota(jnp.int32, logits.shape, 1) < n_tok
         over_tokens = jnp.where(alive, logits, NEG)
         powers = jnp.exp(over_tokens - jnp.max(over_tokens, axis=1, keepdims=True))
@@ -433,25 +444,26 @@
     gda_ref[0] = dot(low_t[3 * LANES :, :], rows_ref[...]).T
 
 
-def turn_kernel(layouts, place_ref, ao_ref, ra_ref, *refs):
+def turn_kernel(layouts, place_ref, ao_ref, bo_ref, ra_ref, *refs):
     refs = list(refs)
     chunks = [[refs.pop(0) for _ in layout[1]] for layout in layouts]
-    qkv_ref, out_ref, route_ref = refs[:3]
-    walls = refs[3:]
+    qkv_ref, out_ref, first_ref, route_ref = refs[:4]
+    walls = refs[4:]
     for chunk, layout, wall in zip(chunks, layouts, walls):
         assemble(place_ref, chunk, layout, wall)
     width = walls[0].shape[0]
     for group, wall in enumerate(walls[:-1]):
         qkv_ref[group * 3 * GROUP : (group + 1) * 3 * GROUP, :] = wall[:, : 3 * GROUP].T
     qkv_ref[3 * width :, :] = walls[0][:, 3 * GROUP : 3 * GROUP + LANES].T
-    out_ref[:width, :] = walls[-1][:, :width].T
-    out_ref[width:, :] = ao_ref[...].T
+    out_ref[:, :width] = walls[-1][:, :width].T
+    out_ref[:, width:] = bo_ref[...]
+    first_ref[...] = ao_ref[...].T
     route_ref[...] = ra_ref[...].T
 
 
 def route_back_kernel(
     n_exp, index_ref, count_ref, cot_ref, x2_ref, uo_ref, ur_ref, disp_ref, comb_ref,
-    att0, att1, att2, ret_ref, bo_ref, wrt_ref, rb_ref, out_ref, route_ref,
+    att0, att1, att2, ret_ref, wrt_ref, rb_ref, out_ref, first_ref, route_ref,
     block_ref, gx2_ref, gatt_ref, pack_ref, pad_b, back_ref, acc_oa, acc_ob, acc_ra, acc_rb,
 ):
     n_img, n_tok, width = cot_ref.shape
@@ -500,21 +512,26 @@
         mixed = dot(three[:, 2 * n_exp :], yexp)
         block_ref[slot] = (living * (x2[rows] + mixed)).astype(BF16)[:n_tok]
         pairs.append(three[:, : 2 * n_exp])
-        belows.append(jnp.concatenate([gslot, wrt_ref[...]], axis=0))
+        belows.append(jnp.concatenate([route_ref[...], gslot, wrt_ref[...]], axis=0))
     glog_rows = jnp.concatenate([pair[:, n_exp:] for pair in pairs], axis=0)
     gur = select_rows(dot(glog_rows, rb_ref[...]), index_ref, first, n_img)
     acc_ra[...] += dot(gur, h2, TN)
-    gh2 = dot(gur, route_ref[...]) + jnp.concatenate(
-        [dot(pair, below) for pair, below in zip(pairs, belows)], axis=0
+    gh2 = jnp.concatenate(
+        [
+            dot(jnp.concatenate([gur[i * total : (i + 1) * total], pairs[i]], axis=1), belows[i])
+            for i in range(n_img)
+        ],
+        axis=0,
     )
     gx2 = jnp.concatenate(upstreams, axis=0) + normalise_back(unit, scale, gh2)
     gbr = gx2.astype(BF16)
     gx2_ref[...] = gbr.reshape(gx2_ref.shape)
     acc_ob[...] += dot(flat(uo_ref), gbr, TN)
-    guo = select_rows(dot(gbr, bo_ref[...]), index_ref, first, n_img)
+    both = dot(gbr, out_ref[...])
+    guo = select_rows(both[:, width:], index_ref, first, n_img)
     att = jnp.concatenate([flat(att0), flat(att1), flat(att2)], axis=1)
     acc_oa[...] += dot(guo, att, TN)
-    gatt = dot(jnp.concatenate([gbr, guo], axis=1), out_ref[...]).astype(BF16)
+    gatt = (both[:, :width] + dot(guo, first_ref[...])).astype(BF16)
     gatt_ref[...] = gatt.reshape(gatt_ref.shape)
 
     @pl.when(pl.program_id(0) == pl.num_programs(0) - 1)
@@ -698,27 +715,23 @@
 
 def pack_call(place, weights, copies):
     rows, columns = weights[0].shape
-    part = (columns // 3 + 6 * LANES) // 4
+    width = columns // 3
+    wide = [width + 6 * LANES, width + 2 * LANES]
+    out = (copies, rows, sum(wide) // 4)
     return call(
         pack_kernel, (place,), (1,), [(weight, whole(weight.shape)) for weight in weights],
-        [((copies, rows, part), BF16, whole((copies, rows, part)))],
-        [pltpu.VMEM((rows, 4 * part), BF16)],
-        rows * columns,
+        [(out, BF16, whole(out))], [pltpu.VMEM((rows, each), BF16) for each in wide], rows * columns,
     )[0]
 
 
 def later_pack_call(place, weights, shards):
-    rows, width = weights[3].shape
-    part, half = (width + 2 * LANES) // 4, width // 2
+    rows, width = weights[1].shape
+    out = (shards, rows, width // 2 + (width + 2 * LANES) // 4)
     return call(
         later_pack_kernel, (place,), (1,), [(weight, whole(weight.shape)) for weight in weights],
-        [
-            ((shards, rows, part), BF16, whole((shards, rows, part))),
-            ((shards, rows, half + part), BF16, whole((shards, rows, half + part))),
-        ],
-        [pltpu.VMEM((rows, columns), BF16) for columns in (4 * part, 2 * half, 4 * part)],
-        rows * width,
-    )
+        [(out, BF16, whole(out))],
+        [pltpu.VMEM((rows, each), BF16) for each in (width, width + 2 * LANES)], rows * width,
+    )[0]
 
 
 def attention_flops(n_img, total, width, parts):
@@ -800,6 +813,7 @@
         [
             pltpu.VMEM((width, columns), BF16),
             pltpu.VMEM((n_exp, LANES), F32),
+            pltpu.VMEM((width, 2 * LANES), BF16),
             pltpu.VMEM((each * total, width), F32),
             pltpu.VMEM((each * total, width), F32),
             pltpu.VMEM(((2 * width // LANES + 1) * n_exp * n_img, LANES), F32),
@@ -985,12 +999,12 @@
     return out.reshape(n_img, n_tok, width)
 
 
-def turn_call(place, bank_ao, bank_ra, packs):
-    width = bank_ao.shape[0]
-    shapes = [(3 * width + LANES, width), (width + LANES, width), (LANES, width)]
+def turn_call(place, banks, packs):
+    width = banks[0].shape[0]
+    shapes = [(3 * width + LANES, width), (width, width + LANES), (LANES, width), (LANES, width)]
     return call(
         functools.partial(turn_kernel, tuple(pack[1] for pack in packs)), (place,), (1,),
-        [(bank, once(bank.shape)) for bank in (bank_ao, bank_ra)]
+        [(bank, once(bank.shape)) for bank in banks]
         + [(chunk, once(chunk.shape)) for pack in packs for chunk in pack[0]],
         [(shape, BF16, once(shape)) for shape in shapes],
         [pltpu.VMEM((width, pack[2]), BF16) for pack in packs],
@@ -1081,62 +1095,63 @@
     ).astype(jnp.int32)
     by_axis = shards == 2 * STRIPS and replicas == 4
 
-    spread0 = pack_call(
+    spread01 = pack_call(
         place,
         (
             query_key_value_weight, query_key_value_first, query_key_value_second.T,
-            output_adapter_first, dispatch_adapter_first,
+            output_adapter_first, dispatch_adapter_first, output_adapter_second.T,
+            frozen_dispatch_weight.T,
         ),
         STRIPS if by_axis else shards,
     )
-    spread1, spread23 = later_pack_call(
-        place,
-        (
-            query_key_value_weight, output_adapter_second.T, frozen_dispatch_weight.T,
-            frozen_output_weight, dispatch_adapter_second.T,
-        ),
-        shards,
+    spread23 = later_pack_call(
+        place, (query_key_value_weight, frozen_output_weight, dispatch_adapter_second.T), shards
     )
     near = functools.partial(swap, axis="replica", size=replicas, bit=1)
     far = functools.partial(swap, axis="replica", size=replicas, bit=2)
     beside = functools.partial(swap, axis="shard", size=shards, bit=1)
+    cut = (width + 6 * LANES) // 4
 
     h1 = norm_call(images, cotangent, total)
     if by_axis:
         lines = [[2 * strip + side for strip in range(STRIPS)] for side in range(2)]
-        own0, spread1, spread23 = tie(over_shard(spread0, lines), spread1, spread23)
-        beside0, far0, h1, spread1 = tie(beside(own0), far(own0), h1, spread1)
-        held = [(own0, 0, 0), (beside0, 0, 1), (far0, 2, 0)]
-        own1 = over_shard(spread1)
-        held.append((far(held[1][0]), 2, 1))
+        own01, spread23, h1 = tie(over_shard(spread01, lines), spread23, h1)
+        own0, own1 = own01[:, :cut], own01[:, cut:]
+        beside0, far0, own1 = tie(beside(own0), far(own0), own1)
+        corner0, beside1, far1 = beside(far0), beside(own1), far(own1)
+        corner0, far1, spread23 = tie(corner0, far1, spread23)
+        held0 = [(own0, 0, 0), (beside0, 0, 1), (far0, 2, 0), (corner0, 2, 1)]
+        held1 = [(own1, 0, 0), (beside1, 0, 1), (far1, 2, 0), (beside(far1), 2, 1)]
     else:
-        own0 = over_shard(spread0)
-        own0, h1, spread1 = tie(own0, h1, spread1)
-        held = [(own0, 0, None), (far(own0), 2, None)]
-        own1 = over_shard(spread1)
-    chunks0 = [chunk for chunk, _, _ in held] + [near(chunk) for chunk, _, _ in held]
-    layout0 = [(replica, side, 0) for _, replica, side in held]
-    layout0 += [(replica ^ 1, side, 0) for _, replica, side in held]
-    *chunks0, own1, spread23 = tie(*chunks0, own1, spread23)
-    pack0 = (tuple(chunks0), (4, tuple(layout0)), 3 * GROUP + 6 * LANES)
-    far1 = far(own1)
+        own01, spread23, h1 = tie(over_shard(spread01), spread23, h1)
+        own0, own1 = own01[:, :cut], own01[:, cut:]
+        held0 = [(own0, 0, None), (far(own0), 2, None)]
+        held1 = [(own1, 0, None), (far(own1), 2, None)]
     own23 = over_shard(spread23)
+
+    def four_pieces(held, columns):
+        layout = [(replica, side, 0) for _, replica, side in held]
+        layout += [(replica ^ 1, side, 0) for _, replica, side in held]
+        chunks = [chunk for chunk, _, _ in held] + [near(chunk) for chunk, _, _ in held]
+        return tuple(chunks), (4, tuple(layout)), columns
+
+    pack0 = four_pieces(held0, width + 6 * LANES)
     qkv0, att0, prob0, uq, bank_a, bank_bt, bank_ao, bank_ra = first_attention_call(
         place, image_adapter_index, h1, pack0, n_tok, shards
     )
-    uq, own1, far1 = tie(uq, own1, far1)
-    four = (4, ((0, None, 0), (1, None, 0), (2, None, 0), (3, None, 0)))
-    pack1 = ((own1, near(own1), far1, near(far1)), four, 3 * GROUP + 2 * LANES)
+    beside1, last1, uq, own23 = tie(held1[1][0], held1[-1][0], uq, own23)
+    held1[1] = (beside1,) + held1[1][1:]
+    held1[-1] = (last1,) + held1[-1][1:]
+    pack1 = four_pieces(held1, width + 2 * LANES)
+    own2, own3 = own23[:, : width // 2], own23[:, width // 2 :]
+    far3 = far(own3)
     qkv1, att1, prob1, bank_bo, bank_wr = next_attention_call(
         place, h1, uq, bank_bt, pack1, n_tok, 1, 2
     )
-    att1, uq, own23 = tie(att1, uq, own23)
-    own2, own3 = own23[:, : width // 2], own23[:, width // 2 :]
-    far3 = far(own3)
-    pack2 = ((own2, near(own2)), (2, ((0, None, 0), (1, None, 0))), 3 * GROUP)
+    att1, uq, own2, own3, far3 = tie(att1, uq, own2, own3, far3)
+    pack2 = ((own2, near(own2)), (2, ((0, None, 0), (1, None, 0))), width)
     qkv2, att2, prob2 = next_attention_call(place, h1, uq, bank_bt, pack2, n_tok, 2, 0)
-    att2, own3, far3 = tie(att2, own3, far3)
-    pack3 = ((own3, near(own3), far3, near(far3)), four, width + 2 * LANES)
+    pack3 = four_pieces([(own3, 0, None), (far3, 2, None)], width + 2 * LANES)
     packs = (pack0, pack1, pack2, pack3)
     atts = (att0, att1, att2)
     x2, uo, ur, disp, comb, sg, bank_wrt, bank_rb = route_call(
@@ -1145,8 +1160,8 @@
     )
 
     landed = lax.all_to_all(sg, "shard", split_axis=0, concat_axis=0, tiled=True)
-    landed, *turned = tie(landed, *turn_call(place, bank_ao, bank_ra, packs))
-    turned_qkv, turned_out, turned_route = turned
+    landed, *turned = tie(landed, *turn_call(place, (bank_ao, bank_bo, bank_ra), packs))
+    turned_qkv, turned_out, turned_first, turned_route = turned
     weights = (
         frozen_up_weight, frozen_down_weight, up_adapter_first, up_adapter_second,
         down_adapter_first, down_adapter_second,
@@ -1162,7 +1177,7 @@
 
     block_out, gx2, gatt, out_pack = route_back_call(
         image_adapter_index, device_image_count, cotangent, x2, uo, ur, disp, comb, atts, back,
-        (bank_bo, bank_wrt, bank_rb, turned_out, turned_route), shards, replicas,
+        (bank_wrt, bank_rb, turned_out, turned_first, turned_route), shards, replicas,
     )
     gatt, *lows = tie(gatt, *[row[3] for row in every])
     held = [array for row, low in zip(every, lows) for array in (*row[:3], low)]

time: 266 us -> 258 us (0.970)
  starting transfers between devices: 55.8 us -> 51.3 us
  Pallas kernels: 162 us -> 158 us
    all_to_all x3 -> x2, starting transfers between devices: 14.5 us -> 8.98 us  [over_shard(): lax.all_to_all(spread, 'shard', split_axis=0, concat_axis=0, tiled=True,...]
    ppermute x30 -> x34, waiting for transfers between devices: 11.7 us -> 16.1 us  [swap(): return lax.ppermute(array, axis, [(i, i ^ bit) for i in range(size)])]
    pallas_call x13, Pallas kernels: 162 us -> 158 us  [call(): pl.pallas_call(kernel, out_shape=shapes, grid_spec=pltpu.PrefetchScalarGr...]
    ppermute x30 -> x34, starting transfers between devices: 27.8 us -> 30.9 us  [swap(): return lax.ppermute(array, axis, [(i, i ^ bit) for i in range(size)])]
    unnamed x61 -> x65, local copies, waits for them, and re-layouts: 12.7 us -> 12.2 us
  transfers between devices with their start and end apart: 36 -> 39, of which waited for: 13 -> 12; matrix products, arithmetic and copies ran while one was open for 3% -> 3% of each run, Pallas kernels for 54% -> 54%
where the time goes in v5:
time: 258 us; the launch traced here: 257 us
  Pallas kernels  158 us (61%)
  starting transfers between devices  51.3 us (20%)
  waiting for transfers between devices  29.4 us (11%)
  local copies, waits for them, and re-layouts  14.3 us (6%)
  other arithmetic  2.82 us (1%)
    pallas_call x13, Pallas kernels, call(): pl.pallas_call(kernel, out_shape=shapes, grid_spec=pltpu.PrefetchScalarGr...  158 us
    ppermute x34, starting transfers between devices, swap(): return lax.ppermute(array, axis, [(i, i ^ bit) for i in range(size)])  30.9 us
    ppermute x34, waiting for transfers between devices, swap(): return lax.ppermute(array, axis, [(i, i ^ bit) for i in range(size)])  16.1 us
    unnamed x65, local copies, waits for them, and re-layouts  12.2 us
    all_to_all x2, starting transfers between devices, over_shard(): lax.all_to_all(spread, 'shard', split_axis=0, concat_axis=0, tiled=True,...  8.98 us
    all_to_all x1, waiting for transfers between devices, per_device(): back = lax.all_to_all(ret, 'shard', split_axis=0, concat_axis=0, tiled=True)  6.82 us
  transfers between devices with their start and end apart: 39, of which 12 were waited for; matrix products, arithmetic and copies ran while one was open for 3% of the time, Pallas kernels for 54%

profile of v5, /device:TPU:1, one launch (start us, length us, event | category | flops | bytes accessed | tf_op | source)
XLA Modules:
  0.0 257.0 jit_solution(2973546281558407152)
XLA Ops:
  1.3 2.8 %shard_map.274 = bf16[4,96,640]{2,1,0:T(8,128)(2,1)} custom-call(s32[3]{0:T(128)} %pad_add_fusion.place_ref, bf16[96,2304]{1,0:T(8,128)(2,1)} %qkv_ref.3, bf16[96,128]{1,0:T(8,128)(2,1)} %a_ref.1, bf16[288,128]{1,0:T(8,128)(2,1)} %bitcast.26, bf16[96,128]{1,0:T(8,128)(2,1)} %ao_ref.1, bf16[96,128]{1,0:T(8,128)(2,1)} %ra_ref.1, bf16[96,128]{1,0:T(8,128)(2,1)} %bitcast.27, ...), custom_call_target="tpu_custom_call" | custom-call | flops 221184 | bytes 1108992 | tf_op jit(solution)/shard_map/pallas_call | solution.py:688
  4.0 5.4 %all-to-all-start = ((bf16[4,96,640]{2,1,0:T(8,128)(2,1)}), bf16[4,96,640]{2,1,0:T(8,128)(2,1)S(1)}, u32[]{:S(2)}, u32[]{:S(2)}) async-start(bf16[4,96,640]{2,1,0:T(8,128)(2,1)} %shard_map.274), calls=%async_computation | async-start | bytes 983040 | tf_op jit(solution)/shard_map/all_to_all | solution.py:1024
  9.4 2.8 %shard_map.275 = bf16[8,96,640]{2,1,0:T(8,128)(2,1)} custom-call(s32[3]{0:T(128)} %pad_add_fusion.place_ref, bf16[96,2304]{1,0:T(8,128)(2,1)} %qkv_ref.3, bf16[96,768]{1,0:T(8,128)(2,1)} %wo_ref.1, bf16[2,128]{1,0:T(2,128)(2,1)} %bitcast.29), custom_call_target="tpu_custom_call" | custom-call | flops 73728 | bytes 1573376 | tf_op jit(solution)/shard_map/pallas_call | solution.py:688
  12.3 1.9 copy.31.image_ref
  14.6 1.9 copy.32._.cot_ref
  16.5 3.7 %shard_map.276.h1_ref.refs_8_ = bf16[8,208,768]{2,1,0:T(8,128)(2,1)} custom-call(bf16[8,197,768]{2,1,0:T(8,128)(2,1)} %copy.31.image_ref, bf16[8,197,768]{2,1,0:T(8,128)(2,1)} %copy.32._.cot_ref), custom_call_target="tpu_custom_call" | custom-call | flops 9682944 | bytes 7397376 | tf_op jit(solution)/shard_map/pallas_call | solution.py:688
  20.2 2.6 %all-to-all-done = bf16[4,96,640]{2,1,0:T(8,128)(2,1)S(1)} async-done(((bf16[4,96,640]{2,1,0:T(8,128)(2,1)}), bf16[4,96,640]{2,1,0:T(8,128)(2,1)S(1)}, u32[]{:S(2)}, u32[]{:S(2)}) %all-to-all-start) | async-done | bytes 491552 | tf_op jit(solution)/shard_map/all_to_all | solution.py:1024
  22.8 1.3 collective-permute-start
  24.1 1.2 collective-permute-start.1
  25.3 4.6 %collective-permute-done.rest_1_.refs_1_ = bf16[384,384]{1,0:T(8,128)(2,1)S(1)} collective-permute-done((bf16[384,384]{1,0:T(8,128)(2,1)S(1)}, bf16[384,384]{1,0:T(8,128)(2,1)S(1)}, u32[]{:S(2)}, u32[]{:S(2)}) %collective-permute-start) | collective-permute-done | bytes 294944 | tf_op jit(solution)/shard_map/ppermute | solution.py:1016
  29.9 0.9 collective-permute-done.1.rest_2_.refs_2_
  31.2 1.2 collective-permute-start.3
  32.4 3.3 %collective-permute-done.3.rest_2_.refs_10_ = bf16[384,256]{1,0:T(8,128)(2,1)S(1)} collective-permute-done((bf16[384,256]{1,0:T(8,128)(2,1)S(1)}, bf16[384,256]{1,0:T(8,128)(2,1)S(1)}, u32[]{:S(2)}, u32[]{:S(2)}) %collective-permute-start.3) | collective-permute-done | bytes 196640 | tf_op jit(solution)/shard_map/ppermute | solution.py:1016
  36.4 3.6 %all-to-all-start.1 = ((bf16[8,96,640]{2,1,0:T(8,128)(2,1)}), bf16[8,96,640]{2,1,0:T(8,128)(2,1)S(1)}, u32[]{:S(2)}, u32[]{:S(2)}) async-start(bf16[8,96,640]{2,1,0:T(8,128)(2,1)} %shard_map.275), calls=%async_computation.1 | async-start | bytes 1966080 | tf_op jit(solution)/shard_map/all_to_all | solution.py:1024
  40.0 4.0 %collective-permute-start.4 = (bf16[384,384]{1,0:T(8,128)(2,1)S(1)}, bf16[384,384]{1,0:T(8,128)(2,1)S(1)}, u32[]{:S(2)}, u32[]{:S(2)}) collective-permute-start(bf16[384,384]{1,0:T(8,128)(2,1)S(1)} %slice.30.rest_0_.refs_0_), channel_id=1, source_target_pairs={{0,8},{8,0},{16,24},{24,16},{1,9},{9,1},{17,25},{25,17},{2,10},{10... | collective-permute-start | bytes 884744 | tf_op jit(solution)/shard_map/ppermute | solution.py:1016
  44.6 1.5 collective-permute-start.8
  46.1 0.8 collective-permute-start.10
  48.7 12.5 %shard_map.277 = (bf16[8,208,768]{2,1,0:T(8,128)(2,1)}, bf16[8,208,256]{2,1,0:T(8,128)(2,1)}, bf16[8,4,208,208]{3,2,1,0:T(8,128)(2,1)}, bf16[8,208,128]{2,1,0:T(...) custom-call(s32[3]{0:T(128)} %pad_add_fusion.place_ref, ...), custom_call_target="tpu_custom_call" | custom-call | flops 2317352960 | bytes 12697600 | tf_op jit(solution)/shard_map/pallas_call | solution.py:688
  61.9 3.6 %collective-permute-start.11 = (bf16[384,256]{1,0:T(8,128)(2,1)}, bf16[384,256]{1,0:T(8,128)(2,1)S(1)}, u32[]{:S(2)}, u32[]{:S(2)}) collective-permute-start(bf16[384,256]{1,0:T(8,128)(2,1)} %copy-done.24), channel_id=1, source_target_pairs={{0,8},{8,0},{16,24},{24,16},{1,9},{9,1},{17,25},{25,17},{2,10},{10... | collective-permute-start | bytes 589832 | tf_op jit(solution)/shard_map/ppermute | solution.py:1016
  65.5 1.3 collective-permute-start.14
  67.8 10.7 %shard_map.278 = (bf16[8,208,768]{2,1,0:T(8,128)(2,1)}, bf16[8,208,256]{2,1,0:T(8,128)(2,1)}, bf16[8,4,208,208]{3,2,1,0:T(8,128)(2,1)}, bf16[768,128]{1,0:T(8,128)(2,1)}, bf16[768,128]{1,0:T(8,128)(2,1)}) custom-call(s32[3]{0:T(128)} %pad_add_fusion.place_ref, bf16[8,208,768]{2,1,0:T(8,128)(2,1)} %shard_map.276.h1_ref.refs_8_, ...), custom_call_target="tpu_custom_call" | custom-call | flops 2317352960 | bytes 11714560 | tf_op jit(solution)/shard_map/pallas_call | solution.py:688
  78.4 0.8 collective-permute-start.15
  80.9 0.8 copy-done.9
  81.7 10.3 %shard_map.279 = (bf16[8,208,768]{2,1,0:T(8,128)(2,1)}, bf16[8,208,256]{2,1,0:T(8,128)(2,1)}, bf16[8,4,208,208]{3,2,1,0:T(8,128)(2,1)}) custom-call(s32[3]{0:T(128)} %pad_add_fusion.place_ref, bf16[8,208,768]{2,1,0:T(8,128)(2,1)} %shard_map.276.h1_ref.refs_8_, bf16[8,208,128]{2,1,0:T(8,128)(2,1)} %get-tuple-element.120.uq_ref.refs_7_, ...), custom_call_target="tpu_custom_call" | custom-call | flops 2317352960 | bytes 10928128 | tf_op jit(solution)/shard_map/pallas_call | solution.py:688
  92.9 15.3 %shard_map.280 = (f32[8,208,768]{2,1,0:T(8,128)}, bf16[8,208,128]{2,1,0:T(8,128)(2,1)}, bf16[8,208,128]{2,1,0:T(8,128)(2,1)}, f32[8,16,208]{2,1,0:T(8,128)}, f32...) custom-call(s32[3]{0:T(128)} %pad_add_fusion.place_ref, ...), custom_call_target="tpu_custom_call" | custom-call | flops 2944401408 | bytes 16388096 | tf_op jit(solution)/shard_map/pallas_call | solution.py:688
  108.2 3.7 %all-to-all-start.2 = ((bf16[8,2,8,1664]{3,2,1,0:T(8,128)(2,1)}), bf16[8,2,8,1664]{3,2,1,0:T(8,128)(2,1)S(1)}, u32[]{:S(2)}, u32[]{:S(2)}) async-start(bf16[8,2,8,1664]{3,2,1,0:T(8,128)(2,1)} %get-tuple-element.140), calls=%async_computation.2 | async-start | bytes 851968 | tf_op jit(solution)/shard_map/all_to_all | solution.py:1162
  111.9 7.8 %shard_map.281 = (bf16[2432,768]{1,0:T(8,128)(2,1)}, bf16[768,896]{1,0:T(8,128)(2,1)}, bf16[128,768]{1,0:T(8,128)(2,1)}, bf16[128,768]{1,0:T(8,128)(2,1)}) custom-call(s32[3]{0:T(128)} %pad_add_fusion.place_ref, bf16[768,128]{1,0:T(8,128)(2,1)} %get-tuple-element.129.ao_ref, bf16[768,128]{1,0:T(8,128)(2,1)} %get-tuple-element.130.bo_ref, ...), custom_call_target="tpu_custom_call" | custom-call | flops 4718592 | bytes 12779520 | tf_op jit(solution)/shard_map/pallas_call | solution.py:688
  119.7 3.8 %all-to-all-done.2.part_ref.refs_0_ = bf16[8,2,8,1664]{3,2,1,0:T(8,128)(2,1)S(1)} async-done(((bf16[8,2,8,1664]{3,2,1,0:T(8,128)(2,1)}), bf16[8,2,8,1664]{3,2,1,0:T(8,128)(2,1)S(1)}, u32[]{:S(2)}, u32[]{:S(2)}) %all-to-all-start.2) | async-done | bytes 426016 | tf_op jit(solution)/shard_map/all_to_all | solution.py:1162
  123.5 0.9 collective-permute-start.18
  124.4 14.9 %shard_map.282 = (bf16[8,2,8,1536]{3,2,1,0:T(8,128)(2,1)}, bf16[2,64,3072]{2,1,0:T(8,128)(2,1)}, bf16[2,64,3072]{2,1,0:T(8,128)(2,1)}, bf16[2,64,512]{2,1,0:T(8,128)(2,1)}) custom-call(bf16[2,768,3072]{2,1,0:T(8,128)(2,1)} %wu_ref.1, bf16[2,3072,768]{2,1,0:T(8,128)(2,1)} %wd_ref.1, bf16[2,768,128]{2,1,0:T(8,128)(2,1)} %ua_ref.1, ...), custom_call_target="tpu_custom_call" | custom-call | flops 2415919104 | bytes 25329664 | tf_op jit(solution)/shard_map/pallas_call | solution.py:688
  139.3 0.8 copy-done.10
  140.1 4.3 %all-to-all-start.3 = ((bf16[8,2,8,1536]{3,2,1,0:T(8,128)(2,1)}), bf16[8,2,8,1536]{3,2,1,0:T(8,128)(2,1)S(1)}, u32[]{:S(2)}, u32[]{:S(2)}) async-start(bf16[8,2,8,1536]{3,2,1,0:T(8,128)(2,1)} %get-tuple-element.147), calls=%async_computation.3 | async-start | bytes 786432 | tf_op jit(solution)/shard_map/all_to_all | solution.py:1172
  146.6 6.8 %all-to-all-done.3.ret_ref = bf16[8,2,8,1536]{3,2,1,0:T(8,128)(2,1)S(1)} async-done(((bf16[8,2,8,1536]{3,2,1,0:T(8,128)(2,1)}), bf16[8,2,8,1536]{3,2,1,0:T(8,128)(2,1)S(1)}, u32[]{:S(2)}, u32[]{:S(2)}) %all-to-all-start.3) | async-done | bytes 393248 | tf_op jit(solution)/shard_map/all_to_all | solution.py:1172
  154.1 21.3 %shard_map.283 = (bf16[8,197,768]{2,1,0:T(8,128)(2,1)}, bf16[8,208,768]{2,1,0:T(8,128)(2,1)}, bf16[8,208,768]{2,1,0:T(8,128)(2,1)}, bf16[8,320,128]{2,1,0:T(8,128)(2,1)}) custom-call(s32[8]{0:T(128)} %index_ref.7, s32[1]{0:T(128)S(6)} %copy.38.count_ref, bf16[8,197,768]{2,1,0:T(8,128)(2,1)} %copy.32._.cot_ref, f32[8,208,768]{2,1,0:T(8,128)} %get-tuple-element.135.x2_ref, ...), custom_call_target="tpu_custom_call" | custom-call | flops 3925868544 | bytes 21532672 | tf_op jit(solution)/shard_map/pallas_call | solution.py:688
  175.5 31.6 %shard_map.284 = (bf16[8,208,768]{2,1,0:T(8,128)(2,1)}, bf16[8,208,768]{2,1,0:T(8,128)(2,1)}, bf16[8,208,768]{2,1,0:T(8,128)(2,1)}, bf16[8,208,128]{2,1,0:T(8,12...) custom-call(s32[3]{0:T(128)} %pad_add_fusion.place_ref, s32[8]{0:T(128)} %index_ref.7, ...), custom_call_target="tpu_custom_call" | custom-call | flops 3639607296 | bytes 32292864 | tf_op jit(solution)/shard_map/pallas_call | solution.py:688
  207.1 3.7 %collective-permute-start.20 = (bf16[8,352,128]{2,1,0:T(8,128)(2,1)}, bf16[8,352,128]{2,1,0:T(8,128)(2,1)S(1)}, u32[]{:S(2)}, u32[]{:S(2)}) collective-permute-start(bf16[8,352,128]{2,1,0:T(8,128)(2,1)} %get-tuple-element.157), channel_id=1, source_target_pairs={{0,8},{8,0},{16,24},{24,16},{1,9},{9,1},{17,25},{25,17},{2,10},{10... | collective-permute-start | bytes 2162696 | tf_op jit(solution)/shard_map/ppermute | solution.py:1016
  210.8 2.0 collective-permute-done.20
  212.9 1.3 add_convert_fusion
  214.2 0.8 collective-permute-start.23
  216.2 15.6 %shard_map.285 = f32[9456,128]{1,0:T(8,128)} custom-call(bf16[8,197,768]{2,1,0:T(8,128)(2,1)} %copy.31.image_ref, bf16[8,208,768]{2,1,0:T(8,128)(2,1)} %get-tuple-element.167.gx2_ref, bf16[8,208,128]{2,1,0:T(8,128)(2,1)} %get-tuple-element.168.guq_ref, bf16[2432,768]{1,0:T(8,128)(2,1)} %get-tuple-element.169.turned_ref, ...), custom_call_target="tpu_custom_call" | custom-call | flops 6215958528 | bytes 21647360 | tf_op jit(solution)/shard_map/pallas_call | solution.py:688
  232.8 0.8 add_convert_fusion.1
  233.6 3.4 %all-to-all-start.4 = ((bf16[8,176,128]{2,1,0:T(8,128)(2,1)}), bf16[8,176,128]{2,1,0:T(8,128)(2,1)S(1)}, u32[]{:S(2)}, u32[]{:S(2)}) async-start(bf16[8,176,128]{2,1,0:T(8,128)(2,1)} %add_convert_fusion.1), calls=%async_computation.4 | async-start | bytes 720896 | tf_op jit(solution)/shard_map/all_to_all | solution.py:1049
  237.4 1.7 collective-permute-done.25.refs_3_
  239.9 8.3 %shard_map.286 = (f32[2,768,128]{2,1,0:T(8,128)}, f32[2,128,3072]{2,1,0:T(8,128)}, f32[2,3072,128]{2,1,0:T(8,128)}, f32[2,128,768]{2,1,0:T(8,128)}) custom-call(bf16[8,2,8,1664]{3,2,1,0:T(8,128)(2,1)} %copy-done, bf16[8,2,8,1664]{3,2,1,0:T(8,128)(2,1)} %copy-done.10, bf16[8,2,8,1664]{3,2,1,0:T(8,128)(2,1)} %collective-permute-done.24.refs_2_, ...), custom_call_target="tpu_custom_call" | custom-call | flops 805306368 | bytes 16384000 | tf_op jit(solution)/shard_map/pallas_call | solution.py:688
  248.3 0.8 collective-permute-start.32
  249.1 2.1 collective-permute-done.32
  251.3 1.9 collective-permute-start.33
  253.2 1.9 copy.37
  (122 shorter events, 16.3 us)
Async XLA Ops:
  4.0 18.7 %all-to-all-start = ((bf16[4,96,640]{2,1,0:T(8,128)(2,1)}), bf16[4,96,640]{2,1,0:T(8,128)(2,1)S(1)}, u32[]{:S(2)}, u32[]{:S(2)}) async-start(bf16[4,96,640]{2,1,0:T(8,128)(2,1)} %shard_map.274), calls=%async_computation | async-start | bytes 983040 | tf_op jit(solution)/shard_map/all_to_all | solution.py:1024
  22.8 25.1 %copy-start.7 = (bf16[384,384]{1,0:T(8,128)(2,1)}, bf16[384,384]{1,0:T(8,128)(2,1)S(1)}, u32[]{:S(2)}) copy-start(bf16[384,384]{1,0:T(8,128)(2,1)S(1)} %slice.30.rest_0_.refs_0_) | copy-start | bytes 884740
  22.8 7.1 %collective-permute-start = (bf16[384,384]{1,0:T(8,128)(2,1)S(1)}, bf16[384,384]{1,0:T(8,128)(2,1)S(1)}, u32[]{:S(2)}, u32[]{:S(2)}) collective-permute-start(bf16[384,384]{1,0:T(8,128)(2,1)S(1)} %slice.30.rest_0_.refs_0_), channel_id=1, source_target_pairs={{0,1},{1,0},{2,3},{3,2},{4,5},{5,4},{6,7},{7,6},{8,9},{9,8},{10,11... | collective-permute-start | bytes 884744 | tf_op jit(solution)/shard_map/ppermute | solution.py:1016
  24.1 6.8 %collective-permute-start.1 = (bf16[384,384]{1,0:T(8,128)(2,1)S(1)}, bf16[384,384]{1,0:T(8,128)(2,1)S(1)}, u32[]{:S(2)}, u32[]{:S(2)}) collective-permute-start(bf16[384,384]{1,0:T(8,128)(2,1)S(1)} %slice.30.rest_0_.refs_0_), channel_id=1, source_target_pairs={{0,16},{8,24},{16,0},{24,8},{1,17},{9,25},{17,1},{25,9},{2,18},{10... | collective-permute-start | bytes 884744 | tf_op jit(solution)/shard_map/ppermute | solution.py:1016
  25.3 35.8 %copy-start.8 = (bf16[384,256]{1,0:T(8,128)(2,1)}, bf16[384,256]{1,0:T(8,128)(2,1)S(1)}, u32[]{:S(2)}) copy-start(bf16[384,256]{1,0:T(8,128)(2,1)S(1)} %slice.31.rest_0_.refs_8_) | copy-start | bytes 589828
  29.9 18.0 %copy-start.16 = (bf16[384,384]{1,0:T(8,128)(2,1)}, bf16[384,384]{1,0:T(8,128)(2,1)S(1)}, u32[]{:S(2)}) copy-start(bf16[384,384]{1,0:T(8,128)(2,1)S(1)} %collective-permute-done.rest_1_.refs_1_) | copy-start | bytes 884740
  30.8 17.1 %copy-start.17 = (bf16[384,384]{1,0:T(8,128)(2,1)}, bf16[384,384]{1,0:T(8,128)(2,1)S(1)}, u32[]{:S(2)}) copy-start(bf16[384,384]{1,0:T(8,128)(2,1)S(1)} %collective-permute-done.1.rest_2_.refs_2_) | copy-start | bytes 884740
  30.8 5.6 %collective-permute-start.2 = (bf16[384,384]{1,0:T(8,128)(2,1)S(1)}, bf16[384,384]{1,0:T(8,128)(2,1)S(1)}, u32[]{:S(2)}, u32[]{:S(2)}) collective-permute-start(bf16[384,384]{1,0:T(8,128)(2,1)S(1)} %collective-permute-done.1.rest_2_.refs_2_), channel_id=1, source_target_pairs={{0,1},{1,0},{2,3},{3,2},{4,5},{5,4},{6,7},{7,6},{8,9},{9,8},{10,11... | collective-permute-start | bytes 884744 | tf_op jit(solution)/shard_map/ppermute | solution.py:1016
  31.2 4.5 %collective-permute-start.3 = (bf16[384,256]{1,0:T(8,128)(2,1)S(1)}, bf16[384,256]{1,0:T(8,128)(2,1)S(1)}, u32[]{:S(2)}, u32[]{:S(2)}) collective-permute-start(bf16[384,256]{1,0:T(8,128)(2,1)S(1)} %slice.31.rest_0_.refs_8_), channel_id=1, source_target_pairs={{0,16},{8,24},{16,0},{24,8},{1,17},{9,25},{17,1},{25,9},{2,18},{10... | collective-permute-start | bytes 589832 | tf_op jit(solution)/shard_map/ppermute | solution.py:1016
  36.4 25.4 %all-to-all-start.1 = ((bf16[8,96,640]{2,1,0:T(8,128)(2,1)}), bf16[8,96,640]{2,1,0:T(8,128)(2,1)S(1)}, u32[]{:S(2)}, u32[]{:S(2)}) async-start(bf16[8,96,640]{2,1,0:T(8,128)(2,1)} %shard_map.275), calls=%async_computation.1 | async-start | bytes 1966080 | tf_op jit(solution)/shard_map/all_to_all | solution.py:1024
  40.0 6.1 %collective-permute-start.4 = (bf16[384,384]{1,0:T(8,128)(2,1)S(1)}, bf16[384,384]{1,0:T(8,128)(2,1)S(1)}, u32[]{:S(2)}, u32[]{:S(2)}) collective-permute-start(bf16[384,384]{1,0:T(8,128)(2,1)S(1)} %slice.30.rest_0_.refs_0_), channel_id=1, source_target_pairs={{0,8},{8,0},{16,24},{24,16},{1,9},{9,1},{17,25},{25,17},{2,10},{10... | collective-permute-start | bytes 884744 | tf_op jit(solution)/shard_map/ppermute | solution.py:1016
  44.0 2.9 %collective-permute-start.5 = (bf16[384,384]{1,0:T(8,128)(2,1)S(1)}, bf16[384,384]{1,0:T(8,128)(2,1)S(1)}, u32[]{:S(2)}, u32[]{:S(2)}) collective-permute-start(bf16[384,384]{1,0:T(8,128)(2,1)S(1)} %collective-permute-done.rest_1_.refs_1_), channel_id=1, source_target_pairs={{0,8},{8,0},{16,24},{24,16},{1,9},{9,1},{17,25},{25,17},{2,10},{10... | collective-permute-start | bytes 884744 | tf_op jit(solution)/shard_map/ppermute | solution.py:1016
  44.1 3.1 %collective-permute-start.6 = (bf16[384,384]{1,0:T(8,128)(2,1)S(1)}, bf16[384,384]{1,0:T(8,128)(2,1)S(1)}, u32[]{:S(2)}, u32[]{:S(2)}) collective-permute-start(bf16[384,384]{1,0:T(8,128)(2,1)S(1)} %collective-permute-done.1.rest_2_.refs_2_), channel_id=1, source_target_pairs={{0,8},{8,0},{16,24},{24,16},{1,9},{9,1},{17,25},{25,17},{2,10},{10... | collective-permute-start | bytes 884744 | tf_op jit(solution)/shard_map/ppermute | solution.py:1016
  44.5 3.4 %collective-permute-start.7 = (bf16[384,384]{1,0:T(8,128)(2,1)S(1)}, bf16[384,384]{1,0:T(8,128)(2,1)S(1)}, u32[]{:S(2)}, u32[]{:S(2)}) collective-permute-start(bf16[384,384]{1,0:T(8,128)(2,1)S(1)} %collective-permute-done.2.rest_3_.refs_3_), channel_id=1, source_target_pairs={{0,8},{8,0},{16,24},{24,16},{1,9},{9,1},{17,25},{25,17},{2,10},{10... | collective-permute-start | bytes 884744 | tf_op jit(solution)/shard_map/ppermute | solution.py:1016
  44.6 16.5 %collective-permute-start.8 = (bf16[384,256]{1,0:T(8,128)(2,1)S(1)}, bf16[384,256]{1,0:T(8,128)(2,1)S(1)}, u32[]{:S(2)}, u32[]{:S(2)}) collective-permute-start(bf16[384,256]{1,0:T(8,128)(2,1)S(1)} %slice.31.rest_0_.refs_8_), channel_id=1, source_target_pairs={{0,1},{1,0},{2,3},{3,2},{4,5},{5,4},{6,7},{7,6},{8,9},{9,8},{10,11... | collective-permute-start | bytes 589832 | tf_op jit(solution)/shard_map/ppermute | solution.py:1016
  46.1 20.7 %collective-permute-start.10 = (bf16[384,256]{1,0:T(8,128)(2,1)S(1)}, bf16[384,256]{1,0:T(8,128)(2,1)}, u32[]{:S(2)}, u32[]{:S(2)}) collective-permute-start(bf16[384,256]{1,0:T(8,128)(2,1)S(1)} %slice.31.rest_0_.refs_8_), channel_id=1, source_target_pairs={{0,8},{8,0},{16,24},{24,16},{1,9},{9,1},{17,25},{25,17},{2,10},{10... | collective-permute-start | bytes 589832 | tf_op jit(solution)/shard_map/ppermute | solution.py:1016
  46.9 14.9 %collective-permute-start.9 = (bf16[384,256]{1,0:T(8,128)(2,1)}, bf16[384,256]{1,0:T(8,128)(2,1)}, u32[]{:S(2)}, u32[]{:S(2)}) collective-permute-start(bf16[384,256]{1,0:T(8,128)(2,1)} %copy-done.23), channel_id=1, source_target_pairs={{0,1},{1,0},{2,3},{3,2},{4,5},{5,4},{6,7},{7,6},{8,9},{9,8},{10,11... | collective-permute-start | bytes 589832 | tf_op jit(solution)/shard_map/ppermute | solution.py:1016
  47.2 19.6 %collective-permute-start.12 = (bf16[384,256]{1,0:T(8,128)(2,1)}, bf16[384,256]{1,0:T(8,128)(2,1)}, u32[]{:S(2)}, u32[]{:S(2)}) collective-permute-start(bf16[384,256]{1,0:T(8,128)(2,1)} %copy-done.23), channel_id=1, source_target_pairs={{0,8},{8,0},{16,24},{24,16},{1,9},{9,1},{17,25},{25,17},{2,10},{10... | collective-permute-start | bytes 589832 | tf_op jit(solution)/shard_map/ppermute | solution.py:1016
  61.9 5.0 %collective-permute-start.11 = (bf16[384,256]{1,0:T(8,128)(2,1)}, bf16[384,256]{1,0:T(8,128)(2,1)S(1)}, u32[]{:S(2)}, u32[]{:S(2)}) collective-permute-start(bf16[384,256]{1,0:T(8,128)(2,1)} %copy-done.24), channel_id=1, source_target_pairs={{0,8},{8,0},{16,24},{24,16},{1,9},{9,1},{17,25},{25,17},{2,10},{10... | collective-permute-start | bytes 589832 | tf_op jit(solution)/shard_map/ppermute | solution.py:1016
  65.4 1.7 collective-permute-start.13
  65.4 13.8 %copy-start.6 = (bf16[768,256]{1,0:T(8,128)(2,1)}, bf16[768,256]{1,0:T(8,128)(2,1)S(1)}, u32[]{:S(2)}) copy-start(bf16[768,256]{1,0:T(8,128)(2,1)S(1)} %slice.33.rest_0_.refs_18_) | copy-start | bytes 1179652
  65.5 13.0 %collective-permute-start.14 = (bf16[768,256]{1,0:T(8,128)(2,1)S(1)}, bf16[768,256]{1,0:T(8,128)(2,1)S(1)}, u32[]{:S(2)}, u32[]{:S(2)}) collective-permute-start(bf16[768,256]{1,0:T(8,128)(2,1)S(1)} %slice.33.rest_0_.refs_18_), channel_id=1, source_target_pairs={{0,16},{8,24},{16,0},{24,8},{1,17},{9,25},{17,1},{25,9},{2,18},{10... | collective-permute-start | bytes 1179656 | tf_op jit(solution)/shard_map/ppermute | solution.py:1016
  66.8 11.6 %copy-start.5 = (bf16[768,384]{1,0:T(8,128)(2,1)}, bf16[768,384]{1,0:T(8,128)(2,1)S(1)}, u32[]{:S(2)}) copy-start(bf16[768,384]{1,0:T(8,128)(2,1)S(1)} %slice.32.rest_0_.refs_16_) | copy-start | bytes 1769476
  78.4 13.6 %copy-start.12 = (bf16[768,256]{1,0:T(8,128)(2,1)}, bf16[768,256]{1,0:T(8,128)(2,1)S(1)}, u32[]{:S(2)}) copy-start(bf16[768,256]{1,0:T(8,128)(2,1)S(1)} %collective-permute-done.14.rest_1_.refs_19_) | copy-start | bytes 1179652
  78.4 2.4 collective-permute-start.15
  79.2 12.7 %collective-permute-start.16 = (bf16[768,256]{1,0:T(8,128)(2,1)S(1)}, bf16[768,256]{1,0:T(8,128)(2,1)S(1)}, u32[]{:S(2)}, u32[]{:S(2)}) collective-permute-start(bf16[768,256]{1,0:T(8,128)(2,1)S(1)} %slice.33.rest_0_.refs_18_), channel_id=1, source_target_pairs={{0,8},{8,0},{16,24},{24,16},{1,9},{9,1},{17,25},{25,17},{2,10},{10... | collective-permute-start | bytes 1179656 | tf_op jit(solution)/shard_map/ppermute | solution.py:1016
  79.3 12.6 %collective-permute-start.17 = (bf16[768,256]{1,0:T(8,128)(2,1)S(1)}, bf16[768,256]{1,0:T(8,128)(2,1)S(1)}, u32[]{:S(2)}, u32[]{:S(2)}) collective-permute-start(bf16[768,256]{1,0:T(8,128)(2,1)S(1)} %collective-permute-done.14.rest_1_.refs_19_), channel_id=1, source_target_pairs={{0,8},{8,0},{16,24},{24,16},{1,9},{9,1},{17,25},{25,17},{2,10},{10... | collective-permute-start | bytes 1179656 | tf_op jit(solution)/shard_map/ppermute | solution.py:1016
  108.2 15.3 %all-to-all-start.2 = ((bf16[8,2,8,1664]{3,2,1,0:T(8,128)(2,1)}), bf16[8,2,8,1664]{3,2,1,0:T(8,128)(2,1)S(1)}, u32[]{:S(2)}, u32[]{:S(2)}) async-start(bf16[8,2,8,1664]{3,2,1,0:T(8,128)(2,1)} %get-tuple-element.140), calls=%async_computation.2 | async-start | bytes 851968 | tf_op jit(solution)/shard_map/all_to_all | solution.py:1162
  123.5 15.7 %collective-permute-start.18 = (bf16[8,2,8,1664]{3,2,1,0:T(8,128)(2,1)S(1)}, bf16[8,2,8,1664]{3,2,1,0:T(8,128)(2,1)S(1)}, u32[]{:S(2)}, u32[]{:S(2)}) collective-permute-start(bf16[8,2,8,1664]{3,2,1,0:T(8,128)(2,1)S(1)} %all-to-all-done.2.part_ref.refs_0_), channel_id=1, source_target_pairs={{0,16},{8,24},{16,0},{24,8},{1,17},{9,25},{17,1},{25,9},{2,18},{10... | collective-permute-start | bytes 1277960 | tf_op jit(solution)/shard_map/ppermute | solution.py:1016
  140.1 13.3 %all-to-all-start.3 = ((bf16[8,2,8,1536]{3,2,1,0:T(8,128)(2,1)}), bf16[8,2,8,1536]{3,2,1,0:T(8,128)(2,1)S(1)}, u32[]{:S(2)}, u32[]{:S(2)}) async-start(bf16[8,2,8,1536]{3,2,1,0:T(8,128)(2,1)} %get-tuple-element.147), calls=%async_computation.3 | async-start | bytes 786432 | tf_op jit(solution)/shard_map/all_to_all | solution.py:1172
  144.4 31.1 %collective-permute-start.19 = (bf16[2,64,512]{2,1,0:T(8,128)(2,1)}, bf16[2,64,512]{2,1,0:T(8,128)(2,1)S(1)}, u32[]{:S(2)}, u32[]{:S(2)}) collective-permute-start(bf16[2,64,512]{2,1,0:T(8,128)(2,1)} %get-tuple-element.181.refs_12_), channel_id=1, source_target_pairs={{0,16},{8,24},{16,0},{24,8},{1,17},{9,25},{17,1},{25,9},{2,18},{10... | collective-permute-start | bytes 393224 | tf_op jit(solution)/shard_map/ppermute | solution.py:1016
  145.1 65.7 %collective-permute-start.21 = (bf16[2,64,3072]{2,1,0:T(8,128)(2,1)}, bf16[2,64,3072]{2,1,0:T(8,128)(2,1)}, u32[]{:S(2)}, u32[]{:S(2)}) collective-permute-start(bf16[2,64,3072]{2,1,0:T(8,128)(2,1)} %get-tuple-element.177.refs_4_), channel_id=1, source_target_pairs={{0,16},{8,24},{16,0},{24,8},{1,17},{9,25},{17,1},{25,9},{2,18},{10... | collective-permute-start | bytes 2359304 | tf_op jit(solution)/shard_map/ppermute | solution.py:1016
  145.8 65.0 %collective-permute-start.22 = (bf16[2,64,3072]{2,1,0:T(8,128)(2,1)}, bf16[2,64,3072]{2,1,0:T(8,128)(2,1)}, u32[]{:S(2)}, u32[]{:S(2)}) collective-permute-start(bf16[2,64,3072]{2,1,0:T(8,128)(2,1)} %get-tuple-element.179.refs_8_), channel_id=1, source_target_pairs={{0,16},{8,24},{16,0},{24,8},{1,17},{9,25},{17,1},{25,9},{2,18},{10... | collective-permute-start | bytes 2359304 | tf_op jit(solution)/shard_map/ppermute | solution.py:1016
  175.5 40.2 %copy-start.28 = (bf16[2,64,512]{2,1,0:T(8,128)(2,1)}, bf16[2,64,512]{2,1,0:T(8,128)(2,1)S(1)}, u32[]{:S(2)}) copy-start(bf16[2,64,512]{2,1,0:T(8,128)(2,1)S(1)} %collective-permute-done.19.refs_13_) | copy-start | bytes 393220
  207.1 5.7 %collective-permute-start.20 = (bf16[8,352,128]{2,1,0:T(8,128)(2,1)}, bf16[8,352,128]{2,1,0:T(8,128)(2,1)S(1)}, u32[]{:S(2)}, u32[]{:S(2)}) collective-permute-start(bf16[8,352,128]{2,1,0:T(8,128)(2,1)} %get-tuple-element.157), channel_id=1, source_target_pairs={{0,8},{8,0},{16,24},{24,16},{1,9},{9,1},{17,25},{25,17},{2,10},{10... | collective-permute-start | bytes 2162696 | tf_op jit(solution)/shard_map/ppermute | solution.py:1016
  214.2 17.6 %collective-permute-start.23 = (bf16[8,176,128]{2,1,0:T(8,128)(2,1)S(1)}, bf16[8,176,128]{2,1,0:T(8,128)(2,1)S(1)}, u32[]{:S(2)}, u32[]{:S(2)}) collective-permute-start(bf16[8,176,128]{2,1,0:T(8,128)(2,1)S(1)} %constant_dynamic-slice_fusion), channel_id=1, source_target_pairs={{0,16},{8,24},{16,0},{24,8},{1,17},{9,25},{17,1},{25,9},{2,18},{10... | collective-permute-start | bytes 1081352 | tf_op jit(solution)/shard_map/ppermute | solution.py:1016
  215.0 22.1 %collective-permute-start.24 = (bf16[8,2,8,1664]{3,2,1,0:T(8,128)(2,1)S(1)}, bf16[8,2,8,1664]{3,2,1,0:T(8,128)(2,1)}, u32[]{:S(2)}, u32[]{:S(2)}) collective-permute-start(bf16[8,2,8,1664]{3,2,1,0:T(8,128)(2,1)S(1)} %copy-done.1), channel_id=1, source_target_pairs={{0,8},{8,0},{16,24},{24,16},{1,9},{9,1},{17,25},{25,17},{2,10},{10... | collective-permute-start | bytes 1277960 | tf_op jit(solution)/shard_map/ppermute | solution.py:1016
  215.6 16.6 %collective-permute-start.30 = (bf16[2,64,512]{2,1,0:T(8,128)(2,1)S(1)}, bf16[2,64,512]{2,1,0:T(8,128)(2,1)S(1)}, u32[]{:S(2)}, u32[]{:S(2)}) collective-permute-start(bf16[2,64,512]{2,1,0:T(8,128)(2,1)S(1)} %copy-done.27), channel_id=1, source_target_pairs={{0,8},{8,0},{16,24},{24,16},{1,9},{9,1},{17,25},{25,17},{2,10},{10... | collective-permute-start | bytes 393224 | tf_op jit(solution)/shard_map/ppermute | solution.py:1016
  215.7 16.6 %collective-permute-start.31 = (bf16[2,64,512]{2,1,0:T(8,128)(2,1)S(1)}, bf16[2,64,512]{2,1,0:T(8,128)(2,1)S(1)}, u32[]{:S(2)}, u32[]{:S(2)}) collective-permute-start(bf16[2,64,512]{2,1,0:T(8,128)(2,1)S(1)} %collective-permute-done.19.refs_13_), channel_id=1, source_target_pairs={{0,8},{8,0},{16,24},{24,16},{1,9},{9,1},{17,25},{25,17},{2,10},{10... | collective-permute-start | bytes 393224 | tf_op jit(solution)/shard_map/ppermute | solution.py:1016
  231.8 7.4 %collective-permute-start.26 = (bf16[2,64,3072]{2,1,0:T(8,128)(2,1)}, bf16[2,64,3072]{2,1,0:T(8,128)(2,1)}, u32[]{:S(2)}, u32[]{:S(2)}) collective-permute-start(bf16[2,64,3072]{2,1,0:T(8,128)(2,1)} %get-tuple-element.177.refs_4_), channel_id=1, source_target_pairs={{0,8},{8,0},{16,24},{24,16},{1,9},{9,1},{17,25},{25,17},{2,10},{10... | collective-permute-start | bytes 2359304 | tf_op jit(solution)/shard_map/ppermute | solution.py:1016
  231.8 7.3 %collective-permute-start.27 = (bf16[2,64,3072]{2,1,0:T(8,128)(2,1)}, bf16[2,64,3072]{2,1,0:T(8,128)(2,1)}, u32[]{:S(2)}, u32[]{:S(2)}) collective-permute-start(bf16[2,64,3072]{2,1,0:T(8,128)(2,1)} %collective-permute-done.21.refs_5_), channel_id=1, source_target_pairs={{0,8},{8,0},{16,24},{24,16},{1,9},{9,1},{17,25},{25,17},{2,10},{10... | collective-permute-start | bytes 2359304 | tf_op jit(solution)/shard_map/ppermute | solution.py:1016
  232.3 6.9 %collective-permute-start.28 = (bf16[2,64,3072]{2,1,0:T(8,128)(2,1)}, bf16[2,64,3072]{2,1,0:T(8,128)(2,1)}, u32[]{:S(2)}, u32[]{:S(2)}) collective-permute-start(bf16[2,64,3072]{2,1,0:T(8,128)(2,1)} %get-tuple-element.179.refs_8_), channel_id=1, source_target_pairs={{0,8},{8,0},{16,24},{24,16},{1,9},{9,1},{17,25},{25,17},{2,10},{10... | collective-permute-start | bytes 2359304 | tf_op jit(solution)/shard_map/ppermute | solution.py:1016
  232.4 6.8 %collective-permute-start.29 = (bf16[2,64,3072]{2,1,0:T(8,128)(2,1)}, bf16[2,64,3072]{2,1,0:T(8,128)(2,1)}, u32[]{:S(2)}, u32[]{:S(2)}) collective-permute-start(bf16[2,64,3072]{2,1,0:T(8,128)(2,1)} %collective-permute-done.22.refs_9_), channel_id=1, source_target_pairs={{0,8},{8,0},{16,24},{24,16},{1,9},{9,1},{17,25},{25,17},{2,10},{10... | collective-permute-start | bytes 2359304 | tf_op jit(solution)/shard_map/ppermute | solution.py:1016
  233.6 14.6 %all-to-all-start.4 = ((bf16[8,176,128]{2,1,0:T(8,128)(2,1)}), bf16[8,176,128]{2,1,0:T(8,128)(2,1)S(1)}, u32[]{:S(2)}, u32[]{:S(2)}) async-start(bf16[8,176,128]{2,1,0:T(8,128)(2,1)} %add_convert_fusion.1), calls=%async_computation.4 | async-start | bytes 720896 | tf_op jit(solution)/shard_map/all_to_all | solution.py:1049
  237.1 16.1 %copy-start.2 = (bf16[8,197,768]{2,1,0:T(8,128)(2,1)S(1)}, bf16[8,197,768]{2,1,0:T(8,128)(2,1)}, u32[]{:S(2)}) copy-start(bf16[8,197,768]{2,1,0:T(8,128)(2,1)} %get-tuple-element.158) | copy-start | bytes 7262212
  237.1 2.0 collective-permute-start.25
  248.3 3.0 %collective-permute-start.32 = (bf16[176,128]{1,0:T(8,128)(2,1)S(1)}, bf16[176,128]{1,0:T(8,128)(2,1)S(1)}, u32[]{:S(2)}, u32[]{:S(2)}) collective-permute-start(bf16[176,128]{1,0:T(8,128)(2,1)S(1)} %reduce_sum.12), channel_id=1, source_target_pairs={{0,16},{8,24},{16,0},{24,8},{1,17},{9,25},{17,1},{25,9},{2,18},{10... | collective-permute-start | bytes 135176 | tf_op jit(solution)/shard_map/ppermute | solution.py:1016
  251.3 3.8 %collective-permute-start.33 = (bf16[352,128]{1,0:T(8,128)(2,1)S(1)}, bf16[352,128]{1,0:T(8,128)(2,1)S(1)}, u32[]{:S(2)}, u32[]{:S(2)}) collective-permute-start(bf16[352,128]{1,0:T(8,128)(2,1)S(1)} %maximum_select_fusion.1), channel_id=1, source_target_pairs={{0,8},{8,0},{16,24},{24,16},{1,9},{9,1},{17,25},{25,17},{2,10},{10... | collective-permute-start | bytes 270344 | tf_op jit(solution)/shard_map/ppermute | solution.py:1016
  (22 other events, 57.2 us)

commit v6 on v5

--- a/solution.py
+++ b/solution.py
@@ -175,13 +175,6 @@
         out_ref[shard] = mine
 
 
-def head_mask(value):
-    lane = lax.broadcasted_iota(jnp.int32, (1, LANES), 1)
-    low = jnp.where(lane < HEAD_DIM, value, 0.0).astype(BF16)
-    high = jnp.where(lane < HEAD_DIM, 0.0, value).astype(BF16)
-    return low, high
-
-
 def each_head(columns, value):
     head = lax.broadcasted_iota(jnp.int32, (1, GROUP), 1) // HEAD_DIM
     return jnp.concatenate(
@@ -318,6 +311,7 @@
     base = both[:, LANES:]
     ur_ref[...] = ur.reshape(ur_ref.shape)
     cot = pad_rows(pad_b, cot_ref)
+    firsts = []
     for slot in range(n_img):
         rows = slice(slot * total, (slot + 1) * total)
         living = (first + slot < count_ref[0]).astype(F32)
@@ -331,6 +325,8 @@
         disp_ref[slot] = disp
         comb_ref[slot] = comb
         upstream = (cot[rows] * living).astype(BF16)
+        firsts.append((rows, disp, comb, upstream))
+    for slot, (rows, disp, comb, upstream) in enumerate(firsts):
         sent = jnp.concatenate(
             [
                 dot(disp.astype(BF16), h2[rows]),
@@ -488,7 +484,7 @@
     x2 = flat(x2_ref)
     unit, scale = normalise(x2)
     h2 = unit.astype(BF16)
-    pairs, belows, upstreams = [], [], []
+    pairs, belows, upstreams, mixes, firsts = [], [], [], [], []
     for slot in range(n_img):
         rows = slice(slot * total, (slot + 1) * total)
         living = (first + slot < count_ref[0]).astype(F32)
@@ -503,19 +499,19 @@
         yexp, gslot = back[:, :width], back[:, width:]
         gcomb = dot(yexp, upstream.astype(BF16), NT)
         gdisp = dot(gslot, h2[rows], NT)
+        firsts.append((rows, living, disp, comb, yexp, gslot, gcomb, gdisp))
+    for slot, (rows, living, disp, comb, yexp, gslot, gcomb, gdisp) in enumerate(firsts):
         glog = (
             disp * (gdisp - jnp.sum(gdisp * disp, axis=1, keepdims=True))
             + comb * (gcomb - jnp.sum(gcomb * comb, axis=0, keepdims=True))
         )
         acc_rb[...] += dot(glog.astype(BF16), ur_ref[slot])
         three = jnp.concatenate([disp, glog, comb], axis=0).T.astype(BF16)
-        mixed = dot(three[:, 2 * n_exp :], yexp)
-        block_ref[slot] = (living * (x2[rows] + mixed)).astype(BF16)[:n_tok]
+        mixes.append((living, three[:, 2 * n_exp :], yexp, rows))
         pairs.append(three[:, : 2 * n_exp])
         belows.append(jnp.concatenate([route_ref[...], gslot, wrt_ref[...]], axis=0))
     glog_rows = jnp.concatenate([pair[:, n_exp:] for pair in pairs], axis=0)
     gur = select_rows(dot(glog_rows, rb_ref[...]), index_ref, first, n_img)
-    acc_ra[...] += dot(gur, h2, TN)
     gh2 = jnp.concatenate(
         [
             dot(jnp.concatenate([gur[i * total : (i + 1) * total], pairs[i]], axis=1), belows[i])
@@ -526,13 +522,16 @@
     gx2 = jnp.concatenate(upstreams, axis=0) + normalise_back(unit, scale, gh2)
     gbr = gx2.astype(BF16)
     gx2_ref[...] = gbr.reshape(gx2_ref.shape)
-    acc_ob[...] += dot(flat(uo_ref), gbr, TN)
     both = dot(gbr, out_ref[...])
     guo = select_rows(both[:, width:], index_ref, first, n_img)
     att = jnp.concatenate([flat(att0), flat(att1), flat(att2)], axis=1)
-    acc_oa[...] += dot(guo, att, TN)
     gatt = (both[:, :width] + dot(guo, first_ref[...])).astype(BF16)
     gatt_ref[...] = gatt.reshape(gatt_ref.shape)
+    acc_ra[...] += dot(gur, h2, TN)
+    acc_ob[...] += dot(flat(uo_ref), gbr, TN)
+    acc_oa[...] += dot(guo, att, TN)
+    for slot, (living, left, yexp, rows) in enumerate(mixes):
+        block_ref[slot] = (living * (x2[rows] + dot(left, yexp))).astype(BF16)[:n_tok]
 
     @pl.when(pl.program_id(0) == pl.num_programs(0) - 1)
     def _():
@@ -555,32 +554,34 @@
 
 
 def attention_backward(qkv, gatt, prob_ref, slot):
-    keep = head_mask(1.0)
+    total = qkv.shape[0]
+    heads = GROUP // HEAD_DIM
+    every = dot(each_head(qkv[:, 2 * GROUP :], 1.0), gatt, NT)
+    gscores = []
+    for head in range(heads):
+        probs = prob_ref[slot, head].astype(F32)
+        gprobs = every[head * total : (head + 1) * total]
+        inner = jnp.sum(gprobs * probs, axis=0, keepdims=True)
+        gscores.append((probs * (gprobs - inner)).astype(BF16))
+
+    def products(lefts, right):
+        outs = []
+        for pair in range(heads // 2):
+            both = dot(
+                jnp.concatenate(lefts[2 * pair : 2 * pair + 2], axis=0),
+                right[:, pair * LANES : (pair + 1) * LANES],
+            )
+            outs.append(merge_pair(both[:total], both[total:]))
+        return outs
+
+    gv = [part.astype(BF16) for part in products([prob_ref[slot, head] for head in range(heads)], gatt)]
+    gk = [(part * 0.125).astype(BF16) for part in products(gscores, qkv[:, :GROUP])]
     key_t = qkv[:, GROUP : 2 * GROUP].T
-    total = qkv.shape[0]
-    gq_parts, gk_parts, gv_parts = [], [], []
-    for pair in range(GROUP // LANES):
-        span = slice(pair * LANES, (pair + 1) * LANES)
-        q_pair, ga_pair = qkv[:, span], gatt[:, span]
-        v_pair = qkv[:, 2 * GROUP + pair * LANES : 2 * GROUP + (pair + 1) * LANES]
-        lows = [prob_ref[slot, 2 * pair], prob_ref[slot, 2 * pair + 1]]
-        gv = dot(jnp.concatenate(lows, axis=0), ga_pair)
-        gprobs = dot(jnp.concatenate([v_pair * keep[0], v_pair * keep[1]], axis=0), ga_pair, NT)
-        gscores = []
-        for side in range(2):
-            probs = lows[side].astype(F32)
-            gprob = gprobs[side * total : (side + 1) * total]
-            inner = jnp.sum(gprob * probs, axis=0, keepdims=True)
-            gscores.append((probs * (gprob - inner)).astype(BF16))
-            head = 2 * pair + side
-            gq_parts.append(
-                (dot(key_t[head * HEAD_DIM : (head + 1) * HEAD_DIM], gscores[side]) * 0.125).astype(BF16)
-            )
-        gk = dot(jnp.concatenate(gscores, axis=0), q_pair)
-        gk_parts.append((merge_pair(gk[:total], gk[total:]) * 0.125).astype(BF16))
-        gv_parts.append(merge_pair(gv[:total], gv[total:]).astype(BF16))
-    gq = jnp.concatenate(gq_parts, axis=0).T
-    return jnp.concatenate([gq] + gk_parts + gv_parts, axis=1)
+    gq = [
+        (dot(key_t[head * HEAD_DIM : (head + 1) * HEAD_DIM], gscores[head]) * 0.125).astype(BF16)
+        for head in range(heads)
+    ]
+    return jnp.concatenate([jnp.concatenate(gq, axis=0).T] + gk + gv, axis=1)
 
 
 def attention_back_kernel(groups, place_ref, index_ref, *refs):

time: 258 us -> 247 us (0.957)
  Pallas kernels: 158 us -> 146 us
    pallas_call x13, Pallas kernels: 158 us -> 146 us  [call(): pl.pallas_call(kernel, out_shape=shapes, grid_spec=pltpu.PrefetchScalarGr...]
  transfers between devices with their start and end apart: 39 -> 39, of which waited for: 12 -> 12; matrix products, arithmetic and copies ran while one was open for 3% -> 3% of each run, Pallas kernels for 54% -> 53%
where the time goes in v6:
time: 247 us; the launch traced here: 246 us
  Pallas kernels  146 us (59%)
  starting transfers between devices  51.3 us (21%)
  waiting for transfers between devices  29.3 us (12%)
  local copies, waits for them, and re-layouts  14.3 us (6%)
  other arithmetic  2.82 us (1%)
    pallas_call x13, Pallas kernels, call(): pl.pallas_call(kernel, out_shape=shapes, grid_spec=pltpu.PrefetchScalarGr...  146 us
    ppermute x34, starting transfers between devices, swap(): return lax.ppermute(array, axis, [(i, i ^ bit) for i in range(size)])  31 us
    ppermute x34, waiting for transfers between devices, swap(): return lax.ppermute(array, axis, [(i, i ^ bit) for i in range(size)])  16.1 us
    unnamed x65, local copies, waits for them, and re-layouts  12.2 us
    all_to_all x2, starting transfers between devices, over_shard(): lax.all_to_all(spread, 'shard', split_axis=0, concat_axis=0, tiled=True,...  8.98 us
    all_to_all x1, waiting for transfers between devices, per_device(): back = lax.all_to_all(ret, 'shard', split_axis=0, concat_axis=0, tiled=True)  6.79 us
  transfers between devices with their start and end apart: 39, of which 12 were waited for; matrix products, arithmetic and copies ran while one was open for 3% of the time, Pallas kernels for 53%

profile of v6, /device:TPU:1, one launch (start us, length us, event | category | flops | bytes accessed | tf_op | source)
XLA Modules:
  0.0 245.9 jit_solution(10295608679608594235)
XLA Ops:
  1.3 2.8 %shard_map.274 = bf16[4,96,640]{2,1,0:T(8,128)(2,1)} custom-call(s32[3]{0:T(128)} %pad_add_fusion.place_ref, bf16[96,2304]{1,0:T(8,128)(2,1)} %qkv_ref.3, bf16[96,128]{1,0:T(8,128)(2,1)} %a_ref.1, bf16[288,128]{1,0:T(8,128)(2,1)} %bitcast.26, bf16[96,128]{1,0:T(8,128)(2,1)} %ao_ref.1, bf16[96,128]{1,0:T(8,128)(2,1)} %ra_ref.1, bf16[96,128]{1,0:T(8,128)(2,1)} %bitcast.27, ...), custom_call_target="tpu_custom_call" | custom-call | flops 221184 | bytes 1108992 | tf_op jit(solution)/shard_map/pallas_call | solution.py:689
  4.0 5.4 %all-to-all-start = ((bf16[4,96,640]{2,1,0:T(8,128)(2,1)}), bf16[4,96,640]{2,1,0:T(8,128)(2,1)S(1)}, u32[]{:S(2)}, u32[]{:S(2)}) async-start(bf16[4,96,640]{2,1,0:T(8,128)(2,1)} %shard_map.274), calls=%async_computation | async-start | bytes 983040 | tf_op jit(solution)/shard_map/all_to_all | solution.py:1025
  9.4 2.8 %shard_map.275 = bf16[8,96,640]{2,1,0:T(8,128)(2,1)} custom-call(s32[3]{0:T(128)} %pad_add_fusion.place_ref, bf16[96,2304]{1,0:T(8,128)(2,1)} %qkv_ref.3, bf16[96,768]{1,0:T(8,128)(2,1)} %wo_ref.1, bf16[2,128]{1,0:T(2,128)(2,1)} %bitcast.29), custom_call_target="tpu_custom_call" | custom-call | flops 73728 | bytes 1573376 | tf_op jit(solution)/shard_map/pallas_call | solution.py:689
  12.3 1.9 copy.31.image_ref
  14.6 1.9 copy.32._.cot_ref
  16.5 3.7 %shard_map.276.h1_ref.refs_8_ = bf16[8,208,768]{2,1,0:T(8,128)(2,1)} custom-call(bf16[8,197,768]{2,1,0:T(8,128)(2,1)} %copy.31.image_ref, bf16[8,197,768]{2,1,0:T(8,128)(2,1)} %copy.32._.cot_ref), custom_call_target="tpu_custom_call" | custom-call | flops 9682944 | bytes 7397376 | tf_op jit(solution)/shard_map/pallas_call | solution.py:689
  20.2 2.6 %all-to-all-done = bf16[4,96,640]{2,1,0:T(8,128)(2,1)S(1)} async-done(((bf16[4,96,640]{2,1,0:T(8,128)(2,1)}), bf16[4,96,640]{2,1,0:T(8,128)(2,1)S(1)}, u32[]{:S(2)}, u32[]{:S(2)}) %all-to-all-start) | async-done | bytes 491552 | tf_op jit(solution)/shard_map/all_to_all | solution.py:1025
  22.8 1.3 collective-permute-start
  24.1 1.2 collective-permute-start.1
  25.3 4.6 %collective-permute-done.rest_1_.refs_1_ = bf16[384,384]{1,0:T(8,128)(2,1)S(1)} collective-permute-done((bf16[384,384]{1,0:T(8,128)(2,1)S(1)}, bf16[384,384]{1,0:T(8,128)(2,1)S(1)}, u32[]{:S(2)}, u32[]{:S(2)}) %collective-permute-start) | collective-permute-done | bytes 294944 | tf_op jit(solution)/shard_map/ppermute | solution.py:1017
  29.9 0.9 collective-permute-done.1.rest_2_.refs_2_
  31.2 1.2 collective-permute-start.3
  32.4 3.3 %collective-permute-done.3.rest_2_.refs_10_ = bf16[384,256]{1,0:T(8,128)(2,1)S(1)} collective-permute-done((bf16[384,256]{1,0:T(8,128)(2,1)S(1)}, bf16[384,256]{1,0:T(8,128)(2,1)S(1)}, u32[]{:S(2)}, u32[]{:S(2)}) %collective-permute-start.3) | collective-permute-done | bytes 196640 | tf_op jit(solution)/shard_map/ppermute | solution.py:1017
  36.4 3.6 %all-to-all-start.1 = ((bf16[8,96,640]{2,1,0:T(8,128)(2,1)}), bf16[8,96,640]{2,1,0:T(8,128)(2,1)S(1)}, u32[]{:S(2)}, u32[]{:S(2)}) async-start(bf16[8,96,640]{2,1,0:T(8,128)(2,1)} %shard_map.275), calls=%async_computation.1 | async-start | bytes 1966080 | tf_op jit(solution)/shard_map/all_to_all | solution.py:1025
  40.0 4.0 %collective-permute-start.4 = (bf16[384,384]{1,0:T(8,128)(2,1)S(1)}, bf16[384,384]{1,0:T(8,128)(2,1)S(1)}, u32[]{:S(2)}, u32[]{:S(2)}) collective-permute-start(bf16[384,384]{1,0:T(8,128)(2,1)S(1)} %slice.30.rest_0_.refs_0_), channel_id=1, source_target_pairs={{0,8},{8,0},{16,24},{24,16},{1,9},{9,1},{17,25},{25,17},{2,10},{10... | collective-permute-start | bytes 884744 | tf_op jit(solution)/shard_map/ppermute | solution.py:1017
  44.6 1.5 collective-permute-start.8
  46.1 0.8 collective-permute-start.10
  48.7 12.5 %shard_map.277 = (bf16[8,208,768]{2,1,0:T(8,128)(2,1)}, bf16[8,208,256]{2,1,0:T(8,128)(2,1)}, bf16[8,4,208,208]{3,2,1,0:T(8,128)(2,1)}, bf16[8,208,128]{2,1,0:T(...) custom-call(s32[3]{0:T(128)} %pad_add_fusion.place_ref, ...), custom_call_target="tpu_custom_call" | custom-call | flops 2317352960 | bytes 12697600 | tf_op jit(solution)/shard_map/pallas_call | solution.py:689
  61.9 3.6 %collective-permute-start.11 = (bf16[384,256]{1,0:T(8,128)(2,1)}, bf16[384,256]{1,0:T(8,128)(2,1)S(1)}, u32[]{:S(2)}, u32[]{:S(2)}) collective-permute-start(bf16[384,256]{1,0:T(8,128)(2,1)} %copy-done.24), channel_id=1, source_target_pairs={{0,8},{8,0},{16,24},{24,16},{1,9},{9,1},{17,25},{25,17},{2,10},{10... | collective-permute-start | bytes 589832 | tf_op jit(solution)/shard_map/ppermute | solution.py:1017
  65.5 1.3 collective-permute-start.14
  67.8 10.7 %shard_map.278 = (bf16[8,208,768]{2,1,0:T(8,128)(2,1)}, bf16[8,208,256]{2,1,0:T(8,128)(2,1)}, bf16[8,4,208,208]{3,2,1,0:T(8,128)(2,1)}, bf16[768,128]{1,0:T(8,128)(2,1)}, bf16[768,128]{1,0:T(8,128)(2,1)}) custom-call(s32[3]{0:T(128)} %pad_add_fusion.place_ref, bf16[8,208,768]{2,1,0:T(8,128)(2,1)} %shard_map.276.h1_ref.refs_8_, ...), custom_call_target="tpu_custom_call" | custom-call | flops 2317352960 | bytes 11714560 | tf_op jit(solution)/shard_map/pallas_call | solution.py:689
  78.4 0.8 collective-permute-start.15
  80.9 0.8 copy-done.9
  81.7 10.3 %shard_map.279 = (bf16[8,208,768]{2,1,0:T(8,128)(2,1)}, bf16[8,208,256]{2,1,0:T(8,128)(2,1)}, bf16[8,4,208,208]{3,2,1,0:T(8,128)(2,1)}) custom-call(s32[3]{0:T(128)} %pad_add_fusion.place_ref, bf16[8,208,768]{2,1,0:T(8,128)(2,1)} %shard_map.276.h1_ref.refs_8_, bf16[8,208,128]{2,1,0:T(8,128)(2,1)} %get-tuple-element.120.uq_ref.refs_7_, ...), custom_call_target="tpu_custom_call" | custom-call | flops 2317352960 | bytes 10928128 | tf_op jit(solution)/shard_map/pallas_call | solution.py:689
  92.9 14.2 %shard_map.280 = (f32[8,208,768]{2,1,0:T(8,128)}, bf16[8,208,128]{2,1,0:T(8,128)(2,1)}, bf16[8,208,128]{2,1,0:T(8,128)(2,1)}, f32[8,16,208]{2,1,0:T(8,128)}, f32...) custom-call(s32[3]{0:T(128)} %pad_add_fusion.place_ref, ...), custom_call_target="tpu_custom_call" | custom-call | flops 2944401408 | bytes 16388096 | tf_op jit(solution)/shard_map/pallas_call | solution.py:689
  107.0 3.7 %all-to-all-start.2 = ((bf16[8,2,8,1664]{3,2,1,0:T(8,128)(2,1)}), bf16[8,2,8,1664]{3,2,1,0:T(8,128)(2,1)S(1)}, u32[]{:S(2)}, u32[]{:S(2)}) async-start(bf16[8,2,8,1664]{3,2,1,0:T(8,128)(2,1)} %get-tuple-element.140), calls=%async_computation.2 | async-start | bytes 851968 | tf_op jit(solution)/shard_map/all_to_all | solution.py:1163
  110.7 7.8 %shard_map.281 = (bf16[2432,768]{1,0:T(8,128)(2,1)}, bf16[768,896]{1,0:T(8,128)(2,1)}, bf16[128,768]{1,0:T(8,128)(2,1)}, bf16[128,768]{1,0:T(8,128)(2,1)}) custom-call(s32[3]{0:T(128)} %pad_add_fusion.place_ref, bf16[768,128]{1,0:T(8,128)(2,1)} %get-tuple-element.129.ao_ref, bf16[768,128]{1,0:T(8,128)(2,1)} %get-tuple-element.130.bo_ref, ...), custom_call_target="tpu_custom_call" | custom-call | flops 4718592 | bytes 12779520 | tf_op jit(solution)/shard_map/pallas_call | solution.py:689
  118.5 3.8 %all-to-all-done.2.part_ref.refs_0_ = bf16[8,2,8,1664]{3,2,1,0:T(8,128)(2,1)S(1)} async-done(((bf16[8,2,8,1664]{3,2,1,0:T(8,128)(2,1)}), bf16[8,2,8,1664]{3,2,1,0:T(8,128)(2,1)S(1)}, u32[]{:S(2)}, u32[]{:S(2)}) %all-to-all-start.2) | async-done | bytes 426016 | tf_op jit(solution)/shard_map/all_to_all | solution.py:1163
  122.3 0.9 collective-permute-start.18
  123.2 14.9 %shard_map.282 = (bf16[8,2,8,1536]{3,2,1,0:T(8,128)(2,1)}, bf16[2,64,3072]{2,1,0:T(8,128)(2,1)}, bf16[2,64,3072]{2,1,0:T(8,128)(2,1)}, bf16[2,64,512]{2,1,0:T(8,128)(2,1)}) custom-call(bf16[2,768,3072]{2,1,0:T(8,128)(2,1)} %wu_ref.1, bf16[2,3072,768]{2,1,0:T(8,128)(2,1)} %wd_ref.1, bf16[2,768,128]{2,1,0:T(8,128)(2,1)} %ua_ref.1, ...), custom_call_target="tpu_custom_call" | custom-call | flops 2415919104 | bytes 25329664 | tf_op jit(solution)/shard_map/pallas_call | solution.py:689
  138.1 0.8 copy-done.10
  138.9 4.3 %all-to-all-start.3 = ((bf16[8,2,8,1536]{3,2,1,0:T(8,128)(2,1)}), bf16[8,2,8,1536]{3,2,1,0:T(8,128)(2,1)S(1)}, u32[]{:S(2)}, u32[]{:S(2)}) async-start(bf16[8,2,8,1536]{3,2,1,0:T(8,128)(2,1)} %get-tuple-element.147), calls=%async_computation.3 | async-start | bytes 786432 | tf_op jit(solution)/shard_map/all_to_all | solution.py:1173
  145.4 6.8 %all-to-all-done.3.ret_ref = bf16[8,2,8,1536]{3,2,1,0:T(8,128)(2,1)S(1)} async-done(((bf16[8,2,8,1536]{3,2,1,0:T(8,128)(2,1)}), bf16[8,2,8,1536]{3,2,1,0:T(8,128)(2,1)S(1)}, u32[]{:S(2)}, u32[]{:S(2)}) %all-to-all-start.3) | async-done | bytes 393248 | tf_op jit(solution)/shard_map/all_to_all | solution.py:1173
  152.9 17.6 %shard_map.283 = (bf16[8,197,768]{2,1,0:T(8,128)(2,1)}, bf16[8,208,768]{2,1,0:T(8,128)(2,1)}, bf16[8,208,768]{2,1,0:T(8,128)(2,1)}, bf16[8,320,128]{2,1,0:T(8,128)(2,1)}) custom-call(s32[8]{0:T(128)} %index_ref.7, s32[1]{0:T(128)S(6)} %copy.38.count_ref, bf16[8,197,768]{2,1,0:T(8,128)(2,1)} %copy.32._.cot_ref, f32[8,208,768]{2,1,0:T(8,128)} %get-tuple-element.135.x2_ref, ...), custom_call_target="tpu_custom_call" | custom-call | flops 3925868544 | bytes 21532672 | tf_op jit(solution)/shard_map/pallas_call | solution.py:689
  170.6 25.4 %shard_map.284 = (bf16[8,208,768]{2,1,0:T(8,128)(2,1)}, bf16[8,208,768]{2,1,0:T(8,128)(2,1)}, bf16[8,208,768]{2,1,0:T(8,128)(2,1)}, bf16[8,208,128]{2,1,0:T(8,12...) custom-call(s32[3]{0:T(128)} %pad_add_fusion.place_ref, s32[8]{0:T(128)} %index_ref.7, ...), custom_call_target="tpu_custom_call" | custom-call | flops 3639607296 | bytes 32292864 | tf_op jit(solution)/shard_map/pallas_call | solution.py:689
  196.0 3.7 %collective-permute-start.20 = (bf16[8,352,128]{2,1,0:T(8,128)(2,1)}, bf16[8,352,128]{2,1,0:T(8,128)(2,1)S(1)}, u32[]{:S(2)}, u32[]{:S(2)}) collective-permute-start(bf16[8,352,128]{2,1,0:T(8,128)(2,1)} %get-tuple-element.157), channel_id=1, source_target_pairs={{0,8},{8,0},{16,24},{24,16},{1,9},{9,1},{17,25},{25,17},{2,10},{10... | collective-permute-start | bytes 2162696 | tf_op jit(solution)/shard_map/ppermute | solution.py:1017
  199.8 2.0 collective-permute-done.20
  201.8 1.3 add_convert_fusion
  203.1 0.8 collective-permute-start.23
  205.1 15.6 %shard_map.285 = f32[9456,128]{1,0:T(8,128)} custom-call(bf16[8,197,768]{2,1,0:T(8,128)(2,1)} %copy.31.image_ref, bf16[8,208,768]{2,1,0:T(8,128)(2,1)} %get-tuple-element.167.gx2_ref, bf16[8,208,128]{2,1,0:T(8,128)(2,1)} %get-tuple-element.168.guq_ref, bf16[2432,768]{1,0:T(8,128)(2,1)} %get-tuple-element.169.turned_ref, ...), custom_call_target="tpu_custom_call" | custom-call | flops 6215958528 | bytes 21647360 | tf_op jit(solution)/shard_map/pallas_call | solution.py:689
  221.7 0.8 add_convert_fusion.1
  222.5 3.4 %all-to-all-start.4 = ((bf16[8,176,128]{2,1,0:T(8,128)(2,1)}), bf16[8,176,128]{2,1,0:T(8,128)(2,1)S(1)}, u32[]{:S(2)}, u32[]{:S(2)}) async-start(bf16[8,176,128]{2,1,0:T(8,128)(2,1)} %add_convert_fusion.1), calls=%async_computation.4 | async-start | bytes 720896 | tf_op jit(solution)/shard_map/all_to_all | solution.py:1050
  226.3 1.7 collective-permute-done.25.refs_3_
  228.8 8.4 %shard_map.286 = (f32[2,768,128]{2,1,0:T(8,128)}, f32[2,128,3072]{2,1,0:T(8,128)}, f32[2,3072,128]{2,1,0:T(8,128)}, f32[2,128,768]{2,1,0:T(8,128)}) custom-call(bf16[8,2,8,1664]{3,2,1,0:T(8,128)(2,1)} %copy-done, bf16[8,2,8,1664]{3,2,1,0:T(8,128)(2,1)} %copy-done.10, bf16[8,2,8,1664]{3,2,1,0:T(8,128)(2,1)} %collective-permute-done.24.refs_2_, ...), custom_call_target="tpu_custom_call" | custom-call | flops 805306368 | bytes 16384000 | tf_op jit(solution)/shard_map/pallas_call | solution.py:689
  237.2 0.8 collective-permute-start.32
  238.1 2.1 collective-permute-done.32
  240.2 1.9 collective-permute-start.33
  242.1 1.9 copy.37
  (122 shorter events, 16.3 us)
Async XLA Ops:
  4.0 18.7 %all-to-all-start = ((bf16[4,96,640]{2,1,0:T(8,128)(2,1)}), bf16[4,96,640]{2,1,0:T(8,128)(2,1)S(1)}, u32[]{:S(2)}, u32[]{:S(2)}) async-start(bf16[4,96,640]{2,1,0:T(8,128)(2,1)} %shard_map.274), calls=%async_computation | async-start | bytes 983040 | tf_op jit(solution)/shard_map/all_to_all | solution.py:1025
  22.8 25.1 %copy-start.7 = (bf16[384,384]{1,0:T(8,128)(2,1)}, bf16[384,384]{1,0:T(8,128)(2,1)S(1)}, u32[]{:S(2)}) copy-start(bf16[384,384]{1,0:T(8,128)(2,1)S(1)} %slice.30.rest_0_.refs_0_) | copy-start | bytes 884740
  22.8 7.1 %collective-permute-start = (bf16[384,384]{1,0:T(8,128)(2,1)S(1)}, bf16[384,384]{1,0:T(8,128)(2,1)S(1)}, u32[]{:S(2)}, u32[]{:S(2)}) collective-permute-start(bf16[384,384]{1,0:T(8,128)(2,1)S(1)} %slice.30.rest_0_.refs_0_), channel_id=1, source_target_pairs={{0,1},{1,0},{2,3},{3,2},{4,5},{5,4},{6,7},{7,6},{8,9},{9,8},{10,11... | collective-permute-start | bytes 884744 | tf_op jit(solution)/shard_map/ppermute | solution.py:1017
  24.1 6.8 %collective-permute-start.1 = (bf16[384,384]{1,0:T(8,128)(2,1)S(1)}, bf16[384,384]{1,0:T(8,128)(2,1)S(1)}, u32[]{:S(2)}, u32[]{:S(2)}) collective-permute-start(bf16[384,384]{1,0:T(8,128)(2,1)S(1)} %slice.30.rest_0_.refs_0_), channel_id=1, source_target_pairs={{0,16},{8,24},{16,0},{24,8},{1,17},{9,25},{17,1},{25,9},{2,18},{10... | collective-permute-start | bytes 884744 | tf_op jit(solution)/shard_map/ppermute | solution.py:1017
  25.3 35.8 %copy-start.8 = (bf16[384,256]{1,0:T(8,128)(2,1)}, bf16[384,256]{1,0:T(8,128)(2,1)S(1)}, u32[]{:S(2)}) copy-start(bf16[384,256]{1,0:T(8,128)(2,1)S(1)} %slice.31.rest_0_.refs_8_) | copy-start | bytes 589828
  29.9 18.0 %copy-start.16 = (bf16[384,384]{1,0:T(8,128)(2,1)}, bf16[384,384]{1,0:T(8,128)(2,1)S(1)}, u32[]{:S(2)}) copy-start(bf16[384,384]{1,0:T(8,128)(2,1)S(1)} %collective-permute-done.rest_1_.refs_1_) | copy-start | bytes 884740
  30.8 17.1 %copy-start.17 = (bf16[384,384]{1,0:T(8,128)(2,1)}, bf16[384,384]{1,0:T(8,128)(2,1)S(1)}, u32[]{:S(2)}) copy-start(bf16[384,384]{1,0:T(8,128)(2,1)S(1)} %collective-permute-done.1.rest_2_.refs_2_) | copy-start | bytes 884740
  30.8 5.6 %collective-permute-start.2 = (bf16[384,384]{1,0:T(8,128)(2,1)S(1)}, bf16[384,384]{1,0:T(8,128)(2,1)S(1)}, u32[]{:S(2)}, u32[]{:S(2)}) collective-permute-start(bf16[384,384]{1,0:T(8,128)(2,1)S(1)} %collective-permute-done.1.rest_2_.refs_2_), channel_id=1, source_target_pairs={{0,1},{1,0},{2,3},{3,2},{4,5},{5,4},{6,7},{7,6},{8,9},{9,8},{10,11... | collective-permute-start | bytes 884744 | tf_op jit(solution)/shard_map/ppermute | solution.py:1017
  31.2 4.5 %collective-permute-start.3 = (bf16[384,256]{1,0:T(8,128)(2,1)S(1)}, bf16[384,256]{1,0:T(8,128)(2,1)S(1)}, u32[]{:S(2)}, u32[]{:S(2)}) collective-permute-start(bf16[384,256]{1,0:T(8,128)(2,1)S(1)} %slice.31.rest_0_.refs_8_), channel_id=1, source_target_pairs={{0,16},{8,24},{16,0},{24,8},{1,17},{9,25},{17,1},{25,9},{2,18},{10... | collective-permute-start | bytes 589832 | tf_op jit(solution)/shard_map/ppermute | solution.py:1017
  36.4 25.4 %all-to-all-start.1 = ((bf16[8,96,640]{2,1,0:T(8,128)(2,1)}), bf16[8,96,640]{2,1,0:T(8,128)(2,1)S(1)}, u32[]{:S(2)}, u32[]{:S(2)}) async-start(bf16[8,96,640]{2,1,0:T(8,128)(2,1)} %shard_map.275), calls=%async_computation.1 | async-start | bytes 1966080 | tf_op jit(solution)/shard_map/all_to_all | solution.py:1025
  40.0 6.1 %collective-permute-start.4 = (bf16[384,384]{1,0:T(8,128)(2,1)S(1)}, bf16[384,384]{1,0:T(8,128)(2,1)S(1)}, u32[]{:S(2)}, u32[]{:S(2)}) collective-permute-start(bf16[384,384]{1,0:T(8,128)(2,1)S(1)} %slice.30.rest_0_.refs_0_), channel_id=1, source_target_pairs={{0,8},{8,0},{16,24},{24,16},{1,9},{9,1},{17,25},{25,17},{2,10},{10... | collective-permute-start | bytes 884744 | tf_op jit(solution)/shard_map/ppermute | solution.py:1017
  44.0 2.9 %collective-permute-start.5 = (bf16[384,384]{1,0:T(8,128)(2,1)S(1)}, bf16[384,384]{1,0:T(8,128)(2,1)S(1)}, u32[]{:S(2)}, u32[]{:S(2)}) collective-permute-start(bf16[384,384]{1,0:T(8,128)(2,1)S(1)} %collective-permute-done.rest_1_.refs_1_), channel_id=1, source_target_pairs={{0,8},{8,0},{16,24},{24,16},{1,9},{9,1},{17,25},{25,17},{2,10},{10... | collective-permute-start | bytes 884744 | tf_op jit(solution)/shard_map/ppermute | solution.py:1017
  44.1 3.1 %collective-permute-start.6 = (bf16[384,384]{1,0:T(8,128)(2,1)S(1)}, bf16[384,384]{1,0:T(8,128)(2,1)S(1)}, u32[]{:S(2)}, u32[]{:S(2)}) collective-permute-start(bf16[384,384]{1,0:T(8,128)(2,1)S(1)} %collective-permute-done.1.rest_2_.refs_2_), channel_id=1, source_target_pairs={{0,8},{8,0},{16,24},{24,16},{1,9},{9,1},{17,25},{25,17},{2,10},{10... | collective-permute-start | bytes 884744 | tf_op jit(solution)/shard_map/ppermute | solution.py:1017
  44.5 3.4 %collective-permute-start.7 = (bf16[384,384]{1,0:T(8,128)(2,1)S(1)}, bf16[384,384]{1,0:T(8,128)(2,1)S(1)}, u32[]{:S(2)}, u32[]{:S(2)}) collective-permute-start(bf16[384,384]{1,0:T(8,128)(2,1)S(1)} %collective-permute-done.2.rest_3_.refs_3_), channel_id=1, source_target_pairs={{0,8},{8,0},{16,24},{24,16},{1,9},{9,1},{17,25},{25,17},{2,10},{10... | collective-permute-start | bytes 884744 | tf_op jit(solution)/shard_map/ppermute | solution.py:1017
  44.6 16.5 %collective-permute-start.8 = (bf16[384,256]{1,0:T(8,128)(2,1)S(1)}, bf16[384,256]{1,0:T(8,128)(2,1)S(1)}, u32[]{:S(2)}, u32[]{:S(2)}) collective-permute-start(bf16[384,256]{1,0:T(8,128)(2,1)S(1)} %slice.31.rest_0_.refs_8_), channel_id=1, source_target_pairs={{0,1},{1,0},{2,3},{3,2},{4,5},{5,4},{6,7},{7,6},{8,9},{9,8},{10,11... | collective-permute-start | bytes 589832 | tf_op jit(solution)/shard_map/ppermute | solution.py:1017
  46.1 20.7 %collective-permute-start.10 = (bf16[384,256]{1,0:T(8,128)(2,1)S(1)}, bf16[384,256]{1,0:T(8,128)(2,1)}, u32[]{:S(2)}, u32[]{:S(2)}) collective-permute-start(bf16[384,256]{1,0:T(8,128)(2,1)S(1)} %slice.31.rest_0_.refs_8_), channel_id=1, source_target_pairs={{0,8},{8,0},{16,24},{24,16},{1,9},{9,1},{17,25},{25,17},{2,10},{10... | collective-permute-start | bytes 589832 | tf_op jit(solution)/shard_map/ppermute | solution.py:1017
  46.9 14.9 %collective-permute-start.9 = (bf16[384,256]{1,0:T(8,128)(2,1)}, bf16[384,256]{1,0:T(8,128)(2,1)}, u32[]{:S(2)}, u32[]{:S(2)}) collective-permute-start(bf16[384,256]{1,0:T(8,128)(2,1)} %copy-done.23), channel_id=1, source_target_pairs={{0,1},{1,0},{2,3},{3,2},{4,5},{5,4},{6,7},{7,6},{8,9},{9,8},{10,11... | collective-permute-start | bytes 589832 | tf_op jit(solution)/shard_map/ppermute | solution.py:1017
  47.2 19.6 %collective-permute-start.12 = (bf16[384,256]{1,0:T(8,128)(2,1)}, bf16[384,256]{1,0:T(8,128)(2,1)}, u32[]{:S(2)}, u32[]{:S(2)}) collective-permute-start(bf16[384,256]{1,0:T(8,128)(2,1)} %copy-done.23), channel_id=1, source_target_pairs={{0,8},{8,0},{16,24},{24,16},{1,9},{9,1},{17,25},{25,17},{2,10},{10... | collective-permute-start | bytes 589832 | tf_op jit(solution)/shard_map/ppermute | solution.py:1017
  61.9 5.0 %collective-permute-start.11 = (bf16[384,256]{1,0:T(8,128)(2,1)}, bf16[384,256]{1,0:T(8,128)(2,1)S(1)}, u32[]{:S(2)}, u32[]{:S(2)}) collective-permute-start(bf16[384,256]{1,0:T(8,128)(2,1)} %copy-done.24), channel_id=1, source_target_pairs={{0,8},{8,0},{16,24},{24,16},{1,9},{9,1},{17,25},{25,17},{2,10},{10... | collective-permute-start | bytes 589832 | tf_op jit(solution)/shard_map/ppermute | solution.py:1017
  65.4 1.7 collective-permute-start.13
  65.4 13.8 %copy-start.6 = (bf16[768,256]{1,0:T(8,128)(2,1)}, bf16[768,256]{1,0:T(8,128)(2,1)S(1)}, u32[]{:S(2)}) copy-start(bf16[768,256]{1,0:T(8,128)(2,1)S(1)} %slice.33.rest_0_.refs_18_) | copy-start | bytes 1179652
  65.5 13.0 %collective-permute-start.14 = (bf16[768,256]{1,0:T(8,128)(2,1)S(1)}, bf16[768,256]{1,0:T(8,128)(2,1)S(1)}, u32[]{:S(2)}, u32[]{:S(2)}) collective-permute-start(bf16[768,256]{1,0:T(8,128)(2,1)S(1)} %slice.33.rest_0_.refs_18_), channel_id=1, source_target_pairs={{0,16},{8,24},{16,0},{24,8},{1,17},{9,25},{17,1},{25,9},{2,18},{10... | collective-permute-start | bytes 1179656 | tf_op jit(solution)/shard_map/ppermute | solution.py:1017
  66.8 11.6 %copy-start.5 = (bf16[768,384]{1,0:T(8,128)(2,1)}, bf16[768,384]{1,0:T(8,128)(2,1)S(1)}, u32[]{:S(2)}) copy-start(bf16[768,384]{1,0:T(8,128)(2,1)S(1)} %slice.32.rest_0_.refs_16_) | copy-start | bytes 1769476
  78.4 13.6 %copy-start.12 = (bf16[768,256]{1,0:T(8,128)(2,1)}, bf16[768,256]{1,0:T(8,128)(2,1)S(1)}, u32[]{:S(2)}) copy-start(bf16[768,256]{1,0:T(8,128)(2,1)S(1)} %collective-permute-done.14.rest_1_.refs_19_) | copy-start | bytes 1179652
  78.4 2.4 collective-permute-start.15
  79.2 12.7 %collective-permute-start.16 = (bf16[768,256]{1,0:T(8,128)(2,1)S(1)}, bf16[768,256]{1,0:T(8,128)(2,1)S(1)}, u32[]{:S(2)}, u32[]{:S(2)}) collective-permute-start(bf16[768,256]{1,0:T(8,128)(2,1)S(1)} %slice.33.rest_0_.refs_18_), channel_id=1, source_target_pairs={{0,8},{8,0},{16,24},{24,16},{1,9},{9,1},{17,25},{25,17},{2,10},{10... | collective-permute-start | bytes 1179656 | tf_op jit(solution)/shard_map/ppermute | solution.py:1017
  79.3 12.6 %collective-permute-start.17 = (bf16[768,256]{1,0:T(8,128)(2,1)S(1)}, bf16[768,256]{1,0:T(8,128)(2,1)S(1)}, u32[]{:S(2)}, u32[]{:S(2)}) collective-permute-start(bf16[768,256]{1,0:T(8,128)(2,1)S(1)} %collective-permute-done.14.rest_1_.refs_19_), channel_id=1, source_target_pairs={{0,8},{8,0},{16,24},{24,16},{1,9},{9,1},{17,25},{25,17},{2,10},{10... | collective-permute-start | bytes 1179656 | tf_op jit(solution)/shard_map/ppermute | solution.py:1017
  107.0 15.3 %all-to-all-start.2 = ((bf16[8,2,8,1664]{3,2,1,0:T(8,128)(2,1)}), bf16[8,2,8,1664]{3,2,1,0:T(8,128)(2,1)S(1)}, u32[]{:S(2)}, u32[]{:S(2)}) async-start(bf16[8,2,8,1664]{3,2,1,0:T(8,128)(2,1)} %get-tuple-element.140), calls=%async_computation.2 | async-start | bytes 851968 | tf_op jit(solution)/shard_map/all_to_all | solution.py:1163
  122.3 15.8 %collective-permute-start.18 = (bf16[8,2,8,1664]{3,2,1,0:T(8,128)(2,1)S(1)}, bf16[8,2,8,1664]{3,2,1,0:T(8,128)(2,1)S(1)}, u32[]{:S(2)}, u32[]{:S(2)}) collective-permute-start(bf16[8,2,8,1664]{3,2,1,0:T(8,128)(2,1)S(1)} %all-to-all-done.2.part_ref.refs_0_), channel_id=1, source_target_pairs={{0,16},{8,24},{16,0},{24,8},{1,17},{9,25},{17,1},{25,9},{2,18},{10... | collective-permute-start | bytes 1277960 | tf_op jit(solution)/shard_map/ppermute | solution.py:1017
  138.9 13.3 %all-to-all-start.3 = ((bf16[8,2,8,1536]{3,2,1,0:T(8,128)(2,1)}), bf16[8,2,8,1536]{3,2,1,0:T(8,128)(2,1)S(1)}, u32[]{:S(2)}, u32[]{:S(2)}) async-start(bf16[8,2,8,1536]{3,2,1,0:T(8,128)(2,1)} %get-tuple-element.147), calls=%async_computation.3 | async-start | bytes 786432 | tf_op jit(solution)/shard_map/all_to_all | solution.py:1173
  143.2 27.4 %collective-permute-start.19 = (bf16[2,64,512]{2,1,0:T(8,128)(2,1)}, bf16[2,64,512]{2,1,0:T(8,128)(2,1)S(1)}, u32[]{:S(2)}, u32[]{:S(2)}) collective-permute-start(bf16[2,64,512]{2,1,0:T(8,128)(2,1)} %get-tuple-element.181.refs_12_), channel_id=1, source_target_pairs={{0,16},{8,24},{16,0},{24,8},{1,17},{9,25},{17,1},{25,9},{2,18},{10... | collective-permute-start | bytes 393224 | tf_op jit(solution)/shard_map/ppermute | solution.py:1017
  143.9 55.8 %collective-permute-start.21 = (bf16[2,64,3072]{2,1,0:T(8,128)(2,1)}, bf16[2,64,3072]{2,1,0:T(8,128)(2,1)}, u32[]{:S(2)}, u32[]{:S(2)}) collective-permute-start(bf16[2,64,3072]{2,1,0:T(8,128)(2,1)} %get-tuple-element.177.refs_4_), channel_id=1, source_target_pairs={{0,16},{8,24},{16,0},{24,8},{1,17},{9,25},{17,1},{25,9},{2,18},{10... | collective-permute-start | bytes 2359304 | tf_op jit(solution)/shard_map/ppermute | solution.py:1017
  144.6 55.1 %collective-permute-start.22 = (bf16[2,64,3072]{2,1,0:T(8,128)(2,1)}, bf16[2,64,3072]{2,1,0:T(8,128)(2,1)}, u32[]{:S(2)}, u32[]{:S(2)}) collective-permute-start(bf16[2,64,3072]{2,1,0:T(8,128)(2,1)} %get-tuple-element.179.refs_8_), channel_id=1, source_target_pairs={{0,16},{8,24},{16,0},{24,8},{1,17},{9,25},{17,1},{25,9},{2,18},{10... | collective-permute-start | bytes 2359304 | tf_op jit(solution)/shard_map/ppermute | solution.py:1017
  170.6 34.1 %copy-start.28 = (bf16[2,64,512]{2,1,0:T(8,128)(2,1)}, bf16[2,64,512]{2,1,0:T(8,128)(2,1)S(1)}, u32[]{:S(2)}) copy-start(bf16[2,64,512]{2,1,0:T(8,128)(2,1)S(1)} %collective-permute-done.19.refs_13_) | copy-start | bytes 393220
  196.0 5.8 %collective-permute-start.20 = (bf16[8,352,128]{2,1,0:T(8,128)(2,1)}, bf16[8,352,128]{2,1,0:T(8,128)(2,1)S(1)}, u32[]{:S(2)}, u32[]{:S(2)}) collective-permute-start(bf16[8,352,128]{2,1,0:T(8,128)(2,1)} %get-tuple-element.157), channel_id=1, source_target_pairs={{0,8},{8,0},{16,24},{24,16},{1,9},{9,1},{17,25},{25,17},{2,10},{10... | collective-permute-start | bytes 2162696 | tf_op jit(solution)/shard_map/ppermute | solution.py:1017
  203.1 17.6 %collective-permute-start.23 = (bf16[8,176,128]{2,1,0:T(8,128)(2,1)S(1)}, bf16[8,176,128]{2,1,0:T(8,128)(2,1)S(1)}, u32[]{:S(2)}, u32[]{:S(2)}) collective-permute-start(bf16[8,176,128]{2,1,0:T(8,128)(2,1)S(1)} %constant_dynamic-slice_fusion), channel_id=1, source_target_pairs={{0,16},{8,24},{16,0},{24,8},{1,17},{9,25},{17,1},{25,9},{2,18},{10... | collective-permute-start | bytes 1081352 | tf_op jit(solution)/shard_map/ppermute | solution.py:1017
  203.9 22.1 %collective-permute-start.24 = (bf16[8,2,8,1664]{3,2,1,0:T(8,128)(2,1)S(1)}, bf16[8,2,8,1664]{3,2,1,0:T(8,128)(2,1)}, u32[]{:S(2)}, u32[]{:S(2)}) collective-permute-start(bf16[8,2,8,1664]{3,2,1,0:T(8,128)(2,1)S(1)} %copy-done.1), channel_id=1, source_target_pairs={{0,8},{8,0},{16,24},{24,16},{1,9},{9,1},{17,25},{25,17},{2,10},{10... | collective-permute-start | bytes 1277960 | tf_op jit(solution)/shard_map/ppermute | solution.py:1017
  204.6 16.6 %collective-permute-start.30 = (bf16[2,64,512]{2,1,0:T(8,128)(2,1)S(1)}, bf16[2,64,512]{2,1,0:T(8,128)(2,1)S(1)}, u32[]{:S(2)}, u32[]{:S(2)}) collective-permute-start(bf16[2,64,512]{2,1,0:T(8,128)(2,1)S(1)} %copy-done.27), channel_id=1, source_target_pairs={{0,8},{8,0},{16,24},{24,16},{1,9},{9,1},{17,25},{25,17},{2,10},{10... | collective-permute-start | bytes 393224 | tf_op jit(solution)/shard_map/ppermute | solution.py:1017
  204.6 16.6 %collective-permute-start.31 = (bf16[2,64,512]{2,1,0:T(8,128)(2,1)S(1)}, bf16[2,64,512]{2,1,0:T(8,128)(2,1)S(1)}, u32[]{:S(2)}, u32[]{:S(2)}) collective-permute-start(bf16[2,64,512]{2,1,0:T(8,128)(2,1)S(1)} %collective-permute-done.19.refs_13_), channel_id=1, source_target_pairs={{0,8},{8,0},{16,24},{24,16},{1,9},{9,1},{17,25},{25,17},{2,10},{10... | collective-permute-start | bytes 393224 | tf_op jit(solution)/shard_map/ppermute | solution.py:1017
  220.7 7.4 %collective-permute-start.26 = (bf16[2,64,3072]{2,1,0:T(8,128)(2,1)}, bf16[2,64,3072]{2,1,0:T(8,128)(2,1)}, u32[]{:S(2)}, u32[]{:S(2)}) collective-permute-start(bf16[2,64,3072]{2,1,0:T(8,128)(2,1)} %get-tuple-element.177.refs_4_), channel_id=1, source_target_pairs={{0,8},{8,0},{16,24},{24,16},{1,9},{9,1},{17,25},{25,17},{2,10},{10... | collective-permute-start | bytes 2359304 | tf_op jit(solution)/shard_map/ppermute | solution.py:1017
  220.7 7.3 %collective-permute-start.27 = (bf16[2,64,3072]{2,1,0:T(8,128)(2,1)}, bf16[2,64,3072]{2,1,0:T(8,128)(2,1)}, u32[]{:S(2)}, u32[]{:S(2)}) collective-permute-start(bf16[2,64,3072]{2,1,0:T(8,128)(2,1)} %collective-permute-done.21.refs_5_), channel_id=1, source_target_pairs={{0,8},{8,0},{16,24},{24,16},{1,9},{9,1},{17,25},{25,17},{2,10},{10... | collective-permute-start | bytes 2359304 | tf_op jit(solution)/shard_map/ppermute | solution.py:1017
  221.2 6.9 %collective-permute-start.28 = (bf16[2,64,3072]{2,1,0:T(8,128)(2,1)}, bf16[2,64,3072]{2,1,0:T(8,128)(2,1)}, u32[]{:S(2)}, u32[]{:S(2)}) collective-permute-start(bf16[2,64,3072]{2,1,0:T(8,128)(2,1)} %get-tuple-element.179.refs_8_), channel_id=1, source_target_pairs={{0,8},{8,0},{16,24},{24,16},{1,9},{9,1},{17,25},{25,17},{2,10},{10... | collective-permute-start | bytes 2359304 | tf_op jit(solution)/shard_map/ppermute | solution.py:1017
  221.3 6.8 %collective-permute-start.29 = (bf16[2,64,3072]{2,1,0:T(8,128)(2,1)}, bf16[2,64,3072]{2,1,0:T(8,128)(2,1)}, u32[]{:S(2)}, u32[]{:S(2)}) collective-permute-start(bf16[2,64,3072]{2,1,0:T(8,128)(2,1)} %collective-permute-done.22.refs_9_), channel_id=1, source_target_pairs={{0,8},{8,0},{16,24},{24,16},{1,9},{9,1},{17,25},{25,17},{2,10},{10... | collective-permute-start | bytes 2359304 | tf_op jit(solution)/shard_map/ppermute | solution.py:1017
  222.5 14.6 %all-to-all-start.4 = ((bf16[8,176,128]{2,1,0:T(8,128)(2,1)}), bf16[8,176,128]{2,1,0:T(8,128)(2,1)S(1)}, u32[]{:S(2)}, u32[]{:S(2)}) async-start(bf16[8,176,128]{2,1,0:T(8,128)(2,1)} %add_convert_fusion.1), calls=%async_computation.4 | async-start | bytes 720896 | tf_op jit(solution)/shard_map/all_to_all | solution.py:1050
  226.0 16.1 %copy-start.2 = (bf16[8,197,768]{2,1,0:T(8,128)(2,1)S(1)}, bf16[8,197,768]{2,1,0:T(8,128)(2,1)}, u32[]{:S(2)}) copy-start(bf16[8,197,768]{2,1,0:T(8,128)(2,1)} %get-tuple-element.158) | copy-start | bytes 7262212
  226.0 2.0 collective-permute-start.25
  237.2 3.0 %collective-permute-start.32 = (bf16[176,128]{1,0:T(8,128)(2,1)S(1)}, bf16[176,128]{1,0:T(8,128)(2,1)S(1)}, u32[]{:S(2)}, u32[]{:S(2)}) collective-permute-start(bf16[176,128]{1,0:T(8,128)(2,1)S(1)} %reduce_sum.12), channel_id=1, source_target_pairs={{0,16},{8,24},{16,0},{24,8},{1,17},{9,25},{17,1},{25,9},{2,18},{10... | collective-permute-start | bytes 135176 | tf_op jit(solution)/shard_map/ppermute | solution.py:1017
  240.2 3.8 %collective-permute-start.33 = (bf16[352,128]{1,0:T(8,128)(2,1)S(1)}, bf16[352,128]{1,0:T(8,128)(2,1)S(1)}, u32[]{:S(2)}, u32[]{:S(2)}) collective-permute-start(bf16[352,128]{1,0:T(8,128)(2,1)S(1)} %maximum_select_fusion.1), channel_id=1, source_target_pairs={{0,8},{8,0},{16,24},{24,16},{1,9},{9,1},{17,25},{25,17},{2,10},{10... | collective-permute-start | bytes 270344 | tf_op jit(solution)/shard_map/ppermute | solution.py:1017
  (22 other events, 57.3 us)

commit v7 on v6

--- a/solution.py
+++ b/solution.py
@@ -356,8 +356,8 @@
 
 
 def expert_tile(slots, gy, u1, gu2, wu_ref, wd_ref, ub_ref, da_ref):
+    ghid = (dot(wd_ref[0], gy, NT) + dot(da_ref[0], gu2, NT)).T
     pre = dot(slots, wu_ref[0]) + dot(u1, ub_ref[0])
-    ghid = (dot(wd_ref[0], gy, NT) + dot(da_ref[0], gu2, NT)).T
     hidden, slope = gelu_both(pre)
     return hidden.astype(BF16), (slope * ghid).astype(BF16)
 
@@ -602,6 +602,7 @@
 
     uq_t = flat(uq_ref).T
     guq = None
+    gqkvs = []
     for group in range(groups):
         parts = []
         for i in range(n_img):
@@ -612,9 +613,11 @@
             gqkv_refs[group][i] = part
             parts.append(part)
         gqkv = jnp.concatenate(parts, axis=0)
-        acc_b[:, group * 3 * GROUP : (group + 1) * 3 * GROUP] += dot(uq_t, gqkv)
         part = dot(gqkv, group_rows(group, width, bt_ref))
         guq = part if guq is None else guq + part
+        gqkvs.append(gqkv)
+    for group, gqkv in enumerate(gqkvs):
+        acc_b[:, group * 3 * GROUP : (group + 1) * 3 * GROUP] += dot(uq_t, gqkv)
     guq = select_rows(guq, index_ref, step * n_img, n_img)
     acc_a[...] += dot(guq, flat(h1_ref), TN)
     guq_ref[...] = guq.reshape(guq_ref.shape)

time: 247 us -> 245 us (level)
  transfers between devices with their start and end apart: 39 -> 39, of which waited for: 12 -> 12; matrix products, arithmetic and copies ran while one was open for 3% -> 3% of each run, Pallas kernels for 53% -> 52%
where the time goes in v7:
time: 245 us; the launch traced here: 244 us
  Pallas kernels  145 us (59%)
  starting transfers between devices  51.3 us (21%)
  waiting for transfers between devices  29.3 us (12%)
  local copies, waits for them, and re-layouts  14.3 us (6%)
  other arithmetic  2.82 us (1%)
    pallas_call x13, Pallas kernels, call(): pl.pallas_call(kernel, out_shape=shapes, grid_spec=pltpu.PrefetchScalarGr...  145 us
    ppermute x34, starting transfers between devices, swap(): return lax.ppermute(array, axis, [(i, i ^ bit) for i in range(size)])  31 us
    ppermute x34, waiting for transfers between devices, swap(): return lax.ppermute(array, axis, [(i, i ^ bit) for i in range(size)])  16.1 us
    unnamed x65, local copies, waits for them, and re-layouts  12.2 us
    all_to_all x2, starting transfers between devices, over_shard(): lax.all_to_all(spread, 'shard', split_axis=0, concat_axis=0, tiled=True,...  8.98 us
    all_to_all x1, waiting for transfers between devices, per_device(): back = lax.all_to_all(ret, 'shard', split_axis=0, concat_axis=0, tiled=True)  6.79 us
  transfers between devices with their start and end apart: 39, of which 12 were waited for; matrix products, arithmetic and copies ran while one was open for 3% of the time, Pallas kernels for 52%

profile of v7, /device:TPU:1, one launch (start us, length us, event | category | flops | bytes accessed | tf_op | source)
XLA Modules:
  0.0 244.2 jit_solution(2218226032074002137)
XLA Ops:
  1.3 2.8 %shard_map.274 = bf16[4,96,640]{2,1,0:T(8,128)(2,1)} custom-call(s32[3]{0:T(128)} %pad_add_fusion.place_ref, bf16[96,2304]{1,0:T(8,128)(2,1)} %qkv_ref.3, bf16[96,128]{1,0:T(8,128)(2,1)} %a_ref.1, bf16[288,128]{1,0:T(8,128)(2,1)} %bitcast.26, bf16[96,128]{1,0:T(8,128)(2,1)} %ao_ref.1, bf16[96,128]{1,0:T(8,128)(2,1)} %ra_ref.1, bf16[96,128]{1,0:T(8,128)(2,1)} %bitcast.27, ...), custom_call_target="tpu_custom_call" | custom-call | flops 221184 | bytes 1108992 | tf_op jit(solution)/shard_map/pallas_call | solution.py:692
  4.0 5.4 %all-to-all-start = ((bf16[4,96,640]{2,1,0:T(8,128)(2,1)}), bf16[4,96,640]{2,1,0:T(8,128)(2,1)S(1)}, u32[]{:S(2)}, u32[]{:S(2)}) async-start(bf16[4,96,640]{2,1,0:T(8,128)(2,1)} %shard_map.274), calls=%async_computation | async-start | bytes 983040 | tf_op jit(solution)/shard_map/all_to_all | solution.py:1028
  9.4 2.8 %shard_map.275 = bf16[8,96,640]{2,1,0:T(8,128)(2,1)} custom-call(s32[3]{0:T(128)} %pad_add_fusion.place_ref, bf16[96,2304]{1,0:T(8,128)(2,1)} %qkv_ref.3, bf16[96,768]{1,0:T(8,128)(2,1)} %wo_ref.1, bf16[2,128]{1,0:T(2,128)(2,1)} %bitcast.29), custom_call_target="tpu_custom_call" | custom-call | flops 73728 | bytes 1573376 | tf_op jit(solution)/shard_map/pallas_call | solution.py:692
  12.3 1.9 copy.31.image_ref
  14.6 1.9 copy.32._.cot_ref
  16.5 3.7 %shard_map.276.h1_ref.refs_8_ = bf16[8,208,768]{2,1,0:T(8,128)(2,1)} custom-call(bf16[8,197,768]{2,1,0:T(8,128)(2,1)} %copy.31.image_ref, bf16[8,197,768]{2,1,0:T(8,128)(2,1)} %copy.32._.cot_ref), custom_call_target="tpu_custom_call" | custom-call | flops 9682944 | bytes 7397376 | tf_op jit(solution)/shard_map/pallas_call | solution.py:692
  20.2 2.6 %all-to-all-done = bf16[4,96,640]{2,1,0:T(8,128)(2,1)S(1)} async-done(((bf16[4,96,640]{2,1,0:T(8,128)(2,1)}), bf16[4,96,640]{2,1,0:T(8,128)(2,1)S(1)}, u32[]{:S(2)}, u32[]{:S(2)}) %all-to-all-start) | async-done | bytes 491552 | tf_op jit(solution)/shard_map/all_to_all | solution.py:1028
  22.8 1.3 collective-permute-start
  24.1 1.2 collective-permute-start.1
  25.3 4.6 %collective-permute-done.rest_1_.refs_1_ = bf16[384,384]{1,0:T(8,128)(2,1)S(1)} collective-permute-done((bf16[384,384]{1,0:T(8,128)(2,1)S(1)}, bf16[384,384]{1,0:T(8,128)(2,1)S(1)}, u32[]{:S(2)}, u32[]{:S(2)}) %collective-permute-start) | collective-permute-done | bytes 294944 | tf_op jit(solution)/shard_map/ppermute | solution.py:1020
  29.9 0.9 collective-permute-done.1.rest_2_.refs_2_
  31.2 1.2 collective-permute-start.3
  32.4 3.3 %collective-permute-done.3.rest_2_.refs_10_ = bf16[384,256]{1,0:T(8,128)(2,1)S(1)} collective-permute-done((bf16[384,256]{1,0:T(8,128)(2,1)S(1)}, bf16[384,256]{1,0:T(8,128)(2,1)S(1)}, u32[]{:S(2)}, u32[]{:S(2)}) %collective-permute-start.3) | collective-permute-done | bytes 196640 | tf_op jit(solution)/shard_map/ppermute | solution.py:1020
  36.4 3.6 %all-to-all-start.1 = ((bf16[8,96,640]{2,1,0:T(8,128)(2,1)}), bf16[8,96,640]{2,1,0:T(8,128)(2,1)S(1)}, u32[]{:S(2)}, u32[]{:S(2)}) async-start(bf16[8,96,640]{2,1,0:T(8,128)(2,1)} %shard_map.275), calls=%async_computation.1 | async-start | bytes 1966080 | tf_op jit(solution)/shard_map/all_to_all | solution.py:1028
  40.0 4.0 %collective-permute-start.4 = (bf16[384,384]{1,0:T(8,128)(2,1)S(1)}, bf16[384,384]{1,0:T(8,128)(2,1)S(1)}, u32[]{:S(2)}, u32[]{:S(2)}) collective-permute-start(bf16[384,384]{1,0:T(8,128)(2,1)S(1)} %slice.30.rest_0_.refs_0_), channel_id=1, source_target_pairs={{0,8},{8,0},{16,24},{24,16},{1,9},{9,1},{17,25},{25,17},{2,10},{10... | collective-permute-start | bytes 884744 | tf_op jit(solution)/shard_map/ppermute | solution.py:1020
  44.6 1.5 collective-permute-start.8
  46.1 0.8 collective-permute-start.10
  48.7 12.5 %shard_map.277 = (bf16[8,208,768]{2,1,0:T(8,128)(2,1)}, bf16[8,208,256]{2,1,0:T(8,128)(2,1)}, bf16[8,4,208,208]{3,2,1,0:T(8,128)(2,1)}, bf16[8,208,128]{2,1,0:T(...) custom-call(s32[3]{0:T(128)} %pad_add_fusion.place_ref, ...), custom_call_target="tpu_custom_call" | custom-call | flops 2317352960 | bytes 12697600 | tf_op jit(solution)/shard_map/pallas_call | solution.py:692
  61.9 3.6 %collective-permute-start.11 = (bf16[384,256]{1,0:T(8,128)(2,1)}, bf16[384,256]{1,0:T(8,128)(2,1)S(1)}, u32[]{:S(2)}, u32[]{:S(2)}) collective-permute-start(bf16[384,256]{1,0:T(8,128)(2,1)} %copy-done.24), channel_id=1, source_target_pairs={{0,8},{8,0},{16,24},{24,16},{1,9},{9,1},{17,25},{25,17},{2,10},{10... | collective-permute-start | bytes 589832 | tf_op jit(solution)/shard_map/ppermute | solution.py:1020
  65.5 1.3 collective-permute-start.14
  67.8 10.7 %shard_map.278 = (bf16[8,208,768]{2,1,0:T(8,128)(2,1)}, bf16[8,208,256]{2,1,0:T(8,128)(2,1)}, bf16[8,4,208,208]{3,2,1,0:T(8,128)(2,1)}, bf16[768,128]{1,0:T(8,128)(2,1)}, bf16[768,128]{1,0:T(8,128)(2,1)}) custom-call(s32[3]{0:T(128)} %pad_add_fusion.place_ref, bf16[8,208,768]{2,1,0:T(8,128)(2,1)} %shard_map.276.h1_ref.refs_8_, ...), custom_call_target="tpu_custom_call" | custom-call | flops 2317352960 | bytes 11714560 | tf_op jit(solution)/shard_map/pallas_call | solution.py:692
  78.4 0.8 collective-permute-start.15
  80.9 0.8 copy-done.9
  81.7 10.3 %shard_map.279 = (bf16[8,208,768]{2,1,0:T(8,128)(2,1)}, bf16[8,208,256]{2,1,0:T(8,128)(2,1)}, bf16[8,4,208,208]{3,2,1,0:T(8,128)(2,1)}) custom-call(s32[3]{0:T(128)} %pad_add_fusion.place_ref, bf16[8,208,768]{2,1,0:T(8,128)(2,1)} %shard_map.276.h1_ref.refs_8_, bf16[8,208,128]{2,1,0:T(8,128)(2,1)} %get-tuple-element.120.uq_ref.refs_7_, ...), custom_call_target="tpu_custom_call" | custom-call | flops 2317352960 | bytes 10928128 | tf_op jit(solution)/shard_map/pallas_call | solution.py:692
  92.9 14.2 %shard_map.280 = (f32[8,208,768]{2,1,0:T(8,128)}, bf16[8,208,128]{2,1,0:T(8,128)(2,1)}, bf16[8,208,128]{2,1,0:T(8,128)(2,1)}, f32[8,16,208]{2,1,0:T(8,128)}, f32...) custom-call(s32[3]{0:T(128)} %pad_add_fusion.place_ref, ...), custom_call_target="tpu_custom_call" | custom-call | flops 2944401408 | bytes 16388096 | tf_op jit(solution)/shard_map/pallas_call | solution.py:692
  107.0 3.7 %all-to-all-start.2 = ((bf16[8,2,8,1664]{3,2,1,0:T(8,128)(2,1)}), bf16[8,2,8,1664]{3,2,1,0:T(8,128)(2,1)S(1)}, u32[]{:S(2)}, u32[]{:S(2)}) async-start(bf16[8,2,8,1664]{3,2,1,0:T(8,128)(2,1)} %get-tuple-element.140), calls=%async_computation.2 | async-start | bytes 851968 | tf_op jit(solution)/shard_map/all_to_all | solution.py:1166
  110.7 7.8 %shard_map.281 = (bf16[2432,768]{1,0:T(8,128)(2,1)}, bf16[768,896]{1,0:T(8,128)(2,1)}, bf16[128,768]{1,0:T(8,128)(2,1)}, bf16[128,768]{1,0:T(8,128)(2,1)}) custom-call(s32[3]{0:T(128)} %pad_add_fusion.place_ref, bf16[768,128]{1,0:T(8,128)(2,1)} %get-tuple-element.129.ao_ref, bf16[768,128]{1,0:T(8,128)(2,1)} %get-tuple-element.130.bo_ref, ...), custom_call_target="tpu_custom_call" | custom-call | flops 4718592 | bytes 12779520 | tf_op jit(solution)/shard_map/pallas_call | solution.py:692
  118.5 3.8 %all-to-all-done.2.part_ref.refs_0_ = bf16[8,2,8,1664]{3,2,1,0:T(8,128)(2,1)S(1)} async-done(((bf16[8,2,8,1664]{3,2,1,0:T(8,128)(2,1)}), bf16[8,2,8,1664]{3,2,1,0:T(8,128)(2,1)S(1)}, u32[]{:S(2)}, u32[]{:S(2)}) %all-to-all-start.2) | async-done | bytes 426016 | tf_op jit(solution)/shard_map/all_to_all | solution.py:1166
  122.3 0.9 collective-permute-start.18
  123.2 14.7 %shard_map.282 = (bf16[8,2,8,1536]{3,2,1,0:T(8,128)(2,1)}, bf16[2,64,3072]{2,1,0:T(8,128)(2,1)}, bf16[2,64,3072]{2,1,0:T(8,128)(2,1)}, bf16[2,64,512]{2,1,0:T(8,128)(2,1)}) custom-call(bf16[2,768,3072]{2,1,0:T(8,128)(2,1)} %wu_ref.1, bf16[2,3072,768]{2,1,0:T(8,128)(2,1)} %wd_ref.1, bf16[2,768,128]{2,1,0:T(8,128)(2,1)} %ua_ref.1, ...), custom_call_target="tpu_custom_call" | custom-call | flops 2415919104 | bytes 25329664 | tf_op jit(solution)/shard_map/pallas_call | solution.py:692
  137.9 0.8 copy-done.10
  138.7 4.3 %all-to-all-start.3 = ((bf16[8,2,8,1536]{3,2,1,0:T(8,128)(2,1)}), bf16[8,2,8,1536]{3,2,1,0:T(8,128)(2,1)S(1)}, u32[]{:S(2)}, u32[]{:S(2)}) async-start(bf16[8,2,8,1536]{3,2,1,0:T(8,128)(2,1)} %get-tuple-element.147), calls=%async_computation.3 | async-start | bytes 786432 | tf_op jit(solution)/shard_map/all_to_all | solution.py:1176
  145.2 6.8 %all-to-all-done.3.ret_ref = bf16[8,2,8,1536]{3,2,1,0:T(8,128)(2,1)S(1)} async-done(((bf16[8,2,8,1536]{3,2,1,0:T(8,128)(2,1)}), bf16[8,2,8,1536]{3,2,1,0:T(8,128)(2,1)S(1)}, u32[]{:S(2)}, u32[]{:S(2)}) %all-to-all-start.3) | async-done | bytes 393248 | tf_op jit(solution)/shard_map/all_to_all | solution.py:1176
  152.7 17.6 %shard_map.283 = (bf16[8,197,768]{2,1,0:T(8,128)(2,1)}, bf16[8,208,768]{2,1,0:T(8,128)(2,1)}, bf16[8,208,768]{2,1,0:T(8,128)(2,1)}, bf16[8,320,128]{2,1,0:T(8,128)(2,1)}) custom-call(s32[8]{0:T(128)} %index_ref.7, s32[1]{0:T(128)S(6)} %copy.38.count_ref, bf16[8,197,768]{2,1,0:T(8,128)(2,1)} %copy.32._.cot_ref, f32[8,208,768]{2,1,0:T(8,128)} %get-tuple-element.135.x2_ref, ...), custom_call_target="tpu_custom_call" | custom-call | flops 3925868544 | bytes 21532672 | tf_op jit(solution)/shard_map/pallas_call | solution.py:692
  170.4 23.9 %shard_map.284 = (bf16[8,208,768]{2,1,0:T(8,128)(2,1)}, bf16[8,208,768]{2,1,0:T(8,128)(2,1)}, bf16[8,208,768]{2,1,0:T(8,128)(2,1)}, bf16[8,208,128]{2,1,0:T(8,12...) custom-call(s32[3]{0:T(128)} %pad_add_fusion.place_ref, s32[8]{0:T(128)} %index_ref.7, ...), custom_call_target="tpu_custom_call" | custom-call | flops 3639607296 | bytes 32292864 | tf_op jit(solution)/shard_map/pallas_call | solution.py:692
  194.3 3.7 %collective-permute-start.20 = (bf16[8,352,128]{2,1,0:T(8,128)(2,1)}, bf16[8,352,128]{2,1,0:T(8,128)(2,1)S(1)}, u32[]{:S(2)}, u32[]{:S(2)}) collective-permute-start(bf16[8,352,128]{2,1,0:T(8,128)(2,1)} %get-tuple-element.157), channel_id=1, source_target_pairs={{0,8},{8,0},{16,24},{24,16},{1,9},{9,1},{17,25},{25,17},{2,10},{10... | collective-permute-start | bytes 2162696 | tf_op jit(solution)/shard_map/ppermute | solution.py:1020
  198.0 2.0 collective-permute-done.20
  200.0 1.3 add_convert_fusion
  201.4 0.8 collective-permute-start.23
  203.3 15.6 %shard_map.285 = f32[9456,128]{1,0:T(8,128)} custom-call(bf16[8,197,768]{2,1,0:T(8,128)(2,1)} %copy.31.image_ref, bf16[8,208,768]{2,1,0:T(8,128)(2,1)} %get-tuple-element.167.gx2_ref, bf16[8,208,128]{2,1,0:T(8,128)(2,1)} %get-tuple-element.168.guq_ref, bf16[2432,768]{1,0:T(8,128)(2,1)} %get-tuple-element.169.turned_ref, ...), custom_call_target="tpu_custom_call" | custom-call | flops 6215958528 | bytes 21647360 | tf_op jit(solution)/shard_map/pallas_call | solution.py:692
  220.0 0.8 add_convert_fusion.1
  220.8 3.4 %all-to-all-start.4 = ((bf16[8,176,128]{2,1,0:T(8,128)(2,1)}), bf16[8,176,128]{2,1,0:T(8,128)(2,1)S(1)}, u32[]{:S(2)}, u32[]{:S(2)}) async-start(bf16[8,176,128]{2,1,0:T(8,128)(2,1)} %add_convert_fusion.1), calls=%async_computation.4 | async-start | bytes 720896 | tf_op jit(solution)/shard_map/all_to_all | solution.py:1053
  224.6 1.7 collective-permute-done.25.refs_3_
  227.1 8.4 %shard_map.286 = (f32[2,768,128]{2,1,0:T(8,128)}, f32[2,128,3072]{2,1,0:T(8,128)}, f32[2,3072,128]{2,1,0:T(8,128)}, f32[2,128,768]{2,1,0:T(8,128)}) custom-call(bf16[8,2,8,1664]{3,2,1,0:T(8,128)(2,1)} %copy-done, bf16[8,2,8,1664]{3,2,1,0:T(8,128)(2,1)} %copy-done.10, bf16[8,2,8,1664]{3,2,1,0:T(8,128)(2,1)} %collective-permute-done.24.refs_2_, ...), custom_call_target="tpu_custom_call" | custom-call | flops 805306368 | bytes 16384000 | tf_op jit(solution)/shard_map/pallas_call | solution.py:692
  235.5 0.8 collective-permute-start.32
  236.3 2.1 collective-permute-done.32
  238.5 1.9 collective-permute-start.33
  240.4 1.9 copy.37
  (122 shorter events, 16.3 us)
Async XLA Ops:
  4.0 18.7 %all-to-all-start = ((bf16[4,96,640]{2,1,0:T(8,128)(2,1)}), bf16[4,96,640]{2,1,0:T(8,128)(2,1)S(1)}, u32[]{:S(2)}, u32[]{:S(2)}) async-start(bf16[4,96,640]{2,1,0:T(8,128)(2,1)} %shard_map.274), calls=%async_computation | async-start | bytes 983040 | tf_op jit(solution)/shard_map/all_to_all | solution.py:1028
  22.8 25.1 %copy-start.7 = (bf16[384,384]{1,0:T(8,128)(2,1)}, bf16[384,384]{1,0:T(8,128)(2,1)S(1)}, u32[]{:S(2)}) copy-start(bf16[384,384]{1,0:T(8,128)(2,1)S(1)} %slice.30.rest_0_.refs_0_) | copy-start | bytes 884740
  22.8 7.1 %collective-permute-start = (bf16[384,384]{1,0:T(8,128)(2,1)S(1)}, bf16[384,384]{1,0:T(8,128)(2,1)S(1)}, u32[]{:S(2)}, u32[]{:S(2)}) collective-permute-start(bf16[384,384]{1,0:T(8,128)(2,1)S(1)} %slice.30.rest_0_.refs_0_), channel_id=1, source_target_pairs={{0,1},{1,0},{2,3},{3,2},{4,5},{5,4},{6,7},{7,6},{8,9},{9,8},{10,11... | collective-permute-start | bytes 884744 | tf_op jit(solution)/shard_map/ppermute | solution.py:1020
  24.1 6.8 %collective-permute-start.1 = (bf16[384,384]{1,0:T(8,128)(2,1)S(1)}, bf16[384,384]{1,0:T(8,128)(2,1)S(1)}, u32[]{:S(2)}, u32[]{:S(2)}) collective-permute-start(bf16[384,384]{1,0:T(8,128)(2,1)S(1)} %slice.30.rest_0_.refs_0_), channel_id=1, source_target_pairs={{0,16},{8,24},{16,0},{24,8},{1,17},{9,25},{17,1},{25,9},{2,18},{10... | collective-permute-start | bytes 884744 | tf_op jit(solution)/shard_map/ppermute | solution.py:1020
  25.3 35.8 %copy-start.8 = (bf16[384,256]{1,0:T(8,128)(2,1)}, bf16[384,256]{1,0:T(8,128)(2,1)S(1)}, u32[]{:S(2)}) copy-start(bf16[384,256]{1,0:T(8,128)(2,1)S(1)} %slice.31.rest_0_.refs_8_) | copy-start | bytes 589828
  29.9 18.0 %copy-start.16 = (bf16[384,384]{1,0:T(8,128)(2,1)}, bf16[384,384]{1,0:T(8,128)(2,1)S(1)}, u32[]{:S(2)}) copy-start(bf16[384,384]{1,0:T(8,128)(2,1)S(1)} %collective-permute-done.rest_1_.refs_1_) | copy-start | bytes 884740
  30.8 17.1 %copy-start.17 = (bf16[384,384]{1,0:T(8,128)(2,1)}, bf16[384,384]{1,0:T(8,128)(2,1)S(1)}, u32[]{:S(2)}) copy-start(bf16[384,384]{1,0:T(8,128)(2,1)S(1)} %collective-permute-done.1.rest_2_.refs_2_) | copy-start | bytes 884740
  30.8 5.6 %collective-permute-start.2 = (bf16[384,384]{1,0:T(8,128)(2,1)S(1)}, bf16[384,384]{1,0:T(8,128)(2,1)S(1)}, u32[]{:S(2)}, u32[]{:S(2)}) collective-permute-start(bf16[384,384]{1,0:T(8,128)(2,1)S(1)} %collective-permute-done.1.rest_2_.refs_2_), channel_id=1, source_target_pairs={{0,1},{1,0},{2,3},{3,2},{4,5},{5,4},{6,7},{7,6},{8,9},{9,8},{10,11... | collective-permute-start | bytes 884744 | tf_op jit(solution)/shard_map/ppermute | solution.py:1020
  31.2 4.5 %collective-permute-start.3 = (bf16[384,256]{1,0:T(8,128)(2,1)S(1)}, bf16[384,256]{1,0:T(8,128)(2,1)S(1)}, u32[]{:S(2)}, u32[]{:S(2)}) collective-permute-start(bf16[384,256]{1,0:T(8,128)(2,1)S(1)} %slice.31.rest_0_.refs_8_), channel_id=1, source_target_pairs={{0,16},{8,24},{16,0},{24,8},{1,17},{9,25},{17,1},{25,9},{2,18},{10... | collective-permute-start | bytes 589832 | tf_op jit(solution)/shard_map/ppermute | solution.py:1020
  36.4 25.4 %all-to-all-start.1 = ((bf16[8,96,640]{2,1,0:T(8,128)(2,1)}), bf16[8,96,640]{2,1,0:T(8,128)(2,1)S(1)}, u32[]{:S(2)}, u32[]{:S(2)}) async-start(bf16[8,96,640]{2,1,0:T(8,128)(2,1)} %shard_map.275), calls=%async_computation.1 | async-start | bytes 1966080 | tf_op jit(solution)/shard_map/all_to_all | solution.py:1028
  40.0 6.1 %collective-permute-start.4 = (bf16[384,384]{1,0:T(8,128)(2,1)S(1)}, bf16[384,384]{1,0:T(8,128)(2,1)S(1)}, u32[]{:S(2)}, u32[]{:S(2)}) collective-permute-start(bf16[384,384]{1,0:T(8,128)(2,1)S(1)} %slice.30.rest_0_.refs_0_), channel_id=1, source_target_pairs={{0,8},{8,0},{16,24},{24,16},{1,9},{9,1},{17,25},{25,17},{2,10},{10... | collective-permute-start | bytes 884744 | tf_op jit(solution)/shard_map/ppermute | solution.py:1020
  44.0 2.9 %collective-permute-start.5 = (bf16[384,384]{1,0:T(8,128)(2,1)S(1)}, bf16[384,384]{1,0:T(8,128)(2,1)S(1)}, u32[]{:S(2)}, u32[]{:S(2)}) collective-permute-start(bf16[384,384]{1,0:T(8,128)(2,1)S(1)} %collective-permute-done.rest_1_.refs_1_), channel_id=1, source_target_pairs={{0,8},{8,0},{16,24},{24,16},{1,9},{9,1},{17,25},{25,17},{2,10},{10... | collective-permute-start | bytes 884744 | tf_op jit(solution)/shard_map/ppermute | solution.py:1020
  44.1 3.1 %collective-permute-start.6 = (bf16[384,384]{1,0:T(8,128)(2,1)S(1)}, bf16[384,384]{1,0:T(8,128)(2,1)S(1)}, u32[]{:S(2)}, u32[]{:S(2)}) collective-permute-start(bf16[384,384]{1,0:T(8,128)(2,1)S(1)} %collective-permute-done.1.rest_2_.refs_2_), channel_id=1, source_target_pairs={{0,8},{8,0},{16,24},{24,16},{1,9},{9,1},{17,25},{25,17},{2,10},{10... | collective-permute-start | bytes 884744 | tf_op jit(solution)/shard_map/ppermute | solution.py:1020
  44.5 3.4 %collective-permute-start.7 = (bf16[384,384]{1,0:T(8,128)(2,1)S(1)}, bf16[384,384]{1,0:T(8,128)(2,1)S(1)}, u32[]{:S(2)}, u32[]{:S(2)}) collective-permute-start(bf16[384,384]{1,0:T(8,128)(2,1)S(1)} %collective-permute-done.2.rest_3_.refs_3_), channel_id=1, source_target_pairs={{0,8},{8,0},{16,24},{24,16},{1,9},{9,1},{17,25},{25,17},{2,10},{10... | collective-permute-start | bytes 884744 | tf_op jit(solution)/shard_map/ppermute | solution.py:1020
  44.6 16.5 %collective-permute-start.8 = (bf16[384,256]{1,0:T(8,128)(2,1)S(1)}, bf16[384,256]{1,0:T(8,128)(2,1)S(1)}, u32[]{:S(2)}, u32[]{:S(2)}) collective-permute-start(bf16[384,256]{1,0:T(8,128)(2,1)S(1)} %slice.31.rest_0_.refs_8_), channel_id=1, source_target_pairs={{0,1},{1,0},{2,3},{3,2},{4,5},{5,4},{6,7},{7,6},{8,9},{9,8},{10,11... | collective-permute-start | bytes 589832 | tf_op jit(solution)/shard_map/ppermute | solution.py:1020
  46.1 20.7 %collective-permute-start.10 = (bf16[384,256]{1,0:T(8,128)(2,1)S(1)}, bf16[384,256]{1,0:T(8,128)(2,1)}, u32[]{:S(2)}, u32[]{:S(2)}) collective-permute-start(bf16[384,256]{1,0:T(8,128)(2,1)S(1)} %slice.31.rest_0_.refs_8_), channel_id=1, source_target_pairs={{0,8},{8,0},{16,24},{24,16},{1,9},{9,1},{17,25},{25,17},{2,10},{10... | collective-permute-start | bytes 589832 | tf_op jit(solution)/shard_map/ppermute | solution.py:1020
  46.9 14.9 %collective-permute-start.9 = (bf16[384,256]{1,0:T(8,128)(2,1)}, bf16[384,256]{1,0:T(8,128)(2,1)}, u32[]{:S(2)}, u32[]{:S(2)}) collective-permute-start(bf16[384,256]{1,0:T(8,128)(2,1)} %copy-done.23), channel_id=1, source_target_pairs={{0,1},{1,0},{2,3},{3,2},{4,5},{5,4},{6,7},{7,6},{8,9},{9,8},{10,11... | collective-permute-start | bytes 589832 | tf_op jit(solution)/shard_map/ppermute | solution.py:1020
  47.2 19.6 %collective-permute-start.12 = (bf16[384,256]{1,0:T(8,128)(2,1)}, bf16[384,256]{1,0:T(8,128)(2,1)}, u32[]{:S(2)}, u32[]{:S(2)}) collective-permute-start(bf16[384,256]{1,0:T(8,128)(2,1)} %copy-done.23), channel_id=1, source_target_pairs={{0,8},{8,0},{16,24},{24,16},{1,9},{9,1},{17,25},{25,17},{2,10},{10... | collective-permute-start | bytes 589832 | tf_op jit(solution)/shard_map/ppermute | solution.py:1020
  61.9 5.0 %collective-permute-start.11 = (bf16[384,256]{1,0:T(8,128)(2,1)}, bf16[384,256]{1,0:T(8,128)(2,1)S(1)}, u32[]{:S(2)}, u32[]{:S(2)}) collective-permute-start(bf16[384,256]{1,0:T(8,128)(2,1)} %copy-done.24), channel_id=1, source_target_pairs={{0,8},{8,0},{16,24},{24,16},{1,9},{9,1},{17,25},{25,17},{2,10},{10... | collective-permute-start | bytes 589832 | tf_op jit(solution)/shard_map/ppermute | solution.py:1020
  65.4 1.7 collective-permute-start.13
  65.4 13.8 %copy-start.6 = (bf16[768,256]{1,0:T(8,128)(2,1)}, bf16[768,256]{1,0:T(8,128)(2,1)S(1)}, u32[]{:S(2)}) copy-start(bf16[768,256]{1,0:T(8,128)(2,1)S(1)} %slice.33.rest_0_.refs_18_) | copy-start | bytes 1179652
  65.5 13.0 %collective-permute-start.14 = (bf16[768,256]{1,0:T(8,128)(2,1)S(1)}, bf16[768,256]{1,0:T(8,128)(2,1)S(1)}, u32[]{:S(2)}, u32[]{:S(2)}) collective-permute-start(bf16[768,256]{1,0:T(8,128)(2,1)S(1)} %slice.33.rest_0_.refs_18_), channel_id=1, source_target_pairs={{0,16},{8,24},{16,0},{24,8},{1,17},{9,25},{17,1},{25,9},{2,18},{10... | collective-permute-start | bytes 1179656 | tf_op jit(solution)/shard_map/ppermute | solution.py:1020
  66.8 11.6 %copy-start.5 = (bf16[768,384]{1,0:T(8,128)(2,1)}, bf16[768,384]{1,0:T(8,128)(2,1)S(1)}, u32[]{:S(2)}) copy-start(bf16[768,384]{1,0:T(8,128)(2,1)S(1)} %slice.32.rest_0_.refs_16_) | copy-start | bytes 1769476
  78.4 13.6 %copy-start.12 = (bf16[768,256]{1,0:T(8,128)(2,1)}, bf16[768,256]{1,0:T(8,128)(2,1)S(1)}, u32[]{:S(2)}) copy-start(bf16[768,256]{1,0:T(8,128)(2,1)S(1)} %collective-permute-done.14.rest_1_.refs_19_) | copy-start | bytes 1179652
  78.4 2.4 collective-permute-start.15
  79.2 12.7 %collective-permute-start.16 = (bf16[768,256]{1,0:T(8,128)(2,1)S(1)}, bf16[768,256]{1,0:T(8,128)(2,1)S(1)}, u32[]{:S(2)}, u32[]{:S(2)}) collective-permute-start(bf16[768,256]{1,0:T(8,128)(2,1)S(1)} %slice.33.rest_0_.refs_18_), channel_id=1, source_target_pairs={{0,8},{8,0},{16,24},{24,16},{1,9},{9,1},{17,25},{25,17},{2,10},{10... | collective-permute-start | bytes 1179656 | tf_op jit(solution)/shard_map/ppermute | solution.py:1020
  79.3 12.6 %collective-permute-start.17 = (bf16[768,256]{1,0:T(8,128)(2,1)S(1)}, bf16[768,256]{1,0:T(8,128)(2,1)S(1)}, u32[]{:S(2)}, u32[]{:S(2)}) collective-permute-start(bf16[768,256]{1,0:T(8,128)(2,1)S(1)} %collective-permute-done.14.rest_1_.refs_19_), channel_id=1, source_target_pairs={{0,8},{8,0},{16,24},{24,16},{1,9},{9,1},{17,25},{25,17},{2,10},{10... | collective-permute-start | bytes 1179656 | tf_op jit(solution)/shard_map/ppermute | solution.py:1020
  107.0 15.3 %all-to-all-start.2 = ((bf16[8,2,8,1664]{3,2,1,0:T(8,128)(2,1)}), bf16[8,2,8,1664]{3,2,1,0:T(8,128)(2,1)S(1)}, u32[]{:S(2)}, u32[]{:S(2)}) async-start(bf16[8,2,8,1664]{3,2,1,0:T(8,128)(2,1)} %get-tuple-element.140), calls=%async_computation.2 | async-start | bytes 851968 | tf_op jit(solution)/shard_map/all_to_all | solution.py:1166
  122.3 15.5 %collective-permute-start.18 = (bf16[8,2,8,1664]{3,2,1,0:T(8,128)(2,1)S(1)}, bf16[8,2,8,1664]{3,2,1,0:T(8,128)(2,1)S(1)}, u32[]{:S(2)}, u32[]{:S(2)}) collective-permute-start(bf16[8,2,8,1664]{3,2,1,0:T(8,128)(2,1)S(1)} %all-to-all-done.2.part_ref.refs_0_), channel_id=1, source_target_pairs={{0,16},{8,24},{16,0},{24,8},{1,17},{9,25},{17,1},{25,9},{2,18},{10... | collective-permute-start | bytes 1277960 | tf_op jit(solution)/shard_map/ppermute | solution.py:1020
  138.7 13.3 %all-to-all-start.3 = ((bf16[8,2,8,1536]{3,2,1,0:T(8,128)(2,1)}), bf16[8,2,8,1536]{3,2,1,0:T(8,128)(2,1)S(1)}, u32[]{:S(2)}, u32[]{:S(2)}) async-start(bf16[8,2,8,1536]{3,2,1,0:T(8,128)(2,1)} %get-tuple-element.147), calls=%async_computation.3 | async-start | bytes 786432 | tf_op jit(solution)/shard_map/all_to_all | solution.py:1176
  143.0 27.4 %collective-permute-start.19 = (bf16[2,64,512]{2,1,0:T(8,128)(2,1)}, bf16[2,64,512]{2,1,0:T(8,128)(2,1)S(1)}, u32[]{:S(2)}, u32[]{:S(2)}) collective-permute-start(bf16[2,64,512]{2,1,0:T(8,128)(2,1)} %get-tuple-element.181.refs_12_), channel_id=1, source_target_pairs={{0,16},{8,24},{16,0},{24,8},{1,17},{9,25},{17,1},{25,9},{2,18},{10... | collective-permute-start | bytes 393224 | tf_op jit(solution)/shard_map/ppermute | solution.py:1020
  143.7 54.3 %collective-permute-start.21 = (bf16[2,64,3072]{2,1,0:T(8,128)(2,1)}, bf16[2,64,3072]{2,1,0:T(8,128)(2,1)}, u32[]{:S(2)}, u32[]{:S(2)}) collective-permute-start(bf16[2,64,3072]{2,1,0:T(8,128)(2,1)} %get-tuple-element.177.refs_4_), channel_id=1, source_target_pairs={{0,16},{8,24},{16,0},{24,8},{1,17},{9,25},{17,1},{25,9},{2,18},{10... | collective-permute-start | bytes 2359304 | tf_op jit(solution)/shard_map/ppermute | solution.py:1020
  144.4 53.6 %collective-permute-start.22 = (bf16[2,64,3072]{2,1,0:T(8,128)(2,1)}, bf16[2,64,3072]{2,1,0:T(8,128)(2,1)}, u32[]{:S(2)}, u32[]{:S(2)}) collective-permute-start(bf16[2,64,3072]{2,1,0:T(8,128)(2,1)} %get-tuple-element.179.refs_8_), channel_id=1, source_target_pairs={{0,16},{8,24},{16,0},{24,8},{1,17},{9,25},{17,1},{25,9},{2,18},{10... | collective-permute-start | bytes 2359304 | tf_op jit(solution)/shard_map/ppermute | solution.py:1020
  170.4 32.5 %copy-start.28 = (bf16[2,64,512]{2,1,0:T(8,128)(2,1)}, bf16[2,64,512]{2,1,0:T(8,128)(2,1)S(1)}, u32[]{:S(2)}) copy-start(bf16[2,64,512]{2,1,0:T(8,128)(2,1)S(1)} %collective-permute-done.19.refs_13_) | copy-start | bytes 393220
  194.3 5.8 %collective-permute-start.20 = (bf16[8,352,128]{2,1,0:T(8,128)(2,1)}, bf16[8,352,128]{2,1,0:T(8,128)(2,1)S(1)}, u32[]{:S(2)}, u32[]{:S(2)}) collective-permute-start(bf16[8,352,128]{2,1,0:T(8,128)(2,1)} %get-tuple-element.157), channel_id=1, source_target_pairs={{0,8},{8,0},{16,24},{24,16},{1,9},{9,1},{17,25},{25,17},{2,10},{10... | collective-permute-start | bytes 2162696 | tf_op jit(solution)/shard_map/ppermute | solution.py:1020
  201.4 17.6 %collective-permute-start.23 = (bf16[8,176,128]{2,1,0:T(8,128)(2,1)S(1)}, bf16[8,176,128]{2,1,0:T(8,128)(2,1)S(1)}, u32[]{:S(2)}, u32[]{:S(2)}) collective-permute-start(bf16[8,176,128]{2,1,0:T(8,128)(2,1)S(1)} %constant_dynamic-slice_fusion), channel_id=1, source_target_pairs={{0,16},{8,24},{16,0},{24,8},{1,17},{9,25},{17,1},{25,9},{2,18},{10... | collective-permute-start | bytes 1081352 | tf_op jit(solution)/shard_map/ppermute | solution.py:1020
  202.1 22.1 %collective-permute-start.24 = (bf16[8,2,8,1664]{3,2,1,0:T(8,128)(2,1)S(1)}, bf16[8,2,8,1664]{3,2,1,0:T(8,128)(2,1)}, u32[]{:S(2)}, u32[]{:S(2)}) collective-permute-start(bf16[8,2,8,1664]{3,2,1,0:T(8,128)(2,1)S(1)} %copy-done.1), channel_id=1, source_target_pairs={{0,8},{8,0},{16,24},{24,16},{1,9},{9,1},{17,25},{25,17},{2,10},{10... | collective-permute-start | bytes 1277960 | tf_op jit(solution)/shard_map/ppermute | solution.py:1020
  202.8 16.6 %collective-permute-start.30 = (bf16[2,64,512]{2,1,0:T(8,128)(2,1)S(1)}, bf16[2,64,512]{2,1,0:T(8,128)(2,1)S(1)}, u32[]{:S(2)}, u32[]{:S(2)}) collective-permute-start(bf16[2,64,512]{2,1,0:T(8,128)(2,1)S(1)} %copy-done.27), channel_id=1, source_target_pairs={{0,8},{8,0},{16,24},{24,16},{1,9},{9,1},{17,25},{25,17},{2,10},{10... | collective-permute-start | bytes 393224 | tf_op jit(solution)/shard_map/ppermute | solution.py:1020
  202.9 16.6 %collective-permute-start.31 = (bf16[2,64,512]{2,1,0:T(8,128)(2,1)S(1)}, bf16[2,64,512]{2,1,0:T(8,128)(2,1)S(1)}, u32[]{:S(2)}, u32[]{:S(2)}) collective-permute-start(bf16[2,64,512]{2,1,0:T(8,128)(2,1)S(1)} %collective-permute-done.19.refs_13_), channel_id=1, source_target_pairs={{0,8},{8,0},{16,24},{24,16},{1,9},{9,1},{17,25},{25,17},{2,10},{10... | collective-permute-start | bytes 393224 | tf_op jit(solution)/shard_map/ppermute | solution.py:1020
  218.9 7.4 %collective-permute-start.26 = (bf16[2,64,3072]{2,1,0:T(8,128)(2,1)}, bf16[2,64,3072]{2,1,0:T(8,128)(2,1)}, u32[]{:S(2)}, u32[]{:S(2)}) collective-permute-start(bf16[2,64,3072]{2,1,0:T(8,128)(2,1)} %get-tuple-element.177.refs_4_), channel_id=1, source_target_pairs={{0,8},{8,0},{16,24},{24,16},{1,9},{9,1},{17,25},{25,17},{2,10},{10... | collective-permute-start | bytes 2359304 | tf_op jit(solution)/shard_map/ppermute | solution.py:1020
  219.0 7.3 %collective-permute-start.27 = (bf16[2,64,3072]{2,1,0:T(8,128)(2,1)}, bf16[2,64,3072]{2,1,0:T(8,128)(2,1)}, u32[]{:S(2)}, u32[]{:S(2)}) collective-permute-start(bf16[2,64,3072]{2,1,0:T(8,128)(2,1)} %collective-permute-done.21.refs_5_), channel_id=1, source_target_pairs={{0,8},{8,0},{16,24},{24,16},{1,9},{9,1},{17,25},{25,17},{2,10},{10... | collective-permute-start | bytes 2359304 | tf_op jit(solution)/shard_map/ppermute | solution.py:1020
  219.4 6.9 %collective-permute-start.28 = (bf16[2,64,3072]{2,1,0:T(8,128)(2,1)}, bf16[2,64,3072]{2,1,0:T(8,128)(2,1)}, u32[]{:S(2)}, u32[]{:S(2)}) collective-permute-start(bf16[2,64,3072]{2,1,0:T(8,128)(2,1)} %get-tuple-element.179.refs_8_), channel_id=1, source_target_pairs={{0,8},{8,0},{16,24},{24,16},{1,9},{9,1},{17,25},{25,17},{2,10},{10... | collective-permute-start | bytes 2359304 | tf_op jit(solution)/shard_map/ppermute | solution.py:1020
  219.5 6.8 %collective-permute-start.29 = (bf16[2,64,3072]{2,1,0:T(8,128)(2,1)}, bf16[2,64,3072]{2,1,0:T(8,128)(2,1)}, u32[]{:S(2)}, u32[]{:S(2)}) collective-permute-start(bf16[2,64,3072]{2,1,0:T(8,128)(2,1)} %collective-permute-done.22.refs_9_), channel_id=1, source_target_pairs={{0,8},{8,0},{16,24},{24,16},{1,9},{9,1},{17,25},{25,17},{2,10},{10... | collective-permute-start | bytes 2359304 | tf_op jit(solution)/shard_map/ppermute | solution.py:1020
  220.8 14.6 %all-to-all-start.4 = ((bf16[8,176,128]{2,1,0:T(8,128)(2,1)}), bf16[8,176,128]{2,1,0:T(8,128)(2,1)S(1)}, u32[]{:S(2)}, u32[]{:S(2)}) async-start(bf16[8,176,128]{2,1,0:T(8,128)(2,1)} %add_convert_fusion.1), calls=%async_computation.4 | async-start | bytes 720896 | tf_op jit(solution)/shard_map/all_to_all | solution.py:1053
  224.2 16.1 %copy-start.2 = (bf16[8,197,768]{2,1,0:T(8,128)(2,1)S(1)}, bf16[8,197,768]{2,1,0:T(8,128)(2,1)}, u32[]{:S(2)}) copy-start(bf16[8,197,768]{2,1,0:T(8,128)(2,1)} %get-tuple-element.158) | copy-start | bytes 7262212
  224.3 2.0 collective-permute-start.25
  235.5 3.0 %collective-permute-start.32 = (bf16[176,128]{1,0:T(8,128)(2,1)S(1)}, bf16[176,128]{1,0:T(8,128)(2,1)S(1)}, u32[]{:S(2)}, u32[]{:S(2)}) collective-permute-start(bf16[176,128]{1,0:T(8,128)(2,1)S(1)} %reduce_sum.12), channel_id=1, source_target_pairs={{0,16},{8,24},{16,0},{24,8},{1,17},{9,25},{17,1},{25,9},{2,18},{10... | collective-permute-start | bytes 135176 | tf_op jit(solution)/shard_map/ppermute | solution.py:1020
  238.5 3.8 %collective-permute-start.33 = (bf16[352,128]{1,0:T(8,128)(2,1)S(1)}, bf16[352,128]{1,0:T(8,128)(2,1)S(1)}, u32[]{:S(2)}, u32[]{:S(2)}) collective-permute-start(bf16[352,128]{1,0:T(8,128)(2,1)S(1)} %maximum_select_fusion.1), channel_id=1, source_target_pairs={{0,8},{8,0},{16,24},{24,16},{1,9},{9,1},{17,25},{25,17},{2,10},{10... | collective-permute-start | bytes 270344 | tf_op jit(solution)/shard_map/ppermute | solution.py:1020
  (22 other events, 57.3 us)

commit v8 on v7

--- a/solution.py
+++ b/solution.py
@@ -658,10 +658,18 @@
     unit, scale = normalise(pad_rows(pad_a, image_ref))
     result = flat(gx2_ref).astype(F32) + normalise_back(unit, scale, gh1)
     for slot in range(n_img):
+        image = step * n_img + slot
+        cut = n_tok // 8 * 8
+        row = lax.broadcasted_iota(jnp.int32, (every, LANES), 0)
         for part in range(parts):
-            out_ref[pl.ds(part * every + step * n_img + slot, n_tok, stride=parts * every), :] = result[
-                slot * total : slot * total + n_tok, part * LANES : (part + 1) * LANES
-            ]
+            columns = result[slot * total : slot * total + n_tok, part * LANES : (part + 1) * LANES]
+            out_ref[pl.ds(part * every + image, cut, stride=parts * every), :] = columns[:cut]
+            for token in range(cut, n_tok):
+                start = (token * parts + part) * every
+                kept = out_ref[start : start + every, :]
+                out_ref[start : start + every, :] = jnp.where(
+                    row == image, columns[token : token + 1], kept
+                )
 
 
 ANY = pl.BlockSpec(memory_space=pl.ANY)
@@ -820,7 +828,7 @@
             pltpu.VMEM((width, 2 * LANES), BF16),
             pltpu.VMEM((each * total, width), F32),
             pltpu.VMEM((each * total, width), F32),
-            pltpu.VMEM(((2 * width // LANES + 1) * n_exp * n_img, LANES), F32),
+            pltpu.VMEM(((2 * width // LANES + 1) * n_exp * n_img + n_img, LANES), F32),
         ],
         n_img * total * 2 * width * (width + 3 * LANES), n_img * total * 2 * n_exp,
     )
@@ -940,7 +948,7 @@
         ],
         [
             pltpu.VMEM((each * total, width), F32),
-            pltpu.VMEM((2 * width // LANES * n_exp * n_img, LANES), F32),
+            pltpu.VMEM((2 * width // LANES * n_exp * n_img + n_img, LANES), F32),
             pltpu.VMEM((LANES, width), F32),
             pltpu.VMEM((LANES, width), F32),
             pltpu.VMEM((LANES, width), F32),

time: 245 us -> 246 us (level)
  transfers between devices with their start and end apart: 39 -> 39, of which waited for: 12 -> 12; matrix products, arithmetic and copies ran while one was open for 3% -> 3% of each run, Pallas kernels for 52% -> 53%
where the time goes in v8:
time: 246 us; the launch traced here: 245 us
  Pallas kernels  146 us (59%)
  starting transfers between devices  51.3 us (21%)
  waiting for transfers between devices  29.3 us (12%)
  local copies, waits for them, and re-layouts  14.3 us (6%)
  other arithmetic  2.82 us (1%)
    pallas_call x13, Pallas kernels, call(): pl.pallas_call(kernel, out_shape=shapes, grid_spec=pltpu.PrefetchScalarGr...  146 us
    ppermute x34, starting transfers between devices, swap(): return lax.ppermute(array, axis, [(i, i ^ bit) for i in range(size)])  30.9 us
    ppermute x34, waiting for transfers between devices, swap(): return lax.ppermute(array, axis, [(i, i ^ bit) for i in range(size)])  16.1 us
    unnamed x65, local copies, waits for them, and re-layouts  12.2 us
    all_to_all x2, starting transfers between devices, over_shard(): lax.all_to_all(spread, 'shard', split_axis=0, concat_axis=0, tiled=True,...  8.98 us
    all_to_all x1, waiting for transfers between devices, per_device(): back = lax.all_to_all(ret, 'shard', split_axis=0, concat_axis=0, tiled=True)  6.81 us
  transfers between devices with their start and end apart: 39, of which 12 were waited for; matrix products, arithmetic and copies ran while one was open for 3% of the time, Pallas kernels for 53%

profile of v8, /device:TPU:1, one launch (start us, length us, event | category | flops | bytes accessed | tf_op | source)
XLA Modules:
  0.0 245.5 jit_solution(17427215002097380359)
XLA Ops:
  1.3 2.8 %shard_map.274 = bf16[4,96,640]{2,1,0:T(8,128)(2,1)} custom-call(s32[3]{0:T(128)} %pad_add_fusion.place_ref, bf16[96,2304]{1,0:T(8,128)(2,1)} %qkv_ref.3, bf16[96,128]{1,0:T(8,128)(2,1)} %a_ref.1, bf16[288,128]{1,0:T(8,128)(2,1)} %bitcast.26, bf16[96,128]{1,0:T(8,128)(2,1)} %ao_ref.1, bf16[96,128]{1,0:T(8,128)(2,1)} %ra_ref.1, bf16[96,128]{1,0:T(8,128)(2,1)} %bitcast.27, ...), custom_call_target="tpu_custom_call" | custom-call | flops 221184 | bytes 1108992 | tf_op jit(solution)/shard_map/pallas_call | solution.py:700
  4.0 5.4 %all-to-all-start = ((bf16[4,96,640]{2,1,0:T(8,128)(2,1)}), bf16[4,96,640]{2,1,0:T(8,128)(2,1)S(1)}, u32[]{:S(2)}, u32[]{:S(2)}) async-start(bf16[4,96,640]{2,1,0:T(8,128)(2,1)} %shard_map.274), calls=%async_computation | async-start | bytes 983040 | tf_op jit(solution)/shard_map/all_to_all | solution.py:1036
  9.4 2.8 %shard_map.275 = bf16[8,96,640]{2,1,0:T(8,128)(2,1)} custom-call(s32[3]{0:T(128)} %pad_add_fusion.place_ref, bf16[96,2304]{1,0:T(8,128)(2,1)} %qkv_ref.3, bf16[96,768]{1,0:T(8,128)(2,1)} %wo_ref.1, bf16[2,128]{1,0:T(2,128)(2,1)} %bitcast.29), custom_call_target="tpu_custom_call" | custom-call | flops 73728 | bytes 1573376 | tf_op jit(solution)/shard_map/pallas_call | solution.py:700
  12.3 1.9 copy.31.image_ref
  14.6 1.9 copy.32._.cot_ref
  16.5 3.7 %shard_map.276.h1_ref.refs_8_ = bf16[8,208,768]{2,1,0:T(8,128)(2,1)} custom-call(bf16[8,197,768]{2,1,0:T(8,128)(2,1)} %copy.31.image_ref, bf16[8,197,768]{2,1,0:T(8,128)(2,1)} %copy.32._.cot_ref), custom_call_target="tpu_custom_call" | custom-call | flops 9682944 | bytes 7397376 | tf_op jit(solution)/shard_map/pallas_call | solution.py:700
  20.2 2.6 %all-to-all-done = bf16[4,96,640]{2,1,0:T(8,128)(2,1)S(1)} async-done(((bf16[4,96,640]{2,1,0:T(8,128)(2,1)}), bf16[4,96,640]{2,1,0:T(8,128)(2,1)S(1)}, u32[]{:S(2)}, u32[]{:S(2)}) %all-to-all-start) | async-done | bytes 491552 | tf_op jit(solution)/shard_map/all_to_all | solution.py:1036
  22.8 1.3 collective-permute-start
  24.1 1.2 collective-permute-start.1
  25.3 4.6 %collective-permute-done.rest_1_.refs_1_ = bf16[384,384]{1,0:T(8,128)(2,1)S(1)} collective-permute-done((bf16[384,384]{1,0:T(8,128)(2,1)S(1)}, bf16[384,384]{1,0:T(8,128)(2,1)S(1)}, u32[]{:S(2)}, u32[]{:S(2)}) %collective-permute-start) | collective-permute-done | bytes 294944 | tf_op jit(solution)/shard_map/ppermute | solution.py:1028
  29.9 0.9 collective-permute-done.1.rest_2_.refs_2_
  31.2 1.2 collective-permute-start.3
  32.4 3.3 %collective-permute-done.3.rest_2_.refs_10_ = bf16[384,256]{1,0:T(8,128)(2,1)S(1)} collective-permute-done((bf16[384,256]{1,0:T(8,128)(2,1)S(1)}, bf16[384,256]{1,0:T(8,128)(2,1)S(1)}, u32[]{:S(2)}, u32[]{:S(2)}) %collective-permute-start.3) | collective-permute-done | bytes 196640 | tf_op jit(solution)/shard_map/ppermute | solution.py:1028
  36.4 3.6 %all-to-all-start.1 = ((bf16[8,96,640]{2,1,0:T(8,128)(2,1)}), bf16[8,96,640]{2,1,0:T(8,128)(2,1)S(1)}, u32[]{:S(2)}, u32[]{:S(2)}) async-start(bf16[8,96,640]{2,1,0:T(8,128)(2,1)} %shard_map.275), calls=%async_computation.1 | async-start | bytes 1966080 | tf_op jit(solution)/shard_map/all_to_all | solution.py:1036
  40.0 4.0 %collective-permute-start.4 = (bf16[384,384]{1,0:T(8,128)(2,1)S(1)}, bf16[384,384]{1,0:T(8,128)(2,1)S(1)}, u32[]{:S(2)}, u32[]{:S(2)}) collective-permute-start(bf16[384,384]{1,0:T(8,128)(2,1)S(1)} %slice.30.rest_0_.refs_0_), channel_id=1, source_target_pairs={{0,8},{8,0},{16,24},{24,16},{1,9},{9,1},{17,25},{25,17},{2,10},{10... | collective-permute-start | bytes 884744 | tf_op jit(solution)/shard_map/ppermute | solution.py:1028
  44.6 1.5 collective-permute-start.8
  46.1 0.8 collective-permute-start.10
  48.7 12.5 %shard_map.277 = (bf16[8,208,768]{2,1,0:T(8,128)(2,1)}, bf16[8,208,256]{2,1,0:T(8,128)(2,1)}, bf16[8,4,208,208]{3,2,1,0:T(8,128)(2,1)}, bf16[8,208,128]{2,1,0:T(...) custom-call(s32[3]{0:T(128)} %pad_add_fusion.place_ref, ...), custom_call_target="tpu_custom_call" | custom-call | flops 2317352960 | bytes 12697600 | tf_op jit(solution)/shard_map/pallas_call | solution.py:700
  61.9 3.6 %collective-permute-start.11 = (bf16[384,256]{1,0:T(8,128)(2,1)}, bf16[384,256]{1,0:T(8,128)(2,1)S(1)}, u32[]{:S(2)}, u32[]{:S(2)}) collective-permute-start(bf16[384,256]{1,0:T(8,128)(2,1)} %copy-done.24), channel_id=1, source_target_pairs={{0,8},{8,0},{16,24},{24,16},{1,9},{9,1},{17,25},{25,17},{2,10},{10... | collective-permute-start | bytes 589832 | tf_op jit(solution)/shard_map/ppermute | solution.py:1028
  65.5 1.3 collective-permute-start.14
  67.8 10.7 %shard_map.278 = (bf16[8,208,768]{2,1,0:T(8,128)(2,1)}, bf16[8,208,256]{2,1,0:T(8,128)(2,1)}, bf16[8,4,208,208]{3,2,1,0:T(8,128)(2,1)}, bf16[768,128]{1,0:T(8,128)(2,1)}, bf16[768,128]{1,0:T(8,128)(2,1)}) custom-call(s32[3]{0:T(128)} %pad_add_fusion.place_ref, bf16[8,208,768]{2,1,0:T(8,128)(2,1)} %shard_map.276.h1_ref.refs_8_, ...), custom_call_target="tpu_custom_call" | custom-call | flops 2317352960 | bytes 11714560 | tf_op jit(solution)/shard_map/pallas_call | solution.py:700
  78.4 0.8 collective-permute-start.15
  80.9 0.8 copy-done.9
  81.7 10.3 %shard_map.279 = (bf16[8,208,768]{2,1,0:T(8,128)(2,1)}, bf16[8,208,256]{2,1,0:T(8,128)(2,1)}, bf16[8,4,208,208]{3,2,1,0:T(8,128)(2,1)}) custom-call(s32[3]{0:T(128)} %pad_add_fusion.place_ref, bf16[8,208,768]{2,1,0:T(8,128)(2,1)} %shard_map.276.h1_ref.refs_8_, bf16[8,208,128]{2,1,0:T(8,128)(2,1)} %get-tuple-element.120.uq_ref.refs_7_, ...), custom_call_target="tpu_custom_call" | custom-call | flops 2317352960 | bytes 10928128 | tf_op jit(solution)/shard_map/pallas_call | solution.py:700
  92.9 14.2 %shard_map.280 = (f32[8,208,768]{2,1,0:T(8,128)}, bf16[8,208,128]{2,1,0:T(8,128)(2,1)}, bf16[8,208,128]{2,1,0:T(8,128)(2,1)}, f32[8,16,208]{2,1,0:T(8,128)}, f32...) custom-call(s32[3]{0:T(128)} %pad_add_fusion.place_ref, ...), custom_call_target="tpu_custom_call" | custom-call | flops 2944401408 | bytes 16388096 | tf_op jit(solution)/shard_map/pallas_call | solution.py:700
  107.0 3.7 %all-to-all-start.2 = ((bf16[8,2,8,1664]{3,2,1,0:T(8,128)(2,1)}), bf16[8,2,8,1664]{3,2,1,0:T(8,128)(2,1)S(1)}, u32[]{:S(2)}, u32[]{:S(2)}) async-start(bf16[8,2,8,1664]{3,2,1,0:T(8,128)(2,1)} %get-tuple-element.140), calls=%async_computation.2 | async-start | bytes 851968 | tf_op jit(solution)/shard_map/all_to_all | solution.py:1174
  110.7 7.8 %shard_map.281 = (bf16[2432,768]{1,0:T(8,128)(2,1)}, bf16[768,896]{1,0:T(8,128)(2,1)}, bf16[128,768]{1,0:T(8,128)(2,1)}, bf16[128,768]{1,0:T(8,128)(2,1)}) custom-call(s32[3]{0:T(128)} %pad_add_fusion.place_ref, bf16[768,128]{1,0:T(8,128)(2,1)} %get-tuple-element.129.ao_ref, bf16[768,128]{1,0:T(8,128)(2,1)} %get-tuple-element.130.bo_ref, ...), custom_call_target="tpu_custom_call" | custom-call | flops 4718592 | bytes 12779520 | tf_op jit(solution)/shard_map/pallas_call | solution.py:700
  118.5 3.8 %all-to-all-done.2.part_ref.refs_0_ = bf16[8,2,8,1664]{3,2,1,0:T(8,128)(2,1)S(1)} async-done(((bf16[8,2,8,1664]{3,2,1,0:T(8,128)(2,1)}), bf16[8,2,8,1664]{3,2,1,0:T(8,128)(2,1)S(1)}, u32[]{:S(2)}, u32[]{:S(2)}) %all-to-all-start.2) | async-done | bytes 426016 | tf_op jit(solution)/shard_map/all_to_all | solution.py:1174
  122.3 0.8 collective-permute-start.18
  123.2 14.7 %shard_map.282 = (bf16[8,2,8,1536]{3,2,1,0:T(8,128)(2,1)}, bf16[2,64,3072]{2,1,0:T(8,128)(2,1)}, bf16[2,64,3072]{2,1,0:T(8,128)(2,1)}, bf16[2,64,512]{2,1,0:T(8,128)(2,1)}) custom-call(bf16[2,768,3072]{2,1,0:T(8,128)(2,1)} %wu_ref.1, bf16[2,3072,768]{2,1,0:T(8,128)(2,1)} %wd_ref.1, bf16[2,768,128]{2,1,0:T(8,128)(2,1)} %ua_ref.1, ...), custom_call_target="tpu_custom_call" | custom-call | flops 2415919104 | bytes 25329664 | tf_op jit(solution)/shard_map/pallas_call | solution.py:700
  137.9 0.8 copy-done.10
  138.7 4.3 %all-to-all-start.3 = ((bf16[8,2,8,1536]{3,2,1,0:T(8,128)(2,1)}), bf16[8,2,8,1536]{3,2,1,0:T(8,128)(2,1)S(1)}, u32[]{:S(2)}, u32[]{:S(2)}) async-start(bf16[8,2,8,1536]{3,2,1,0:T(8,128)(2,1)} %get-tuple-element.147), calls=%async_computation.3 | async-start | bytes 786432 | tf_op jit(solution)/shard_map/all_to_all | solution.py:1184
  145.2 6.8 %all-to-all-done.3.ret_ref = bf16[8,2,8,1536]{3,2,1,0:T(8,128)(2,1)S(1)} async-done(((bf16[8,2,8,1536]{3,2,1,0:T(8,128)(2,1)}), bf16[8,2,8,1536]{3,2,1,0:T(8,128)(2,1)S(1)}, u32[]{:S(2)}, u32[]{:S(2)}) %all-to-all-start.3) | async-done | bytes 393248 | tf_op jit(solution)/shard_map/all_to_all | solution.py:1184
  152.7 17.6 %shard_map.283 = (bf16[8,197,768]{2,1,0:T(8,128)(2,1)}, bf16[8,208,768]{2,1,0:T(8,128)(2,1)}, bf16[8,208,768]{2,1,0:T(8,128)(2,1)}, bf16[8,320,128]{2,1,0:T(8,128)(2,1)}) custom-call(s32[8]{0:T(128)} %index_ref.7, s32[1]{0:T(128)S(6)} %copy.38.count_ref, bf16[8,197,768]{2,1,0:T(8,128)(2,1)} %copy.32._.cot_ref, f32[8,208,768]{2,1,0:T(8,128)} %get-tuple-element.135.x2_ref, ...), custom_call_target="tpu_custom_call" | custom-call | flops 3925868544 | bytes 21532672 | tf_op jit(solution)/shard_map/pallas_call | solution.py:700
  170.4 23.9 %shard_map.284 = (bf16[8,208,768]{2,1,0:T(8,128)(2,1)}, bf16[8,208,768]{2,1,0:T(8,128)(2,1)}, bf16[8,208,768]{2,1,0:T(8,128)(2,1)}, bf16[8,208,128]{2,1,0:T(8,12...) custom-call(s32[3]{0:T(128)} %pad_add_fusion.place_ref, s32[8]{0:T(128)} %index_ref.7, ...), custom_call_target="tpu_custom_call" | custom-call | flops 3639607296 | bytes 32292864 | tf_op jit(solution)/shard_map/pallas_call | solution.py:700
  194.3 3.7 %collective-permute-start.20 = (bf16[8,352,128]{2,1,0:T(8,128)(2,1)}, bf16[8,352,128]{2,1,0:T(8,128)(2,1)S(1)}, u32[]{:S(2)}, u32[]{:S(2)}) collective-permute-start(bf16[8,352,128]{2,1,0:T(8,128)(2,1)} %get-tuple-element.157), channel_id=1, source_target_pairs={{0,8},{8,0},{16,24},{24,16},{1,9},{9,1},{17,25},{25,17},{2,10},{10... | collective-permute-start | bytes 2162696 | tf_op jit(solution)/shard_map/ppermute | solution.py:1028
  198.0 2.0 collective-permute-done.20
  200.0 1.3 add_convert_fusion
  201.4 0.8 collective-permute-start.23
  203.3 16.9 %shard_map.285 = f32[9456,128]{1,0:T(8,128)} custom-call(bf16[8,197,768]{2,1,0:T(8,128)(2,1)} %copy.31.image_ref, bf16[8,208,768]{2,1,0:T(8,128)(2,1)} %get-tuple-element.167.gx2_ref, bf16[8,208,128]{2,1,0:T(8,128)(2,1)} %get-tuple-element.168.guq_ref, bf16[2432,768]{1,0:T(8,128)(2,1)} %get-tuple-element.169.turned_ref, ...), custom_call_target="tpu_custom_call" | custom-call | flops 6215958528 | bytes 21647360 | tf_op jit(solution)/shard_map/pallas_call | solution.py:700
  221.2 0.8 add_convert_fusion.1
  222.1 3.4 %all-to-all-start.4 = ((bf16[8,176,128]{2,1,0:T(8,128)(2,1)}), bf16[8,176,128]{2,1,0:T(8,128)(2,1)S(1)}, u32[]{:S(2)}, u32[]{:S(2)}) async-start(bf16[8,176,128]{2,1,0:T(8,128)(2,1)} %add_convert_fusion.1), calls=%async_computation.4 | async-start | bytes 720896 | tf_op jit(solution)/shard_map/all_to_all | solution.py:1061
  225.9 1.7 collective-permute-done.25.refs_3_
  228.3 8.4 %shard_map.286 = (f32[2,768,128]{2,1,0:T(8,128)}, f32[2,128,3072]{2,1,0:T(8,128)}, f32[2,3072,128]{2,1,0:T(8,128)}, f32[2,128,768]{2,1,0:T(8,128)}) custom-call(bf16[8,2,8,1664]{3,2,1,0:T(8,128)(2,1)} %copy-done, bf16[8,2,8,1664]{3,2,1,0:T(8,128)(2,1)} %copy-done.10, bf16[8,2,8,1664]{3,2,1,0:T(8,128)(2,1)} %collective-permute-done.24.refs_2_, ...), custom_call_target="tpu_custom_call" | custom-call | flops 805306368 | bytes 16384000 | tf_op jit(solution)/shard_map/pallas_call | solution.py:700
  236.8 0.8 collective-permute-start.32
  237.6 2.1 collective-permute-done.32
  239.7 1.9 collective-permute-start.33
  241.6 1.9 copy.37
  (122 shorter events, 16.3 us)
Async XLA Ops:
  4.0 18.7 %all-to-all-start = ((bf16[4,96,640]{2,1,0:T(8,128)(2,1)}), bf16[4,96,640]{2,1,0:T(8,128)(2,1)S(1)}, u32[]{:S(2)}, u32[]{:S(2)}) async-start(bf16[4,96,640]{2,1,0:T(8,128)(2,1)} %shard_map.274), calls=%async_computation | async-start | bytes 983040 | tf_op jit(solution)/shard_map/all_to_all | solution.py:1036
  22.8 25.1 %copy-start.7 = (bf16[384,384]{1,0:T(8,128)(2,1)}, bf16[384,384]{1,0:T(8,128)(2,1)S(1)}, u32[]{:S(2)}) copy-start(bf16[384,384]{1,0:T(8,128)(2,1)S(1)} %slice.30.rest_0_.refs_0_) | copy-start | bytes 884740
  22.8 7.1 %collective-permute-start = (bf16[384,384]{1,0:T(8,128)(2,1)S(1)}, bf16[384,384]{1,0:T(8,128)(2,1)S(1)}, u32[]{:S(2)}, u32[]{:S(2)}) collective-permute-start(bf16[384,384]{1,0:T(8,128)(2,1)S(1)} %slice.30.rest_0_.refs_0_), channel_id=1, source_target_pairs={{0,1},{1,0},{2,3},{3,2},{4,5},{5,4},{6,7},{7,6},{8,9},{9,8},{10,11... | collective-permute-start | bytes 884744 | tf_op jit(solution)/shard_map/ppermute | solution.py:1028
  24.1 6.8 %collective-permute-start.1 = (bf16[384,384]{1,0:T(8,128)(2,1)S(1)}, bf16[384,384]{1,0:T(8,128)(2,1)S(1)}, u32[]{:S(2)}, u32[]{:S(2)}) collective-permute-start(bf16[384,384]{1,0:T(8,128)(2,1)S(1)} %slice.30.rest_0_.refs_0_), channel_id=1, source_target_pairs={{0,16},{8,24},{16,0},{24,8},{1,17},{9,25},{17,1},{25,9},{2,18},{10... | collective-permute-start | bytes 884744 | tf_op jit(solution)/shard_map/ppermute | solution.py:1028
  25.3 35.8 %copy-start.8 = (bf16[384,256]{1,0:T(8,128)(2,1)}, bf16[384,256]{1,0:T(8,128)(2,1)S(1)}, u32[]{:S(2)}) copy-start(bf16[384,256]{1,0:T(8,128)(2,1)S(1)} %slice.31.rest_0_.refs_8_) | copy-start | bytes 589828
  29.9 18.0 %copy-start.16 = (bf16[384,384]{1,0:T(8,128)(2,1)}, bf16[384,384]{1,0:T(8,128)(2,1)S(1)}, u32[]{:S(2)}) copy-start(bf16[384,384]{1,0:T(8,128)(2,1)S(1)} %collective-permute-done.rest_1_.refs_1_) | copy-start | bytes 884740
  30.8 17.1 %copy-start.17 = (bf16[384,384]{1,0:T(8,128)(2,1)}, bf16[384,384]{1,0:T(8,128)(2,1)S(1)}, u32[]{:S(2)}) copy-start(bf16[384,384]{1,0:T(8,128)(2,1)S(1)} %collective-permute-done.1.rest_2_.refs_2_) | copy-start | bytes 884740
  30.8 5.6 %collective-permute-start.2 = (bf16[384,384]{1,0:T(8,128)(2,1)S(1)}, bf16[384,384]{1,0:T(8,128)(2,1)S(1)}, u32[]{:S(2)}, u32[]{:S(2)}) collective-permute-start(bf16[384,384]{1,0:T(8,128)(2,1)S(1)} %collective-permute-done.1.rest_2_.refs_2_), channel_id=1, source_target_pairs={{0,1},{1,0},{2,3},{3,2},{4,5},{5,4},{6,7},{7,6},{8,9},{9,8},{10,11... | collective-permute-start | bytes 884744 | tf_op jit(solution)/shard_map/ppermute | solution.py:1028
  31.2 4.5 %collective-permute-start.3 = (bf16[384,256]{1,0:T(8,128)(2,1)S(1)}, bf16[384,256]{1,0:T(8,128)(2,1)S(1)}, u32[]{:S(2)}, u32[]{:S(2)}) collective-permute-start(bf16[384,256]{1,0:T(8,128)(2,1)S(1)} %slice.31.rest_0_.refs_8_), channel_id=1, source_target_pairs={{0,16},{8,24},{16,0},{24,8},{1,17},{9,25},{17,1},{25,9},{2,18},{10... | collective-permute-start | bytes 589832 | tf_op jit(solution)/shard_map/ppermute | solution.py:1028
  36.4 25.4 %all-to-all-start.1 = ((bf16[8,96,640]{2,1,0:T(8,128)(2,1)}), bf16[8,96,640]{2,1,0:T(8,128)(2,1)S(1)}, u32[]{:S(2)}, u32[]{:S(2)}) async-start(bf16[8,96,640]{2,1,0:T(8,128)(2,1)} %shard_map.275), calls=%async_computation.1 | async-start | bytes 1966080 | tf_op jit(solution)/shard_map/all_to_all | solution.py:1036
  40.0 6.1 %collective-permute-start.4 = (bf16[384,384]{1,0:T(8,128)(2,1)S(1)}, bf16[384,384]{1,0:T(8,128)(2,1)S(1)}, u32[]{:S(2)}, u32[]{:S(2)}) collective-permute-start(bf16[384,384]{1,0:T(8,128)(2,1)S(1)} %slice.30.rest_0_.refs_0_), channel_id=1, source_target_pairs={{0,8},{8,0},{16,24},{24,16},{1,9},{9,1},{17,25},{25,17},{2,10},{10... | collective-permute-start | bytes 884744 | tf_op jit(solution)/shard_map/ppermute | solution.py:1028
  44.0 2.9 %collective-permute-start.5 = (bf16[384,384]{1,0:T(8,128)(2,1)S(1)}, bf16[384,384]{1,0:T(8,128)(2,1)S(1)}, u32[]{:S(2)}, u32[]{:S(2)}) collective-permute-start(bf16[384,384]{1,0:T(8,128)(2,1)S(1)} %collective-permute-done.rest_1_.refs_1_), channel_id=1, source_target_pairs={{0,8},{8,0},{16,24},{24,16},{1,9},{9,1},{17,25},{25,17},{2,10},{10... | collective-permute-start | bytes 884744 | tf_op jit(solution)/shard_map/ppermute | solution.py:1028
  44.1 3.1 %collective-permute-start.6 = (bf16[384,384]{1,0:T(8,128)(2,1)S(1)}, bf16[384,384]{1,0:T(8,128)(2,1)S(1)}, u32[]{:S(2)}, u32[]{:S(2)}) collective-permute-start(bf16[384,384]{1,0:T(8,128)(2,1)S(1)} %collective-permute-done.1.rest_2_.refs_2_), channel_id=1, source_target_pairs={{0,8},{8,0},{16,24},{24,16},{1,9},{9,1},{17,25},{25,17},{2,10},{10... | collective-permute-start | bytes 884744 | tf_op jit(solution)/shard_map/ppermute | solution.py:1028
  44.5 3.4 %collective-permute-start.7 = (bf16[384,384]{1,0:T(8,128)(2,1)S(1)}, bf16[384,384]{1,0:T(8,128)(2,1)S(1)}, u32[]{:S(2)}, u32[]{:S(2)}) collective-permute-start(bf16[384,384]{1,0:T(8,128)(2,1)S(1)} %collective-permute-done.2.rest_3_.refs_3_), channel_id=1, source_target_pairs={{0,8},{8,0},{16,24},{24,16},{1,9},{9,1},{17,25},{25,17},{2,10},{10... | collective-permute-start | bytes 884744 | tf_op jit(solution)/shard_map/ppermute | solution.py:1028
  44.6 16.5 %collective-permute-start.8 = (bf16[384,256]{1,0:T(8,128)(2,1)S(1)}, bf16[384,256]{1,0:T(8,128)(2,1)S(1)}, u32[]{:S(2)}, u32[]{:S(2)}) collective-permute-start(bf16[384,256]{1,0:T(8,128)(2,1)S(1)} %slice.31.rest_0_.refs_8_), channel_id=1, source_target_pairs={{0,1},{1,0},{2,3},{3,2},{4,5},{5,4},{6,7},{7,6},{8,9},{9,8},{10,11... | collective-permute-start | bytes 589832 | tf_op jit(solution)/shard_map/ppermute | solution.py:1028
  46.1 20.7 %collective-permute-start.10 = (bf16[384,256]{1,0:T(8,128)(2,1)S(1)}, bf16[384,256]{1,0:T(8,128)(2,1)}, u32[]{:S(2)}, u32[]{:S(2)}) collective-permute-start(bf16[384,256]{1,0:T(8,128)(2,1)S(1)} %slice.31.rest_0_.refs_8_), channel_id=1, source_target_pairs={{0,8},{8,0},{16,24},{24,16},{1,9},{9,1},{17,25},{25,17},{2,10},{10... | collective-permute-start | bytes 589832 | tf_op jit(solution)/shard_map/ppermute | solution.py:1028
  46.9 14.9 %collective-permute-start.9 = (bf16[384,256]{1,0:T(8,128)(2,1)}, bf16[384,256]{1,0:T(8,128)(2,1)}, u32[]{:S(2)}, u32[]{:S(2)}) collective-permute-start(bf16[384,256]{1,0:T(8,128)(2,1)} %copy-done.23), channel_id=1, source_target_pairs={{0,1},{1,0},{2,3},{3,2},{4,5},{5,4},{6,7},{7,6},{8,9},{9,8},{10,11... | collective-permute-start | bytes 589832 | tf_op jit(solution)/shard_map/ppermute | solution.py:1028
  47.2 19.6 %collective-permute-start.12 = (bf16[384,256]{1,0:T(8,128)(2,1)}, bf16[384,256]{1,0:T(8,128)(2,1)}, u32[]{:S(2)}, u32[]{:S(2)}) collective-permute-start(bf16[384,256]{1,0:T(8,128)(2,1)} %copy-done.23), channel_id=1, source_target_pairs={{0,8},{8,0},{16,24},{24,16},{1,9},{9,1},{17,25},{25,17},{2,10},{10... | collective-permute-start | bytes 589832 | tf_op jit(solution)/shard_map/ppermute | solution.py:1028
  61.9 5.0 %collective-permute-start.11 = (bf16[384,256]{1,0:T(8,128)(2,1)}, bf16[384,256]{1,0:T(8,128)(2,1)S(1)}, u32[]{:S(2)}, u32[]{:S(2)}) collective-permute-start(bf16[384,256]{1,0:T(8,128)(2,1)} %copy-done.24), channel_id=1, source_target_pairs={{0,8},{8,0},{16,24},{24,16},{1,9},{9,1},{17,25},{25,17},{2,10},{10... | collective-permute-start | bytes 589832 | tf_op jit(solution)/shard_map/ppermute | solution.py:1028
  65.4 1.7 collective-permute-start.13
  65.4 13.8 %copy-start.6 = (bf16[768,256]{1,0:T(8,128)(2,1)}, bf16[768,256]{1,0:T(8,128)(2,1)S(1)}, u32[]{:S(2)}) copy-start(bf16[768,256]{1,0:T(8,128)(2,1)S(1)} %slice.33.rest_0_.refs_18_) | copy-start | bytes 1179652
  65.5 13.0 %collective-permute-start.14 = (bf16[768,256]{1,0:T(8,128)(2,1)S(1)}, bf16[768,256]{1,0:T(8,128)(2,1)S(1)}, u32[]{:S(2)}, u32[]{:S(2)}) collective-permute-start(bf16[768,256]{1,0:T(8,128)(2,1)S(1)} %slice.33.rest_0_.refs_18_), channel_id=1, source_target_pairs={{0,16},{8,24},{16,0},{24,8},{1,17},{9,25},{17,1},{25,9},{2,18},{10... | collective-permute-start | bytes 1179656 | tf_op jit(solution)/shard_map/ppermute | solution.py:1028
  66.8 11.6 %copy-start.5 = (bf16[768,384]{1,0:T(8,128)(2,1)}, bf16[768,384]{1,0:T(8,128)(2,1)S(1)}, u32[]{:S(2)}) copy-start(bf16[768,384]{1,0:T(8,128)(2,1)S(1)} %slice.32.rest_0_.refs_16_) | copy-start | bytes 1769476
  78.4 13.6 %copy-start.12 = (bf16[768,256]{1,0:T(8,128)(2,1)}, bf16[768,256]{1,0:T(8,128)(2,1)S(1)}, u32[]{:S(2)}) copy-start(bf16[768,256]{1,0:T(8,128)(2,1)S(1)} %collective-permute-done.14.rest_1_.refs_19_) | copy-start | bytes 1179652
  78.4 2.4 collective-permute-start.15
  79.2 12.7 %collective-permute-start.16 = (bf16[768,256]{1,0:T(8,128)(2,1)S(1)}, bf16[768,256]{1,0:T(8,128)(2,1)S(1)}, u32[]{:S(2)}, u32[]{:S(2)}) collective-permute-start(bf16[768,256]{1,0:T(8,128)(2,1)S(1)} %slice.33.rest_0_.refs_18_), channel_id=1, source_target_pairs={{0,8},{8,0},{16,24},{24,16},{1,9},{9,1},{17,25},{25,17},{2,10},{10... | collective-permute-start | bytes 1179656 | tf_op jit(solution)/shard_map/ppermute | solution.py:1028
  79.3 12.6 %collective-permute-start.17 = (bf16[768,256]{1,0:T(8,128)(2,1)S(1)}, bf16[768,256]{1,0:T(8,128)(2,1)S(1)}, u32[]{:S(2)}, u32[]{:S(2)}) collective-permute-start(bf16[768,256]{1,0:T(8,128)(2,1)S(1)} %collective-permute-done.14.rest_1_.refs_19_), channel_id=1, source_target_pairs={{0,8},{8,0},{16,24},{24,16},{1,9},{9,1},{17,25},{25,17},{2,10},{10... | collective-permute-start | bytes 1179656 | tf_op jit(solution)/shard_map/ppermute | solution.py:1028
  107.0 15.3 %all-to-all-start.2 = ((bf16[8,2,8,1664]{3,2,1,0:T(8,128)(2,1)}), bf16[8,2,8,1664]{3,2,1,0:T(8,128)(2,1)S(1)}, u32[]{:S(2)}, u32[]{:S(2)}) async-start(bf16[8,2,8,1664]{3,2,1,0:T(8,128)(2,1)} %get-tuple-element.140), calls=%async_computation.2 | async-start | bytes 851968 | tf_op jit(solution)/shard_map/all_to_all | solution.py:1174
  122.3 15.5 %collective-permute-start.18 = (bf16[8,2,8,1664]{3,2,1,0:T(8,128)(2,1)S(1)}, bf16[8,2,8,1664]{3,2,1,0:T(8,128)(2,1)S(1)}, u32[]{:S(2)}, u32[]{:S(2)}) collective-permute-start(bf16[8,2,8,1664]{3,2,1,0:T(8,128)(2,1)S(1)} %all-to-all-done.2.part_ref.refs_0_), channel_id=1, source_target_pairs={{0,16},{8,24},{16,0},{24,8},{1,17},{9,25},{17,1},{25,9},{2,18},{10... | collective-permute-start | bytes 1277960 | tf_op jit(solution)/shard_map/ppermute | solution.py:1028
  138.7 13.3 %all-to-all-start.3 = ((bf16[8,2,8,1536]{3,2,1,0:T(8,128)(2,1)}), bf16[8,2,8,1536]{3,2,1,0:T(8,128)(2,1)S(1)}, u32[]{:S(2)}, u32[]{:S(2)}) async-start(bf16[8,2,8,1536]{3,2,1,0:T(8,128)(2,1)} %get-tuple-element.147), calls=%async_computation.3 | async-start | bytes 786432 | tf_op jit(solution)/shard_map/all_to_all | solution.py:1184
  143.0 27.4 %collective-permute-start.19 = (bf16[2,64,512]{2,1,0:T(8,128)(2,1)}, bf16[2,64,512]{2,1,0:T(8,128)(2,1)S(1)}, u32[]{:S(2)}, u32[]{:S(2)}) collective-permute-start(bf16[2,64,512]{2,1,0:T(8,128)(2,1)} %get-tuple-element.181.refs_12_), channel_id=1, source_target_pairs={{0,16},{8,24},{16,0},{24,8},{1,17},{9,25},{17,1},{25,9},{2,18},{10... | collective-permute-start | bytes 393224 | tf_op jit(solution)/shard_map/ppermute | solution.py:1028
  143.7 54.3 %collective-permute-start.21 = (bf16[2,64,3072]{2,1,0:T(8,128)(2,1)}, bf16[2,64,3072]{2,1,0:T(8,128)(2,1)}, u32[]{:S(2)}, u32[]{:S(2)}) collective-permute-start(bf16[2,64,3072]{2,1,0:T(8,128)(2,1)} %get-tuple-element.177.refs_4_), channel_id=1, source_target_pairs={{0,16},{8,24},{16,0},{24,8},{1,17},{9,25},{17,1},{25,9},{2,18},{10... | collective-permute-start | bytes 2359304 | tf_op jit(solution)/shard_map/ppermute | solution.py:1028
  144.4 53.6 %collective-permute-start.22 = (bf16[2,64,3072]{2,1,0:T(8,128)(2,1)}, bf16[2,64,3072]{2,1,0:T(8,128)(2,1)}, u32[]{:S(2)}, u32[]{:S(2)}) collective-permute-start(bf16[2,64,3072]{2,1,0:T(8,128)(2,1)} %get-tuple-element.179.refs_8_), channel_id=1, source_target_pairs={{0,16},{8,24},{16,0},{24,8},{1,17},{9,25},{17,1},{25,9},{2,18},{10... | collective-permute-start | bytes 2359304 | tf_op jit(solution)/shard_map/ppermute | solution.py:1028
  170.3 32.5 %copy-start.28 = (bf16[2,64,512]{2,1,0:T(8,128)(2,1)}, bf16[2,64,512]{2,1,0:T(8,128)(2,1)S(1)}, u32[]{:S(2)}) copy-start(bf16[2,64,512]{2,1,0:T(8,128)(2,1)S(1)} %collective-permute-done.19.refs_13_) | copy-start | bytes 393220
  194.3 5.8 %collective-permute-start.20 = (bf16[8,352,128]{2,1,0:T(8,128)(2,1)}, bf16[8,352,128]{2,1,0:T(8,128)(2,1)S(1)}, u32[]{:S(2)}, u32[]{:S(2)}) collective-permute-start(bf16[8,352,128]{2,1,0:T(8,128)(2,1)} %get-tuple-element.157), channel_id=1, source_target_pairs={{0,8},{8,0},{16,24},{24,16},{1,9},{9,1},{17,25},{25,17},{2,10},{10... | collective-permute-start | bytes 2162696 | tf_op jit(solution)/shard_map/ppermute | solution.py:1028
  201.4 18.9 %collective-permute-start.23 = (bf16[8,176,128]{2,1,0:T(8,128)(2,1)S(1)}, bf16[8,176,128]{2,1,0:T(8,128)(2,1)S(1)}, u32[]{:S(2)}, u32[]{:S(2)}) collective-permute-start(bf16[8,176,128]{2,1,0:T(8,128)(2,1)S(1)} %constant_dynamic-slice_fusion), channel_id=1, source_target_pairs={{0,16},{8,24},{16,0},{24,8},{1,17},{9,25},{17,1},{25,9},{2,18},{10... | collective-permute-start | bytes 1081352 | tf_op jit(solution)/shard_map/ppermute | solution.py:1028
  202.1 23.4 %collective-permute-start.24 = (bf16[8,2,8,1664]{3,2,1,0:T(8,128)(2,1)S(1)}, bf16[8,2,8,1664]{3,2,1,0:T(8,128)(2,1)}, u32[]{:S(2)}, u32[]{:S(2)}) collective-permute-start(bf16[8,2,8,1664]{3,2,1,0:T(8,128)(2,1)S(1)} %copy-done.1), channel_id=1, source_target_pairs={{0,8},{8,0},{16,24},{24,16},{1,9},{9,1},{17,25},{25,17},{2,10},{10... | collective-permute-start | bytes 1277960 | tf_op jit(solution)/shard_map/ppermute | solution.py:1028
  202.8 17.9 %collective-permute-start.30 = (bf16[2,64,512]{2,1,0:T(8,128)(2,1)S(1)}, bf16[2,64,512]{2,1,0:T(8,128)(2,1)S(1)}, u32[]{:S(2)}, u32[]{:S(2)}) collective-permute-start(bf16[2,64,512]{2,1,0:T(8,128)(2,1)S(1)} %copy-done.27), channel_id=1, source_target_pairs={{0,8},{8,0},{16,24},{24,16},{1,9},{9,1},{17,25},{25,17},{2,10},{10... | collective-permute-start | bytes 393224 | tf_op jit(solution)/shard_map/ppermute | solution.py:1028
  202.9 17.9 %collective-permute-start.31 = (bf16[2,64,512]{2,1,0:T(8,128)(2,1)S(1)}, bf16[2,64,512]{2,1,0:T(8,128)(2,1)S(1)}, u32[]{:S(2)}, u32[]{:S(2)}) collective-permute-start(bf16[2,64,512]{2,1,0:T(8,128)(2,1)S(1)} %collective-permute-done.19.refs_13_), channel_id=1, source_target_pairs={{0,8},{8,0},{16,24},{24,16},{1,9},{9,1},{17,25},{25,17},{2,10},{10... | collective-permute-start | bytes 393224 | tf_op jit(solution)/shard_map/ppermute | solution.py:1028
  220.2 7.4 %collective-permute-start.26 = (bf16[2,64,3072]{2,1,0:T(8,128)(2,1)}, bf16[2,64,3072]{2,1,0:T(8,128)(2,1)}, u32[]{:S(2)}, u32[]{:S(2)}) collective-permute-start(bf16[2,64,3072]{2,1,0:T(8,128)(2,1)} %get-tuple-element.177.refs_4_), channel_id=1, source_target_pairs={{0,8},{8,0},{16,24},{24,16},{1,9},{9,1},{17,25},{25,17},{2,10},{10... | collective-permute-start | bytes 2359304 | tf_op jit(solution)/shard_map/ppermute | solution.py:1028
  220.3 7.3 %collective-permute-start.27 = (bf16[2,64,3072]{2,1,0:T(8,128)(2,1)}, bf16[2,64,3072]{2,1,0:T(8,128)(2,1)}, u32[]{:S(2)}, u32[]{:S(2)}) collective-permute-start(bf16[2,64,3072]{2,1,0:T(8,128)(2,1)} %collective-permute-done.21.refs_5_), channel_id=1, source_target_pairs={{0,8},{8,0},{16,24},{24,16},{1,9},{9,1},{17,25},{25,17},{2,10},{10... | collective-permute-start | bytes 2359304 | tf_op jit(solution)/shard_map/ppermute | solution.py:1028
  220.7 6.9 %collective-permute-start.28 = (bf16[2,64,3072]{2,1,0:T(8,128)(2,1)}, bf16[2,64,3072]{2,1,0:T(8,128)(2,1)}, u32[]{:S(2)}, u32[]{:S(2)}) collective-permute-start(bf16[2,64,3072]{2,1,0:T(8,128)(2,1)} %get-tuple-element.179.refs_8_), channel_id=1, source_target_pairs={{0,8},{8,0},{16,24},{24,16},{1,9},{9,1},{17,25},{25,17},{2,10},{10... | collective-permute-start | bytes 2359304 | tf_op jit(solution)/shard_map/ppermute | solution.py:1028
  220.8 6.8 %collective-permute-start.29 = (bf16[2,64,3072]{2,1,0:T(8,128)(2,1)}, bf16[2,64,3072]{2,1,0:T(8,128)(2,1)}, u32[]{:S(2)}, u32[]{:S(2)}) collective-permute-start(bf16[2,64,3072]{2,1,0:T(8,128)(2,1)} %collective-permute-done.22.refs_9_), channel_id=1, source_target_pairs={{0,8},{8,0},{16,24},{24,16},{1,9},{9,1},{17,25},{25,17},{2,10},{10... | collective-permute-start | bytes 2359304 | tf_op jit(solution)/shard_map/ppermute | solution.py:1028
  222.1 14.6 %all-to-all-start.4 = ((bf16[8,176,128]{2,1,0:T(8,128)(2,1)}), bf16[8,176,128]{2,1,0:T(8,128)(2,1)S(1)}, u32[]{:S(2)}, u32[]{:S(2)}) async-start(bf16[8,176,128]{2,1,0:T(8,128)(2,1)} %add_convert_fusion.1), calls=%async_computation.4 | async-start | bytes 720896 | tf_op jit(solution)/shard_map/all_to_all | solution.py:1061
  225.5 16.1 %copy-start.2 = (bf16[8,197,768]{2,1,0:T(8,128)(2,1)S(1)}, bf16[8,197,768]{2,1,0:T(8,128)(2,1)}, u32[]{:S(2)}) copy-start(bf16[8,197,768]{2,1,0:T(8,128)(2,1)} %get-tuple-element.158) | copy-start | bytes 7262212
  225.5 2.0 collective-permute-start.25
  236.8 3.0 %collective-permute-start.32 = (bf16[176,128]{1,0:T(8,128)(2,1)S(1)}, bf16[176,128]{1,0:T(8,128)(2,1)S(1)}, u32[]{:S(2)}, u32[]{:S(2)}) collective-permute-start(bf16[176,128]{1,0:T(8,128)(2,1)S(1)} %reduce_sum.12), channel_id=1, source_target_pairs={{0,16},{8,24},{16,0},{24,8},{1,17},{9,25},{17,1},{25,9},{2,18},{10... | collective-permute-start | bytes 135176 | tf_op jit(solution)/shard_map/ppermute | solution.py:1028
  239.7 3.8 %collective-permute-start.33 = (bf16[352,128]{1,0:T(8,128)(2,1)S(1)}, bf16[352,128]{1,0:T(8,128)(2,1)S(1)}, u32[]{:S(2)}, u32[]{:S(2)}) collective-permute-start(bf16[352,128]{1,0:T(8,128)(2,1)S(1)} %maximum_select_fusion.1), channel_id=1, source_target_pairs={{0,8},{8,0},{16,24},{24,16},{1,9},{9,1},{17,25},{25,17},{2,10},{10... | collective-permute-start | bytes 270344 | tf_op jit(solution)/shard_map/ppermute | solution.py:1028
  (22 other events, 57.2 us)
